TPU v7x, 32 devices: a whole 2x2x4 slice. The times are simulated.
32 devices in a mesh: dp: 8 (over z, y), fsdp: 4 (over x, core).
Axes of the slice: x: 2, y: 2, z: 4, core: 2. Of those that a mesh axis runs over, the one named last changes fastest.
Arguments:
- tokens: bfloat16 [32768, 768], P(('dp', 'fsdp')), may hold values from -6 to 6
- lengths: int32 [32, 5], P(('dp', 'fsdp')), may hold values from 0 to 768, as said below
- ln1_gain: bfloat16 [768], P(('dp', 'fsdp')), may hold values from 0.099609375 to 1.8984375
- ln1_bias: bfloat16 [768], P(('dp', 'fsdp')), may hold values from -4 to 4
- w_qkv: bfloat16 [768, 2304], P(('dp', 'fsdp')), may hold values from -0.21875 to 0.21875
- qv_bias: bfloat16 [1536], P(('dp', 'fsdp')), may hold values from -4 to 4
- w_proj: bfloat16 [768, 768], P(('dp', 'fsdp')), may hold values from -6 to 6
- proj_bias: bfloat16 [768], P(('dp', 'fsdp')), may hold values from -6 to 6
- ln2_gain: bfloat16 [768], P(('dp', 'fsdp')), may hold values from 0.099609375 to 1.8984375
- ln2_bias: bfloat16 [768], P(('dp', 'fsdp')), may hold values from -4 to 4
- w_fc: bfloat16 [768, 3072], P(('dp', 'fsdp')), may hold values from -0.21875 to 0.21875
- fc_bias: bfloat16 [3072], P(('dp', 'fsdp')), may hold values from -6 to 6
- w_out: bfloat16 [3072, 768], P(('dp', 'fsdp')), may hold values from -3 to 3
- out_bias: bfloat16 [768], P(('dp', 'fsdp')), may hold values from -6 to 6
- cotangent: bfloat16 [32768, 768], P(('dp', 'fsdp')), may hold values from -6 to 6
Outputs:
- block_out: bfloat16 [32768, 768], P(('dp', 'fsdp'))
- grad_tokens: bfloat16 [32768, 768], P(('dp', 'fsdp'))
- grad_ln1_gain: float32 [768], P(('dp', 'fsdp'))
- grad_ln1_bias: float32 [768], P(('dp', 'fsdp'))
- grad_w_qkv: float32 [768, 2304], P(('dp', 'fsdp'))
- grad_qv_bias: float32 [1536], P(('dp', 'fsdp'))
- grad_w_proj: float32 [768, 768], P(('dp', 'fsdp'))
- grad_proj_bias: float32 [768], P(('dp', 'fsdp'))
- grad_ln2_gain: float32 [768], P(('dp', 'fsdp'))
- grad_ln2_bias: float32 [768], P(('dp', 'fsdp'))
- grad_w_fc: float32 [768, 3072], P(('dp', 'fsdp'))
- grad_fc_bias: float32 [3072], P(('dp', 'fsdp'))
- grad_w_out: float32 [3072, 768], P(('dp', 'fsdp'))
- grad_out_bias: float32 [768], P(('dp', 'fsdp'))
Inputs may be any that keep to these rules, and one draw needn't show every extreme that they name: Row r lists, in order, the lengths of the 4 sequences of pack r, each 64 or more, and, last, the number of pad rows after them, below 64; each row sums to 1024, and in every row one sequence has exactly 768 rows.
All inputs are finite; a program needn't handle non-finite values.
Results may differ from a plain program's by a relative error of at most 0.012.
Values may be sent and summed in bfloat16 or wider, within the bound.
No kernel may reach another device: no remote copies, remote signals or barrier semaphores. Data moves between devices by JAX's collectives and lax.ppermute only.
A program may use at most 256 MiB of HBM per device.

v0:
```python
import math

import jax
import jax.numpy as jnp
from jax import lax
from jax.sharding import PartitionSpec as P

HD = 64


epsilon = 1e-05
branch_scale = 1.0 / math.sqrt(48.0)
masked_score = -1e30


def layer_norm(values, gain, bias):
    centred = values - jnp.mean(values, axis=-1, keepdims=True)
    variance = jnp.mean(centred * centred, axis=-1, keepdims=True)
    return centred * lax.rsqrt(variance + epsilon) * gain + bias


def pack_layout(counts, row_count):
    seq_ends = jnp.cumsum(counts)
    position = jnp.arange(row_count, dtype=jnp.int32)
    segment = jnp.sum((position[:, None] >= seq_ends[None, :]).astype(jnp.int32), axis=1)
    row_valid = segment < counts.shape[0] - 1
    return (position, segment, row_valid)


def permitted(position, segment, row_valid, first_row, block_rows):
    query_pos = lax.dynamic_slice_in_dim(position, first_row, block_rows)
    query_seg = lax.dynamic_slice_in_dim(segment, first_row, block_rows)
    same_seq = (
        (query_seg[:, None] == segment[None, :])
        & (query_pos[:, None] >= position[None, :])
        & row_valid[None, :]
    )
    return same_seq | (query_pos[:, None] == position[None, :])


def contract_rows(left_side, right_side):
    return lax.dot_general(
        left_side, right_side, (((0,), (0,)), ((), ())), preferred_element_type=jnp.float32
    )


def contract_last(left_side, right_side):
    return lax.dot_general(
        left_side, right_side, (((1,), (1,)), ((), ())), preferred_element_type=jnp.float32
    )


def gelu_tanh(values):
    return jax.nn.gelu(values, approximate=True)


def per_device(
    tokens,
    lengths,
    ln1_gain,
    ln1_bias,
    w_qkv,
    qv_bias,
    w_proj,
    proj_bias,
    ln2_gain,
    ln2_bias,
    w_fc,
    fc_bias,
    w_out,
    out_bias,
    cotangent,
):
    row_count, model_width = tokens.shape
    head_count = model_width // HD
    score_scale = HD ** (-0.5)
    block_rows = min(512, row_count)
    starts = jnp.arange(row_count // block_rows, dtype=jnp.int32) * block_rows
    position, segment, row_valid = pack_layout(lengths[0], row_count)
    gain_one, bias_one, qkv_full, qv_full, proj_full, proj_bias_full = (
        lax.all_gather(ln1_gain, ("dp", "fsdp"), axis=0, tiled=True),
        lax.all_gather(ln1_bias, ("dp", "fsdp"), axis=0, tiled=True),
        lax.all_gather(w_qkv, ("dp", "fsdp"), axis=0, tiled=True),
        lax.all_gather(qv_bias, ("dp", "fsdp"), axis=0, tiled=True),
        lax.all_gather(w_proj, ("dp", "fsdp"), axis=0, tiled=True),
        lax.all_gather(proj_bias, ("dp", "fsdp"), axis=0, tiled=True),
    )
    inputs = tokens.astype(jnp.float32)
    normed = layer_norm(inputs, gain_one.astype(jnp.float32), bias_one.astype(jnp.float32)).astype(
        jnp.bfloat16
    )
    qkv_bias = jnp.concatenate(
        [qv_full[:model_width], jnp.zeros((model_width,), jnp.bfloat16), qv_full[model_width:]]
    ).astype(jnp.float32)
    joined = (jnp.dot(normed, qkv_full, preferred_element_type=jnp.float32) + qkv_bias).astype(
        jnp.bfloat16
    )
    queries = joined[:, :model_width].reshape(row_count, head_count, HD)
    key_heads = joined[:, model_width : 2 * model_width].reshape(row_count, head_count, HD)
    value_heads = joined[:, 2 * model_width :].reshape(row_count, head_count, HD)

    def attend(first_row):
        query_block = lax.dynamic_slice_in_dim(queries, first_row, block_rows)
        allowed = permitted(position, segment, row_valid, first_row, block_rows)
        scores = (
            jnp.einsum("qhd,khd->hqk", query_block, key_heads, preferred_element_type=jnp.float32)
            * score_scale
        )
        scores = jnp.where(allowed[None], scores, masked_score)
        row_max = jnp.max(scores, axis=-1, keepdims=True)
        exponent = jnp.exp(scores - row_max)
        row_total = jnp.sum(exponent, axis=-1, keepdims=True)
        prob_low = (exponent / row_total).astype(jnp.bfloat16)
        mixed_heads = jnp.einsum(
            "hqk,khd->qhd", prob_low, value_heads, preferred_element_type=jnp.float32
        )
        return (mixed_heads.astype(jnp.bfloat16), row_max[..., 0] + jnp.log(row_total[..., 0]))

    mixed_blocks, log_totals = lax.map(attend, starts)
    attended = mixed_blocks.reshape(row_count, model_width)
    branch = jnp.dot(
        attended, proj_full, preferred_element_type=jnp.float32
    ) + proj_bias_full.astype(jnp.float32)
    middle = inputs + branch_scale * branch
    gain_two, bias_two, fc_full, fc_bias_full, out_full, out_bias_full = (
        lax.all_gather(ln2_gain, ("dp", "fsdp"), axis=0, tiled=True),
        lax.all_gather(ln2_bias, ("dp", "fsdp"), axis=0, tiled=True),
        lax.all_gather(w_fc, ("dp", "fsdp"), axis=0, tiled=True),
        lax.all_gather(fc_bias, ("dp", "fsdp"), axis=0, tiled=True),
        lax.all_gather(w_out, ("dp", "fsdp"), axis=0, tiled=True),
        lax.all_gather(out_bias, ("dp", "fsdp"), axis=0, tiled=True),
    )
    normed_two = layer_norm(
        middle, gain_two.astype(jnp.float32), bias_two.astype(jnp.float32)
    ).astype(jnp.bfloat16)
    pre_act = jnp.dot(
        normed_two, fc_full, preferred_element_type=jnp.float32
    ) + fc_bias_full.astype(jnp.float32)
    activated = gelu_tanh(pre_act).astype(jnp.bfloat16)
    mlp_out = jnp.dot(
        activated, out_full, preferred_element_type=jnp.float32
    ) + out_bias_full.astype(jnp.float32)
    outputs = middle + branch_scale * mlp_out
    gain_one_b, bias_one_b, qkv_back, qv_back, proj_back, proj_bias_back = (
        lax.all_gather(ln1_gain, ("dp", "fsdp"), axis=0, tiled=True),
        lax.all_gather(ln1_bias, ("dp", "fsdp"), axis=0, tiled=True),
        lax.all_gather(w_qkv, ("dp", "fsdp"), axis=0, tiled=True),
        lax.all_gather(qv_bias, ("dp", "fsdp"), axis=0, tiled=True),
        lax.all_gather(w_proj, ("dp", "fsdp"), axis=0, tiled=True),
        lax.all_gather(proj_bias, ("dp", "fsdp"), axis=0, tiled=True),
    )
    gain_two_b, bias_two_b, fc_back, fc_bias_back, out_back, out_bias_back = (
        lax.all_gather(ln2_gain, ("dp", "fsdp"), axis=0, tiled=True),
        lax.all_gather(ln2_bias, ("dp", "fsdp"), axis=0, tiled=True),
        lax.all_gather(w_fc, ("dp", "fsdp"), axis=0, tiled=True),
        lax.all_gather(fc_bias, ("dp", "fsdp"), axis=0, tiled=True),
        lax.all_gather(w_out, ("dp", "fsdp"), axis=0, tiled=True),
        lax.all_gather(out_bias, ("dp", "fsdp"), axis=0, tiled=True),
    )
    out_grad = cotangent.astype(jnp.float32) * row_valid[:, None].astype(jnp.float32)
    mlp_grad = (branch_scale * out_grad).astype(jnp.bfloat16)
    grad_out_bias = jnp.sum(mlp_grad, axis=0, dtype=jnp.float32)
    grad_w_out = contract_rows(activated, mlp_grad)
    grad_act = contract_last(mlp_grad, out_back)
    grad_pre = jax.vjp(gelu_tanh, pre_act)[1](grad_act)[0].astype(jnp.bfloat16)
    grad_fc_bias = jnp.sum(grad_pre, axis=0, dtype=jnp.float32)
    grad_w_fc = contract_rows(normed_two, grad_pre)
    grad_normed_two = contract_last(grad_pre, fc_back)
    grad_middle_ln, grad_gain_two, grad_bias_two = jax.vjp(
        layer_norm, middle, gain_two_b.astype(jnp.float32), bias_two_b.astype(jnp.float32)
    )[1](grad_normed_two)
    grad_middle = out_grad + grad_middle_ln
    mlp_shares = (
        lax.psum_scatter(grad_gain_two, ("dp", "fsdp"), scatter_dimension=0, tiled=True),
        lax.psum_scatter(grad_bias_two, ("dp", "fsdp"), scatter_dimension=0, tiled=True),
        lax.psum_scatter(grad_w_fc, ("dp", "fsdp"), scatter_dimension=0, tiled=True),
        lax.psum_scatter(grad_fc_bias, ("dp", "fsdp"), scatter_dimension=0, tiled=True),
        lax.psum_scatter(grad_w_out, ("dp", "fsdp"), scatter_dimension=0, tiled=True),
        lax.psum_scatter(grad_out_bias, ("dp", "fsdp"), scatter_dimension=0, tiled=True),
    )
    proj_grad = (branch_scale * grad_middle).astype(jnp.bfloat16)
    grad_proj_bias = jnp.sum(proj_grad, axis=0, dtype=jnp.float32)
    grad_w_proj = contract_rows(attended, proj_grad)
    grad_attended = (
        contract_last(proj_grad, proj_back).astype(jnp.bfloat16).reshape(row_count, head_count, HD)
    )

    def attend_back(accum_state, block_item):
        first_row, log_block = block_item
        grad_keys, grad_values = accum_state
        query_block = lax.dynamic_slice_in_dim(queries, first_row, block_rows)
        grad_block = lax.dynamic_slice_in_dim(grad_attended, first_row, block_rows)
        allowed = permitted(position, segment, row_valid, first_row, block_rows)
        scores = (
            jnp.einsum("qhd,khd->hqk", query_block, key_heads, preferred_element_type=jnp.float32)
            * score_scale
        )
        scores = jnp.where(allowed[None], scores, masked_score)
        probs = jnp.exp(scores - log_block[..., None])
        prob_low = probs.astype(jnp.bfloat16)
        grad_probs = jnp.einsum(
            "qhd,khd->hqk", grad_block, value_heads, preferred_element_type=jnp.float32
        )
        centre = jnp.sum(grad_probs * probs, axis=-1, keepdims=True)
        grad_scores = (probs * (grad_probs - centre)).astype(jnp.bfloat16)
        grad_query = (
            jnp.einsum("hqk,khd->qhd", grad_scores, key_heads, preferred_element_type=jnp.float32)
            * score_scale
        )
        grad_keys = (
            grad_keys
            + jnp.einsum(
                "hqk,qhd->khd", grad_scores, query_block, preferred_element_type=jnp.float32
            )
            * score_scale
        )
        grad_values = grad_values + jnp.einsum(
            "hqk,qhd->khd", prob_low, grad_block, preferred_element_type=jnp.float32
        )
        return ((grad_keys, grad_values), grad_query)

    zero_heads = jnp.zeros((row_count, head_count, HD), jnp.float32)
    key_values_grad, grad_queries = lax.scan(
        attend_back, (zero_heads, zero_heads), (starts, log_totals)
    )
    grad_joined = jnp.concatenate(
        [
            grad_queries.reshape(row_count, model_width),
            key_values_grad[0].reshape(row_count, model_width),
            key_values_grad[1].reshape(row_count, model_width),
        ],
        axis=1,
    ).astype(jnp.bfloat16)
    grad_qv_bias = jnp.concatenate(
        [
            jnp.sum(grad_joined[:, :model_width], axis=0, dtype=jnp.float32),
            jnp.sum(grad_joined[:, 2 * model_width :], axis=0, dtype=jnp.float32),
        ]
    )
    grad_w_qkv = contract_rows(normed, grad_joined)
    grad_normed = contract_last(grad_joined, qkv_back)
    grad_inputs_ln, grad_gain_one, grad_bias_one = jax.vjp(
        layer_norm, inputs, gain_one_b.astype(jnp.float32), bias_one_b.astype(jnp.float32)
    )[1](grad_normed)
    grad_inputs = (grad_middle + grad_inputs_ln).astype(jnp.bfloat16)
    attn_shares = (
        lax.psum_scatter(grad_gain_one, ("dp", "fsdp"), scatter_dimension=0, tiled=True),
        lax.psum_scatter(grad_bias_one, ("dp", "fsdp"), scatter_dimension=0, tiled=True),
        lax.psum_scatter(grad_w_qkv, ("dp", "fsdp"), scatter_dimension=0, tiled=True),
        lax.psum_scatter(grad_qv_bias, ("dp", "fsdp"), scatter_dimension=0, tiled=True),
        lax.psum_scatter(grad_w_proj, ("dp", "fsdp"), scatter_dimension=0, tiled=True),
        lax.psum_scatter(grad_proj_bias, ("dp", "fsdp"), scatter_dimension=0, tiled=True),
    )
    all_shares = attn_shares + mlp_shares
    return (
        outputs.astype(jnp.bfloat16),
        grad_inputs,
        all_shares[0],
        all_shares[1],
        all_shares[2],
        all_shares[3],
        all_shares[4],
        all_shares[5],
        all_shares[6],
        all_shares[7],
        all_shares[8],
        all_shares[9],
        all_shares[10],
        all_shares[11],
    )


def solution(mesh):
    in_specs = (
        P(("dp", "fsdp"), None),
        P(("dp", "fsdp"), None),
        P(("dp", "fsdp")),
        P(("dp", "fsdp")),
        P(("dp", "fsdp"), None),
        P(("dp", "fsdp")),
        P(("dp", "fsdp"), None),
        P(("dp", "fsdp")),
        P(("dp", "fsdp")),
        P(("dp", "fsdp")),
        P(("dp", "fsdp"), None),
        P(("dp", "fsdp")),
        P(("dp", "fsdp"), None),
        P(("dp", "fsdp")),
        P(("dp", "fsdp"), None),
    )
    out_specs = (
        P(("dp", "fsdp"), None),
        P(("dp", "fsdp"), None),
        P(("dp", "fsdp")),
        P(("dp", "fsdp")),
        P(("dp", "fsdp"), None),
        P(("dp", "fsdp")),
        P(("dp", "fsdp"), None),
        P(("dp", "fsdp")),
        P(("dp", "fsdp")),
        P(("dp", "fsdp")),
        P(("dp", "fsdp"), None),
        P(("dp", "fsdp")),
        P(("dp", "fsdp"), None),
        P(("dp", "fsdp")),
    )
    return jax.shard_map(
        per_device, mesh=mesh, in_specs=in_specs, out_specs=out_specs, check_vma=False
    )
```

profile of v0, /device:TPU:0, one launch (start us, length us, event | category | flops | bytes accessed | tf_op | source)
XLA Modules:
  0.0 908.6 jit_solution(8445728518475810348)
XLA Ops:
  18.3 42.9 %all-reduce.17 = (bf16[1536]{0:T(1024)(128)(2,1)S(1)}, bf16[768]{0:T(1024)(128)(2,1)S(1)}, bf16[768]{0:T(1024)(128)(2,1)S(1)}, bf16[768]{0:T(1024)(128)(2,1)S(1)...) all-reduce(bf16[1536]{0:T(1024)(128)(2,1)S(1)} %dynamic-update-slic, ...), channel_id=1, replica_groups=mesh['dp'=8,'fsdp'=4] {'dp','fsdp'}, use_global_device_ids=true, to_apply=%add.2 | all-reduce | flops 9216 | bytes 36864
  67.9 6.0 all-gather.5.cloned.1.call-done
  73.9 6.4 add_convert_fusion
  85.9 76.7 %while.29 = (s32[]{:T(128)}, bf16[2,512,12,64]{1,3,2,0:T(8,128)(2,1)}, f32[2,12,512]{2,1,0:T(8,128)S(1)}, s32[2]{0:T(128)S(1)}, s32[1024]{0:T(1024)S(1)}, /*inde...) while((s32[]{:T(128)}, ...), condition=%wide.region_7.8_spmd.clone, body=%wide.region_4.7_spmd.clone.sunk | while | flops 1689643008 | bytes 189510896 | solution.py:119
  89.6 10.8 %fusion.107 = (f32[12,512]{1,0:T(8,128)S(1)}, f32[12,512,1024]{2,1,0:T(8,128)}) fusion(pred[512,1024]{1,0:T(8,128)(4,1)S(1)} %compare_or_fusion.4, bf16[1024,12,64]{0,2,1:T(8,128)(2,1)S(1)} %get-tuple-element.604, bf16[1024,12,64]{0,2,1:T(8,128)(2,1)S(1)} %get-tuple-element.603, s32[]{:T(128)S(6)} %select_n.61), kind=kOutput, calls=%fused_computation.3.clone.1 | convolution fusion | flops 824174592 | bytes 28073988 | tf_op jit(solution)/shard_map/while/body/eval_jaxpr/qhd,khd->hqk/dot_general | solution.py:106
  100.4 12.3 %fusion.108 = f32[12,512]{1,0:T(8,128)S(1)} fusion(f32[12,512,1024]{2,1,0:T(8,128)} %get-tuple-element.553, f32[12,512]{1,0:T(8,128)S(1)} %get-tuple-element.554, pred[512,1024]{1,0:T(8,128)(4,1)S(1)} %compare_or_fusion.4), kind=kLoop, calls=%fused_computation.4.clone.1 | loop fusion | flops 25159680 | bytes 25739264 | tf_op jit(solution)/shard_map/while/body/eval_jaxpr/reduce_sum | solution.py:112
  112.7 3.1 copy-done
  115.8 8.5 fusion.109
  127.8 10.8 %fusion.107 = (f32[12,512]{1,0:T(8,128)S(1)}, f32[12,512,1024]{2,1,0:T(8,128)}) fusion(pred[512,1024]{1,0:T(8,128)(4,1)S(1)} %compare_or_fusion.4, bf16[1024,12,64]{0,2,1:T(8,128)(2,1)S(1)} %get-tuple-element.604, bf16[1024,12,64]{0,2,1:T(8,128)(2,1)S(1)} %get-tuple-element.603, s32[]{:T(128)S(6)} %select_n.61), kind=kOutput, calls=%fused_computation.3.clone.1 | convolution fusion | flops 824174592 | bytes 28073988 | tf_op jit(solution)/shard_map/while/body/eval_jaxpr/qhd,khd->hqk/dot_general | solution.py:106
  138.6 12.4 %fusion.108 = f32[12,512]{1,0:T(8,128)S(1)} fusion(f32[12,512,1024]{2,1,0:T(8,128)} %get-tuple-element.553, f32[12,512]{1,0:T(8,128)S(1)} %get-tuple-element.554, pred[512,1024]{1,0:T(8,128)(4,1)S(1)} %compare_or_fusion.4), kind=kLoop, calls=%fused_computation.4.clone.1 | loop fusion | flops 25159680 | bytes 25739264 | tf_op jit(solution)/shard_map/while/body/eval_jaxpr/reduce_sum | solution.py:112
  151.0 3.1 copy-done
  154.1 8.5 fusion.109
  162.6 3.0 copy.76
  167.3 4.0 fusion.65
  173.3 21.9 %all-gather.9.cloned.1.call-done = bf16[768,3072]{1,0:T(8,128)(2,1)} async-done(((bf16[24,3072]{1,0:T(8,128)(2,1)}), bf16[768,3072]{1,0:T(8,128)(2,1)}) %all-gather.9.cloned.1.call-update) | async-done | bytes 4718608 | tf_op jit(solution)/shard_map/all_gather | solution.py:128
  195.2 11.2 %fusion.60 = f32[1024,3072]{1,0:T(8,128)} fusion(bf16[768,3072]{1,0:T(8,128)(2,1)} %all-gather.9.cloned.1.call-done, f32[1024,768]{0,1:T(8,128)} %copy-done.7, f32[768]{0:T(1024)S(1)} %copy-done.28, f32[768]{0:T(1024)S(1)} %copy-done.24, f32[1024]{0:T(1024)S(1)} %fusion.52, f32[1024]{0:T(1024)S(1)} %broadcast_multiply_fusion), kind=kOutput, calls=%fused_computation.108 | convolution fusion | flops 4835770368 | bytes 20461568 | tf_op jit(solution)/shard_map/dot_general | solution.py:136
  206.4 54.0 %all-gather.11.cloned.1.call-done = bf16[3072,768]{1,0:T(8,128)(2,1)} async-done(((bf16[96,768]{1,0:T(8,128)(2,1)}), bf16[3072,768]{1,0:T(8,128)(2,1)}) %all-gather.11.cloned.1.call-update) | async-done | bytes 4718608 | tf_op jit(solution)/shard_map/all_gather | solution.py:130
  260.5 17.7 %convert_reduce_fusion = (f32[3072]{0:T(1024)}, bf16[1024,3072]{1,0:T(8,128)(2,1)S(1)}) fusion(f32[1024,3072]{1,0:T(8,128)} %fusion.60, f32[3072]{0:T(1024)S(1)} %copy-done.45, bf16[3072,768]{1,0:T(8,128)(2,1)} %all-gather.11.cloned.1.call-done, bf16[1024,768]{0,1:T(8,128)(2,1)} %copy.78, f32[1024]{0:T(1024)S(1)} %copy-done.34), kind=kOutput, calls=%fused_computation.48 | convolution fusion | flops 4907332608 | bytes 25194496 | tf_op jit(solution)/shard_map/dot_general | solution.py:48
  278.2 7.3 fusion.67
  285.5 3.5 copy.79
  289.0 4.5 multiply_reduce_fusion.1
  300.8 4.3 convolution_convert_fusion
  305.1 179.2 %while.30 = (s32[]{:T(128)}, f32[1024,12,64]{0,2,1:T(8,128)}, f32[1024,12,64]{0,2,1:T(8,128)}, bf16[2,512,12,64]{1,3,2,0:T(8,128)(2,1)}, s32[2]{0:T(128)S(1)}, /...) while((s32[]{:T(128)}, f32[1024,12,64]{0,2,1:T(8,128)}, ...), condition=%wide.region_14.15_spmd.clone.clone, body=%wide.region_12.14_spmd.clone.clone.sunk | while | flops 4128368640 | bytes 231937360 | solution.py:223
  308.8 13.4 %fusion.119 = f32[12,512,1024]{2,1,0:T(8,128)} fusion(bf16[1024,12,64]{0,2,1:T(8,128)(2,1)S(1)} %get-tuple-element.650, bf16[1024,12,64]{0,2,1:T(8,128)(2,1)} %copy-done.2, s32[]{:T(128)S(6)} %select_n.65), kind=kOutput, calls=%fused_computation.30.clone.1 | convolution fusion | flops 805306368 | bytes 27525124 | tf_op jit(solution)/shard_map/while/body/eval_jaxpr/qhd,khd->hqk/dot_general | solution.py:195
  322.2 13.7 %bitcast_add_fusion.5 = f32[1024,12,64]{0,2,1:T(8,128)} fusion(f32[1024,12,64]{0,2,1:T(8,128)} %get-tuple-element.627, f32[12,512,1024]{2,1,0:T(8,128)} %fusion.119, f32[12,512]{1,0:T(8,128)S(1)} %dynamic-slice_bitcast_fusion.2, pred[512,1024]{1,0:T(8,128)(4,1)S(1)} %compare_or_fusion.5, pred[]{:T(512)S(6)} %compare.3, ...), kind=kOutput, calls=%fused_computation.22.clone.1 | convolution fusion | flops 832045056 | bytes 32800772 | tf_op jit(solution)/shard_map/while/body/eval_jaxpr/hqk,qhd->khd/dot_general | solution.py:217
  336.0 18.3 %multiply_reduce_fusion.5 = (f32[12,512]{1,0:T(8,128)S(1)}, f32[12,512,1024]{2,1,0:T(8,128)}) fusion(f32[12,512,1024]{2,1,0:T(8,128)} %fusion.119, f32[12,512]{1,0:T(8,128)S(1)} %dynamic-slice_bitcast_fusion.2, pred[512,1024]{1,0:T(8,128)(4,1)S(1)} %compare_or_fusion.5, bf16[1024,12,64]{0,2,1:T(8,128)(2,1)} %get-tuple-element.653, ...), kind=kOutput, calls=%fused_computation.17.clone.1 | convolution fusion | flops 836757504 | bytes 53264388 | tf_op jit(solution)/shard_map/while/body/eval_jaxpr/qhd,khd->hqk/dot_general | solution.py:201
  354.2 21.9 %multiply_convert_fusion.10 = bf16[12,512,1024]{2,1,0:T(8,128)(2,1)} fusion(f32[12,512,1024]{2,1,0:T(8,128)} %get-tuple-element.568, f32[12,512,1024]{2,1,0:T(8,128)} %fusion.119, f32[12,512]{1,0:T(8,128)S(1)} %get-tuple-element.569, f32[12,512]{1,0:T(8,128)S(1)} %dynamic-slice_bitcast_fusion.2, pred[512,1024]{1,0:T(8,128)(4,1)S(1)} %compare_or_fusion.5), kind=kLoop, calls=%fused_computation.16.clone.1 | loop fusion | flops 37748736 | bytes 63488000 | tf_op jit(solution)/shard_map/while/body/eval_jaxpr/convert_element_type | solution.py:205
  376.1 9.6 %bitcast_dynamic-update-slice_fusion.5 = bf16[2,512,12,64]{1,3,2,0:T(8,128)(2,1)} fusion(bf16[2,512,12,64]{1,3,2,0:T(8,128)(2,1)} %get-tuple-element.628, s32[]{:T(128)S(6)} %copy.113, bf16[12,512,1024]{2,1,0:T(8,128)(2,1)} %multiply_convert_fusion.10, bf16[1024,12,64]{0,2,1:T(8,128)(2,1)S(1)} %get-tuple-element.650), kind=kOutput, calls=%fused_computation.25.clone.1 | convolution fusion | flops 805699584 | bytes 15728644 | tf_op jit(solution)/shard_map/while/body/eval_jaxpr/hqk,khd->qhd/dot_general | solution.py:207
  385.7 8.7 bitcast_add_fusion.4
  398.0 13.1 %fusion.119 = f32[12,512,1024]{2,1,0:T(8,128)} fusion(bf16[1024,12,64]{0,2,1:T(8,128)(2,1)S(1)} %get-tuple-element.650, bf16[1024,12,64]{0,2,1:T(8,128)(2,1)} %copy-done.2, s32[]{:T(128)S(6)} %select_n.65), kind=kOutput, calls=%fused_computation.30.clone.1 | convolution fusion | flops 805306368 | bytes 27525124 | tf_op jit(solution)/shard_map/while/body/eval_jaxpr/qhd,khd->hqk/dot_general | solution.py:195
  411.1 14.5 %bitcast_add_fusion.5 = f32[1024,12,64]{0,2,1:T(8,128)} fusion(f32[1024,12,64]{0,2,1:T(8,128)} %get-tuple-element.627, f32[12,512,1024]{2,1,0:T(8,128)} %fusion.119, f32[12,512]{1,0:T(8,128)S(1)} %dynamic-slice_bitcast_fusion.2, pred[512,1024]{1,0:T(8,128)(4,1)S(1)} %compare_or_fusion.5, pred[]{:T(512)S(6)} %compare.3, ...), kind=kOutput, calls=%fused_computation.22.clone.1 | convolution fusion | flops 832045056 | bytes 32800772 | tf_op jit(solution)/shard_map/while/body/eval_jaxpr/hqk,qhd->khd/dot_general | solution.py:217
  425.6 18.2 %multiply_reduce_fusion.5 = (f32[12,512]{1,0:T(8,128)S(1)}, f32[12,512,1024]{2,1,0:T(8,128)}) fusion(f32[12,512,1024]{2,1,0:T(8,128)} %fusion.119, f32[12,512]{1,0:T(8,128)S(1)} %dynamic-slice_bitcast_fusion.2, pred[512,1024]{1,0:T(8,128)(4,1)S(1)} %compare_or_fusion.5, bf16[1024,12,64]{0,2,1:T(8,128)(2,1)} %get-tuple-element.653, ...), kind=kOutput, calls=%fused_computation.17.clone.1 | convolution fusion | flops 836757504 | bytes 53264388 | tf_op jit(solution)/shard_map/while/body/eval_jaxpr/qhd,khd->hqk/dot_general | solution.py:201
  443.8 21.2 %multiply_convert_fusion.10 = bf16[12,512,1024]{2,1,0:T(8,128)(2,1)} fusion(f32[12,512,1024]{2,1,0:T(8,128)} %get-tuple-element.568, f32[12,512,1024]{2,1,0:T(8,128)} %fusion.119, f32[12,512]{1,0:T(8,128)S(1)} %get-tuple-element.569, f32[12,512]{1,0:T(8,128)S(1)} %dynamic-slice_bitcast_fusion.2, pred[512,1024]{1,0:T(8,128)(4,1)S(1)} %compare_or_fusion.5), kind=kLoop, calls=%fused_computation.16.clone.1 | loop fusion | flops 37748736 | bytes 63488000 | tf_op jit(solution)/shard_map/while/body/eval_jaxpr/convert_element_type | solution.py:205
  465.0 9.5 %bitcast_dynamic-update-slice_fusion.5 = bf16[2,512,12,64]{1,3,2,0:T(8,128)(2,1)} fusion(bf16[2,512,12,64]{1,3,2,0:T(8,128)(2,1)} %get-tuple-element.628, s32[]{:T(128)S(6)} %copy.113, bf16[12,512,1024]{2,1,0:T(8,128)(2,1)} %multiply_convert_fusion.10, bf16[1024,12,64]{0,2,1:T(8,128)(2,1)S(1)} %get-tuple-element.650), kind=kOutput, calls=%fused_computation.25.clone.1 | convolution fusion | flops 805699584 | bytes 15728644 | tf_op jit(solution)/shard_map/while/body/eval_jaxpr/hqk,khd->qhd/dot_general | solution.py:207
  474.5 9.6 %bitcast_add_fusion.4 = f32[1024,12,64]{0,2,1:T(8,128)} fusion(f32[1024,12,64]{0,2,1:T(8,128)} %get-tuple-element.626, bf16[12,512,1024]{2,1,0:T(8,128)(2,1)} %multiply_convert_fusion.10, pred[]{:T(512)S(6)} %compare.3, bf16[1024,12,64]{0,2,1:T(8,128)(2,1)S(1)} %copy-done.3, s32[]{:T(128)S(6)} %select_n.65), kind=kOutput, calls=%fused_computation.23.clone.1 | convolution fusion | flops 807665664 | bytes 19660804 | tf_op jit(solution)/shard_map/while/body/eval_jaxpr/hqk,qhd->khd/dot_general | solution.py:212
  484.4 3.2 copy.80
  488.3 3.0 convert_reduce_fusion.4
  492.5 7.0 fusion.47
  500.9 13.9 %fusion.49 = f32[3072,768]{1,0:T(8,128)} fusion(bf16[1024,768]{0,1:T(8,128)(2,1)S(1)} %copy-done.13, f32[1024]{0:T(1024)S(1)} %copy-done.35, f32[1024,3072]{1,0:T(8,128)} %fusion.60, f32[3072]{0:T(1024)S(1)} %copy-done.46), kind=kOutput, calls=%fused_computation.85 | convolution fusion | flops 4866441216 | bytes 23609344 | tf_op jit(solution)/shard_map/dot_general | solution.py:42
  515.5 11.3 %fusion.59 = f32[768,3072]{1,0:T(8,128)} fusion(bf16[1024,3072]{1,0:T(8,128)(2,1)} %copy-done.53, f32[1024,768]{0,1:T(8,128)} %copy-done.7, f32[768]{0:T(1024)S(1)} %copy-done.29, f32[768]{0:T(1024)S(1)} %copy-done.25, f32[1024]{0:T(1024)S(1)} %copy-done.27, f32[1024]{0:T(1024)S(1)} %copy-done.23), kind=kOutput, calls=%fused_computation.107 | convolution fusion | flops 4835770368 | bytes 18888704 | tf_op jit(solution)/shard_map/dot_general | solution.py:42
  527.5 12.6 %add_convert_fusion.2 = bf16[1024,768]{0,1:T(8,128)(2,1)} fusion(f32[1024,768]{0,1:T(8,128)} %copy-done.7, bf16[3072,768]{1,0:T(8,128)(2,1)} %all-gather.11.cloned.1.call-done, f32[768]{0:T(1024)S(1)} %convert_element_type.121, f32[1024,3072]{1,0:T(8,128)} %fusion.60, f32[3072]{0:T(1024)S(1)} %copy-done.46), kind=kOutput, calls=%fused_computation.79 | convolution fusion | flops 4866441216 | bytes 22035456 | tf_op jit(solution)/shard_map/dot_general | solution.py:140
  542.7 9.0 fusion.66
  551.6 3.6 copy.81
  561.1 41.3 %all-reduce.16 = (f32[768]{0:T(1024)S(1)}, f32[768]{0:T(1024)S(1)}, f32[1536]{0:T(1024)S(1)}, f32[768]{0:T(1024)S(1)}, f32[768]{0:T(1024)S(1)}, /*index=5*/f32[7...) all-reduce(f32[768]{0:T(1024)S(1)} %get-tuple-element.332, ...), channel_id=2, replica_groups=mesh['dp'=8,'fsdp'=4] {'dp','fsdp'}, use_global_device_ids=true, to_apply=%region_18.19.clone | all-reduce | flops 9216 | bytes 73728
  605.9 5.6 add_convert_fusion.1
  615.3 2.8 reduce-scatter.5.cloned.1.call-done
  618.1 141.4 %reduce-scatter.11.cloned.1.call-done = f32[96,768]{1,0:T(8,128)} async-done(((f32[3072,768]{1,0:T(8,128)}), f32[96,768]{1,0:T(8,128)}) %reduce-scatter.11.cloned.1.call-update) | async-done | bytes 294928 | tf_op jit(solution)/shard_map/reduce_scatter | solution.py:178
  759.5 142.0 %reduce-scatter.9.cloned.1.call-done = f32[24,3072]{1,0:T(8,128)} async-done(((f32[768,3072]{1,0:T(8,128)}), f32[24,3072]{1,0:T(8,128)}) %reduce-scatter.9.cloned.1.call-update) | async-done | bytes 294928 | tf_op jit(solution)/shard_map/reduce_scatter | solution.py:176
  (228 shorter events, 60.2 us)
Async XLA Ops:
  7.2 66.8 %all-gather.5.cloned.1.call-start = ((), (), s32[]{:S(2)}) async-start(), calls=%async_computation.4 | async-start | bytes 3649536 | tf_op jit(solution)/shard_map/all_gather | solution.py:83
  7.9 159.3 %all-gather.7.cloned.1.call-start = ((), (), s32[]{:S(2)}) async-start(), calls=%async_computation.5 | async-start | bytes 1216512 | tf_op jit(solution)/shard_map/all_gather | solution.py:85
  8.7 186.6 %all-gather.9.cloned.1.call-start = ((), (), s32[]{:S(2)}) async-start(), calls=%async_computation.6 | async-start | bytes 4866048 | tf_op jit(solution)/shard_map/all_gather | solution.py:128
  9.4 251.1 %all-gather.11.cloned.1.call-start = ((), (), s32[]{:S(2)}) async-start(), calls=%async_computation.7 | async-start | bytes 4866048 | tf_op jit(solution)/shard_map/all_gather | solution.py:130
  10.0 605.3 %reduce-scatter.7.cloned.1.call-start = ((), (), s32[]{:S(2)}) async-start(), calls=%async_computation.9 | async-start | bytes 2433024 | tf_op jit(solution)/shard_map/reduce_scatter | solution.py:251
  61.2 12.7 %copy-start.32 = (f32[768]{0:T(1024)}, f32[768]{0:T(1024)S(1)}, u32[]{:S(2)}) copy-start(f32[768]{0:T(1024)S(1)} %convert_element_type.110) | copy-start | bytes 9220
  61.8 12.1 %copy-start.48 = (f32[768]{0:T(1024)}, f32[768]{0:T(1024)S(1)}, u32[]{:S(2)}) copy-start(f32[768]{0:T(1024)S(1)} %convert_element_type.111) | copy-start | bytes 9220
  63.6 2.6 copy-start.17
  65.5 8.5 copy-start.5
  65.7 14.6 %copy-start.30 = (f32[1024]{0:T(1024)}, f32[1024]{0:T(1024)S(1)}, u32[]{:S(2)}) copy-start(f32[1024]{0:T(1024)S(1)} %broadcast_multiply_fusion.1) | copy-start | bytes 12292
  66.2 14.1 %copy-start.40 = (f32[1024]{0:T(1024)}, f32[1024]{0:T(1024)S(1)}, u32[]{:S(2)}) copy-start(f32[1024]{0:T(1024)S(1)} %fusion.45) | copy-start | bytes 12292
  66.2 14.1 %copy-start.36 = (f32[1024]{0:T(1024)}, f32[1024]{0:T(1024)S(1)}, u32[]{:S(2)}) copy-start(f32[1024]{0:T(1024)S(1)} %fusion.51) | copy-start | bytes 12292
  89.6 23.1 %copy-start.4 = (bf16[1024,12,64]{0,2,1:T(8,128)(2,1)S(1)}, bf16[1024,12,64]{0,2,1:T(8,128)(2,1)}, u32[]{:S(2)}) copy-start(bf16[1024,12,64]{0,2,1:T(8,128)(2,1)} %get-tuple-element.605) | copy-start | bytes 4718596 | tf_op jit(solution)/shard_map/while
  100.4 15.4 %copy-start = (f32[12,512,1024]{2,1,0:T(8,128)S(1)}, f32[12,512,1024]{2,1,0:T(8,128)}, u32[]{:S(2)}) copy-start(f32[12,512,1024]{2,1,0:T(8,128)} %get-tuple-element.553) | copy-start | bytes 75497472 | tf_op jit(solution)/shard_map/while
  127.8 23.2 %copy-start.4 = (bf16[1024,12,64]{0,2,1:T(8,128)(2,1)S(1)}, bf16[1024,12,64]{0,2,1:T(8,128)(2,1)}, u32[]{:S(2)}) copy-start(bf16[1024,12,64]{0,2,1:T(8,128)(2,1)} %get-tuple-element.605) | copy-start | bytes 4718596 | tf_op jit(solution)/shard_map/while
  138.6 15.6 %copy-start = (f32[12,512,1024]{2,1,0:T(8,128)S(1)}, f32[12,512,1024]{2,1,0:T(8,128)}, u32[]{:S(2)}) copy-start(f32[12,512,1024]{2,1,0:T(8,128)} %get-tuple-element.553) | copy-start | bytes 75497472 | tf_op jit(solution)/shard_map/while
  162.6 4.6 copy-start.50
  171.3 24.0 %copy-start.24 = (f32[768]{0:T(1024)S(1)}, f32[768]{0:T(1024)}, u32[]{:S(2)}) copy-start(f32[768]{0:T(1024)} %convert_element_type.116) | copy-start | bytes 9220
  171.3 23.9 %copy-start.28 = (f32[768]{0:T(1024)S(1)}, f32[768]{0:T(1024)}, u32[]{:S(2)}) copy-start(f32[768]{0:T(1024)} %convert_element_type.117) | copy-start | bytes 9220
  171.3 122.3 %copy-start.22 = (f32[1024]{0:T(1024)}, f32[1024]{0:T(1024)S(1)}, u32[]{:S(2)}) copy-start(f32[1024]{0:T(1024)S(1)} %broadcast_multiply_fusion) | copy-start | bytes 12292
  173.3 120.2 %copy-start.26 = (f32[1024]{0:T(1024)}, f32[1024]{0:T(1024)S(1)}, u32[]{:S(2)}) copy-start(f32[1024]{0:T(1024)S(1)} %fusion.52) | copy-start | bytes 12292
  173.3 87.1 %copy-start.34 = (f32[1024]{0:T(1024)S(1)}, f32[1024]{0:T(1024)}, u32[]{:S(2)}) copy-start(f32[1024]{0:T(1024)} %get-tuple-element.402) | copy-start | bytes 12292
  173.3 87.1 %copy-start.45 = (f32[3072]{0:T(1024)S(1)}, f32[3072]{0:T(1024)}, u32[]{:S(2)}) copy-start(f32[3072]{0:T(1024)} %convert_element_type.119) | copy-start | bytes 36868
  260.5 17.7 %copy-start.16 = (bf16[768,3072]{1,0:T(8,128)(2,1)S(1)}, bf16[768,3072]{1,0:T(8,128)(2,1)}, u32[]{:S(2)}) copy-start(bf16[768,3072]{1,0:T(8,128)(2,1)} %all-gather.9.cloned.1.call-done) | copy-start | bytes 14155780
  278.2 7.3 copy-start.53
  289.0 4.5 copy-start.8
  289.0 4.7 copy-start.11
  295.2 2.7 copy-start.18
  300.8 317.3 %reduce-scatter.5.cloned.1.call-start = ((), (), s32[]{:S(2)}) async-start(), calls=%async_computation.8 | async-start | bytes 7299072 | tf_op jit(solution)/shard_map/reduce_scatter | solution.py:249
  305.3 2.8 copy-start.2
  308.8 13.4 %copy-start.14 = (bf16[1024,12,64]{0,2,1:T(8,128)(2,1)S(1)}, bf16[1024,12,64]{0,2,1:T(8,128)(2,1)}, u32[]{:S(2)}) copy-start(bf16[1024,12,64]{0,2,1:T(8,128)(2,1)} %get-tuple-element.652) | copy-start | bytes 4718596 | tf_op jit(solution)/shard_map/while
  376.1 9.6 %copy-start.3 = (bf16[1024,12,64]{0,2,1:T(8,128)(2,1)S(1)}, bf16[1024,12,64]{0,2,1:T(8,128)(2,1)}, u32[]{:S(2)}) copy-start(bf16[1024,12,64]{0,2,1:T(8,128)(2,1)} %copy-done.2) | copy-start | bytes 4718596 | tf_op jit(solution)/shard_map/while
  394.4 2.8 copy-start.2
  398.0 13.1 %copy-start.14 = (bf16[1024,12,64]{0,2,1:T(8,128)(2,1)S(1)}, bf16[1024,12,64]{0,2,1:T(8,128)(2,1)}, u32[]{:S(2)}) copy-start(bf16[1024,12,64]{0,2,1:T(8,128)(2,1)} %get-tuple-element.652) | copy-start | bytes 4718596 | tf_op jit(solution)/shard_map/while
  465.0 9.5 %copy-start.3 = (bf16[1024,12,64]{0,2,1:T(8,128)(2,1)S(1)}, bf16[1024,12,64]{0,2,1:T(8,128)(2,1)}, u32[]{:S(2)}) copy-start(bf16[1024,12,64]{0,2,1:T(8,128)(2,1)} %copy-done.2) | copy-start | bytes 4718596 | tf_op jit(solution)/shard_map/while
  484.4 3.6 copy-start.1
  488.0 3.4 copy-start.15
  488.2 3.1 copy-start.19
  488.2 4.2 copy-start.6
  488.2 4.2 copy-start.31
  488.3 4.2 copy-start.33
  488.3 4.2 copy-start.37
  488.3 4.2 copy-start.49
  499.5 260.0 %reduce-scatter.11.cloned.1.call-start = ((), (), s32[]{:S(2)}) async-start(), calls=%async_computation.11 | async-start | bytes 9732096 | tf_op jit(solution)/shard_map/reduce_scatter | solution.py:178
  514.9 386.7 %reduce-scatter.9.cloned.1.call-start = ((), (), s32[]{:S(2)}) async-start(), calls=%async_computation.10 | async-start | bytes 9732096 | tf_op jit(solution)/shard_map/reduce_scatter | solution.py:176
  555.3 4.3 copy-start.41
  555.3 4.4 copy-start.9
  559.7 46.3 %copy-start.39 = (f32[1024]{0:T(1024)S(1)}, f32[1024]{0:T(1024)}, u32[]{:S(2)}) copy-start(f32[1024]{0:T(1024)} %copy-done.38) | copy-start | bytes 12292
  (19 other events, 24.5 us)
Sparse Core Ops, SparseCore 0:
  10.9 62.9 all-gather.4
  76.8 52.8 all-gather.6
  132.6 62.5 all-gather.8
  198.0 62.4 all-gather.10
  300.9 97.8 reduce-scatter.6
  499.6 118.4 reduce-scatter.4
  624.6 134.9 reduce-scatter.10
  767.0 134.5 reduce-scatter.8
where the time goes:
time: 915 us; the launch traced here: 909 us
  waiting for transfers between devices  371 us (41%)
  matrix products  275 us (30%)
  other arithmetic  97.2 us (11%)
  blocking collectives  84.3 us (9%)
  local copies, waits for them, and re-layouts  57.6 us (6%)
  between operations  15 us (2%)
    reduce_scatter x1, waiting for transfers between devices, per_device(): lax.psum_scatter(grad_w_fc, ('dp', 'fsdp'), scatter_dimension=0, tiled=True)  142 us
    reduce_scatter x1, waiting for transfers between devices, per_device(): lax.psum_scatter(grad_w_out, ('dp', 'fsdp'), scatter_dimension=0, tiled=T...  141 us
    unnamed x2, blocking collectives  84.3 us
    all_gather x1, waiting for transfers between devices, per_device(): lax.all_gather(w_out, ('dp', 'fsdp'), axis=0, tiled=True)  54 us
    convert_element_type x2, other arithmetic, attend_back(): grad_scores = (probs * (grad_probs - centre)).astype(jnp.bfloat16)  43.1 us
    dot_general x4, matrix products, contract_last(): lax.dot_general(left_side, right_side, (((1,), (1,)), ((), ())), preferre...  38.3 us
    dot_general x2, matrix products, attend_back(): jnp.einsum('qhd,khd->hqk', grad_block, value_heads, preferred_element_typ...  36.5 us
    dot_general x4, matrix products, contract_rows(): lax.dot_general(left_side, right_side, (((0,), (0,)), ((), ())), preferre...  35 us
  transfers between devices with their start and end apart: 8, of which 6 were waited for; matrix products, arithmetic and copies ran while one was open for 42% of the time, Pallas kernels for 0%

commit v1 on v0

v1 whole, which is shorter than its diff:
```python
import functools
import math

import jax
import jax.numpy as jnp
from jax import lax
from jax.experimental import pallas as pl
from jax.experimental.pallas import tpu as pltpu
from jax.sharding import PartitionSpec as P

HD = 64
LONG = 768
EPS = 1e-05
BS = 1.0 / math.sqrt(48.0)
NEG = -1e30
F32 = jnp.float32
BF = jnp.bfloat16
VMEM_LIMIT = 58 * 1024 * 1024
AXES = ("dp", "fsdp")
GC0 = math.sqrt(2.0 / math.pi)
GC1 = 0.044715


def dot(a, b):
    return lax.dot_general(a, b, (((1,), (0,)), ((), ())), preferred_element_type=F32)


def dot_t(a, b):
    return lax.dot_general(a, b, (((1,), (1,)), ((), ())), preferred_element_type=F32)


def dot_0(a, b):
    return lax.dot_general(a, b, (((0,), (0,)), ((), ())), preferred_element_type=F32)


def params(grid_len=1):
    return pltpu.CompilerParams(
        dimension_semantics=("arbitrary",) * grid_len, vmem_limit_bytes=VMEM_LIMIT
    )


def cost(flops, nbytes, trans=0):
    return pl.CostEstimate(flops=int(flops), bytes_accessed=int(nbytes), transcendentals=int(trans))


def normalize(values):
    centred = values - jnp.mean(values, axis=-1, keepdims=True)
    rstd = lax.rsqrt(jnp.mean(centred * centred, axis=-1, keepdims=True) + EPS)
    return centred * rstd, rstd


def ln_back(dy, xhat, rstd, gain):
    dx = dy * gain
    m1 = jnp.mean(dx, axis=-1, keepdims=True)
    m2 = jnp.mean(dx * xhat, axis=-1, keepdims=True)
    return rstd * (dx - m1 - xhat * m2)


def full_spec(shape):
    return pl.BlockSpec(shape, lambda *_: (0,) * len(shape))


def qkv_kernel(x_ref, g_ref, b_ref, w_ref, bias_ref, o_ref, n_ref):
    rows = x_ref.shape[0]

    @pl.when(pl.program_id(0) == 0)
    def _():
        for r in range(0, rows, 256):
            xhat, _ = normalize(x_ref[r : r + 256, :].astype(F32))
            n_ref[r : r + 256, :] = (xhat * g_ref[...] + b_ref[...]).astype(BF)

    for r in range(0, rows, 256):
        o_ref[r : r + 256, :] = (dot(n_ref[r : r + 256, :], w_ref[...]) + bias_ref[...]).astype(BF)


def qkv_call(x, g, b, w, bias):
    rows, d = x.shape
    cols = w.shape[1]
    bc = 384
    return pl.pallas_call(
        qkv_kernel,
        grid=(cols // bc,),
        in_specs=[
            full_spec((rows, d)),
            full_spec((1, d)),
            full_spec((1, d)),
            pl.BlockSpec((d, bc), lambda j: (0, j)),
            pl.BlockSpec((1, bc), lambda j: (0, j)),
        ],
        out_specs=pl.BlockSpec((rows, bc), lambda j: (0, j)),
        out_shape=jax.ShapeDtypeStruct((rows, cols), BF),
        scratch_shapes=[pltpu.VMEM((rows, d), BF)],
        compiler_params=params(),
        cost_estimate=cost(2 * rows * d * cols, rows * d * 8 + d * cols * 2),
        name="qkv",
    )(x, g, b, w, bias)


def lane_masks(rows):
    lane = lax.broadcasted_iota(jnp.int32, (rows, 128), 1)
    return lane < HD


def split_heads(block):
    low = lane_masks(block.shape[0])
    zero = jnp.zeros_like(block)
    return jnp.where(low, block, zero), jnp.where(low, zero, block)


def q_tiles(rows):
    tiles = [(r, 0, r + 256, True) for r in range(0, LONG, 256)]
    tiles += [(LONG, LONG, rows, False)]
    return tiles


def diag_allowed(is_long, seg_row, seg_col):
    kv = lax.broadcasted_iota(jnp.int32, (256, 256), 0)
    qp = lax.broadcasted_iota(jnp.int32, (256, 256), 1)
    allowed = kv <= qp
    if not is_long:
        allowed = allowed & (seg_col == seg_row)
    return allowed


def attn_kernel(q_ref, k_ref, v_ref, segr_ref, segc_ref, o_ref, lse_ref):
    rows = q_ref.shape[0]
    k0, k1 = split_heads(k_ref[...] * BF(HD**-0.5))
    v0, v1 = split_heads(v_ref[...])
    for q0, kv0, kv1, is_long in q_tiles(rows):
        q = q_ref[q0 : q0 + 256, :]
        allowed = diag_allowed(is_long, segr_ref[...], segc_ref[...])
        outs = []
        for h, (k, v) in enumerate(((k0, v0), (k1, v1))):
            s = dot_t(k[kv0:kv1], q)
            diag = jnp.where(allowed, s[q0 - kv0 : q0 - kv0 + 256], NEG)
            parts = [diag] if kv1 - kv0 == 256 else [s[: q0 - kv0], diag]
            top = functools.reduce(
                jnp.maximum, [jnp.max(p, axis=0, keepdims=True) for p in parts]
            )
            exps = [jnp.exp(p - top) for p in parts]
            total = functools.reduce(
                jnp.add, [jnp.sum(e, axis=0, keepdims=True) for e in exps]
            )
            lse_ref[0, h : h + 1, q0 : q0 + 256] = top + jnp.log(total)
            probs = jnp.concatenate([e.astype(BF) for e in exps], axis=0)
            outs.append(dot_0(v[kv0:kv1], probs) * (1.0 / total))
        o_ref[q0 : q0 + 256, :] = (outs[0] + outs[1]).T.astype(BF)


def attn_call(joined, seg_row, seg_col):
    rows = joined.shape[0]
    pairs = joined.shape[1] // 384
    return pl.pallas_call(
        attn_kernel,
        grid=(pairs,),
        in_specs=[
            pl.BlockSpec((rows, 128), lambda p: (0, p)),
            pl.BlockSpec((rows, 128), lambda p: (0, pairs + p)),
            pl.BlockSpec((rows, 128), lambda p: (0, 2 * pairs + p)),
            full_spec((1, 256)),
            full_spec((256, 1)),
        ],
        out_specs=[
            pl.BlockSpec((rows, 128), lambda p: (0, p)),
            pl.BlockSpec((1, 2, rows), lambda p: (p, 0, 0)),
        ],
        out_shape=[
            jax.ShapeDtypeStruct((rows, pairs * 128), BF),
            jax.ShapeDtypeStruct((pairs, 2, rows), F32),
        ],
        compiler_params=params(),
        cost_estimate=cost(12e9, 8e6, 5.5e6),
        name="attn",
    )(joined, joined, joined, seg_row, seg_col)


def attn_back_kernel(
    q_ref, k_ref, v_ref, do_ref, lse_ref, del_ref, segr_ref, segc_ref, dq_ref, dk_ref, dv_ref,
    dk_acc, dv_acc,
):
    rows = q_ref.shape[0]
    scale = HD**-0.5
    k0, k1 = split_heads(k_ref[...] * BF(scale))
    v0, v1 = split_heads(v_ref[...])
    for q0, kv0, kv1, is_long in q_tiles(rows)[::-1]:
        q = q_ref[q0 : q0 + 256, :]
        do = do_ref[q0 : q0 + 256, :]
        qh = split_heads(q)
        doh = split_heads(do)
        allowed = diag_allowed(is_long, segr_ref[...], segc_ref[...])
        low_p, low_s = [], []
        dq = None
        for h, (k, v) in enumerate(((k0, v0), (k1, v1))):
            s = dot_t(k[kv0:kv1], q)
            dp = dot_t(v[kv0:kv1], do)
            lse = lse_ref[0, h : h + 1, q0 : q0 + 256]
            dlt = del_ref[0, h : h + 1, q0 : q0 + 256]
            diag = jnp.where(allowed, s[q0 - kv0 : q0 - kv0 + 256], NEG)
            parts = [diag] if kv1 - kv0 == 256 else [s[: q0 - kv0], diag]
            probs = jnp.concatenate([jnp.exp(p - lse) for p in parts], axis=0)
            ds = (probs * (dp - dlt)).astype(BF)
            low_p.append(probs.astype(BF))
            low_s.append(ds)
            part = dot_0(k[kv0:kv1], ds)
            dq = part if dq is None else dq + part
        dq_ref[q0 : q0 + 256, :] = dq.T.astype(BF)
        dv = dot(jnp.concatenate(low_p, axis=1), jnp.concatenate(doh, axis=0))
        dk = dot(jnp.concatenate(low_s, axis=1), jnp.concatenate(qh, axis=0))
        if q0 in (LONG, LONG - 256):
            dk_acc[kv0:kv1, :] = dk
            dv_acc[kv0:kv1, :] = dv
        else:
            dk_acc[kv0:kv1, :] += dk
            dv_acc[kv0:kv1, :] += dv
    dk_ref[...] = (dk_acc[...] * scale).astype(BF)
    dv_ref[...] = dv_acc[...].astype(BF)


def attn_back_call(joined, grad_att, lse, delta, seg_row, seg_col):
    rows = joined.shape[0]
    pairs = joined.shape[1] // 384
    blk = lambda off: pl.BlockSpec((rows, 128), lambda p: (0, off + p))
    stat = pl.BlockSpec((1, 2, rows), lambda p: (p, 0, 0))
    return pl.pallas_call(
        attn_back_kernel,
        grid=(pairs,),
        in_specs=[
            blk(0), blk(pairs), blk(2 * pairs), blk(0), stat, stat,
            full_spec((1, 256)), full_spec((256, 1)),
        ],
        out_specs=[blk(0), blk(0), blk(0)],
        out_shape=[jax.ShapeDtypeStruct((rows, pairs * 128), BF)] * 3,
        scratch_shapes=[pltpu.VMEM((rows, 128), F32)] * 2,
        compiler_params=params(),
        cost_estimate=cost(30e9, 12e6, 5.5e6),
        name="attn_back",
    )(joined, joined, joined, grad_att, lse, delta, seg_row, seg_col)


def proj_kernel(x_ref, a_ref, w_ref, pb_ref, g_ref, b_ref, mid_ref, n_ref):
    branch = dot(a_ref[...], w_ref[...]) + pb_ref[...]
    middle = x_ref[...].astype(F32) + BS * branch
    mid_ref[...] = middle
    xhat, _ = normalize(middle)
    n_ref[...] = (xhat * g_ref[...] + b_ref[...]).astype(BF)


def proj_call(x, att, w, pb, g, b):
    rows, d = x.shape
    br = 256
    row = pl.BlockSpec((br, d), lambda i: (i, 0))
    return pl.pallas_call(
        proj_kernel,
        grid=(rows // br,),
        in_specs=[row, row, full_spec((d, d)), full_spec((1, d)), full_spec((1, d)), full_spec((1, d))],
        out_specs=[row, row],
        out_shape=[jax.ShapeDtypeStruct((rows, d), F32), jax.ShapeDtypeStruct((rows, d), BF)],
        compiler_params=params(),
        cost_estimate=cost(2 * rows * d * d, rows * d * 10 + d * d * 2),
        name="proj",
    )(x, att, w, pb, g, b)


def mlp_kernel(
    n_ref, c_ref, mid_ref, wf_ref, fb_ref, wo_ref, ob_ref,
    out_ref, gn_ref, gwf_ref, gwo_ref, gfb_ref, gob_ref,
    nt_scr, mg_scr, acc_scr, act_scr, gp_scr,
):
    j = pl.program_id(0)
    rows = n_ref.shape[0]
    br = 256

    @pl.when(j == 0)
    def _():
        nt_scr[...] = n_ref[...].T
        total = jnp.zeros_like(gob_ref)
        for r in range(0, rows, br):
            mg = (BS * c_ref[r : r + br, :].astype(F32)).astype(BF)
            mg_scr[r : r + br, :] = mg
            total += jnp.sum(mg.astype(F32), axis=0, keepdims=True)
        gob_ref[...] = total

    bias_sum = jnp.zeros_like(gfb_ref)
    for r in range(0, rows, br):
        rr = slice(r, r + br)
        pre = dot(n_ref[rr, :], wf_ref[...]) + fb_ref[...]
        ga = dot_t(mg_scr[rr, :], wo_ref[...])
        sq = pre * pre
        t = jnp.tanh(GC0 * pre * (1.0 + GC1 * sq))
        half = 0.5 * (1.0 + t)
        act = (pre * half).astype(BF)
        slope = half + (0.5 * GC0) * pre * (1.0 - t * t) * (1.0 + (3.0 * GC1) * sq)
        gp = (slope * ga).astype(BF)
        act_scr[rr, :] = act
        gp_scr[rr, :] = gp
        bias_sum += jnp.sum(gp.astype(F32), axis=0, keepdims=True)
        fwd = dot(act, wo_ref[...])
        back = dot_t(gp, wf_ref[...])

        @pl.when(j == 0)
        def _():
            acc_scr[rr, :] = fwd
            gn_ref[rr, :] = back

        @pl.when(j > 0)
        def _():
            acc_scr[rr, :] += fwd
            gn_ref[rr, :] += back

    gfb_ref[...] = bias_sum
    gwf_ref[...] = dot(nt_scr[...], gp_scr[...]).astype(BF)
    gwo_ref[...] = dot_0(act_scr[...], mg_scr[...]).astype(BF)

    @pl.when(j == pl.num_programs(0) - 1)
    def _():
        for r in range(0, rows, br):
            rr = slice(r, r + br)
            out_ref[rr, :] = (mid_ref[rr, :] + BS * (acc_scr[rr, :] + ob_ref[...])).astype(BF)


def mlp_call(normed, cot, middle, w_fc, fc_bias, w_out, out_bias):
    rows, d = normed.shape
    ff = w_fc.shape[1]
    bc = 512
    return pl.pallas_call(
        mlp_kernel,
        grid=(ff // bc,),
        in_specs=[
            full_spec((rows, d)), full_spec((rows, d)), full_spec((rows, d)),
            pl.BlockSpec((d, bc), lambda j: (0, j)),
            pl.BlockSpec((1, bc), lambda j: (0, j)),
            pl.BlockSpec((bc, d), lambda j: (j, 0)),
            full_spec((1, d)),
        ],
        out_specs=[
            full_spec((rows, d)), full_spec((rows, d)),
            pl.BlockSpec((d, bc), lambda j: (0, j)),
            pl.BlockSpec((bc, d), lambda j: (j, 0)),
            pl.BlockSpec((1, bc), lambda j: (0, j)),
            full_spec((1, d)),
        ],
        out_shape=[
            jax.ShapeDtypeStruct((rows, d), BF),
            jax.ShapeDtypeStruct((rows, d), F32),
            jax.ShapeDtypeStruct((d, ff), BF),
            jax.ShapeDtypeStruct((ff, d), BF),
            jax.ShapeDtypeStruct((1, ff), F32),
            jax.ShapeDtypeStruct((1, d), F32),
        ],
        scratch_shapes=[
            pltpu.VMEM((d, rows), BF), pltpu.VMEM((rows, d), BF), pltpu.VMEM((rows, d), F32),
            pltpu.VMEM((rows, bc), BF), pltpu.VMEM((rows, bc), BF),
        ],
        compiler_params=params(),
        cost_estimate=cost(12 * rows * d * ff, 30e6, rows * ff),
        name="mlp",
    )(normed, cot, middle, w_fc, fc_bias, w_out, out_bias)


def proj_back_kernel(
    gn_ref, mid_ref, c_ref, a_ref, w_ref, g_ref, ind_ref,
    gm_ref, ga_ref, gw_ref, del_ref, gg_ref, gb_ref, gpb_ref, gw_acc,
):
    i = pl.program_id(0)

    @pl.when(i == 0)
    def _():
        gw_acc[...] = jnp.zeros_like(gw_acc)
        gg_ref[...] = jnp.zeros_like(gg_ref)
        gb_ref[...] = jnp.zeros_like(gb_ref)
        gpb_ref[...] = jnp.zeros_like(gpb_ref)

    dy = gn_ref[...]
    xhat, rstd = normalize(mid_ref[...])
    gg_ref[...] += jnp.sum(dy * xhat, axis=0, keepdims=True)
    gb_ref[...] += jnp.sum(dy, axis=0, keepdims=True)
    gm = c_ref[...].astype(F32) + ln_back(dy, xhat, rstd, g_ref[...])
    gm_ref[...] = gm
    pg = (BS * gm).astype(BF)
    gpb_ref[...] += jnp.sum(pg.astype(F32), axis=0, keepdims=True)
    gw_acc[...] += dot_0(a_ref[...], pg)
    ga = dot_t(pg, w_ref[...]).astype(BF)
    ga_ref[...] = ga
    prod = ga.astype(F32) * a_ref[...].astype(F32)
    high = prod.astype(BF)
    low = (prod - high.astype(F32)).astype(BF)
    del_ref[...] = dot_t(ind_ref[...], high) + dot_t(ind_ref[...], low)

    @pl.when(i == pl.num_programs(0) - 1)
    def _():
        gw_ref[...] = gw_acc[...].astype(BF)


def proj_back_call(gn, middle, cot, att, w, g, heads):
    rows, d = middle.shape
    br = 256
    row = pl.BlockSpec((br, d), lambda i: (i, 0))
    ind = (jnp.arange(16)[:, None] == jnp.arange(d)[None, :] // HD).astype(BF)
    vec = full_spec((1, d))
    vshape = jax.ShapeDtypeStruct((1, d), F32)
    return pl.pallas_call(
        proj_back_kernel,
        grid=(rows // br,),
        in_specs=[row, row, row, row, full_spec((d, d)), vec, full_spec((16, d))],
        out_specs=[row, row, full_spec((d, d)), pl.BlockSpec((16, br), lambda i: (0, i)), vec, vec, vec],
        out_shape=[
            jax.ShapeDtypeStruct((rows, d), F32),
            jax.ShapeDtypeStruct((rows, d), BF),
            jax.ShapeDtypeStruct((d, d), BF),
            jax.ShapeDtypeStruct((16, rows), F32),
            vshape, vshape, vshape,
        ],
        scratch_shapes=[pltpu.VMEM((d, d), F32)],
        compiler_params=params(),
        cost_estimate=cost(4 * rows * d * d, rows * d * 16),
        name="proj_back",
    )(gn, middle, cot, att, w, g, ind)


def qkv_back_kernel(
    x_ref, gm_ref, gq_ref, gk_ref, gv_ref, w_ref, g_ref, b_ref,
    gx_ref, gw_ref, gg_ref, gb_ref, gqb_ref, gvb_ref, nt_scr, acc_scr,
):
    j = pl.program_id(0)
    rows, d = x_ref.shape
    br = 256

    def block(src):
        gw_ref[...] = dot(nt_scr[...], src[...]).astype(BF)

        for r in range(0, rows, br):
            rr = slice(r, r + br)
            back = dot_t(src[rr, :], w_ref[...])

            @pl.when(j == 0)
            def _():
                acc_scr[rr, :] = back

            @pl.when(j > 0)
            def _():
                acc_scr[rr, :] += back

    def column_sum(src):
        total = jnp.zeros((1, d), F32)
        for r in range(0, rows, br):
            total += jnp.sum(src[r : r + br, :].astype(F32), axis=0, keepdims=True)
        return total

    @pl.when(j == 0)
    def _():
        for r in range(0, rows, br):
            xhat, _ = normalize(x_ref[r : r + br, :].astype(F32))
            nt_scr[:, r : r + br] = (xhat * g_ref[...] + b_ref[...]).astype(BF).T
        gqb_ref[...] = column_sum(gq_ref)
        gvb_ref[...] = column_sum(gv_ref)
        block(gq_ref)

    @pl.when(j == 1)
    def _():
        block(gk_ref)

    @pl.when(j == 2)
    def _():
        block(gv_ref)
        gg = jnp.zeros((1, d), F32)
        gb = jnp.zeros((1, d), F32)
        for r in range(0, rows, br):
            rr = slice(r, r + br)
            xhat, rstd = normalize(x_ref[rr, :].astype(F32))
            dy = acc_scr[rr, :]
            gg += jnp.sum(dy * xhat, axis=0, keepdims=True)
            gb += jnp.sum(dy, axis=0, keepdims=True)
            gx_ref[rr, :] = (gm_ref[rr, :] + ln_back(dy, xhat, rstd, g_ref[...])).astype(BF)
        gg_ref[...] = gg
        gb_ref[...] = gb


def qkv_back_call(x, gm, gq, gk, gv, w, g, b):
    rows, d = x.shape
    act = full_spec((rows, d))
    vec = full_spec((1, d))
    vshape = jax.ShapeDtypeStruct((1, d), F32)
    return pl.pallas_call(
        qkv_back_kernel,
        grid=(3,),
        in_specs=[act, act, act, act, act, pl.BlockSpec((d, d), lambda j: (0, j)), vec, vec],
        out_specs=[act, pl.BlockSpec((d, d), lambda j: (0, j)), vec, vec, vec, vec],
        out_shape=[
            jax.ShapeDtypeStruct((rows, d), BF),
            jax.ShapeDtypeStruct((d, 3 * d), BF),
            vshape, vshape, vshape, vshape,
        ],
        scratch_shapes=[pltpu.VMEM((d, rows), BF), pltpu.VMEM((rows, d), F32)],
        compiler_params=params(),
        cost_estimate=cost(12 * rows * d * d, rows * d * 20),
        name="qkv_back",
    )(x, gm, gq, gk, gv, w, g, b)


def pack_plan(counts, rows):
    c = [counts[i] for i in range(counts.shape[0])]
    ends, run = [], jnp.int32(0)
    for v in c:
        run = run + v
        ends.append(run)
    start = jnp.int32(0)
    for i in range(len(c) - 1):
        start = jnp.where(c[i] == LONG, ends[i] - c[i], start)
    rolled = jnp.arange(rows, dtype=jnp.int32)
    pos = rolled + start
    pos = jnp.where(pos >= rows, pos - rows, pos)
    seg = functools.reduce(jnp.add, [(pos >= e).astype(jnp.int32) for e in ends])
    valid = seg < len(c) - 1
    seg = jnp.where(valid, seg, 1000 + rolled)
    return start, seg[LONG:], valid


def roll_rows(array, shift):
    return lax.dynamic_slice_in_dim(jnp.concatenate([array, array], axis=0), shift, array.shape[0])


def per_device(
    tokens, lengths, ln1_gain, ln1_bias, w_qkv, qv_bias, w_proj, proj_bias, ln2_gain, ln2_bias,
    w_fc, fc_bias, w_out, out_bias, cotangent,
):
    rows, d = tokens.shape
    heads = d // HD
    r = w_qkv.shape[0]
    devices = d // r
    gather = lambda v: lax.all_gather(v, AXES, axis=0, tiled=True)
    scatter = lambda v: lax.psum_scatter(v, AXES, scatter_dimension=0, tiled=True)

    start, seg, valid = pack_plan(lengths[0], rows)
    seg_row, seg_col = seg[None, :], seg[:, None]
    x = roll_rows(tokens, start)
    cot = jnp.where(valid[:, None], roll_rows(cotangent, start), BF(0))

    vectors = [ln1_gain, ln1_bias, qv_bias, proj_bias, ln2_gain, ln2_bias, fc_bias, out_bias]
    flat = jnp.concatenate(vectors)
    flat = jnp.pad(flat, (0, r * 128 - flat.shape[0])).reshape(r, 128)
    first = gather(jnp.concatenate([w_qkv, w_proj, flat], axis=1))
    w_fc_all = gather(w_fc)
    w_out_all = gather(w_out)
    w_qkv_all = first[:, : 3 * d]
    w_proj_all = first[:, 3 * d : 4 * d]
    table = first[:, 4 * d :].reshape(devices, r * 128)
    rows_of, at = [], 0
    for v in vectors:
        size = v.shape[0]
        rows_of.append(table[:, at : at + size].reshape(1, -1).astype(F32))
        at += size
    g1, b1, qvb, pb, g2, b2, fb, ob = rows_of
    bias = jnp.concatenate([qvb[:, :d], jnp.zeros((1, d), F32), qvb[:, d:]], axis=1)

    joined = qkv_call(x, g1, b1, w_qkv_all, bias)
    att, lse = attn_call(joined, seg_row, seg_col)
    middle, normed_two = proj_call(x, att, w_proj_all, pb, g2, b2)
    out, gn, gw_fc, gw_out, gfb, gob = mlp_call(normed_two, cot, middle, w_fc_all, fb, w_out_all, ob)
    rs_fc = scatter(gw_fc)
    rs_out = scatter(gw_out)
    gm, ga, gw_proj, delta, gg2, gb2, gpb = proj_back_call(gn, middle, cot, att, w_proj_all, g2, heads)
    delta = delta[:heads].reshape(heads // 2, 2, rows)
    gq, gk, gv = attn_back_call(joined, ga, lse, delta, seg_row, seg_col)
    gx, gw_qkv, gg1, gb1, gqb, gvb = qkv_back_call(x, gm, gq, gk, gv, w_qkv_all, g1, b1)
    gqv = jnp.concatenate([gqb, gvb], axis=1)
    grads = [gg1, gb1, gqv, gpb, gg2, gb2, gfb, gob]
    back = jnp.concatenate([v.reshape(devices, -1) for v in grads], axis=1)
    back = jnp.pad(back, ((0, 0), (0, r * 128 - back.shape[1]))).reshape(d, 128)
    last = scatter(jnp.concatenate([gw_qkv, gw_proj, back.astype(BF)], axis=1))
    small = last[:, 4 * d :].reshape(-1).astype(F32)
    shares, at = [], 0
    for v in vectors:
        shares.append(small[at : at + v.shape[0]])
        at += v.shape[0]
    rg1, rb1, rqv, rpb, rg2, rb2, rfb, rob = shares
    restore = rows - start
    return (
        roll_rows(out, restore),
        roll_rows(gx, restore),
        rg1, rb1, last[:, : 3 * d].astype(F32), rqv, last[:, 3 * d : 4 * d].astype(F32), rpb,
        rg2, rb2, rs_fc.astype(F32), rfb, rs_out.astype(F32), rob,
    )


def solution(mesh):
    row, vec = P(AXES, None), P(AXES)
    in_specs = (row, row, vec, vec, row, vec, row, vec, vec, vec, row, vec, row, vec, row)
    out_specs = (row, row, vec, vec, row, vec, row, vec, vec, vec, row, vec, row, vec)
    return jax.shard_map(
        per_device, mesh=mesh, in_specs=in_specs, out_specs=out_specs, check_vma=False
    )
```

time: 915 us -> 711 us (0.78)
  matrix products: 275 us -> 0 us
  Pallas kernels: 0 us -> 141 us
  waiting for transfers between devices: 371 us -> 485 us
  blocking collectives: 84.3 us -> 0 us
  other arithmetic: 97.2 us -> 31 us
  local copies, waits for them, and re-layouts: 57.6 us -> 25.7 us
    dot_general x26 -> x0, matrix products: 275 us -> none  [the longest x4 38.3 us: contract_last(): lax.dot_general(left_side, right_side, (((1,), (1,)), ((), ())), preferre...]
    pallas_call x0 -> x7, Pallas kernels: none -> 141 us  [the longest x1 49.9 us: mlp_call(): pl.pallas_call(mlp_kernel, grid=(ff // bc,), in_specs=[full_spec((rows, d...]
    unnamed x8 -> x7, waiting for transfers between devices: 2.65 us -> 139 us
    unnamed x2 -> x0, blocking collectives: 84.3 us -> none
    reduce_scatter x4 -> x2, waiting for transfers between devices: 286 us -> 217 us  [per_device(): lax.psum_scatter(v, AXES, scatter_dimension=0, tiled=True)]
    all_gather x4 -> x3, waiting for transfers between devices: 81.9 us -> 129 us  [per_device(): gather = lambda v: lax.all_gather(v, AXES, axis=0, tiled=True)]
    convert_element_type x12 -> x9, other arithmetic: 51.6 us -> 8 us  [the longest x1 1.64 us: per_device(): rs_fc.astype(F32)]
    reduce_sum x13 -> x0, other arithmetic: 41.4 us -> none  [the longest x2 24.7 us: attend(): row_total = jnp.sum(exponent, axis=-1, keepdims=True)]
  transfers between devices with their start and end apart: 8 -> 6, of which waited for: 6 -> 6; matrix products, arithmetic and copies ran while one was open for 42% -> 5% of each run, Pallas kernels for 0% -> 5%
where the time goes in v1:
time: 711 us; the launch traced here: 703 us
  waiting for transfers between devices  485 us (68%)
  Pallas kernels  141 us (20%)
  other arithmetic  31 us (4%)
  local copies, waits for them, and re-layouts  25.7 us (4%)
  between operations  20.6 us (3%)
    reduce_scatter x2, waiting for transfers between devices, per_device(): lax.psum_scatter(v, AXES, scatter_dimension=0, tiled=True)  217 us
    unnamed x7, waiting for transfers between devices  139 us
    all_gather x3, waiting for transfers between devices, per_device(): gather = lambda v: lax.all_gather(v, AXES, axis=0, tiled=True)  129 us
    pallas_call x1, Pallas kernels, mlp_call(): pl.pallas_call(mlp_kernel, grid=(ff // bc,), in_specs=[full_spec((rows, d...  49.9 us
    pallas_call x1, Pallas kernels, qkv_back_call(): pl.pallas_call(qkv_back_kernel, grid=(3,), in_specs=[act, act, act, act,...  21.5 us
    pallas_call x1, Pallas kernels, attn_call(): pl.pallas_call(attn_kernel, grid=(pairs,), in_specs=[pl.BlockSpec((rows,...  21.1 us
    pallas_call x1, Pallas kernels, attn_back_call(): pl.pallas_call(attn_back_kernel, grid=(pairs,), in_specs=[blk(0), blk(pai...  20 us
  transfers between devices with their start and end apart: 6, of which 6 were waited for; matrix products, arithmetic and copies ran while one was open for 5% of the time, Pallas kernels for 5%

profile of v1, /device:TPU:0, one launch (start us, length us, event | category | flops | bytes accessed | tf_op | source)
XLA Modules:
  0.0 703.0 jit_solution(7685234217011254118)
XLA Ops:
  7.2 5.5 concatenate.33
  12.8 1.6 pad_maximum_fusion.1
  14.5 0.7 all-gather.6.cloned.1.call-update
  15.2 0.7 all-gather.8.cloned.1.call-update
  15.9 1.4 fusion.18
  23.2 0.7 add_select_fusion.1
  23.9 0.8 copy.31.segc_ref
  24.7 0.7 broadcast_compare_fusion
  25.4 4.0 fusion.4.x_ref
  29.4 0.6 fusion.5.ind_ref
  30.0 2.3 fusion.3.c_ref
  32.4 49.3 %all-gather.4.cloned.1.call-done = bf16[768,3200]{1,0:T(8,128)(2,1)} async-done(((bf16[24,3200]{1,0:T(8,128)(2,1)}), bf16[768,3200]{1,0:T(8,128)(2,1)}) %all-gather.4.cloned.1.call-update) | async-done | bytes 4915216 | tf_op jit(solution)/shard_map/all_gather | solution.py:530
  81.6 0.9 slice.129
  82.9 0.7 reshape.274.g_ref
  83.6 0.7 reshape.275.b_ref
  84.3 0.7 reshape.278.g_ref
  85.0 0.7 reshape.277.pb_ref
  85.7 0.7 reshape.279.b_ref
  86.3 0.7 reshape.281.ob_ref
  87.1 0.7 reshape.280.fb_ref
  87.8 4.1 slice.132.w_ref
  91.9 2.4 slice.136.w_ref
  94.2 0.6 fusion.6.bias_ref
  94.9 10.5 %qkv.1.q_ref.k_ref.v_ref = bf16[1024,2304]{1,0:T(8,128)(2,1)} custom-call(bf16[1024,768]{1,0:T(8,128)(2,1)} %fusion.4.x_ref, f32[1,768]{1,0:T(1,128)} %reshape.274.g_ref, f32[1,768]{1,0:T(1,128)} %reshape.275.b_ref, bf16[768,2304]{1,0:T(8,128)(2,1)} %slice.132.w_ref, f32[1,2304]{1,0:T(1,128)} %fusion.6.bias_ref), custom_call_target="tpu_custom_call" | custom-call | flops 3623878656 | bytes 9830400 | tf_op jit(solution)/shard_map/qkv/pallas_call | solution.py:80
  105.3 21.1 %attn.1 = (bf16[1024,768]{1,0:T(8,128)(2,1)}, f32[6,2,1024]{2,1,0:T(2,128)}) custom-call(bf16[1024,2304]{1,0:T(8,128)(2,1)} %qkv.1.q_ref.k_ref.v_ref, bf16[1024,2304]{1,0:T(8,128)(2,1)} %qkv.1.q_ref.k_ref.v_ref, bf16[1024,2304]{1,0:T(8,128)(2,1)} %qkv.1.q_ref.k_ref.v_ref, s32[1,256]{1,0:T(1,128)} %bitcast.17, s32[256,1]{1,0:T(8,128)} %copy.31.segc_ref), custom_call_target="tpu_custom_call" | custom-call | flops 12000000000 | bytes 8000000 | tf_op jit(solution)/shard_map/attn/pallas_call | solution.py:153
  126.5 6.4 proj.1
  132.9 14.1 %all-gather.6.cloned.1.call-done.wf_ref = bf16[768,3072]{1,0:T(8,128)(2,1)} async-done(((bf16[24,3072]{1,0:T(8,128)(2,1)}), bf16[768,3072]{1,0:T(8,128)(2,1)}) %all-gather.6.cloned.1.call-update) | async-done | bytes 4718608 | tf_op jit(solution)/shard_map/all_gather | solution.py:530
  147.0 65.4 %all-gather.8.cloned.1.call-done.wo_ref = bf16[3072,768]{1,0:T(8,128)(2,1)} async-done(((bf16[96,768]{1,0:T(8,128)(2,1)}), bf16[3072,768]{1,0:T(8,128)(2,1)}) %all-gather.8.cloned.1.call-update) | async-done | bytes 4718608 | tf_op jit(solution)/shard_map/all_gather | solution.py:530
  212.4 49.9 %mlp.1 = (bf16[1024,768]{1,0:T(8,128)(2,1)}, f32[1024,768]{1,0:T(8,128)}, bf16[768,3072]{1,0:T(8,128)(2,1)}, bf16[3072,768]{1,0:T(8,128)(2,1)}, f32[1,3072]{1,0:T(1,128)}, /*index=5*/f32[1,768]{1,0:T(1,128)}) custom-call(bf16[1024,768]{1,0:T(8,128)(2,1)} %get-tuple-element.41.n_ref, bf16[1024,768]{1,0:T(8,128)(2,1)} %fusion.3.c_ref, ...), custom_call_target="tpu_custom_call" | custom-call | flops 28991029248 | bytes 30000000 | tf_op jit(solution)/shard_map/mlp/pallas_call | solution.py:325
  262.3 11.4 %proj_back.1 = (f32[1024,768]{1,0:T(8,128)}, bf16[1024,768]{1,0:T(8,128)(2,1)}, bf16[768,768]{1,0:T(8,128)(2,1)}, f32[16,1024]{1,0:T(8,128)}, f32[1,768]{1,0:T(1...) custom-call(f32[1024,768]{1,0:T(8,128)} %get-tuple-element.44.gn_ref, f32[1024,768]{1,0:T(8,128)} %get-tuple-element.42.mid_ref, ...), custom_call_target="tpu_custom_call" | custom-call | flops 2415919104 | bytes 12582912 | tf_op jit(solution)/shard_map/proj_back/pallas_call | solution.py:401
  273.8 0.7 convert_reduce_fusion.2
  274.7 1.5 reshape.265.del_ref
  276.2 20.0 %attn_back.1 = (bf16[1024,768]{1,0:T(8,128)(2,1)}, bf16[1024,768]{1,0:T(8,128)(2,1)}, bf16[1024,768]{1,0:T(8,128)(2,1)}) custom-call(bf16[1024,2304]{1,0:T(8,128)(2,1)} %qkv.1.q_ref.k_ref.v_ref, bf16[1024,2304]{1,0:T(8,128)(2,1)} %qkv.1.q_ref.k_ref.v_ref, bf16[1024,2304]{1,0:T(8,128)(2,1)} %qkv.1.q_ref.k_ref.v_ref, ...), custom_call_target="tpu_custom_call" | custom-call | flops 30000001024 | bytes 12000000 | tf_op jit(solution)/shard_map/attn_back/pallas_call | solution.py:224
  296.2 21.5 %qkv_back.1 = (bf16[1024,768]{1,0:T(8,128)(2,1)}, bf16[768,2304]{1,0:T(8,128)(2,1)}, f32[1,768]{1,0:T(1,128)}, f32[1,768]{1,0:T(1,128)}, f32[1,768]{1,0:T(1,128)}, /*index=5*/f32[1,768]{1,0:T(1,128)}) custom-call(bf16[1024,768]{1,0:T(8,128)(2,1)} %fusion.4.x_ref, f32[1024,768]{1,0:T(8,128)} %get-tuple-element.45.gm_ref, ...), custom_call_target="tpu_custom_call" | custom-call | flops 7247757312 | bytes 15728640 | tf_op jit(solution)/shard_map/qkv_back/pallas_call | solution.py:483
  317.7 0.7 convert.49
  318.4 0.7 convert.50
  319.2 0.7 convert_reduce_fusion.5
  320.8 4.9 pad_maximum_fusion
  326.8 0.8 copy-done.1
  328.1 5.4 fusion
  333.5 136.8 %all-reduce.5.cloned.1.call-done = bf16[768,3200]{1,0:T(8,128)(2,1)} async-done(((bf16[768,3200]{1,0:T(8,128)(2,1)}), bf16[768,3200]{1,0:T(8,128)(2,1)}) %all-reduce.5.cloned.1.call-update) | async-done | bytes 4915216
  470.2 0.8 fusion.7
  472.2 1.5 dynamic-slice_convert_fusion.1
  474.3 1.6 dynamic-slice_convert_fusion
  475.9 105.9 %reduce-scatter.3.cloned.1.call-done = bf16[24,3072]{1,0:T(8,128)(2,1)} async-done(((bf16[768,3072]{1,0:T(8,128)(2,1)}), bf16[24,3072]{1,0:T(8,128)(2,1)}) %reduce-scatter.3.cloned.1.call-update) | async-done | bytes 147472 | tf_op jit(solution)/shard_map/reduce_scatter | solution.py:531
  581.8 1.6 convert_element_type.140
  583.4 110.7 %reduce-scatter.5.cloned.1.call-done = bf16[96,768]{1,0:T(8,128)(2,1)} async-done(((bf16[3072,768]{1,0:T(8,128)(2,1)}), bf16[96,768]{1,0:T(8,128)(2,1)}) %reduce-scatter.5.cloned.1.call-update) | async-done | bytes 147472 | tf_op jit(solution)/shard_map/reduce_scatter | solution.py:531
  694.1 1.6 convert_element_type.141
  (54 shorter events, 5.1 us)
Async XLA Ops:
  7.2 22.9 %copy-start = (bf16[1024,768]{1,0:T(8,128)(2,1)S(1)}, bf16[1024,768]{1,0:T(8,128)(2,1)}, u32[]{:S(2)}) copy-start(bf16[1024,768]{1,0:T(8,128)(2,1)} %param.29) | copy-start | bytes 4718596
  7.2 74.4 %all-gather.4.cloned.1.call-start = ((), (), s32[]{:S(2)}) async-start(), calls=%async_computation.2 | async-start | bytes 5068800 | tf_op jit(solution)/shard_map/all_gather | solution.py:530
  14.4 132.6 %all-gather.6.cloned.1.call-start = ((), (), s32[]{:S(2)}) async-start(), calls=%async_computation.3 | async-start | bytes 4866048 | tf_op jit(solution)/shard_map/all_gather | solution.py:530
  15.2 197.3 %all-gather.8.cloned.1.call-start = ((), (), s32[]{:S(2)}) async-start(), calls=%async_computation.4 | async-start | bytes 4866048 | tf_op jit(solution)/shard_map/all_gather | solution.py:530
  15.9 454.3 %all-reduce.5.cloned.1.call-start = ((), (), s32[]{:S(2)}) async-start(), calls=%async_computation.7 | async-start | bytes 9830400
  23.9 8.5 %copy-start.5 = (s32[256]{0:T(256)}, s32[256]{0:T(256)S(1)}, u32[]{:S(2)}) copy-start(s32[256]{0:T(256)S(1)} %slice.110) | copy-start | bytes 3076
  296.1 24.0 %copy-start.7 = (f32[1,768]{1,0:T(1,128)S(1)}, f32[1,768]{1,0:T(1,128)}, u32[]{:S(2)}) copy-start(f32[1,768]{1,0:T(1,128)} %get-tuple-element.59) | copy-start | bytes 9220
  296.1 24.1 %copy-start.4 = (f32[1,3072]{1,0:T(1,128)S(1)}, f32[1,3072]{1,0:T(1,128)}, u32[]{:S(2)}) copy-start(f32[1,3072]{1,0:T(1,128)} %get-tuple-element.62) | copy-start | bytes 36868
  296.1 24.3 %copy-start.6 = (f32[1,768]{1,0:T(1,128)S(1)}, f32[1,768]{1,0:T(1,128)}, u32[]{:S(2)}) copy-start(f32[1,768]{1,0:T(1,128)} %get-tuple-element.63) | copy-start | bytes 9220
  296.2 24.6 %copy-start.3 = (bf16[768,768]{1,0:T(8,128)(2,1)S(1)}, bf16[768,768]{1,0:T(8,128)(2,1)}, u32[]{:S(2)}) copy-start(bf16[768,768]{1,0:T(8,128)(2,1)} %get-tuple-element.54) | copy-start | bytes 3538948
  325.6 256.1 %reduce-scatter.3.cloned.1.call-start = ((), (), s32[]{:S(2)}) async-start(), calls=%async_computation.5 | async-start | bytes 4866048 | tf_op jit(solution)/shard_map/reduce_scatter | solution.py:531
  326.2 1.4 copy-start.1
  326.2 1.9 copy-start.2
  326.3 367.9 %reduce-scatter.5.cloned.1.call-start = ((), (), s32[]{:S(2)}) async-start(), calls=%async_computation.6 | async-start | bytes 4866048 | tf_op jit(solution)/shard_map/reduce_scatter | solution.py:531
Sparse Core Ops, SparseCore 0:
  14.5 67.0 all-gather.3
  84.5 62.4 all-gather.5
  149.9 62.4 all-gather.7
  325.8 144.4 all-reduce.4
  475.6 106.1 reduce-scatter.2
  588.0 106.0 reduce-scatter.4

commit v2 on v1

v2 whole, which is shorter than its diff:
```python
import functools
import math

import jax
import jax.numpy as jnp
from jax import lax
from jax.experimental import pallas as pl
from jax.experimental.pallas import tpu as pltpu
from jax.sharding import PartitionSpec as P

HD = 64
LONG = 768
EPS = 1e-05
BS = 1.0 / math.sqrt(48.0)
NEG = -1e30
F32 = jnp.float32
BF = jnp.bfloat16
VMEM_LIMIT = 58 * 1024 * 1024
AXES = ("dp", "fsdp")
GC0 = math.sqrt(2.0 / math.pi)
GC1 = 0.044715


def dot(a, b):
    return lax.dot_general(a, b, (((1,), (0,)), ((), ())), preferred_element_type=F32)


def dot_t(a, b):
    return lax.dot_general(a, b, (((1,), (1,)), ((), ())), preferred_element_type=F32)


def dot_0(a, b):
    return lax.dot_general(a, b, (((0,), (0,)), ((), ())), preferred_element_type=F32)


def params(grid_len=1):
    return pltpu.CompilerParams(
        dimension_semantics=("arbitrary",) * grid_len, vmem_limit_bytes=VMEM_LIMIT
    )


def cost(flops, nbytes, trans=0):
    return pl.CostEstimate(flops=int(flops), bytes_accessed=int(nbytes), transcendentals=int(trans))


def normalize(values):
    centred = values - jnp.mean(values, axis=-1, keepdims=True)
    rstd = lax.rsqrt(jnp.mean(centred * centred, axis=-1, keepdims=True) + EPS)
    return centred * rstd, rstd


def ln_back(dy, xhat, rstd, gain):
    dx = dy * gain
    m1 = jnp.mean(dx, axis=-1, keepdims=True)
    m2 = jnp.mean(dx * xhat, axis=-1, keepdims=True)
    return rstd * (dx - m1 - xhat * m2)


def full_spec(shape):
    return pl.BlockSpec(shape, lambda *_: (0,) * len(shape))


def lane_masks(rows):
    lane = lax.broadcasted_iota(jnp.int32, (rows, 128), 1)
    return lane < HD


def split_heads(block):
    low = lane_masks(block.shape[0])
    zero = jnp.zeros_like(block)
    return jnp.where(low, block, zero), jnp.where(low, zero, block)


def q_tiles(rows):
    tiles = [(r, 0, r + 256, True) for r in range(0, LONG, 256)]
    tiles += [(LONG, LONG, rows, False)]
    return tiles


def diag_allowed(is_long, seg_row, seg_col):
    kv = lax.broadcasted_iota(jnp.int32, (256, 256), 0)
    qp = lax.broadcasted_iota(jnp.int32, (256, 256), 1)
    allowed = kv <= qp
    if not is_long:
        allowed = allowed & (seg_col == seg_row)
    return allowed


def attn_kernel(q_ref, k_ref, v_ref, segr_ref, segc_ref, o_ref, lse_ref):
    rows = q_ref.shape[0]
    k0, k1 = split_heads(k_ref[...] * BF(HD**-0.5))
    v0, v1 = split_heads(v_ref[...])
    for q0, kv0, kv1, is_long in q_tiles(rows):
        q = q_ref[q0 : q0 + 256, :]
        allowed = diag_allowed(is_long, segr_ref[...], segc_ref[...])
        outs = []
        for h, (k, v) in enumerate(((k0, v0), (k1, v1))):
            s = dot_t(k[kv0:kv1], q)
            diag = jnp.where(allowed, s[q0 - kv0 : q0 - kv0 + 256], NEG)
            parts = [diag] if kv1 - kv0 == 256 else [s[: q0 - kv0], diag]
            top = functools.reduce(
                jnp.maximum, [jnp.max(p, axis=0, keepdims=True) for p in parts]
            )
            exps = [jnp.exp(p - top) for p in parts]
            total = functools.reduce(
                jnp.add, [jnp.sum(e, axis=0, keepdims=True) for e in exps]
            )
            lse_ref[0, h : h + 1, q0 : q0 + 256] = top + jnp.log(total)
            probs = jnp.concatenate([e.astype(BF) for e in exps], axis=0)
            outs.append(dot_0(v[kv0:kv1], probs) * (1.0 / total))
        o_ref[q0 : q0 + 256, :] = (outs[0] + outs[1]).T.astype(BF)


def attn_call(joined, seg_row, seg_col):
    rows = joined.shape[0]
    pairs = joined.shape[1] // 384
    return pl.pallas_call(
        attn_kernel,
        grid=(pairs,),
        in_specs=[pl.BlockSpec((rows, 128), lambda p, t=t: (0, pair_block(p, pairs) * 3 + t)) for t in range(3)]
        + [full_spec((1, 256)), full_spec((256, 1))],
        out_specs=[
            pl.BlockSpec((rows, 128), lambda p: (0, p)),
            pl.BlockSpec((1, 2, rows), lambda p: (p, 0, 0)),
        ],
        out_shape=[
            jax.ShapeDtypeStruct((rows, pairs * 128), BF),
            jax.ShapeDtypeStruct((pairs, 2, rows), F32),
        ],
        compiler_params=params(),
        cost_estimate=cost(24e9, 8e6, 5.5e6),
        name="attn",
    )(joined, joined, joined, seg_row, seg_col)


def pair_block(p, pairs):
    return (p % 2) * (pairs // 2) + p // 2


ANY = pl.BlockSpec(memory_space=pl.ANY)
SMEM = pl.BlockSpec(memory_space=pltpu.SMEM)


def local_copy(src, dst, sem):
    return pltpu.make_async_copy(src, dst, sem)


def chips_of(dims, where_ref):
    z_n, y_n, x_n = dims
    zi, yi, xi = [where_ref[i] for i in range(3)]
    for i in range(y_n * x_n):
        for j in range(z_n):
            yield i, j, lax.rem(zi + j, z_n), lax.rem(yi + i // x_n, y_n), lax.rem(xi + i % x_n, x_n)


def piece_at(dims, arrays, i, j):
    at = i * dims[0] + j
    for a in arrays:
        if at < a.shape[0]:
            return a.at[at]
        at -= a.shape[0]


def load_columns(dims, where_ref, own, oth, first, cols, dst, sem):
    ci = where_ref[3]
    for i, j, z, y, x in chips_of(dims, where_ref):
        for half, src in ((ci, own), (1 - ci, oth)):
            block = piece_at(dims, src, i, j).at[:, pl.ds(first, cols)]
            local_copy(block, dst.at[half, z, y, x], sem.at[half, z, y, x]).start()


def wait_columns(dims, dst, sem, half):
    for z in range(dims[0]):
        for y in range(dims[1]):
            for x in range(dims[2]):
                block = dst.at[half, z, y, x]
                local_copy(block, block, sem.at[half, z, y, x]).wait()


def flat2(value):
    return value.reshape(-1, value.shape[-1])


def store_columns(dims, where_ref, src, own, oth, half, first, cols, sem):
    ci = where_ref[3]
    for other, out in ((False, own), (True, oth)):

        @pl.when((half != ci) if other else (half == ci))
        def _():
            for i, j, z, y, x in chips_of(dims, where_ref):
                local_copy(src.at[z, y, x], out.at[i, j, :, pl.ds(first, cols)], sem.at[i, j]).start()


def wait_store(dims, src, out, first, cols, sem):
    for i in range(dims[1] * dims[2]):
        for j in range(dims[0]):
            local_copy(src.at[0, 0, 0], out.at[i, j, :, pl.ds(first, cols)], sem.at[i, j]).wait()


def weight_scratch(dims, n, cols):
    return [
        pltpu.VMEM((2,) + dims + (n, cols), BF),
        pltpu.SemaphoreType.DMA((2,) + dims),
    ]


def vector_plan(d, devices):
    r = d // devices
    return {
        "g1": (0, 0, r), "b1": (0, r, r), "qv": (0, 2 * r, 2 * r), "fb": (1, 0, 4 * r),
        "pb": (2, 0, r), "g2": (2, r, r), "b2": (2, 2 * r, r), "ob": (2, 3 * r, r),
    }


VECTOR_ROWS = ("g1", "b1", "qv", "pb", "g2", "b2", "fb", "ob")


def owner_of(shape, size, axis):
    c = lax.broadcasted_iota(jnp.int32, shape, axis).astype(F32)
    owner = jnp.floor((c + 0.5) * (1.0 / size))
    return owner, c - owner * size


def row_pick(devices, d, row):
    r = d // devices
    at = lax.broadcasted_iota(jnp.int32, (devices, d), 1)
    dev = lax.broadcasted_iota(jnp.int32, (devices, d), 0)
    return (at == dev * r + row).astype(BF)


def vector_maps(devices, n, first, size):
    owner, place = owner_of((devices, n), size, 1)
    mine = owner == lax.broadcasted_iota(jnp.int32, (devices, n), 0).astype(F32)
    _, place = owner_of((128, n), size, 1)
    spot = (place + first == lax.broadcasted_iota(jnp.int32, (128, n), 0).astype(F32)).astype(BF)
    return mine, spot


def unpack_vectors(table, d, devices, out_ref):
    plan = vector_plan(d, devices)
    picked = [dot(row_pick(devices, d, k), table).astype(BF) for k in range(3)]
    for i, name in enumerate(VECTOR_ROWS):
        k, first, size = plan[name]
        n = size * devices
        mine, spot = vector_maps(devices, n, first, size)
        spread = dot(picked[k], spot)
        out_ref[i : i + 1, :n] = jnp.sum(jnp.where(mine, spread, 0.0), axis=0, keepdims=True)


def pack_vectors(rows, d, devices):
    plan = vector_plan(d, devices)
    parts = [None] * 3
    for name in VECTOR_ROWS:
        k, first, size = plan[name]
        n = size * devices
        mine, spot = vector_maps(devices, n, first, size)
        part = dot_t(jnp.where(mine, rows[name], 0.0).astype(BF), spot)
        parts[k] = part if parts[k] is None else parts[k] + part
    total = None
    for k in range(3):
        piece = dot_0(row_pick(devices, d, k), parts[k].astype(BF))
        total = piece if total is None else total + piece
    return total.astype(BF)


def qkv_kernel(dims, count, devices, where_ref, x_ref, *refs):
    own, oth = refs[:count], refs[count : 2 * count]
    o_ref, vec_ref, w_scr, w_sem, t_scr, t_sem, n_scr, bias_scr = refs[2 * count :]
    rows, d = x_ref.shape
    cols = w_scr.shape[-1]
    table_at = own[0].shape[-1] - 128
    step = pl.program_id(0)

    @pl.when(step == 0)
    def _():
        for i, j, z, y, x in chips_of(dims, where_ref):
            block = piece_at(dims, own, i, j).at[:, pl.ds(table_at, 128)]
            local_copy(block, t_scr.at[z, y, x], t_sem.at[z, y, x]).start()
        load_columns(dims, where_ref, own, oth, 0, cols, w_scr, w_sem)
        for z in range(dims[0]):
            for y in range(dims[1]):
                for x in range(dims[2]):
                    block = t_scr.at[z, y, x]
                    local_copy(block, block, t_sem.at[z, y, x]).wait()
        vec_ref[...] = jnp.zeros_like(vec_ref)
        unpack_vectors(flat2(t_scr[...]), d, devices, vec_ref)
        zero = jnp.zeros((1, 128), F32)
        pairs = d // 128
        for p in range(pairs):
            at = pair_block(p, pairs) * 384
            half, at = at // cols, at % cols
            bias_scr[half, :, at : at + 128] = vec_ref[2:3, p * 128 : (p + 1) * 128]
            bias_scr[half, :, at + 128 : at + 256] = zero
            bias_scr[half, :, at + 256 : at + 384] = vec_ref[2:3, d + p * 128 : d + (p + 1) * 128]
        for r in range(0, rows, 256):
            xhat, _ = normalize(x_ref[r : r + 256, :].astype(F32))
            n_scr[r : r + 256, :] = (xhat * vec_ref[0:1, :d] + vec_ref[1:2, :d]).astype(BF)
        wait_columns(dims, w_scr, w_sem, 0)

    @pl.when(step == 1)
    def _():
        wait_columns(dims, w_scr, w_sem, 1)

    w = flat2(w_scr[step])
    for r in range(0, rows, 256):
        o_ref[r : r + 256, :] = (dot(n_scr[r : r + 256, :], w) + bias_scr[step]).astype(BF)


def qkv_call(dims, where, x, own, oth, devices):
    rows, d = x.shape
    n = own[0].shape[1]
    cols = 3 * d // 2
    return pl.pallas_call(
        functools.partial(qkv_kernel, dims, len(own), devices),
        grid=(2,),
        in_specs=[SMEM, full_spec((rows, d))] + [ANY] * (2 * len(own)),
        out_specs=[pl.BlockSpec((rows, cols), lambda j: (0, j)), full_spec((8, 4 * d))],
        out_shape=[
            jax.ShapeDtypeStruct((rows, 2 * cols), BF), jax.ShapeDtypeStruct((8, 4 * d), F32)
        ],
        scratch_shapes=weight_scratch(dims, n, cols)
        + [
            pltpu.VMEM(dims + (n, 128), BF), pltpu.SemaphoreType.DMA(dims),
            pltpu.VMEM((rows, d), BF), pltpu.VMEM((2, 1, cols), F32),
        ],
        compiler_params=params(),
        cost_estimate=cost(4 * rows * d * cols, rows * d * 8 + d * cols * 4),
        name="qkv",
    )(where, x, *own, *oth)


def proj_kernel(dims, count, first, where_ref, x_ref, a_ref, vec_ref, *refs):
    own, oth = refs[:count], refs[count : 2 * count]
    mid_ref, n_ref, w_scr, w_sem = refs[2 * count :]
    d = x_ref.shape[1]

    @pl.when(pl.program_id(0) == 0)
    def _():
        load_columns(dims, where_ref, own, oth, first, w_scr.shape[-1], w_scr, w_sem)
        for h in range(2):
            wait_columns(dims, w_scr, w_sem, h)

    a = a_ref[...]
    branch = jnp.concatenate([dot(a, flat2(w_scr[h])) for h in range(2)], axis=1) + vec_ref[3:4, :d]
    middle = x_ref[...].astype(F32) + BS * branch
    mid_ref[...] = middle
    xhat, _ = normalize(middle)
    n_ref[...] = (xhat * vec_ref[4:5, :d] + vec_ref[5:6, :d]).astype(BF)


def proj_call(dims, where, x, att, vec, own, oth):
    rows, d = x.shape
    br = 256
    row = pl.BlockSpec((br, d), lambda i: (i, 0))
    return pl.pallas_call(
        functools.partial(proj_kernel, dims, len(own), 3 * d // 2),
        grid=(rows // br,),
        in_specs=[SMEM, row, row, full_spec(vec.shape)] + [ANY] * (2 * len(own)),
        out_specs=[row, row],
        out_shape=[jax.ShapeDtypeStruct((rows, d), F32), jax.ShapeDtypeStruct((rows, d), BF)],
        scratch_shapes=weight_scratch(dims, own[0].shape[1], d // 2),
        compiler_params=params(),
        cost_estimate=cost(2 * rows * d * d, rows * d * 10 + d * d * 2),
        name="proj",
    )(where, x, att, vec, *own, *oth)


def hidden_parts(dims, n, d):
    per = min(n, d)
    return per, d // per


def mlp_kernel(dims, count, where_ref, n_ref, c_ref, mid_ref, vec_ref, *refs):
    fc_own, fc_oth = refs[: count[0]], refs[count[0] : 2 * count[0]]
    refs = refs[2 * count[0] :]
    out_own, out_oth = refs[: count[1]], refs[count[1] : 2 * count[1]]
    (
        out_ref, gn_ref, gfb_ref, gob_ref, gf_own, gf_oth, go_own, go_oth,
        nt_scr, mg_scr, acc_scr, act_scr, gp_scr, f_scr, f_sem, o_scr, o_sem, gf_scr, gf_sem, go_scr, go_sem,
    ) = refs[2 * count[1] :]
    z_n, y_n, x_n = dims
    zi, yi, xi, ci = [where_ref[i] for i in range(4)]
    j = pl.program_id(0)
    blocks = o_scr.shape[0]
    rows, d = n_ref.shape
    n = out_own[0].shape[1]
    per, parts = hidden_parts(dims, n, d)
    br = 256

    @pl.when(j == 0)
    def _():
        load_columns(dims, where_ref, fc_own, fc_oth, 0, f_scr.shape[-1], f_scr, f_sem)
        for i, s, z, y, x in chips_of(dims, where_ref):
            for core, src in ((ci, out_own), (1 - ci, out_oth)):
                for q in range(n // per):
                    at = (((z * y_n + y) * x_n + x) * 2 + core) * n + q * per
                    blk, off = at // d, lax.rem(at, d)
                    local_copy(
                        piece_at(dims, src, i, s).at[pl.ds(q * per, per), :],
                        o_scr.at[blk, pl.ds(pl.multiple_of(off, 16), per), :],
                        o_sem.at[blk, off // per],
                    ).start()
        nt_scr[...] = n_ref[...].T
        total = jnp.zeros_like(gob_ref)
        for r in range(0, rows, br):
            mg = (BS * c_ref[r : r + br, :].astype(F32)).astype(BF)
            mg_scr[r : r + br, :] = mg
            total += jnp.sum(mg.astype(F32), axis=0, keepdims=True)
        gob_ref[...] = total
        wait_columns(dims, f_scr, f_sem, 0)

    @pl.when(j == blocks // 2)
    def _():
        wait_columns(dims, f_scr, f_sem, 1)

    for q in range(parts):
        part = o_scr.at[j, pl.ds(q * per, per), :]
        local_copy(part, part, o_sem.at[j, q]).wait()

    half = j // (blocks // 2)
    first = pl.multiple_of(lax.rem(j, blocks // 2) * d, 128)
    wf = flat2(f_scr[half, :, :, :, :, pl.ds(first, d)])
    wo = o_scr[j]
    fb = vec_ref[6:7, pl.ds(pl.multiple_of(j * d, 128), d)]
    bias_sum = jnp.zeros((1, d), F32)
    for r in range(0, rows, br):
        rr = slice(r, r + br)
        pre = dot(n_ref[rr, :], wf) + fb
        ga = dot_t(mg_scr[rr, :], wo)
        sq = pre * pre
        t = jnp.tanh(GC0 * pre * (1.0 + GC1 * sq))
        half_t = 0.5 * (1.0 + t)
        act = (pre * half_t).astype(BF)
        slope = half_t + (0.5 * GC0) * pre * (1.0 - t * t) * (1.0 + (3.0 * GC1) * sq)
        gp = (slope * ga).astype(BF)
        act_scr[rr, :] = act
        gp_scr[rr, :] = gp
        bias_sum += jnp.sum(gp.astype(F32), axis=0, keepdims=True)
        fwd = dot(act, wo)
        back = dot_t(gp, wf)

        @pl.when(j == 0)
        def _():
            acc_scr[rr, :] = fwd
            gn_ref[rr, :] = back

        @pl.when(j > 0)
        def _():
            acc_scr[rr, :] += fwd
            gn_ref[rr, :] += back

    gfb_ref[...] = bias_sum
    gf_scr[j] = dot(nt_scr[...], gp_scr[...]).astype(BF).reshape(gf_scr.shape[1:])
    store_columns(dims, where_ref, gf_scr.at[j], gf_own, gf_oth, half, first, d, gf_sem.at[j])
    go_scr[j] = dot_0(act_scr[...], mg_scr[...]).astype(BF)
    for q in range(parts):
        at = j * d + q * per
        dev = at // n
        core = lax.rem(dev, 2)
        x = lax.rem(dev // 2, x_n)
        y = lax.rem(dev // (2 * x_n), y_n)
        z = dev // (2 * x_n * y_n)
        piece = lax.rem(y - yi + y_n, y_n) * x_n + lax.rem(x - xi + x_n, x_n)
        slot = lax.rem(z - zi + z_n, z_n)
        off = pl.multiple_of(lax.rem(at, n), 16)
        for other, out in ((False, go_own), (True, go_oth)):

            @pl.when((core != ci) if other else (core == ci))
            def _():
                local_copy(
                    go_scr.at[j, pl.ds(q * per, per), :], out.at[piece, slot, pl.ds(off, per), :], go_sem.at[j, q]
                ).start()

    @pl.when(j == blocks - 1)
    def _():
        for r in range(0, rows, br):
            rr = slice(r, r + br)
            out_ref[rr, :] = (mid_ref[rr, :] + BS * (acc_scr[rr, :] + vec_ref[7:8, :d])).astype(BF)
        for b in range(blocks):
            wait_store(dims, gf_scr.at[b], gf_own, 0, d, gf_sem.at[b])
            for q in range(parts):
                part = go_scr.at[b, pl.ds(q * per, per), :]
                local_copy(part, part, go_sem.at[b, q]).wait()


def mlp_call(dims, where, normed, cot, middle, vec, fc, out):
    rows, d = normed.shape
    n, half = fc[0][0].shape[1:]
    blocks = 2 * half // d
    n_out = out[0][0].shape[1]
    per, parts = hidden_parts(dims, n_out, d)
    count = dims[1] * dims[2]
    act = full_spec((rows, d))
    f_piece = jax.ShapeDtypeStruct((count, dims[0], n, half), BF)
    o_piece = jax.ShapeDtypeStruct((count, dims[0], n_out, d), BF)
    return pl.pallas_call(
        functools.partial(mlp_kernel, dims, (len(fc[0]), len(out[0]))),
        grid=(blocks,),
        in_specs=[SMEM, act, act, act, full_spec(vec.shape)] + [ANY] * (2 * (len(fc[0]) + len(out[0]))),
        out_specs=[act, act, pl.BlockSpec((1, d), lambda j: (0, j)), full_spec((1, d))] + [ANY] * 4,
        out_shape=[
            jax.ShapeDtypeStruct((rows, d), BF),
            jax.ShapeDtypeStruct((rows, d), F32),
            jax.ShapeDtypeStruct((1, 2 * half), F32),
            jax.ShapeDtypeStruct((1, d), F32),
            f_piece, f_piece, o_piece, o_piece,
        ],
        scratch_shapes=[
            pltpu.VMEM((d, rows), BF), pltpu.VMEM((rows, d), BF), pltpu.VMEM((rows, d), F32),
            pltpu.VMEM((rows, d), BF), pltpu.VMEM((rows, d), BF),
        ]
        + weight_scratch(dims, n, half)
        + [
            pltpu.VMEM((blocks, d, d), BF), pltpu.SemaphoreType.DMA((blocks, parts)),
            pltpu.VMEM((blocks,) + dims + (n, d), BF), pltpu.SemaphoreType.DMA((blocks, count, dims[0])),
            pltpu.VMEM((blocks, d, d), BF), pltpu.SemaphoreType.DMA((blocks, parts)),
        ],
        compiler_params=params(),
        cost_estimate=cost(24 * rows * d * half, 30e6, rows * half),
        name="mlp",
    )(where, normed, cot, middle, vec, *fc[0], *fc[1], *out[0], *out[1])


def proj_back_kernel(dims, count, first, where_ref, gn_ref, mid_ref, c_ref, a_ref, vec_ref, ind_ref, *refs):
    own, oth = refs[:count], refs[count : 2 * count]
    (
        gm_ref, ga_ref, gw_ref, del_ref, gg_ref, gb_ref, gpb_ref, gw_acc, w_scr, w_sem,
    ) = refs[2 * count :]
    i = pl.program_id(0)
    d = mid_ref.shape[1]
    m = d // 2

    @pl.when(i == 0)
    def _():
        load_columns(dims, where_ref, own, oth, first, m, w_scr, w_sem)
        gw_acc[...] = jnp.zeros_like(gw_acc)
        gg_ref[...] = jnp.zeros_like(gg_ref)
        gb_ref[...] = jnp.zeros_like(gb_ref)
        gpb_ref[...] = jnp.zeros_like(gpb_ref)
        for h in range(2):
            wait_columns(dims, w_scr, w_sem, h)

    dy = gn_ref[...]
    xhat, rstd = normalize(mid_ref[...])
    gg_ref[...] += jnp.sum(dy * xhat, axis=0, keepdims=True)
    gb_ref[...] += jnp.sum(dy, axis=0, keepdims=True)
    gm = c_ref[...].astype(F32) + ln_back(dy, xhat, rstd, vec_ref[4:5, :d])
    gm_ref[...] = gm
    pg = (BS * gm).astype(BF)
    gpb_ref[...] += jnp.sum(pg.astype(F32), axis=0, keepdims=True)
    gw_acc[...] += dot_0(a_ref[...], pg)
    ga = (dot_t(pg[:, :m], flat2(w_scr[0])) + dot_t(pg[:, m:], flat2(w_scr[1]))).astype(BF)
    ga_ref[...] = ga
    prod = ga.astype(F32) * a_ref[...].astype(F32)
    high = prod.astype(BF)
    low = (prod - high.astype(F32)).astype(BF)
    del_ref[...] = dot_t(ind_ref[...], high) + dot_t(ind_ref[...], low)

    @pl.when(i == pl.num_programs(0) - 1)
    def _():
        gw_ref[...] = gw_acc[...].astype(BF)


def proj_back_call(dims, where, gn, middle, cot, att, vec, own, oth):
    rows, d = middle.shape
    br = 256
    row = pl.BlockSpec((br, d), lambda i: (i, 0))
    ind = (jnp.arange(16)[:, None] == jnp.arange(d)[None, :] // HD).astype(BF)
    one = full_spec((1, d))
    vshape = jax.ShapeDtypeStruct((1, d), F32)
    return pl.pallas_call(
        functools.partial(proj_back_kernel, dims, len(own), 3 * d // 2),
        grid=(rows // br,),
        in_specs=[SMEM, row, row, row, row, full_spec(vec.shape), full_spec((16, d))] + [ANY] * (2 * len(own)),
        out_specs=[row, row, full_spec((d, d)), pl.BlockSpec((16, br), lambda i: (0, i)), one, one, one],
        out_shape=[
            jax.ShapeDtypeStruct((rows, d), F32),
            jax.ShapeDtypeStruct((rows, d), BF),
            jax.ShapeDtypeStruct((d, d), BF),
            jax.ShapeDtypeStruct((16, rows), F32),
            vshape, vshape, vshape,
        ],
        scratch_shapes=[pltpu.VMEM((d, d), F32)] + weight_scratch(dims, own[0].shape[1], d // 2),
        compiler_params=params(),
        cost_estimate=cost(4 * rows * d * d, rows * d * 16),
        name="proj_back",
    )(where, gn, middle, cot, att, vec, ind, *own, *oth)


def pair_back(j_ref, do_ref, lse_ref, del_ref, segr_ref, segc_ref, dj_ref, dk_acc, dv_acc):
    rows = j_ref.shape[0]
    scale = HD**-0.5
    k0, k1 = split_heads(j_ref[:, 128:256] * BF(scale))
    v0, v1 = split_heads(j_ref[:, 256:384])
    for q0, kv0, kv1, is_long in q_tiles(rows)[::-1]:
        q = j_ref[q0 : q0 + 256, 0:128]
        do = do_ref[q0 : q0 + 256, :]
        qh = split_heads(q)
        doh = split_heads(do)
        allowed = diag_allowed(is_long, segr_ref[...], segc_ref[...])
        low_p, low_s = [], []
        dq = None
        for h, (k, v) in enumerate(((k0, v0), (k1, v1))):
            s = dot_t(k[kv0:kv1], q)
            dp = dot_t(v[kv0:kv1], do)
            lse = lse_ref[0, h : h + 1, q0 : q0 + 256]
            dlt = del_ref[0, h : h + 1, q0 : q0 + 256]
            diag = jnp.where(allowed, s[q0 - kv0 : q0 - kv0 + 256], NEG)
            parts = [diag] if kv1 - kv0 == 256 else [s[: q0 - kv0], diag]
            probs = jnp.concatenate([jnp.exp(p - lse) for p in parts], axis=0)
            low_p.append(probs.astype(BF))
            ds = (probs * (dp - dlt)).astype(BF)
            low_s.append(ds)
            part = dot_0(k[kv0:kv1], ds)
            dq = part if dq is None else dq + part
        dj_ref[q0 : q0 + 256, 0:128] = dq.T.astype(BF)
        dv = dot(jnp.concatenate(low_p, axis=1), jnp.concatenate(doh, axis=0))
        dk = dot(jnp.concatenate(low_s, axis=1), jnp.concatenate(qh, axis=0))
        if q0 in (LONG, LONG - 256):
            dk_acc[kv0:kv1, :] = dk
            dv_acc[kv0:kv1, :] = dv
        else:
            dk_acc[kv0:kv1, :] += dk
            dv_acc[kv0:kv1, :] += dv
    dj_ref[:, 128:256] = (dk_acc[...] * scale).astype(BF)
    dj_ref[:, 256:384] = dv_acc[...].astype(BF)


def attn_back_kernel(
    dims, count, group0, groups, last, devices, where_ref, j_ref, do_ref, lse_ref, del_ref, segr_ref, segc_ref,
    x_ref, vec_ref, *refs,
):
    own, oth, refs = refs[:count], refs[count : 2 * count], refs[2 * count :]
    if last:
        gnin_ref, qvin_ref, gm_ref, gfb_ref, gob_ref, gg2_ref, gb2_ref, gpb_ref = refs[:8]
        gx_ref, g_own, g_oth = refs[8:11]
        refs = refs[11:]
    else:
        gwp_ref, gn_out, qv_out, g_own, g_oth = refs[:5]
        refs = refs[5:]
    w_scr, w_sem, nt_scr, gn_scr, dj_scr, dk_acc, dv_acc, gw_scr, gw_sem, e_scr, e_sem, qv_scr = refs
    i = pl.program_id(0)
    rows, d = x_ref.shape
    half, group = lax.rem(i, 2), i // 2
    br = 256
    extra_at = groups * 384

    @pl.when(i == 0)
    def _():
        load_columns(dims, where_ref, own, oth, group0 * 384, groups * 384, w_scr, w_sem)
        if not last:
            for h in range(2):
                e_scr[h] = gwp_ref[:, h * (d // 2) : (h + 1) * (d // 2)].reshape(e_scr.shape[1:])
                store_columns(dims, where_ref, e_scr.at[h], g_own, g_oth, h, extra_at, d // 2, e_sem.at[h])
            qv_scr[...] = jnp.zeros_like(qv_scr)
            gn_scr[...] = jnp.zeros_like(gn_scr)
        else:
            qv_scr[...] = qvin_ref[...]
            gn_scr[...] = gnin_ref[...]
        for r in range(0, rows, br):
            xhat, _ = normalize(x_ref[r : r + br, :].astype(F32))
            nt_scr[:, r : r + br] = (xhat * vec_ref[0:1, :d] + vec_ref[1:2, :d]).astype(BF).T
        for h in range(2):
            wait_columns(dims, w_scr, w_sem, h)

    pair_back(j_ref, do_ref, lse_ref, del_ref, segr_ref, segc_ref, dj_scr, dk_acc, dv_acc)
    first = pl.multiple_of(group * 384, 128)
    dj = dj_scr[...]
    pair = group0 * 2 + i
    qv_scr[:, pl.ds(pl.multiple_of(pair * 128, 128), 128)] = jnp.sum(
        dj[:, 0:128].astype(F32), axis=0, keepdims=True
    )
    qv_scr[:, pl.ds(pl.multiple_of(d + pair * 128, 128), 128)] = jnp.sum(
        dj[:, 256:384].astype(F32), axis=0, keepdims=True
    )
    gw_scr[i] = dot(nt_scr[...], dj).astype(BF).reshape(gw_scr.shape[1:])
    store_columns(dims, where_ref, gw_scr.at[i], g_own, g_oth, half, first, 384, gw_sem.at[i])
    w = flat2(w_scr[half, :, :, :, :, pl.ds(first, 384)])
    for r in range(0, rows, br):
        gn_scr[r : r + br, :] += dot_t(dj[r : r + br, :], w)

    @pl.when(i == 2 * groups - 1)
    def _():
        if last:
            gg = jnp.zeros((1, d), F32)
            gb = jnp.zeros((1, d), F32)
            for r in range(0, rows, br):
                rr = slice(r, r + br)
                xhat, rstd = normalize(x_ref[rr, :].astype(F32))
                dy = gn_scr[rr, :]
                gg += jnp.sum(dy * xhat, axis=0, keepdims=True)
                gb += jnp.sum(dy, axis=0, keepdims=True)
                gx_ref[rr, :] = (gm_ref[rr, :] + ln_back(dy, xhat, rstd, vec_ref[0:1, :d])).astype(BF)
            table = pack_vectors(
                {
                    "g1": gg, "b1": gb, "qv": qv_scr[...], "fb": gfb_ref[...], "pb": gpb_ref[...],
                    "g2": gg2_ref[...], "b2": gb2_ref[...], "ob": gob_ref[...],
                },
                d, devices,
            ).reshape(e_scr.shape[1:])
            for h in range(2):
                e_scr[h] = table
                store_columns(dims, where_ref, e_scr.at[h], g_own, g_oth, h, extra_at, 128, e_sem.at[h])
        else:
            gn_out[...] = gn_scr[...]
            qv_out[...] = qv_scr[...]
        for b in range(2 * groups):
            wait_store(dims, gw_scr.at[b], g_own, 0, 384, gw_sem.at[b])
        for h in range(2):
            wait_store(dims, e_scr.at[h], g_own, extra_at, e_scr.shape[-1], e_sem.at[h])


def attn_back_call(dims, where, joined, ga, lse, delta, seg_row, seg_col, x, vec, own, oth, group0, groups, extra, last, devices):
    rows, d = x.shape
    n = own[0].shape[1]
    pairs = d // 128
    act = full_spec((rows, d))
    one = full_spec((1, d))
    wide = d // 2 if not last else 128
    stat = pl.BlockSpec((1, 2, rows), lambda i: (group0 * 2 + i, 0, 0))
    arrays, count = len(own), dims[1] * dims[2]
    piece = jax.ShapeDtypeStruct((count, dims[0], n, groups * 384 + wide), BF)
    in_specs = [
        SMEM,
        pl.BlockSpec((rows, 384), lambda i: (0, pair_block(group0 * 2 + i, pairs))),
        pl.BlockSpec((rows, 128), lambda i: (0, group0 * 2 + i)),
        stat, stat, full_spec((1, 256)), full_spec((256, 1)), act, full_spec(vec.shape),
    ] + [ANY] * (2 * arrays)
    if last:
        in_specs += [act, full_spec((1, 2 * d)), act, full_spec((1, 4 * d))] + [one] * 4
        out_specs = [act, ANY, ANY]
        out_shape = [jax.ShapeDtypeStruct((rows, d), BF), piece, piece]
    else:
        in_specs += [full_spec((d, d))]
        out_specs = [act, full_spec((1, 2 * d)), ANY, ANY]
        out_shape = [jax.ShapeDtypeStruct((rows, d), F32), jax.ShapeDtypeStruct((1, 2 * d), F32), piece, piece]
    return pl.pallas_call(
        functools.partial(attn_back_kernel, dims, arrays, group0, groups, last, devices),
        grid=(2 * groups,),
        in_specs=in_specs,
        out_specs=out_specs,
        out_shape=out_shape,
        scratch_shapes=weight_scratch(dims, n, groups * 384)
        + [
            pltpu.VMEM((d, rows), BF), pltpu.VMEM((rows, d), F32), pltpu.VMEM((rows, 384), BF),
            pltpu.VMEM((rows, 128), F32), pltpu.VMEM((rows, 128), F32),
            pltpu.VMEM((2 * groups,) + dims + (n, 384), BF), pltpu.SemaphoreType.DMA((2 * groups, count, dims[0])),
            pltpu.VMEM((2,) + dims + (n, wide), BF), pltpu.SemaphoreType.DMA((2, count, dims[0])),
            pltpu.VMEM((1, 2 * d), F32),
        ],
        compiler_params=params(),
        cost_estimate=cost(groups * 20e9, 12e6, 5.5e6),
        name="attn_back_last" if last else "attn_back",
    )(where, joined, ga, lse, delta, seg_row, seg_col, x, vec, *own, *oth, *extra)


def pack_plan(counts, rows):
    c = [counts[i] for i in range(counts.shape[0])]
    ends, run = [], jnp.int32(0)
    for v in c:
        run = run + v
        ends.append(run)
    start = jnp.int32(0)
    for i in range(len(c) - 1):
        start = jnp.where(c[i] == LONG, ends[i] - c[i], start)
    rolled = jnp.arange(rows, dtype=jnp.int32)
    pos = rolled + start
    pos = jnp.where(pos >= rows, pos - rows, pos)
    seg = functools.reduce(jnp.add, [(pos >= e).astype(jnp.int32) for e in ends])
    valid = seg < len(c) - 1
    seg = jnp.where(valid, seg, 1000 + rolled)
    return start, seg[LONG:], valid


def roll_rows(array, shift):
    return lax.dynamic_slice_in_dim(jnp.concatenate([array, array], axis=0), shift, array.shape[0])


def half_columns(w, h, joined=False):
    r, cols = w.shape
    if not joined:
        return w[:, h * (cols // 2) : (h + 1) * (cols // 2)]
    pairs = cols // 384
    parts = w.reshape(r, 3, pairs // 2, 2, 128)[:, :, :, h]
    return jnp.swapaxes(parts, 1, 2).reshape(r, cols // 2)


def join_columns(left, right):
    r, m = left.shape
    both = jnp.stack([v.reshape(r, m // 384, 3, 128) for v in (left, right)], axis=2)
    return both.transpose(0, 3, 1, 2, 4).reshape(r, 2 * m)


def add_all(values):
    return functools.reduce(jnp.add, [v.astype(F32) for v in values])


class Plain:
    def __init__(self, dp, fsdp):
        self.dims = (1, 1, 1)
        index = lax.axis_index("dp") * fsdp + lax.axis_index("fsdp")
        self.ci = index % 2

    def where(self):
        zero = jnp.zeros((), jnp.int32)
        return jnp.stack([zero, zero, zero, self.ci.astype(jnp.int32)])

    def pick(self, pair):
        return jnp.where(self.ci == 0, pair[0], pair[1]), jnp.where(self.ci == 0, pair[1], pair[0])

    def gather(self, w_qkv, w_proj, table, w_fc, w_out):
        whole = lambda v: lax.all_gather(v, AXES, axis=0, tiled=True)
        attn = whole(jnp.concatenate([w_qkv, w_proj, table], axis=1))
        cut = w_qkv.shape[1], w_qkv.shape[1] + w_proj.shape[1]
        fc, out = whole(w_fc), whole(w_out)
        first = [
            jnp.concatenate(
                [half_columns(attn[:, : cut[0]], h, True), half_columns(attn[:, cut[0] : cut[1]], h), attn[:, cut[1] :]],
                axis=1,
            )
            for h in range(2)
        ]
        second = [half_columns(fc, h) for h in range(2)]
        third = [out[: out.shape[0] // 2], out[out.shape[0] // 2 :]]
        listed = []
        for pair in (first, second, third):
            own, oth = self.pick(pair)
            listed.append(([own[None]], [oth[None]]))
        return listed

    def scatter(self, own, oth, rows=False):
        pair = self.pick([own[0, 0], oth[0, 0]])
        if rows:
            return lax.psum_scatter(jnp.concatenate(pair, axis=0), AXES, scatter_dimension=0, tiled=True).astype(F32)
        m = pair[0].shape[1]
        mine = lax.psum_scatter(jnp.concatenate(pair, axis=1), AXES, scatter_dimension=0, tiled=True).astype(F32)
        return mine[:, :m], mine[:, m:]


class Chips:
    def __init__(self, dp, fsdp):
        x_n, z_n = fsdp // 2, 4
        self.dims = (z_n, dp // z_n, x_n)
        index = lax.axis_index("dp") * fsdp + lax.axis_index("fsdp")
        self.ci = index % 2
        self.at = (index // (2 * x_n * self.dims[1]), (index // (2 * x_n)) % self.dims[1], (index // 2) % x_n, self.ci)

    def where(self):
        return jnp.stack(self.at).astype(jnp.int32)

    def pick(self, pair):
        return jnp.where(self.ci == 0, pair[0], pair[1]), jnp.where(self.ci == 0, pair[1], pair[0])

    def send(self, array, dz=0, dy=0, dx=0, dc=0):
        z_n, y_n, x_n = self.dims
        pairs = []
        for z in range(z_n):
            for y in range(y_n):
                for x in range(x_n):
                    for c in range(2):
                        here = ((z * y_n + y) * x_n + x) * 2 + c
                        there = (((z + dz) % z_n * y_n + (y + dy) % y_n) * x_n + (x + dx) % x_n) * 2 + (c + dc) % 2
                        pairs.append((here, there))
        return lax.ppermute(array, AXES, pairs)

    def cut_halves(self, w_qkv, w_proj, table, w_fc):
        halves = [
            jnp.concatenate(
                [half_columns(w_qkv, h, True), half_columns(w_proj, h), table, half_columns(w_fc, h)], axis=1
            )
            for h in range(2)
        ]
        keep, give = self.pick(halves)
        rows = jnp.concatenate(self.pick([keep, self.send(give, dc=1)]), axis=0)
        cut = (w_qkv.shape[1] + w_proj.shape[1]) // 2 + 128
        return rows[:, :cut], rows[:, cut:]

    def along_z(self, piece):
        return jnp.stack([piece] + [self.send(piece, dz=-k) for k in range(1, self.dims[0])])

    def swap(self, arrays):
        return [self.send(v, dc=1) for v in arrays]

    def add_core(self, own, theirs):
        return [add_all([own[i], theirs[i]]).astype(BF) for i in range(own.shape[0])]

    def add_chips(self, block, arrived):
        return [add_all([block[j]] + [a[j] for a in arrived]).astype(BF) for j in range(self.dims[0])]

    def sum_z(self, column):
        return add_all([column[0]] + [self.send(column[j], dz=j) for j in range(1, self.dims[0])])

    def rows_back(self, total):
        n = total.shape[0] // 2
        mine, give = self.pick([total[:n], total[n:]])
        return self.pick([mine, self.send(give, dc=1)])


def together(*trees):
    return lax.optimization_barrier(trees)


def prepare(tokens, lengths, cotangent):
    start, seg, valid = pack_plan(lengths[0], tokens.shape[0])
    x = roll_rows(tokens, start)
    cot = jnp.where(valid[:, None], roll_rows(cotangent, start), BF(0))
    return start, seg[None, :], seg[:, None], x, cot


def vector_table(r, ln1_gain, ln1_bias, qv_bias, proj_bias, ln2_gain, ln2_bias, fc_bias, out_bias):
    flat = [
        jnp.concatenate([ln1_gain, ln1_bias, qv_bias]), fc_bias,
        jnp.concatenate([proj_bias, ln2_gain, ln2_bias, out_bias]),
    ]
    return jnp.pad(jnp.stack(flat), ((0, r - 3), (0, 128 - 4 * r)))


def results(r, start, out, gx, s_fc, s_out, s_one, s_two):
    rows = out.shape[0]
    wide = 2 * 384
    s_qkv = join_columns(*[jnp.concatenate([a[:, :wide], b[:, :-128]], axis=1) for a, b in zip(s_one, s_two)])
    s_proj = jnp.concatenate([v[:, wide:] for v in s_one], axis=1)
    small = s_two[0][:, -128:]
    row0, row1, row2 = [small[k, : 4 * r] for k in range(3)]
    restore = rows - start
    return (
        roll_rows(out, restore), roll_rows(gx, restore),
        row0[:r], row0[r : 2 * r], s_qkv, row0[2 * r :], s_proj, row2[:r],
        row2[r : 2 * r], row2[2 * r : 3 * r], jnp.concatenate(s_fc, axis=1), row1, s_out, row2[3 * r :],
    )


def block_plain(
    links, tokens, lengths, ln1_gain, ln1_bias, w_qkv, qv_bias, w_proj, proj_bias, ln2_gain, ln2_bias,
    w_fc, fc_bias, w_out, out_bias, cotangent,
):
    rows, d = tokens.shape
    r = w_qkv.shape[0]
    devices = d // r
    dims, where = links.dims, links.where()
    table = vector_table(r, ln1_gain, ln1_bias, qv_bias, proj_bias, ln2_gain, ln2_bias, fc_bias, out_bias)
    attn_w, fc_w, out_w = links.gather(w_qkv, w_proj, table, w_fc, w_out)
    start, seg_row, seg_col, x, cot = prepare(tokens, lengths, cotangent)
    joined, vec = qkv_call(dims, where, x, *attn_w, devices)
    att, lse = attn_call(joined, seg_row, seg_col)
    middle, normed_two = proj_call(dims, where, x, att, vec, *attn_w)
    out, gn, gfb, gob, gf_own, gf_oth, go_own, go_oth = mlp_call(
        dims, where, normed_two, cot, middle, vec, fc_w, out_w
    )
    s_fc = links.scatter(gf_own, gf_oth)
    s_out = links.scatter(go_own, go_oth, rows=True)
    gm, ga, gw_proj, delta, gg2, gb2, gpb = proj_back_call(dims, where, gn, middle, cot, att, vec, *attn_w)
    delta = delta[: d // HD].reshape(d // 128, 2, rows)
    shared = (dims, where, joined, ga, lse, delta, seg_row, seg_col, x, vec, *attn_w)
    gn1, qv1, g_own, g_oth = attn_back_call(*shared, 0, 2, (gw_proj,), False, devices)
    s_one = links.scatter(g_own, g_oth)
    gx, g_own, g_oth = attn_back_call(
        *shared, 2, d // 256 - 2, (gn1, qv1, gm, gfb, gob, gg2, gb2, gpb), True, devices
    )
    s_two = links.scatter(g_own, g_oth)
    return results(r, start, out, gx, s_fc, s_out, s_one, s_two)


def block_chips(
    links, tokens, lengths, ln1_gain, ln1_bias, w_qkv, qv_bias, w_proj, proj_bias, ln2_gain, ln2_bias,
    w_fc, fc_bias, w_out, out_bias, cotangent,
):
    rows, d = tokens.shape
    r = w_qkv.shape[0]
    devices = d // r
    dims, where, send = links.dims, links.where(), links.send
    table = vector_table(r, ln1_gain, ln1_bias, qv_bias, proj_bias, ln2_gain, ln2_bias, fc_bias, out_bias)
    a, b = links.cut_halves(w_qkv, w_proj, table, w_fc)
    start, seg_row, seg_col, x, cot = prepare(tokens, lengths, cotangent)

    a0 = links.along_z(a)
    a0, b, c = together(a0, b, w_out)
    ax, ay = send(a0, dx=1), send(a0, dy=1)
    b0 = links.along_z(b)
    ax, ay, b0, c = together(ax, ay, b0, c)
    ad = [send(ax[:2], dy=1), send(ay[2:], dx=1)]
    a_oth = links.swap([a0, ax, ay])
    c0 = links.along_z(c)
    ad, a_oth, c0, b0 = together(ad, a_oth, c0, b0)
    attn_w = [a0, ax, ay] + ad, a_oth + links.swap(ad)
    attn_w, b0, c0, x = together(attn_w, b0, c0, x)

    joined, vec = qkv_call(dims, where, x, *attn_w, devices)
    bx, by = send(b0, dx=1), send(b0, dy=1)
    joined, bx, by, c0 = together(joined, bx, by, c0)

    att, lse = attn_call(joined, seg_row, seg_col)
    bd = send(bx, dy=1)
    cx, cy = send(c0, dx=1), send(c0, dy=1)
    b_oth = links.swap([b0, bx, by])
    att, bd, cx, cy, b_oth = together(att, bd, cx, cy, b_oth)

    middle, normed_two = proj_call(dims, where, x, att, vec, *attn_w)
    cd = send(cy, dx=1)
    b_oth = b_oth + links.swap([bd])
    c_oth = links.swap([c0, cx, cy])
    normed_two, cd, b_oth, c_oth = together(normed_two, cd, b_oth, c_oth)
    c_oth = c_oth + links.swap([cd])

    out, gn, gfb, gob, gf_own, gf_oth, go_own, go_oth = mlp_call(
        dims, where, normed_two, cot, middle, vec, ([b0, bx, by, bd], b_oth), ([c0, cx, cy, cd], c_oth)
    )

    gm, ga, gw_proj, delta, gg2, gb2, gpb = proj_back_call(dims, where, gn, middle, cot, att, vec, *attn_w)
    delta = delta[: d // HD].reshape(d // 128, 2, rows)
    gf_oth, go_oth = links.swap([gf_oth, go_oth])
    fc = links.add_core(gf_own, gf_oth)
    wo = links.add_core(go_own, go_oth)
    ga, fc, wo = together(ga, fc, wo)

    shared = (dims, where, joined, ga, lse, delta, seg_row, seg_col, x, vec, *attn_w)
    gn1, qv1, g_own, g_oth = attn_back_call(*shared, 0, 2, (gw_proj,), False, devices)
    fd, fy = send(fc[3], dy=1), send(fc[2], dy=1)
    wd, wx = send(wo[3], dx=1), send(wo[1], dx=1)
    fcx = add_all([fc[1], fd]).astype(BF)
    woy = add_all([wo[2], wd]).astype(BF)
    gn1, g_own, g_oth, fcx, woy, fy, wx = together(gn1, g_own, g_oth, fcx, woy, fy, wx)

    gx, h_own, h_oth = attn_back_call(
        *shared, 2, d // 256 - 2, (gn1, qv1, gm, gfb, gob, gg2, gb2, gpb), True, devices
    )
    fx, wy = send(fcx, dx=1), send(woy, dy=1)
    (g_oth,) = links.swap([g_oth])
    fc = links.add_chips(fc[0], [fx, fy])
    wo = links.add_chips(wo[0], [wx, wy])
    one = links.add_core(g_own, g_oth)
    gx, h_own, h_oth, fc, wo, one = together(gx, h_own, h_oth, fc, wo, one)

    fc, wo = links.sum_z(fc), links.sum_z(wo)
    one = links.add_chips(one[0], [send(one[1], dx=1), send(one[2], dy=1), send(one[3], dx=1, dy=1)])
    (h_oth,) = links.swap([h_oth])
    two = links.add_core(h_own, h_oth)
    two, one, fc, wo = together(two, one, fc, wo)
    two = links.add_chips(two[0], [send(two[1], dx=1), send(two[2], dy=1), send(two[3], dx=1, dy=1)])
    one = links.sum_z(one)
    s_fc = links.rows_back(fc)
    two, one, s_fc = together(two, one, s_fc)
    s_two = links.rows_back(links.sum_z(two))
    s_one = links.rows_back(one)
    return results(r, start, out, gx, s_fc, wo, s_one, s_two)


def solution(mesh):
    dp, fsdp = mesh.shape["dp"], mesh.shape["fsdp"]

    def per_device(*args):
        if (dp, fsdp) == (8, 4) and args[4].shape[0] % 8 == 0:
            return block_chips(Chips(dp, fsdp), *args)
        return block_plain(Plain(dp, fsdp), *args)

    row, vec = P(AXES, None), P(AXES)
    in_specs = (row, row, vec, vec, row, vec, row, vec, vec, vec, row, vec, row, vec, row)
    out_specs = (row, row, vec, vec, row, vec, row, vec, vec, vec, row, vec, row, vec)
    return jax.shard_map(
        per_device, mesh=mesh, in_specs=in_specs, out_specs=out_specs, check_vma=False
    )
```

time: 711 us -> 364 us (0.51)
  waiting for transfers between devices: 485 us -> 92.7 us
  starting transfers between devices: 0.24 us -> 61.1 us
  Pallas kernels: 141 us -> 158 us
  local copies, waits for them, and re-layouts: 25.7 us -> 11.1 us
  between operations: 20.6 us -> 7.68 us
    reduce_scatter x2 -> x0, waiting for transfers between devices: 217 us -> none  [per_device(): lax.psum_scatter(v, AXES, scatter_dimension=0, tiled=True)]
    unnamed x7 -> x0, waiting for transfers between devices: 139 us -> none
    all_gather x3 -> x0, waiting for transfers between devices: 129 us -> none  [per_device(): gather = lambda v: lax.all_gather(v, AXES, axis=0, tiled=True)]
    ppermute x0 -> x64, waiting for transfers between devices: none -> 92.7 us  [send(): return lax.ppermute(array, AXES, pairs)]
    ppermute x0 -> x64, starting transfers between devices: none -> 61.1 us  [send(): return lax.ppermute(array, AXES, pairs)]
    pallas_call x6, Pallas kernels: 120 us -> 137 us  [the longest x1 53.4 us: mlp_call(): pl.pallas_call(functools.partial(mlp_kernel, dims, (len(fc[0]), len(out[0...]
  transfers between devices with their start and end apart: 6 -> 64, of which waited for: 6 -> 23; matrix products, arithmetic and copies ran while one was open for 5% -> 8% of each run, Pallas kernels for 5% -> 29%
where the time goes in v2:
time: 364 us; the launch traced here: 360 us
  Pallas kernels  158 us (43%)
  waiting for transfers between devices  92.7 us (25%)
  starting transfers between devices  61.1 us (17%)
  other arithmetic  29.2 us (8%)
  local copies, waits for them, and re-layouts  11.1 us (3%)
  between operations  7.68 us (2%)
    ppermute x64, waiting for transfers between devices, send(): return lax.ppermute(array, AXES, pairs)  92.7 us
    ppermute x64, starting transfers between devices, send(): return lax.ppermute(array, AXES, pairs)  61.1 us
    pallas_call x1, Pallas kernels, mlp_call(): pl.pallas_call(functools.partial(mlp_kernel, dims, (len(fc[0]), len(out[0...  53.4 us
    pallas_call x2, Pallas kernels, attn_back_call(): pl.pallas_call(functools.partial(attn_back_kernel, dims, arrays, group0,...  50.2 us
    pallas_call x1, Pallas kernels, attn_call(): pl.pallas_call(attn_kernel, grid=(pairs,), in_specs=[pl.BlockSpec((rows,...  21.2 us
    pallas_call x1, Pallas kernels, proj_back_call(): pl.pallas_call(functools.partial(proj_back_kernel, dims, len(own), 3 * d...  13.3 us
    pallas_call x1, Pallas kernels, qkv_call(): pl.pallas_call(functools.partial(qkv_kernel, dims, len(own), devices), gr...  12.3 us
    concatenate x3, other arithmetic, roll_rows(): jnp.concatenate([array, array], axis=0)  12 us
  transfers between devices with their start and end apart: 64, of which 23 were waited for; matrix products, arithmetic and copies ran while one was open for 8% of the time, Pallas kernels for 29%

profile of v2, /device:TPU:0, one launch (start us, length us, event | category | flops | bytes accessed | tf_op | source)
XLA Modules:
  0.0 359.5 jit_solution(12937019181510694235)
XLA Ops:
  4.9 5.0 %collective-permute-start.1 = (bf16[48,1664]{1,0:T(8,128)(2,1)S(1)}, bf16[48,1664]{1,0:T(8,128)(2,1)S(1)}, u32[]{:S(2)}, u32[]{:S(2)}) collective-permute-start(bf16[48,1664]{1,0:T(8,128)(2,1)S(1)} %fusion.21), channel_id=1, source_target_pairs={{0,24},{1,25},{2,26},{3,27},{4,28},{5,29},{6,30},{7,31},{8,0},{9,1... | collective-permute-start | bytes 479240 | tf_op jit(solution)/shard_map/ppermute | solution.py:864
  11.0 3.5 collective-permute-done.1
  14.5 9.3 %collective-permute-done.2 = bf16[48,1664]{1,0:T(8,128)(2,1)S(1)} collective-permute-done((bf16[48,1664]{1,0:T(8,128)(2,1)S(1)}, bf16[48,1664]{1,0:T(8,128)(2,1)S(1)}, u32[]{:S(2)}, u32[]{:S(2)}) %collective-permute-start.2) | collective-permute-done | bytes 159776 | tf_op jit(solution)/shard_map/ppermute | solution.py:864
  23.9 1.6 collective-permute-start.4
  25.4 1.5 collective-permute-start.5
  28.1 1.7 collective-permute-start.7
  29.8 2.0 collective-permute-start.8
  33.0 9.0 %collective-permute-done.7 = bf16[48,1536]{1,0:T(8,128)(2,1)S(1)} collective-permute-done((bf16[48,1536]{1,0:T(8,128)(2,1)S(1)}, bf16[48,1536]{1,0:T(8,128)(2,1)S(1)}, u32[]{:S(2)}, u32[]{:S(2)}) %collective-permute-start.7) | collective-permute-done | bytes 147488 | tf_op jit(solution)/shard_map/ppermute | solution.py:864
  44.5 5.7 %collective-permute-done.14 = bf16[96,768]{1,0:T(8,128)(2,1)S(1)} collective-permute-done((bf16[96,768]{1,0:T(8,128)(2,1)S(1)}, bf16[96,768]{1,0:T(8,128)(2,1)S(1)}, u32[]{:S(2)}, u32[]{:S(2)}) %collective-permute-start.14) | collective-permute-done | bytes 147488 | tf_op jit(solution)/shard_map/ppermute | solution.py:864
  50.3 7.8 %collective-permute-done.15 = bf16[96,768]{1,0:T(8,128)(2,1)S(1)} collective-permute-done((bf16[96,768]{1,0:T(8,128)(2,1)S(1)}, bf16[96,768]{1,0:T(8,128)(2,1)S(1)}, u32[]{:S(2)}, u32[]{:S(2)}) %collective-permute-start.15) | collective-permute-done | bytes 147488 | tf_op jit(solution)/shard_map/ppermute | solution.py:864
  60.5 6.6 %collective-permute-done.10.refs_4_ = bf16[2,48,1664]{2,1,0:T(8,128)(2,1)S(1)} collective-permute-done((bf16[2,48,1664]{2,1,0:T(8,128)(2,1)S(1)}, bf16[2,48,1664]{2,1,0:T(8,128)(2,1)S(1)}, u32[]{:S(2)}, u32[]{:S(2)}) %collective-permute-start.10) | collective-permute-done | bytes 319520 | tf_op jit(solution)/shard_map/ppermute | solution.py:864
  73.9 4.0 %fusion.4.x_ref = bf16[1024,768]{1,0:T(8,128)(2,1)} fusion(s32[]{:T(128)S(6)} %select_n.162, bf16[1024,768]{1,0:T(8,128)(2,1)} %param.15), kind=kLoop, calls=%fused_computation.12 | loop fusion | flops 3145728 | bytes 3145732 | tf_op jit(solution)/shard_map/concatenate | solution.py:776
  78.0 1.5 collective-permute-start.19
  83.8 12.3 %qkv.1 = (bf16[1024,2304]{1,0:T(8,128)(2,1)}, f32[8,3072]{1,0:T(8,128)}) custom-call(s32[4]{0:T(128)} %pad_add_fusion.where_ref, bf16[1024,768]{1,0:T(8,128)(2,1)} %fusion.4.x_ref, bf16[4,48,1664]{2,1,0:T(8,128)(2,1)} %copy-done, bf16[4,48,1664]{2,1,0:T(8,128)(2,1)} %copy-done.1, bf16[4,48,1664]{2,1,0:T(8,128)(2,1)} %copy-done.2, ...), custom_call_target="tpu_custom_call" | custom-call | flops 3623878656 | bytes 9830400 | tf_op jit(solution)/shard_map/qkv/pallas_call | solution.py:313
  99.3 21.2 %attn.1 = (bf16[1024,768]{1,0:T(8,128)(2,1)}, f32[6,2,1024]{2,1,0:T(2,128)}) custom-call(bf16[1024,2304]{1,0:T(8,128)(2,1)} %get-tuple-element.165.q_ref.k_ref.v_ref.j_ref, bf16[1024,2304]{1,0:T(8,128)(2,1)} %get-tuple-element.165.q_ref.k_ref.v_ref.j_ref, bf16[1024,2304]{1,0:T(8,128)(2,1)} %get-tuple-element.165.q_ref.k_ref.v_ref.j_ref, s32[1,256]{1,0:T(1,128)} %bitcast.133, ...), custom_call_target="tpu_custom_call" | custom-call | flops 24000000000 | bytes 8000000 | tf_op jit(solution)/shard_map/attn/pallas_call | solution.py:117
  120.4 4.4 %collective-permute-done.21.refs_3_ = bf16[4,48,1536]{2,1,0:T(8,128)(2,1)S(1)} collective-permute-done((bf16[4,48,1536]{2,1,0:T(8,128)(2,1)S(1)}, bf16[4,48,1536]{2,1,0:T(8,128)(2,1)S(1)}, u32[]{:S(2)}, u32[]{:S(2)}) %collective-permute-start.21) | collective-permute-done | bytes 589856 | tf_op jit(solution)/shard_map/ppermute | solution.py:864
  124.9 1.6 collective-permute-start.27
  127.2 7.4 %proj.1 = (f32[1024,768]{1,0:T(8,128)}, bf16[1024,768]{1,0:T(8,128)(2,1)}) custom-call(s32[4]{0:T(128)} %pad_add_fusion.where_ref, bf16[1024,768]{1,0:T(8,128)(2,1)} %fusion.4.x_ref, bf16[1024,768]{1,0:T(8,128)(2,1)} %get-tuple-element.170.a_ref, f32[8,3072]{1,0:T(8,128)} %get-tuple-element.171.vec_ref, bf16[4,48,1664]{2,1,0:T(8,128)(2,1)} %copy-done, ...), custom_call_target="tpu_custom_call" | custom-call | flops 1207959552 | bytes 9043968 | tf_op jit(solution)/shard_map/proj/pallas_call | solution.py:355
  134.7 6.0 %collective-permute-done.27.refs_11_ = bf16[4,96,768]{2,1,0:T(8,128)(2,1)S(1)} collective-permute-done((bf16[4,96,768]{2,1,0:T(8,128)(2,1)S(1)}, bf16[4,96,768]{2,1,0:T(8,128)(2,1)S(1)}, u32[]{:S(2)}, u32[]{:S(2)}) %collective-permute-start.27) | collective-permute-done | bytes 589856 | tf_op jit(solution)/shard_map/ppermute | solution.py:864
  141.5 2.3 fusion.3.c_ref
  144.7 53.4 %mlp.1 = (bf16[1024,768]{1,0:T(8,128)(2,1)}, f32[1024,768]{1,0:T(8,128)}, f32[1,3072]{1,0:T(1,128)}, f32[1,768]{1,0:T(1,128)}, bf16[4,4,48,1536]{3,2,1,0:T(8,128...) custom-call(s32[4]{0:T(128)} %pad_add_fusion.where_ref, ...), custom_call_target="tpu_custom_call" | custom-call | flops 28991029248 | bytes 30000000 | tf_op jit(solution)/shard_map/mlp/pallas_call | solution.py:496
  199.4 13.3 %proj_back.1 = (f32[1024,768]{1,0:T(8,128)}, bf16[1024,768]{1,0:T(8,128)(2,1)}, bf16[768,768]{1,0:T(8,128)(2,1)}, f32[16,1024]{1,0:T(8,128)}, f32[1,768]{1,0:T(1...) custom-call(s32[4]{0:T(128)} %pad_add_fusion.where_ref, f32[1024,768]{1,0:T(8,128)} %get-tuple-element.190.gn_ref, ...), custom_call_target="tpu_custom_call" | custom-call | flops 2415919104 | bytes 12582912 | tf_op jit(solution)/shard_map/proj_back/pallas_call | solution.py:571
  212.8 1.5 reshape.299.del_ref
  214.2 4.2 %fusion.1 = bf16[1024,768]{1,0:T(8,128)(2,1)} fusion(s32[]{:T(128)S(6)} %select_n.166, bf16[1024,768]{1,0:T(8,128)(2,1)} %get-tuple-element.189), kind=kLoop, calls=%fused_computation.9 | loop fusion | flops 3145728 | bytes 3145732 | tf_op jit(solution)/shard_map/concatenate | solution.py:776
  218.5 3.3 fusion.12
  221.8 1.6 fusion.8
  223.3 1.5 collective-permute-start.36
  227.4 28.0 %attn_back.1 = (f32[1024,768]{1,0:T(8,128)}, f32[1,1536]{1,0:T(1,128)}, bf16[4,4,48,1152]{3,2,1,0:T(8,128)(2,1)}, bf16[4,4,48,1152]{3,2,1,0:T(8,128)(2,1)}) custom-call(s32[4]{0:T(128)} %pad_add_fusion.where_ref, bf16[1024,2304]{1,0:T(8,128)(2,1)} %get-tuple-element.165.q_ref.k_ref.v_ref.j_ref, bf16[1024,768]{1,0:T(8,128)(2,1)} %get-tuple-element.196.do_ref, ...), custom_call_target="tpu_custom_call" | custom-call | flops 40000000000 | bytes 12000000 | tf_op jit(solution)/shard_map/attn_back/pallas_call | solution.py:737
  257.1 1.5 collective-permute-start.39
  258.6 22.2 %attn_back_last.1 = (bf16[1024,768]{1,0:T(8,128)(2,1)}, bf16[4,4,48,512]{3,2,1,0:T(8,128)(2,1)}, bf16[4,4,48,512]{3,2,1,0:T(8,128)(2,1)}) custom-call(s32[4]{0:T(128)} %pad_add_fusion.where_ref, bf16[1024,2304]{1,0:T(8,128)(2,1)} %get-tuple-element.165.q_ref.k_ref.v_ref.j_ref, bf16[1024,768]{1,0:T(8,128)(2,1)} %get-tuple-element.196.do_ref, ...), custom_call_target="tpu_custom_call" | custom-call | flops 20000000000 | bytes 12000000 | tf_op jit(solution)/shard_map/attn_back_last/pallas_call | solution.py:737
  280.8 1.3 fusion.31
  285.4 3.2 collective-permute-start.46
  288.8 2.3 collective-permute-start.48
  291.1 3.8 %fusion = bf16[1024,768]{1,0:T(8,128)(2,1)} fusion(s32[]{:T(128)S(6)} %select_n.166, bf16[1024,768]{1,0:T(8,128)(2,1)S(1)} %copy-done.10), kind=kLoop, calls=%fused_computation.8 | loop fusion | flops 3145728 | bytes 3145732 | tf_op jit(solution)/shard_map/concatenate | solution.py:776
  294.8 2.0 collective-permute-start.51
  296.9 7.5 %collective-permute-done.50 = bf16[96,768]{1,0:T(8,128)(2,1)S(1)} collective-permute-done((bf16[96,768]{1,0:T(8,128)(2,1)S(1)}, bf16[96,768]{1,0:T(8,128)(2,1)S(1)}, u32[]{:S(2)}, u32[]{:S(2)}) %collective-permute-start.50) | collective-permute-done | bytes 147488 | tf_op jit(solution)/shard_map/ppermute | solution.py:864
  305.8 1.7 collective-permute-done.47
  309.3 8.2 %collective-permute-done.43 = bf16[4,48,1152]{2,1,0:T(8,128)(2,1)S(1)} collective-permute-done((bf16[4,48,1152]{2,1,0:T(8,128)(2,1)S(1)}, bf16[4,48,1152]{2,1,0:T(8,128)(2,1)S(1)}, u32[]{:S(2)}, u32[]{:S(2)}) %collective-permute-start.43) | collective-permute-done | bytes 442400 | tf_op jit(solution)/shard_map/ppermute | solution.py:864
  317.8 6.7 %collective-permute-done.45 = bf16[4,48,1152]{2,1,0:T(8,128)(2,1)S(1)} collective-permute-done((bf16[4,48,1152]{2,1,0:T(8,128)(2,1)S(1)}, bf16[4,48,1152]{2,1,0:T(8,128)(2,1)S(1)}, u32[]{:S(2)}, u32[]{:S(2)}) %collective-permute-start.45) | collective-permute-done | bytes 442400 | tf_op jit(solution)/shard_map/ppermute | solution.py:864
  325.0 4.5 %collective-permute-start.55 = (bf16[48,1152]{1,0:T(8,128)(2,1)S(1)}, bf16[48,1152]{1,0:T(8,128)(2,1)S(1)}, u32[]{:S(2)}, u32[]{:S(2)}) collective-permute-start(bf16[48,1152]{1,0:T(8,128)(2,1)S(1)} %get-tuple-element.248), channel_id=1, source_target_pairs={{0,8},{1,9},{2,10},{3,11},{4,12},{5,13},{6,14},{7,15},{8,16},{9,17... | collective-permute-start | bytes 331784 | tf_op jit(solution)/shard_map/ppermute | solution.py:864
  329.5 2.0 collective-permute-start.56
  331.5 2.8 collective-permute-start.57
  336.1 1.4 collective-permute-done.56
  338.1 4.1 %collective-permute-done.52 = bf16[4,48,512]{2,1,0:T(8,128)(2,1)S(1)} collective-permute-done((bf16[4,48,512]{2,1,0:T(8,128)(2,1)S(1)}, bf16[4,48,512]{2,1,0:T(8,128)(2,1)S(1)}, u32[]{:S(2)}, u32[]{:S(2)}) %collective-permute-start.52) | collective-permute-done | bytes 196640 | tf_op jit(solution)/shard_map/ppermute | solution.py:864
  342.2 4.6 %collective-permute-done.53 = bf16[4,48,512]{2,1,0:T(8,128)(2,1)S(1)} collective-permute-done((bf16[4,48,512]{2,1,0:T(8,128)(2,1)S(1)}, bf16[4,48,512]{2,1,0:T(8,128)(2,1)S(1)}, u32[]{:S(2)}, u32[]{:S(2)}) %collective-permute-start.53) | collective-permute-done | bytes 196640 | tf_op jit(solution)/shard_map/ppermute | solution.py:864
  347.7 2.1 collective-permute-start.60
  349.8 1.5 collective-permute-start.61
  351.5 1.6 collective-permute-done.59
  (238 shorter events, 45.7 us)
Async XLA Ops:
  4.9 9.6 %collective-permute-start.1 = (bf16[48,1664]{1,0:T(8,128)(2,1)S(1)}, bf16[48,1664]{1,0:T(8,128)(2,1)S(1)}, u32[]{:S(2)}, u32[]{:S(2)}) collective-permute-start(bf16[48,1664]{1,0:T(8,128)(2,1)S(1)} %fusion.21), channel_id=1, source_target_pairs={{0,24},{1,25},{2,26},{3,27},{4,28},{5,29},{6,30},{7,31},{8,0},{9,1... | collective-permute-start | bytes 479240 | tf_op jit(solution)/shard_map/ppermute | solution.py:864
  9.9 13.8 %collective-permute-start.2 = (bf16[48,1664]{1,0:T(8,128)(2,1)S(1)}, bf16[48,1664]{1,0:T(8,128)(2,1)S(1)}, u32[]{:S(2)}, u32[]{:S(2)}) collective-permute-start(bf16[48,1664]{1,0:T(8,128)(2,1)S(1)} %fusion.21), channel_id=1, source_target_pairs={{0,16},{1,17},{2,18},{3,19},{4,20},{5,21},{6,22},{7,23},{8,24},{9,... | collective-permute-start | bytes 479240 | tf_op jit(solution)/shard_map/ppermute | solution.py:864
  9.9 13.8 %collective-permute-start.3 = (bf16[48,1664]{1,0:T(8,128)(2,1)S(1)}, bf16[48,1664]{1,0:T(8,128)(2,1)S(1)}, u32[]{:S(2)}, u32[]{:S(2)}) collective-permute-start(bf16[48,1664]{1,0:T(8,128)(2,1)S(1)} %fusion.21), channel_id=1, source_target_pairs={{0,8},{1,9},{2,10},{3,11},{4,12},{5,13},{6,14},{7,15},{8,16},{9,17... | collective-permute-start | bytes 479240 | tf_op jit(solution)/shard_map/ppermute | solution.py:864
  23.9 19.0 %collective-permute-start.4 = (bf16[4,48,1664]{2,1,0:T(8,128)(2,1)S(1)}, bf16[4,48,1664]{2,1,0:T(8,128)(2,1)S(1)}, u32[]{:S(2)}, u32[]{:S(2)}) collective-permute-start(bf16[4,48,1664]{2,1,0:T(8,128)(2,1)S(1)} %pad_maximum_fusion.refs_0_), channel_id=1, source_target_pairs={{0,2},{1,3},{2,0},{3,1},{4,6},{5,7},{6,4},{7,5},{8,10},{9,11},{10,... | collective-permute-start | bytes 1916936 | tf_op jit(solution)/shard_map/ppermute | solution.py:864
  25.4 17.4 %collective-permute-start.5 = (bf16[4,48,1664]{2,1,0:T(8,128)(2,1)S(1)}, bf16[4,48,1664]{2,1,0:T(8,128)(2,1)S(1)}, u32[]{:S(2)}, u32[]{:S(2)}) collective-permute-start(bf16[4,48,1664]{2,1,0:T(8,128)(2,1)S(1)} %pad_maximum_fusion.refs_0_), channel_id=1, source_target_pairs={{0,4},{1,5},{2,6},{3,7},{4,0},{5,1},{6,2},{7,3},{8,12},{9,13},{10,... | collective-permute-start | bytes 1916936 | tf_op jit(solution)/shard_map/ppermute | solution.py:864
  28.1 13.9 %collective-permute-start.7 = (bf16[48,1536]{1,0:T(8,128)(2,1)S(1)}, bf16[48,1536]{1,0:T(8,128)(2,1)S(1)}, u32[]{:S(2)}, u32[]{:S(2)}) collective-permute-start(bf16[48,1536]{1,0:T(8,128)(2,1)S(1)} %pad_maximum_fusion.6), channel_id=1, source_target_pairs={{0,16},{1,17},{2,18},{3,19},{4,20},{5,21},{6,22},{7,23},{8,24},{9,... | collective-permute-start | bytes 442376 | tf_op jit(solution)/shard_map/ppermute | solution.py:864
  29.8 12.2 %collective-permute-start.8 = (bf16[48,1536]{1,0:T(8,128)(2,1)S(1)}, bf16[48,1536]{1,0:T(8,128)(2,1)S(1)}, u32[]{:S(2)}, u32[]{:S(2)}) collective-permute-start(bf16[48,1536]{1,0:T(8,128)(2,1)S(1)} %pad_maximum_fusion.6), channel_id=1, source_target_pairs={{0,8},{1,9},{2,10},{3,11},{4,12},{5,13},{6,14},{7,15},{8,16},{9,17... | collective-permute-start | bytes 442376 | tf_op jit(solution)/shard_map/ppermute | solution.py:864
  33.0 27.6 %collective-permute-start.11 = (bf16[4,48,1664]{2,1,0:T(8,128)(2,1)S(1)}, bf16[4,48,1664]{2,1,0:T(8,128)(2,1)S(1)}, u32[]{:S(2)}, u32[]{:S(2)}) collective-permute-start(bf16[4,48,1664]{2,1,0:T(8,128)(2,1)S(1)} %pad_maximum_fusion.refs_0_), channel_id=1, source_target_pairs={{0,1},{1,0},{2,3},{3,2},{4,5},{5,4},{6,7},{7,6},{8,9},{9,8},{10,11... | collective-permute-start | bytes 1916936 | tf_op jit(solution)/shard_map/ppermute | solution.py:864
  42.9 24.5 %collective-permute-start.12 = (bf16[4,48,1664]{2,1,0:T(8,128)(2,1)S(1)}, bf16[4,48,1664]{2,1,0:T(8,128)(2,1)S(1)}, u32[]{:S(2)}, u32[]{:S(2)}) collective-permute-start(bf16[4,48,1664]{2,1,0:T(8,128)(2,1)S(1)} %collective-permute-done.4.refs_1_), channel_id=1, source_target_pairs={{0,1},{1,0},{2,3},{3,2},{4,5},{5,4},{6,7},{7,6},{8,9},{9,8},{10,11... | collective-permute-start | bytes 1916936 | tf_op jit(solution)/shard_map/ppermute | solution.py:864
  43.0 24.4 %collective-permute-start.13 = (bf16[4,48,1664]{2,1,0:T(8,128)(2,1)S(1)}, bf16[4,48,1664]{2,1,0:T(8,128)(2,1)S(1)}, u32[]{:S(2)}, u32[]{:S(2)}) collective-permute-start(bf16[4,48,1664]{2,1,0:T(8,128)(2,1)S(1)} %collective-permute-done.5.refs_2_), channel_id=1, source_target_pairs={{0,1},{1,0},{2,3},{3,2},{4,5},{5,4},{6,7},{7,6},{8,9},{9,8},{10,11... | collective-permute-start | bytes 1916936 | tf_op jit(solution)/shard_map/ppermute | solution.py:864
  43.5 14.6 %collective-permute-start.15 = (bf16[96,768]{1,0:T(8,128)(2,1)S(1)}, bf16[96,768]{1,0:T(8,128)(2,1)S(1)}, u32[]{:S(2)}, u32[]{:S(2)}) collective-permute-start(bf16[96,768]{1,0:T(8,128)(2,1)S(1)} %copy-done.16), channel_id=1, source_target_pairs={{0,16},{1,17},{2,18},{3,19},{4,20},{5,21},{6,22},{7,23},{8,24},{9,... | collective-permute-start | bytes 442376 | tf_op jit(solution)/shard_map/ppermute | solution.py:864
  68.2 9.7 %collective-permute-start.17 = (bf16[2,48,1664]{2,1,0:T(8,128)(2,1)S(1)}, bf16[2,48,1664]{2,1,0:T(8,128)(2,1)S(1)}, u32[]{:S(2)}, u32[]{:S(2)}) collective-permute-start(bf16[2,48,1664]{2,1,0:T(8,128)(2,1)S(1)} %collective-permute-done.9.refs_3_), channel_id=1, source_target_pairs={{0,1},{1,0},{2,3},{3,2},{4,5},{5,4},{6,7},{7,6},{8,9},{9,8},{10,11... | collective-permute-start | bytes 958472 | tf_op jit(solution)/shard_map/ppermute | solution.py:864
  68.2 9.7 %collective-permute-start.18 = (bf16[2,48,1664]{2,1,0:T(8,128)(2,1)S(1)}, bf16[2,48,1664]{2,1,0:T(8,128)(2,1)}, u32[]{:S(2)}, u32[]{:S(2)}) collective-permute-start(bf16[2,48,1664]{2,1,0:T(8,128)(2,1)S(1)} %collective-permute-done.10.refs_4_), channel_id=1, source_target_pairs={{0,1},{1,0},{2,3},{3,2},{4,5},{5,4},{6,7},{7,6},{8,9},{9,8},{10,11... | collective-permute-start | bytes 958472 | tf_op jit(solution)/shard_map/ppermute | solution.py:864
  78.0 18.1 %collective-permute-start.19 = (bf16[4,48,1536]{2,1,0:T(8,128)(2,1)}, bf16[4,48,1536]{2,1,0:T(8,128)(2,1)S(1)}, u32[]{:S(2)}, u32[]{:S(2)}) collective-permute-start(bf16[4,48,1536]{2,1,0:T(8,128)(2,1)} %pad_maximum_fusion.1.refs_0_), channel_id=1, source_target_pairs={{0,2},{1,3},{2,0},{3,1},{4,6},{5,7},{6,4},{7,5},{8,10},{9,11},{10,... | collective-permute-start | bytes 1769480 | tf_op jit(solution)/shard_map/ppermute | solution.py:864
  79.5 16.6 %collective-permute-start.20 = (bf16[4,48,1536]{2,1,0:T(8,128)(2,1)}, bf16[4,48,1536]{2,1,0:T(8,128)(2,1)S(1)}, u32[]{:S(2)}, u32[]{:S(2)}) collective-permute-start(bf16[4,48,1536]{2,1,0:T(8,128)(2,1)} %pad_maximum_fusion.1.refs_0_), channel_id=1, source_target_pairs={{0,4},{1,5},{2,6},{3,7},{4,0},{5,1},{6,2},{7,3},{8,12},{9,13},{10,... | collective-permute-start | bytes 1769480 | tf_op jit(solution)/shard_map/ppermute | solution.py:864
  80.4 18.4 %collective-permute-start.24 = (bf16[4,48,1536]{2,1,0:T(8,128)(2,1)}, bf16[4,48,1536]{2,1,0:T(8,128)(2,1)S(1)}, u32[]{:S(2)}, u32[]{:S(2)}) collective-permute-start(bf16[4,48,1536]{2,1,0:T(8,128)(2,1)} %pad_maximum_fusion.1.refs_0_), channel_id=1, source_target_pairs={{0,1},{1,0},{2,3},{3,2},{4,5},{5,4},{6,7},{7,6},{8,9},{9,8},{10,11... | collective-permute-start | bytes 1769480 | tf_op jit(solution)/shard_map/ppermute | solution.py:864
  96.1 28.7 %collective-permute-start.22 = (bf16[4,96,768]{2,1,0:T(8,128)(2,1)S(1)}, bf16[4,96,768]{2,1,0:T(8,128)(2,1)S(1)}, u32[]{:S(2)}, u32[]{:S(2)}) collective-permute-start(bf16[4,96,768]{2,1,0:T(8,128)(2,1)S(1)} %copy-done.15), channel_id=1, source_target_pairs={{0,2},{1,3},{2,0},{3,1},{4,6},{5,7},{6,4},{7,5},{8,10},{9,11},{10,... | collective-permute-start | bytes 1769480 | tf_op jit(solution)/shard_map/ppermute | solution.py:864
  96.7 28.1 %collective-permute-start.23 = (bf16[4,96,768]{2,1,0:T(8,128)(2,1)S(1)}, bf16[4,96,768]{2,1,0:T(8,128)(2,1)S(1)}, u32[]{:S(2)}, u32[]{:S(2)}) collective-permute-start(bf16[4,96,768]{2,1,0:T(8,128)(2,1)S(1)} %copy-done.15), channel_id=1, source_target_pairs={{0,4},{1,5},{2,6},{3,7},{4,0},{5,1},{6,2},{7,3},{8,12},{9,13},{10,... | collective-permute-start | bytes 1769480 | tf_op jit(solution)/shard_map/ppermute | solution.py:864
  97.9 26.9 %collective-permute-start.21 = (bf16[4,48,1536]{2,1,0:T(8,128)(2,1)S(1)}, bf16[4,48,1536]{2,1,0:T(8,128)(2,1)S(1)}, u32[]{:S(2)}, u32[]{:S(2)}) collective-permute-start(bf16[4,48,1536]{2,1,0:T(8,128)(2,1)S(1)} %collective-permute-done.19.refs_1_), channel_id=1, source_target_pairs={{0,4},{1,5},{2,6},{3,7},{4,0},{5,1},{6,2},{7,3},{8,12},{9,13},{10,... | collective-permute-start | bytes 1769480 | tf_op jit(solution)/shard_map/ppermute | solution.py:864
  98.7 26.1 %collective-permute-start.25 = (bf16[4,48,1536]{2,1,0:T(8,128)(2,1)S(1)}, bf16[4,48,1536]{2,1,0:T(8,128)(2,1)S(1)}, u32[]{:S(2)}, u32[]{:S(2)}) collective-permute-start(bf16[4,48,1536]{2,1,0:T(8,128)(2,1)S(1)} %collective-permute-done.19.refs_1_), channel_id=1, source_target_pairs={{0,1},{1,0},{2,3},{3,2},{4,5},{5,4},{6,7},{7,6},{8,9},{9,8},{10,11... | collective-permute-start | bytes 1769480 | tf_op jit(solution)/shard_map/ppermute | solution.py:864
  98.8 26.1 %collective-permute-start.26 = (bf16[4,48,1536]{2,1,0:T(8,128)(2,1)S(1)}, bf16[4,48,1536]{2,1,0:T(8,128)(2,1)S(1)}, u32[]{:S(2)}, u32[]{:S(2)}) collective-permute-start(bf16[4,48,1536]{2,1,0:T(8,128)(2,1)S(1)} %collective-permute-done.20.refs_2_), channel_id=1, source_target_pairs={{0,1},{1,0},{2,3},{3,2},{4,5},{5,4},{6,7},{7,6},{8,9},{9,8},{10,11... | collective-permute-start | bytes 1769480 | tf_op jit(solution)/shard_map/ppermute | solution.py:864
  124.8 9.8 %collective-permute-start.29 = (bf16[4,96,768]{2,1,0:T(8,128)(2,1)S(1)}, bf16[4,96,768]{2,1,0:T(8,128)(2,1)S(1)}, u32[]{:S(2)}, u32[]{:S(2)}) collective-permute-start(bf16[4,96,768]{2,1,0:T(8,128)(2,1)S(1)} %copy-done.15), channel_id=1, source_target_pairs={{0,1},{1,0},{2,3},{3,2},{4,5},{5,4},{6,7},{7,6},{8,9},{9,8},{10,11... | collective-permute-start | bytes 1769480 | tf_op jit(solution)/shard_map/ppermute | solution.py:864
  124.9 15.8 %collective-permute-start.27 = (bf16[4,96,768]{2,1,0:T(8,128)(2,1)S(1)}, bf16[4,96,768]{2,1,0:T(8,128)(2,1)S(1)}, u32[]{:S(2)}, u32[]{:S(2)}) collective-permute-start(bf16[4,96,768]{2,1,0:T(8,128)(2,1)S(1)} %collective-permute-done.23.refs_10_), channel_id=1, source_target_pairs={{0,2},{1,3},{2,0},{3,1},{4,6},{5,7},{6,4},{7,5},{8,10},{9,11},{10,... | collective-permute-start | bytes 1769480 | tf_op jit(solution)/shard_map/ppermute | solution.py:864
  126.5 14.2 %collective-permute-start.28 = (bf16[4,48,1536]{2,1,0:T(8,128)(2,1)S(1)}, bf16[4,48,1536]{2,1,0:T(8,128)(2,1)S(1)}, u32[]{:S(2)}, u32[]{:S(2)}) collective-permute-start(bf16[4,48,1536]{2,1,0:T(8,128)(2,1)S(1)} %collective-permute-done.21.refs_3_), channel_id=1, source_target_pairs={{0,1},{1,0},{2,3},{3,2},{4,5},{5,4},{6,7},{7,6},{8,9},{9,8},{10,11... | collective-permute-start | bytes 1769480 | tf_op jit(solution)/shard_map/ppermute | solution.py:864
  126.7 14.0 %collective-permute-start.30 = (bf16[4,96,768]{2,1,0:T(8,128)(2,1)S(1)}, bf16[4,96,768]{2,1,0:T(8,128)(2,1)}, u32[]{:S(2)}, u32[]{:S(2)}) collective-permute-start(bf16[4,96,768]{2,1,0:T(8,128)(2,1)S(1)} %collective-permute-done.22.refs_9_), channel_id=1, source_target_pairs={{0,1},{1,0},{2,3},{3,2},{4,5},{5,4},{6,7},{7,6},{8,9},{9,8},{10,11... | collective-permute-start | bytes 1769480 | tf_op jit(solution)/shard_map/ppermute | solution.py:864
  127.0 13.7 %collective-permute-start.31 = (bf16[4,96,768]{2,1,0:T(8,128)(2,1)S(1)}, bf16[4,96,768]{2,1,0:T(8,128)(2,1)}, u32[]{:S(2)}, u32[]{:S(2)}) collective-permute-start(bf16[4,96,768]{2,1,0:T(8,128)(2,1)S(1)} %collective-permute-done.23.refs_10_), channel_id=1, source_target_pairs={{0,1},{1,0},{2,3},{3,2},{4,5},{5,4},{6,7},{7,6},{8,9},{9,8},{10,11... | collective-permute-start | bytes 1769480 | tf_op jit(solution)/shard_map/ppermute | solution.py:864
  198.1 20.4 %collective-permute-start.34 = (bf16[4,4,96,768]{3,2,1,0:T(8,128)(2,1)}, bf16[4,4,96,768]{3,2,1,0:T(8,128)(2,1)}, u32[]{:S(2)}, u32[]{:S(2)}) collective-permute-start(bf16[4,4,96,768]{3,2,1,0:T(8,128)(2,1)} %get-tuple-element.195), channel_id=1, source_target_pairs={{0,1},{1,0},{2,3},{3,2},{4,5},{5,4},{6,7},{7,6},{8,9},{9,8},{10,11... | collective-permute-start | bytes 7077896 | tf_op jit(solution)/shard_map/ppermute | solution.py:864
  198.8 23.0 %collective-permute-start.33 = (bf16[4,4,48,1536]{3,2,1,0:T(8,128)(2,1)}, bf16[4,4,48,1536]{3,2,1,0:T(8,128)(2,1)S(1)}, u32[]{:S(2)}, u32[]{:S(2)}) collective-permute-start(bf16[4,4,48,1536]{3,2,1,0:T(8,128)(2,1)} %get-tuple-element.193), channel_id=1, source_target_pairs={{0,1},{1,0},{2,3},{3,2},{4,5},{5,4},{6,7},{7,6},{8,9},{9,8},{10,11... | collective-permute-start | bytes 7077896 | tf_op jit(solution)/shard_map/ppermute | solution.py:864
  223.3 32.0 %collective-permute-start.36 = (bf16[4,96,768]{2,1,0:T(8,128)(2,1)}, bf16[4,96,768]{2,1,0:T(8,128)(2,1)S(1)}, u32[]{:S(2)}, u32[]{:S(2)}) collective-permute-start(bf16[4,96,768]{2,1,0:T(8,128)(2,1)} %get-tuple-element.206), channel_id=1, source_target_pairs={{0,2},{1,3},{2,0},{3,1},{4,6},{5,7},{6,4},{7,5},{8,10},{9,11},{10,... | collective-permute-start | bytes 1769480 | tf_op jit(solution)/shard_map/ppermute | solution.py:864
  224.9 30.7 %collective-permute-start.35 = (bf16[4,48,1536]{2,1,0:T(8,128)(2,1)}, bf16[4,48,1536]{2,1,0:T(8,128)(2,1)S(1)}, u32[]{:S(2)}, u32[]{:S(2)}) collective-permute-start(bf16[4,48,1536]{2,1,0:T(8,128)(2,1)} %get-tuple-element.204), channel_id=1, source_target_pairs={{0,4},{1,5},{2,6},{3,7},{4,0},{5,1},{6,2},{7,3},{8,12},{9,13},{10,... | collective-permute-start | bytes 1769480 | tf_op jit(solution)/shard_map/ppermute | solution.py:864
  226.1 29.6 %collective-permute-start.37 = (bf16[4,48,1536]{2,1,0:T(8,128)(2,1)S(1)}, bf16[4,48,1536]{2,1,0:T(8,128)(2,1)S(1)}, u32[]{:S(2)}, u32[]{:S(2)}) collective-permute-start(bf16[4,48,1536]{2,1,0:T(8,128)(2,1)S(1)} %get-tuple-element.207), channel_id=1, source_target_pairs={{0,4},{1,5},{2,6},{3,7},{4,0},{5,1},{6,2},{7,3},{8,12},{9,13},{10,... | collective-permute-start | bytes 1769480 | tf_op jit(solution)/shard_map/ppermute | solution.py:864
  226.9 28.8 %collective-permute-start.38 = (bf16[4,96,768]{2,1,0:T(8,128)(2,1)S(1)}, bf16[4,96,768]{2,1,0:T(8,128)(2,1)}, u32[]{:S(2)}, u32[]{:S(2)}) collective-permute-start(bf16[4,96,768]{2,1,0:T(8,128)(2,1)S(1)} %get-tuple-element.208), channel_id=1, source_target_pairs={{0,2},{1,3},{2,0},{3,1},{4,6},{5,7},{6,4},{7,5},{8,10},{9,11},{10,... | collective-permute-start | bytes 1769480 | tf_op jit(solution)/shard_map/ppermute | solution.py:864
  255.7 26.7 %collective-permute-start.41 = (bf16[4,4,48,1152]{3,2,1,0:T(8,128)(2,1)}, bf16[4,4,48,1152]{3,2,1,0:T(8,128)(2,1)S(1)}, u32[]{:S(2)}, u32[]{:S(2)}) collective-permute-start(bf16[4,4,48,1152]{3,2,1,0:T(8,128)(2,1)} %get-tuple-element.227), channel_id=1, source_target_pairs={{0,1},{1,0},{2,3},{3,2},{4,5},{5,4},{6,7},{7,6},{8,9},{9,8},{10,11... | collective-permute-start | bytes 5308424 | tf_op jit(solution)/shard_map/ppermute | solution.py:864
  255.8 25.0 %collective-permute-start.40 = (bf16[4,96,768]{2,1,0:T(8,128)(2,1)S(1)}, bf16[4,96,768]{2,1,0:T(8,128)(2,1)S(1)}, u32[]{:S(2)}, u32[]{:S(2)}) collective-permute-start(bf16[4,96,768]{2,1,0:T(8,128)(2,1)S(1)} %add_convert_fusion), channel_id=1, source_target_pairs={{0,4},{1,5},{2,6},{3,7},{4,0},{5,1},{6,2},{7,3},{8,12},{9,13},{10,... | collective-permute-start | bytes 1769480 | tf_op jit(solution)/shard_map/ppermute | solution.py:864
  257.1 25.1 %collective-permute-start.39 = (bf16[4,48,1536]{2,1,0:T(8,128)(2,1)S(1)}, bf16[4,48,1536]{2,1,0:T(8,128)(2,1)S(1)}, u32[]{:S(2)}, u32[]{:S(2)}) collective-permute-start(bf16[4,48,1536]{2,1,0:T(8,128)(2,1)S(1)} %add_convert_fusion.1), channel_id=1, source_target_pairs={{0,2},{1,3},{2,0},{3,1},{4,6},{5,7},{6,4},{7,5},{8,10},{9,11},{10,... | collective-permute-start | bytes 1769480 | tf_op jit(solution)/shard_map/ppermute | solution.py:864
  284.1 10.7 %collective-permute-start.49 = (bf16[96,768]{1,0:T(8,128)(2,1)S(1)}, bf16[96,768]{1,0:T(8,128)(2,1)S(1)}, u32[]{:S(2)}, u32[]{:S(2)}) collective-permute-start(bf16[96,768]{1,0:T(8,128)(2,1)S(1)} %get-tuple-element.240), channel_id=1, source_target_pairs={{0,8},{1,9},{2,10},{3,11},{4,12},{5,13},{6,14},{7,15},{8,16},{9,17... | collective-permute-start | bytes 442376 | tf_op jit(solution)/shard_map/ppermute | solution.py:864
  284.2 20.2 %collective-permute-start.50 = (bf16[96,768]{1,0:T(8,128)(2,1)S(1)}, bf16[96,768]{1,0:T(8,128)(2,1)S(1)}, u32[]{:S(2)}, u32[]{:S(2)}) collective-permute-start(bf16[96,768]{1,0:T(8,128)(2,1)S(1)} %get-tuple-element.241), channel_id=1, source_target_pairs={{0,16},{1,17},{2,18},{3,19},{4,20},{5,21},{6,22},{7,23},{8,24},{9,... | collective-permute-start | bytes 442376 | tf_op jit(solution)/shard_map/ppermute | solution.py:864
  285.4 19.7 %collective-permute-start.46 = (bf16[48,1536]{1,0:T(8,128)(2,1)S(1)}, bf16[48,1536]{1,0:T(8,128)(2,1)S(1)}, u32[]{:S(2)}, u32[]{:S(2)}) collective-permute-start(bf16[48,1536]{1,0:T(8,128)(2,1)S(1)} %get-tuple-element.236), channel_id=1, source_target_pairs={{0,8},{1,9},{2,10},{3,11},{4,12},{5,13},{6,14},{7,15},{8,16},{9,17... | collective-permute-start | bytes 442376 | tf_op jit(solution)/shard_map/ppermute | solution.py:864
  288.6 19.0 %collective-permute-start.47 = (bf16[48,1536]{1,0:T(8,128)(2,1)S(1)}, bf16[48,1536]{1,0:T(8,128)(2,1)S(1)}, u32[]{:S(2)}, u32[]{:S(2)}) collective-permute-start(bf16[48,1536]{1,0:T(8,128)(2,1)S(1)} %get-tuple-element.237), channel_id=1, source_target_pairs={{0,16},{1,17},{2,18},{3,19},{4,20},{5,21},{6,22},{7,23},{8,24},{9,... | collective-permute-start | bytes 442376 | tf_op jit(solution)/shard_map/ppermute | solution.py:864
  288.8 19.6 %collective-permute-start.48 = (bf16[48,1536]{1,0:T(8,128)(2,1)S(1)}, bf16[48,1536]{1,0:T(8,128)(2,1)S(1)}, u32[]{:S(2)}, u32[]{:S(2)}) collective-permute-start(bf16[48,1536]{1,0:T(8,128)(2,1)S(1)} %get-tuple-element.238), channel_id=1, source_target_pairs={{0,24},{1,25},{2,26},{3,27},{4,28},{5,29},{6,30},{7,31},{8,0},{9,1... | collective-permute-start | bytes 442376 | tf_op jit(solution)/shard_map/ppermute | solution.py:864
  294.8 13.7 %collective-permute-start.51 = (bf16[96,768]{1,0:T(8,128)(2,1)S(1)}, bf16[96,768]{1,0:T(8,128)(2,1)S(1)}, u32[]{:S(2)}, u32[]{:S(2)}) collective-permute-start(bf16[96,768]{1,0:T(8,128)(2,1)S(1)} %get-tuple-element.242), channel_id=1, source_target_pairs={{0,24},{1,25},{2,26},{3,27},{4,28},{5,29},{6,30},{7,31},{8,0},{9,1... | collective-permute-start | bytes 442376 | tf_op jit(solution)/shard_map/ppermute | solution.py:864
  304.4 13.1 %collective-permute-start.43 = (bf16[4,48,1152]{2,1,0:T(8,128)(2,1)S(1)}, bf16[4,48,1152]{2,1,0:T(8,128)(2,1)S(1)}, u32[]{:S(2)}, u32[]{:S(2)}) collective-permute-start(bf16[4,48,1152]{2,1,0:T(8,128)(2,1)S(1)} %get-tuple-element.232), channel_id=1, source_target_pairs={{0,2},{1,3},{2,0},{3,1},{4,6},{5,7},{6,4},{7,5},{8,10},{9,11},{10,... | collective-permute-start | bytes 1327112 | tf_op jit(solution)/shard_map/ppermute | solution.py:864
  305.1 12.7 %collective-permute-start.44 = (bf16[4,48,1152]{2,1,0:T(8,128)(2,1)S(1)}, bf16[4,48,1152]{2,1,0:T(8,128)(2,1)S(1)}, u32[]{:S(2)}, u32[]{:S(2)}) collective-permute-start(bf16[4,48,1152]{2,1,0:T(8,128)(2,1)S(1)} %get-tuple-element.233), channel_id=1, source_target_pairs={{0,4},{1,5},{2,6},{3,7},{4,0},{5,1},{6,2},{7,3},{8,12},{9,13},{10,... | collective-permute-start | bytes 1327112 | tf_op jit(solution)/shard_map/ppermute | solution.py:864
  307.5 17.0 %collective-permute-start.45 = (bf16[4,48,1152]{2,1,0:T(8,128)(2,1)S(1)}, bf16[4,48,1152]{2,1,0:T(8,128)(2,1)S(1)}, u32[]{:S(2)}, u32[]{:S(2)}) collective-permute-start(bf16[4,48,1152]{2,1,0:T(8,128)(2,1)S(1)} %get-tuple-element.234), channel_id=1, source_target_pairs={{0,6},{1,7},{2,4},{3,5},{4,2},{5,3},{6,0},{7,1},{8,14},{9,15},{10,... | collective-permute-start | bytes 1327112 | tf_op jit(solution)/shard_map/ppermute | solution.py:864
  308.4 16.4 %collective-permute-start.42 = (bf16[4,4,48,512]{3,2,1,0:T(8,128)(2,1)S(1)}, bf16[4,4,48,512]{3,2,1,0:T(8,128)(2,1)S(1)}, u32[]{:S(2)}, u32[]{:S(2)}) collective-permute-start(bf16[4,4,48,512]{3,2,1,0:T(8,128)(2,1)S(1)} %copy-done.28), channel_id=1, source_target_pairs={{0,1},{1,0},{2,3},{3,2},{4,5},{5,4},{6,7},{7,6},{8,9},{9,8},{10,11... | collective-permute-start | bytes 2359304 | tf_op jit(solution)/shard_map/ppermute | solution.py:864
  325.0 10.7 %collective-permute-start.55 = (bf16[48,1152]{1,0:T(8,128)(2,1)S(1)}, bf16[48,1152]{1,0:T(8,128)(2,1)S(1)}, u32[]{:S(2)}, u32[]{:S(2)}) collective-permute-start(bf16[48,1152]{1,0:T(8,128)(2,1)S(1)} %get-tuple-element.248), channel_id=1, source_target_pairs={{0,8},{1,9},{2,10},{3,11},{4,12},{5,13},{6,14},{7,15},{8,16},{9,17... | collective-permute-start | bytes 331784 | tf_op jit(solution)/shard_map/ppermute | solution.py:864
  335.7 11.2 %collective-permute-start.53 = (bf16[4,48,512]{2,1,0:T(8,128)(2,1)S(1)}, bf16[4,48,512]{2,1,0:T(8,128)(2,1)S(1)}, u32[]{:S(2)}, u32[]{:S(2)}) collective-permute-start(bf16[4,48,512]{2,1,0:T(8,128)(2,1)S(1)} %get-tuple-element.245), channel_id=1, source_target_pairs={{0,4},{1,5},{2,6},{3,7},{4,0},{5,1},{6,2},{7,3},{8,12},{9,13},{10,... | collective-permute-start | bytes 589832 | tf_op jit(solution)/shard_map/ppermute | solution.py:864
  337.5 9.4 %collective-permute-start.54 = (bf16[4,48,512]{2,1,0:T(8,128)(2,1)S(1)}, bf16[4,48,512]{2,1,0:T(8,128)(2,1)S(1)}, u32[]{:S(2)}, u32[]{:S(2)}) collective-permute-start(bf16[4,48,512]{2,1,0:T(8,128)(2,1)S(1)} %get-tuple-element.246), channel_id=1, source_target_pairs={{0,6},{1,7},{2,4},{3,5},{4,2},{5,3},{6,0},{7,1},{8,14},{9,15},{10,... | collective-permute-start | bytes 589832 | tf_op jit(solution)/shard_map/ppermute | solution.py:864
  (57 other events, 574.4 us)

commit v3 on v2

--- a/solution.py
+++ b/solution.py
@@ -57,7 +57,7 @@
 
 
 def full_spec(shape):
-    return pl.BlockSpec(shape, lambda *_: (0,) * len(shape))
+    return pl.BlockSpec(shape, lambda *_: (0,) * len(shape), pipeline_mode=pl.Buffered(1))
 
 
 def lane_masks(rows):
@@ -111,24 +111,24 @@
         o_ref[q0 : q0 + 256, :] = (outs[0] + outs[1]).T.astype(BF)
 
 
-def attn_call(joined, seg_row, seg_col):
+def attn_call(joined, seg_row, seg_col, group0, groups):
     rows = joined.shape[0]
     pairs = joined.shape[1] // 384
+    at = lambda t: pl.BlockSpec((rows, 128), lambda p: (0, pair_block(group0 * 2 + p, pairs) * 3 + t))
     return pl.pallas_call(
         attn_kernel,
-        grid=(pairs,),
-        in_specs=[pl.BlockSpec((rows, 128), lambda p, t=t: (0, pair_block(p, pairs) * 3 + t)) for t in range(3)]
-        + [full_spec((1, 256)), full_spec((256, 1))],
+        grid=(2 * groups,),
+        in_specs=[at(0), at(1), at(2), full_spec((1, 256)), full_spec((256, 1))],
         out_specs=[
             pl.BlockSpec((rows, 128), lambda p: (0, p)),
             pl.BlockSpec((1, 2, rows), lambda p: (p, 0, 0)),
         ],
         out_shape=[
-            jax.ShapeDtypeStruct((rows, pairs * 128), BF),
-            jax.ShapeDtypeStruct((pairs, 2, rows), F32),
+            jax.ShapeDtypeStruct((rows, groups * 256), BF),
+            jax.ShapeDtypeStruct((2 * groups, 2, rows), F32),
         ],
         compiler_params=params(),
-        cost_estimate=cost(24e9, 8e6, 5.5e6),
+        cost_estimate=cost(groups * 8e9, 8e6, 5.5e6),
         name="attn",
     )(joined, joined, joined, seg_row, seg_col)
 
@@ -212,7 +212,7 @@
     }
 
 
-VECTOR_ROWS = ("g1", "b1", "qv", "pb", "g2", "b2", "fb", "ob")
+VECTOR_ROWS = {"g1": 0, "b1": 1, "qv": 2, "pb": 3, "g2": 4, "b2": 5, "fb": 6, "ob": 7}
 
 
 def owner_of(shape, size, axis):
@@ -239,7 +239,7 @@
 def unpack_vectors(table, d, devices, out_ref):
     plan = vector_plan(d, devices)
     picked = [dot(row_pick(devices, d, k), table).astype(BF) for k in range(3)]
-    for i, name in enumerate(VECTOR_ROWS):
+    for name, i in VECTOR_ROWS.items():
         k, first, size = plan[name]
         n = size * devices
         mine, spot = vector_maps(devices, n, first, size)
@@ -261,6 +261,41 @@
         piece = dot_0(row_pick(devices, d, k), parts[k].astype(BF))
         total = piece if total is None else total + piece
     return total.astype(BF)
+
+
+def cut_kernel(where_ref, w_ref, p_ref, t_ref, keep_ref, give_ref):
+    ci = where_ref[3]
+    pairs = w_ref.shape[1] // 384
+    half = p_ref.shape[1] // 2
+    for h in range(2):
+        for other, out in ((False, keep_ref), (True, give_ref)):
+
+            @pl.when((ci != h) if other else (ci == h))
+            def _():
+                at = 0
+                for p in range(h, pairs, 2):
+                    for t in range(3):
+                        first = (t * pairs + p) * 128
+                        out[:, at : at + 128] = w_ref[:, first : first + 128]
+                        at += 128
+                out[:, at : at + half] = p_ref[:, h * half : (h + 1) * half]
+                out[:, at + half :] = t_ref[...]
+
+
+def cut_call(where, w_qkv, w_proj, table):
+    r = w_qkv.shape[0]
+    cols = (w_qkv.shape[1] + w_proj.shape[1]) // 2 + 128
+    shapes = [full_spec(v.shape) for v in (w_qkv, w_proj, table)]
+    return pl.pallas_call(
+        cut_kernel,
+        grid=(1,),
+        in_specs=[SMEM] + shapes,
+        out_specs=[full_spec((r, cols))] * 2,
+        out_shape=[jax.ShapeDtypeStruct((r, cols), BF)] * 2,
+        compiler_params=params(),
+        cost_estimate=cost(0, 4 * r * cols),
+        name="cut",
+    )(where, w_qkv, w_proj, table)
 
 
 def qkv_kernel(dims, count, devices, where_ref, x_ref, *refs):
@@ -329,7 +364,7 @@
     )(where, x, *own, *oth)
 
 
-def proj_kernel(dims, count, first, where_ref, x_ref, a_ref, vec_ref, *refs):
+def proj_kernel(dims, count, first, where_ref, x_ref, a0_ref, a1_ref, vec_ref, *refs):
     own, oth = refs[:count], refs[count : 2 * count]
     mid_ref, n_ref, w_scr, w_sem = refs[2 * count :]
     d = x_ref.shape[1]
@@ -340,7 +375,7 @@
         for h in range(2):
             wait_columns(dims, w_scr, w_sem, h)
 
-    a = a_ref[...]
+    a = jnp.concatenate([a0_ref[...], a1_ref[...]], axis=1)
     branch = jnp.concatenate([dot(a, flat2(w_scr[h])) for h in range(2)], axis=1) + vec_ref[3:4, :d]
     middle = x_ref[...].astype(F32) + BS * branch
     mid_ref[...] = middle
@@ -355,50 +390,45 @@
     return pl.pallas_call(
         functools.partial(proj_kernel, dims, len(own), 3 * d // 2),
         grid=(rows // br,),
-        in_specs=[SMEM, row, row, full_spec(vec.shape)] + [ANY] * (2 * len(own)),
+        in_specs=[SMEM, row] + [pl.BlockSpec((br, v.shape[1]), lambda i: (i, 0)) for v in att]
+        + [full_spec(vec.shape)] + [ANY] * (2 * len(own)),
         out_specs=[row, row],
         out_shape=[jax.ShapeDtypeStruct((rows, d), F32), jax.ShapeDtypeStruct((rows, d), BF)],
         scratch_shapes=weight_scratch(dims, own[0].shape[1], d // 2),
         compiler_params=params(),
         cost_estimate=cost(2 * rows * d * d, rows * d * 10 + d * d * 2),
         name="proj",
-    )(where, x, att, vec, *own, *oth)
-
-
-def hidden_parts(dims, n, d):
-    per = min(n, d)
-    return per, d // per
+    )(where, x, *att, vec, *own, *oth)
 
 
 def mlp_kernel(dims, count, where_ref, n_ref, c_ref, mid_ref, vec_ref, *refs):
-    fc_own, fc_oth = refs[: count[0]], refs[count[0] : 2 * count[0]]
-    refs = refs[2 * count[0] :]
-    out_own, out_oth = refs[: count[1]], refs[count[1] : 2 * count[1]]
+    own, oth = refs[:count], refs[count : 2 * count]
     (
-        out_ref, gn_ref, gfb_ref, gob_ref, gf_own, gf_oth, go_own, go_oth,
+        out_ref, gn_ref, gfb_ref, gob_ref, g_own, g_oth,
         nt_scr, mg_scr, acc_scr, act_scr, gp_scr, f_scr, f_sem, o_scr, o_sem, gf_scr, gf_sem, go_scr, go_sem,
-    ) = refs[2 * count[1] :]
+    ) = refs[2 * count :]
     z_n, y_n, x_n = dims
     zi, yi, xi, ci = [where_ref[i] for i in range(4)]
     j = pl.program_id(0)
     blocks = o_scr.shape[0]
     rows, d = n_ref.shape
-    n = out_own[0].shape[1]
-    per, parts = hidden_parts(dims, n, d)
+    n = own[0].shape[1]
+    wide = f_scr.shape[-1]
+    parts = d // n
     br = 256
 
     @pl.when(j == 0)
     def _():
-        load_columns(dims, where_ref, fc_own, fc_oth, 0, f_scr.shape[-1], f_scr, f_sem)
+        load_columns(dims, where_ref, own, oth, 0, wide, f_scr, f_sem)
         for i, s, z, y, x in chips_of(dims, where_ref):
-            for core, src in ((ci, out_own), (1 - ci, out_oth)):
-                for q in range(n // per):
-                    at = (((z * y_n + y) * x_n + x) * 2 + core) * n + q * per
-                    blk, off = at // d, lax.rem(at, d)
+            for core, src in ((ci, own), (1 - ci, oth)):
+                for t in range(2):
+                    at = (((z * y_n + y) * x_n + x) * 2 + core) * 2 + t
+                    q = lax.rem(at, parts)
                     local_copy(
-                        piece_at(dims, src, i, s).at[pl.ds(q * per, per), :],
-                        o_scr.at[blk, pl.ds(pl.multiple_of(off, 16), per), :],
-                        o_sem.at[blk, off // per],
+                        piece_at(dims, src, i, s).at[:, pl.ds(wide + t * d, d)],
+                        o_scr.at[at // parts, pl.ds(pl.multiple_of(q * n, 16), n), :],
+                        o_sem.at[at // parts, q],
                     ).start()
         nt_scr[...] = n_ref[...].T
         total = jnp.zeros_like(gob_ref)
@@ -414,7 +444,7 @@
         wait_columns(dims, f_scr, f_sem, 1)
 
     for q in range(parts):
-        part = o_scr.at[j, pl.ds(q * per, per), :]
+        part = o_scr.at[j, pl.ds(q * n, n), :]
         local_copy(part, part, o_sem.at[j, q]).wait()
 
     half = j // (blocks // 2)
@@ -451,25 +481,23 @@
 
     gfb_ref[...] = bias_sum
     gf_scr[j] = dot(nt_scr[...], gp_scr[...]).astype(BF).reshape(gf_scr.shape[1:])
-    store_columns(dims, where_ref, gf_scr.at[j], gf_own, gf_oth, half, first, d, gf_sem.at[j])
+    store_columns(dims, where_ref, gf_scr.at[j], g_own, g_oth, half, first, d, gf_sem.at[j])
     go_scr[j] = dot_0(act_scr[...], mg_scr[...]).astype(BF)
     for q in range(parts):
-        at = j * d + q * per
-        dev = at // n
+        at = j * parts + q
+        dev, t = at // 2, lax.rem(at, 2)
         core = lax.rem(dev, 2)
         x = lax.rem(dev // 2, x_n)
         y = lax.rem(dev // (2 * x_n), y_n)
         z = dev // (2 * x_n * y_n)
         piece = lax.rem(y - yi + y_n, y_n) * x_n + lax.rem(x - xi + x_n, x_n)
         slot = lax.rem(z - zi + z_n, z_n)
-        off = pl.multiple_of(lax.rem(at, n), 16)
-        for other, out in ((False, go_own), (True, go_oth)):
+        to = pl.ds(pl.multiple_of(wide + t * d, 128), d)
+        for other, out in ((False, g_own), (True, g_oth)):
 
             @pl.when((core != ci) if other else (core == ci))
             def _():
-                local_copy(
-                    go_scr.at[j, pl.ds(q * per, per), :], out.at[piece, slot, pl.ds(off, per), :], go_sem.at[j, q]
-                ).start()
+                local_copy(go_scr.at[j, pl.ds(q * n, n), :], out.at[piece, slot, :, to], go_sem.at[j, q]).start()
 
     @pl.when(j == blocks - 1)
     def _():
@@ -477,51 +505,49 @@
             rr = slice(r, r + br)
             out_ref[rr, :] = (mid_ref[rr, :] + BS * (acc_scr[rr, :] + vec_ref[7:8, :d])).astype(BF)
         for b in range(blocks):
-            wait_store(dims, gf_scr.at[b], gf_own, 0, d, gf_sem.at[b])
+            wait_store(dims, gf_scr.at[b], g_own, 0, d, gf_sem.at[b])
             for q in range(parts):
-                part = go_scr.at[b, pl.ds(q * per, per), :]
+                part = go_scr.at[b, pl.ds(q * n, n), :]
                 local_copy(part, part, go_sem.at[b, q]).wait()
 
 
-def mlp_call(dims, where, normed, cot, middle, vec, fc, out):
+def mlp_call(dims, where, normed, cot, middle, vec, own, oth):
     rows, d = normed.shape
-    n, half = fc[0][0].shape[1:]
-    blocks = 2 * half // d
-    n_out = out[0][0].shape[1]
-    per, parts = hidden_parts(dims, n_out, d)
+    n, cols = own[0].shape[1:]
+    wide = cols - 2 * d
+    blocks = 2 * wide // d
     count = dims[1] * dims[2]
     act = full_spec((rows, d))
-    f_piece = jax.ShapeDtypeStruct((count, dims[0], n, half), BF)
-    o_piece = jax.ShapeDtypeStruct((count, dims[0], n_out, d), BF)
+    piece = jax.ShapeDtypeStruct((count, dims[0], n, cols), BF)
     return pl.pallas_call(
-        functools.partial(mlp_kernel, dims, (len(fc[0]), len(out[0]))),
+        functools.partial(mlp_kernel, dims, len(own)),
         grid=(blocks,),
-        in_specs=[SMEM, act, act, act, full_spec(vec.shape)] + [ANY] * (2 * (len(fc[0]) + len(out[0]))),
-        out_specs=[act, act, pl.BlockSpec((1, d), lambda j: (0, j)), full_spec((1, d))] + [ANY] * 4,
+        in_specs=[SMEM, act, act, act, full_spec(vec.shape)] + [ANY] * (2 * len(own)),
+        out_specs=[act, act, pl.BlockSpec((1, d), lambda j: (0, j)), full_spec((1, d))] + [ANY] * 2,
         out_shape=[
             jax.ShapeDtypeStruct((rows, d), BF),
             jax.ShapeDtypeStruct((rows, d), F32),
-            jax.ShapeDtypeStruct((1, 2 * half), F32),
+            jax.ShapeDtypeStruct((1, blocks * d), F32),
             jax.ShapeDtypeStruct((1, d), F32),
-            f_piece, f_piece, o_piece, o_piece,
+            piece, piece,
         ],
         scratch_shapes=[
             pltpu.VMEM((d, rows), BF), pltpu.VMEM((rows, d), BF), pltpu.VMEM((rows, d), F32),
             pltpu.VMEM((rows, d), BF), pltpu.VMEM((rows, d), BF),
         ]
-        + weight_scratch(dims, n, half)
+        + weight_scratch(dims, n, wide)
         + [
-            pltpu.VMEM((blocks, d, d), BF), pltpu.SemaphoreType.DMA((blocks, parts)),
+            pltpu.VMEM((blocks, d, d), BF), pltpu.SemaphoreType.DMA((blocks, d // n)),
             pltpu.VMEM((blocks,) + dims + (n, d), BF), pltpu.SemaphoreType.DMA((blocks, count, dims[0])),
-            pltpu.VMEM((blocks, d, d), BF), pltpu.SemaphoreType.DMA((blocks, parts)),
+            pltpu.VMEM((blocks, d, d), BF), pltpu.SemaphoreType.DMA((blocks, d // n)),
         ],
         compiler_params=params(),
-        cost_estimate=cost(24 * rows * d * half, 30e6, rows * half),
+        cost_estimate=cost(24 * rows * d * wide, 30e6, 2 * rows * wide),
         name="mlp",
-    )(where, normed, cot, middle, vec, *fc[0], *fc[1], *out[0], *out[1])
-
-
-def proj_back_kernel(dims, count, first, where_ref, gn_ref, mid_ref, c_ref, a_ref, vec_ref, ind_ref, *refs):
+    )(where, normed, cot, middle, vec, *own, *oth)
+
+
+def proj_back_kernel(dims, count, first, where_ref, gn_ref, mid_ref, c_ref, a0_ref, a1_ref, vec_ref, ind_ref, *refs):
     own, oth = refs[:count], refs[count : 2 * count]
     (
         gm_ref, ga_ref, gw_ref, del_ref, gg_ref, gb_ref, gpb_ref, gw_acc, w_scr, w_sem,
@@ -548,10 +574,11 @@
     gm_ref[...] = gm
     pg = (BS * gm).astype(BF)
     gpb_ref[...] += jnp.sum(pg.astype(F32), axis=0, keepdims=True)
-    gw_acc[...] += dot_0(a_ref[...], pg)
+    a = jnp.concatenate([a0_ref[...], a1_ref[...]], axis=1)
+    gw_acc[...] += dot_0(a, pg)
     ga = (dot_t(pg[:, :m], flat2(w_scr[0])) + dot_t(pg[:, m:], flat2(w_scr[1]))).astype(BF)
     ga_ref[...] = ga
-    prod = ga.astype(F32) * a_ref[...].astype(F32)
+    prod = ga.astype(F32) * a.astype(F32)
     high = prod.astype(BF)
     low = (prod - high.astype(F32)).astype(BF)
     del_ref[...] = dot_t(ind_ref[...], high) + dot_t(ind_ref[...], low)
@@ -571,7 +598,8 @@
     return pl.pallas_call(
         functools.partial(proj_back_kernel, dims, len(own), 3 * d // 2),
         grid=(rows // br,),
-        in_specs=[SMEM, row, row, row, row, full_spec(vec.shape), full_spec((16, d))] + [ANY] * (2 * len(own)),
+        in_specs=[SMEM, row, row, row] + [pl.BlockSpec((br, v.shape[1]), lambda i: (i, 0)) for v in att]
+        + [full_spec(vec.shape), full_spec((16, d))] + [ANY] * (2 * len(own)),
         out_specs=[row, row, full_spec((d, d)), pl.BlockSpec((16, br), lambda i: (0, i)), one, one, one],
         out_shape=[
             jax.ShapeDtypeStruct((rows, d), F32),
@@ -584,7 +612,7 @@
         compiler_params=params(),
         cost_estimate=cost(4 * rows * d * d, rows * d * 16),
         name="proj_back",
-    )(where, gn, middle, cot, att, vec, ind, *own, *oth)
+    )(where, gn, middle, cot, *att, vec, ind, *own, *oth)
 
 
 def pair_back(j_ref, do_ref, lse_ref, del_ref, segr_ref, segc_ref, dj_ref, dk_acc, dv_acc):
@@ -724,7 +752,7 @@
         SMEM,
         pl.BlockSpec((rows, 384), lambda i: (0, pair_block(group0 * 2 + i, pairs))),
         pl.BlockSpec((rows, 128), lambda i: (0, group0 * 2 + i)),
-        stat, stat, full_spec((1, 256)), full_spec((256, 1)), act, full_spec(vec.shape),
+        pl.BlockSpec((1, 2, rows), lambda i: (i, 0, 0)), stat, full_spec((1, 256)), full_spec((256, 1)), act, full_spec(vec.shape),
     ] + [ANY] * (2 * arrays)
     if last:
         in_specs += [act, full_spec((1, 2 * d)), act, full_spec((1, 4 * d))] + [one] * 4
@@ -781,8 +809,8 @@
     if not joined:
         return w[:, h * (cols // 2) : (h + 1) * (cols // 2)]
     pairs = cols // 384
-    parts = w.reshape(r, 3, pairs // 2, 2, 128)[:, :, :, h]
-    return jnp.swapaxes(parts, 1, 2).reshape(r, cols // 2)
+    starts = [(t * pairs + p) * 128 for p in range(h, pairs, 2) for t in range(3)]
+    return jnp.concatenate([w[:, s : s + 128] for s in starts], axis=1)
 
 
 def join_columns(left, right):
@@ -813,28 +841,33 @@
         attn = whole(jnp.concatenate([w_qkv, w_proj, table], axis=1))
         cut = w_qkv.shape[1], w_qkv.shape[1] + w_proj.shape[1]
         fc, out = whole(w_fc), whole(w_out)
-        first = [
-            jnp.concatenate(
-                [half_columns(attn[:, : cut[0]], h, True), half_columns(attn[:, cut[0] : cut[1]], h), attn[:, cut[1] :]],
-                axis=1,
+        d = out.shape[1]
+        lists = [[], []]
+        for h in range(2):
+            qkv, proj, table = attn[:, : cut[0]], attn[:, cut[0] : cut[1]], attn[:, cut[1] :]
+            lists[0].append(jnp.concatenate([half_columns(qkv, h, True), half_columns(proj, h), table], axis=1))
+            lists[1].append(
+                jnp.concatenate([half_columns(fc, h)] + [out[(2 * h + t) * d : (2 * h + t + 1) * d] for t in range(2)], axis=1)
             )
-            for h in range(2)
-        ]
-        second = [half_columns(fc, h) for h in range(2)]
-        third = [out[: out.shape[0] // 2], out[out.shape[0] // 2 :]]
         listed = []
-        for pair in (first, second, third):
+        for pair in lists:
             own, oth = self.pick(pair)
             listed.append(([own[None]], [oth[None]]))
         return listed
 
-    def scatter(self, own, oth, rows=False):
+    def scatter(self, own, oth):
         pair = self.pick([own[0, 0], oth[0, 0]])
-        if rows:
-            return lax.psum_scatter(jnp.concatenate(pair, axis=0), AXES, scatter_dimension=0, tiled=True).astype(F32)
         m = pair[0].shape[1]
         mine = lax.psum_scatter(jnp.concatenate(pair, axis=1), AXES, scatter_dimension=0, tiled=True).astype(F32)
         return mine[:, :m], mine[:, m:]
+
+    def scatter_hidden(self, own, oth):
+        pair = self.pick([own[0, 0], oth[0, 0]])
+        d = pair[0].shape[0]
+        wide = pair[0].shape[1] - 2 * d
+        fc = self.scatter(own[..., :wide], oth[..., :wide])
+        out = jnp.concatenate([v[:, wide + t * d : wide + (t + 1) * d] for v in pair for t in range(2)], axis=0)
+        return fc, lax.psum_scatter(out, AXES, scatter_dimension=0, tiled=True).astype(F32)
 
 
 class Chips:
@@ -863,32 +896,20 @@
                         pairs.append((here, there))
         return lax.ppermute(array, AXES, pairs)
 
-    def cut_halves(self, w_qkv, w_proj, table, w_fc):
-        halves = [
-            jnp.concatenate(
-                [half_columns(w_qkv, h, True), half_columns(w_proj, h), table, half_columns(w_fc, h)], axis=1
-            )
-            for h in range(2)
-        ]
-        keep, give = self.pick(halves)
-        rows = jnp.concatenate(self.pick([keep, self.send(give, dc=1)]), axis=0)
-        cut = (w_qkv.shape[1] + w_proj.shape[1]) // 2 + 128
-        return rows[:, :cut], rows[:, cut:]
+    def trade(self, halves):
+        return self.rows_of(*self.pick(halves))
+
+    def rows_of(self, keep, give):
+        return jnp.concatenate(self.pick([keep, self.send(give, dc=1)]), axis=0)
 
     def along_z(self, piece):
-        return jnp.stack([piece] + [self.send(piece, dz=-k) for k in range(1, self.dims[0])])
+        return [piece] + [self.send(piece, dz=-k) for k in range(1, self.dims[0])]
 
     def swap(self, arrays):
         return [self.send(v, dc=1) for v in arrays]
 
     def add_core(self, own, theirs):
         return [add_all([own[i], theirs[i]]).astype(BF) for i in range(own.shape[0])]
-
-    def add_chips(self, block, arrived):
-        return [add_all([block[j]] + [a[j] for a in arrived]).astype(BF) for j in range(self.dims[0])]
-
-    def sum_z(self, column):
-        return add_all([column[0]] + [self.send(column[j], dz=j) for j in range(1, self.dims[0])])
 
     def rows_back(self, total):
         n = total.shape[0] // 2
@@ -915,19 +936,23 @@
     return jnp.pad(jnp.stack(flat), ((0, r - 3), (0, 128 - 4 * r)))
 
 
-def results(r, start, out, gx, s_fc, s_out, s_one, s_two):
-    rows = out.shape[0]
-    wide = 2 * 384
-    s_qkv = join_columns(*[jnp.concatenate([a[:, :wide], b[:, :-128]], axis=1) for a, b in zip(s_one, s_two)])
-    s_proj = jnp.concatenate([v[:, wide:] for v in s_one], axis=1)
-    small = s_two[0][:, -128:]
-    row0, row1, row2 = [small[k, : 4 * r] for k in range(3)]
+def results(r, start, out, gx, s_fc, s_out, s_attn):
+    rows, d = out.shape
+    cut = 3 * d // 2
+    s_qkv = join_columns(*[v[:, :cut] for v in s_attn])
+    s_proj = jnp.concatenate([v[:, cut:-128] for v in s_attn], axis=1)
+    row0, row1, row2 = [s_attn[0][k, 2 * d : 2 * d + 4 * r] for k in range(3)]
     restore = rows - start
     return (
         roll_rows(out, restore), roll_rows(gx, restore),
         row0[:r], row0[r : 2 * r], s_qkv, row0[2 * r :], s_proj, row2[:r],
         row2[r : 2 * r], row2[2 * r : 3 * r], jnp.concatenate(s_fc, axis=1), row1, s_out, row2[3 * r :],
     )
+
+
+def merge_parts(one, two):
+    a, b = one.shape[-1], two.shape[-1]
+    return jnp.concatenate([one[..., : 2 * 384], two[..., : b - 128], one[..., 2 * 384 : a], two[..., b - 128 :]], axis=-1)
 
 
 def block_plain(
@@ -939,26 +964,24 @@
     devices = d // r
     dims, where = links.dims, links.where()
     table = vector_table(r, ln1_gain, ln1_bias, qv_bias, proj_bias, ln2_gain, ln2_bias, fc_bias, out_bias)
-    attn_w, fc_w, out_w = links.gather(w_qkv, w_proj, table, w_fc, w_out)
+    attn_w, mlp_w = links.gather(w_qkv, w_proj, table, w_fc, w_out)
     start, seg_row, seg_col, x, cot = prepare(tokens, lengths, cotangent)
     joined, vec = qkv_call(dims, where, x, *attn_w, devices)
-    att, lse = attn_call(joined, seg_row, seg_col)
+    att0, lse0 = attn_call(joined, seg_row, seg_col, 0, 2)
+    att1, lse1 = attn_call(joined, seg_row, seg_col, 2, d // 256 - 2)
+    att = att0, att1
     middle, normed_two = proj_call(dims, where, x, att, vec, *attn_w)
-    out, gn, gfb, gob, gf_own, gf_oth, go_own, go_oth = mlp_call(
-        dims, where, normed_two, cot, middle, vec, fc_w, out_w
-    )
-    s_fc = links.scatter(gf_own, gf_oth)
-    s_out = links.scatter(go_own, go_oth, rows=True)
+    out, gn, gfb, gob, *m_g = mlp_call(dims, where, normed_two, cot, middle, vec, *mlp_w)
+    s_fc, s_out = links.scatter_hidden(*m_g)
     gm, ga, gw_proj, delta, gg2, gb2, gpb = proj_back_call(dims, where, gn, middle, cot, att, vec, *attn_w)
     delta = delta[: d // HD].reshape(d // 128, 2, rows)
-    shared = (dims, where, joined, ga, lse, delta, seg_row, seg_col, x, vec, *attn_w)
-    gn1, qv1, g_own, g_oth = attn_back_call(*shared, 0, 2, (gw_proj,), False, devices)
-    s_one = links.scatter(g_own, g_oth)
-    gx, g_own, g_oth = attn_back_call(
-        *shared, 2, d // 256 - 2, (gn1, qv1, gm, gfb, gob, gg2, gb2, gpb), True, devices
+    stats = (delta, seg_row, seg_col, x, vec, *attn_w)
+    gn1, qv1, g_own, g_oth = attn_back_call(dims, where, joined, ga, lse0, *stats, 0, 2, (gw_proj,), False, devices)
+    gx, h_own, h_oth = attn_back_call(
+        dims, where, joined, ga, lse1, *stats, 2, d // 256 - 2, (gn1, qv1, gm, gfb, gob, gg2, gb2, gpb), True, devices
     )
-    s_two = links.scatter(g_own, g_oth)
-    return results(r, start, out, gx, s_fc, s_out, s_one, s_two)
+    s_attn = links.scatter(merge_parts(g_own, h_own), merge_parts(g_oth, h_oth))
+    return results(r, start, out, gx, s_fc, s_out, s_attn)
 
 
 def block_chips(
@@ -968,81 +991,85 @@
     rows, d = tokens.shape
     r = w_qkv.shape[0]
     devices = d // r
-    dims, where, send = links.dims, links.where(), links.send
+    dims, where, send, swap = links.dims, links.where(), links.send, links.swap
     table = vector_table(r, ln1_gain, ln1_bias, qv_bias, proj_bias, ln2_gain, ln2_bias, fc_bias, out_bias)
-    a, b = links.cut_halves(w_qkv, w_proj, table, w_fc)
-    start, seg_row, seg_col, x, cot = prepare(tokens, lengths, cotangent)
-
+
+    def xy(column):
+        return send(column, dx=1), send(column, dy=1)
+
+    def corner(x_part, y_part):
+        return [send(x_part[:2], dy=1), send(y_part[2:], dx=1)]
+
+    a = links.rows_of(*cut_call(where, w_qkv, w_proj, table))
+    a, tokens, lengths, cotangent, w_fc = together(a, tokens, lengths, cotangent, w_fc)
     a0 = links.along_z(a)
-    a0, b, c = together(a0, b, w_out)
-    ax, ay = send(a0, dx=1), send(a0, dy=1)
-    b0 = links.along_z(b)
-    ax, ay, b0, c = together(ax, ay, b0, c)
-    ad = [send(ax[:2], dy=1), send(ay[2:], dx=1)]
-    a_oth = links.swap([a0, ax, ay])
-    c0 = links.along_z(c)
-    ad, a_oth, c0, b0 = together(ad, a_oth, c0, b0)
-    attn_w = [a0, ax, ay] + ad, a_oth + links.swap(ad)
-    attn_w, b0, c0, x = together(attn_w, b0, c0, x)
+    fc = links.trade([half_columns(w_fc, h) for h in range(2)])
+    m = jnp.concatenate([fc, w_out[: 2 * r], w_out[2 * r :]], axis=1)
+    prep = prepare(tokens, lengths, cotangent)
+    a0, prep, m = together(a0, prep, m)
+    start, seg_row, seg_col, x, cot = prep
+    a0 = jnp.stack(a0)
+    ax, ay = xy(a0)
+    m1, m3 = send(m, dz=-1), send(m, dz=-3)
+    ax, ay, m, m1, m3 = together(ax, ay, m, m1, m3)
+    ad = corner(ax, ay)
+    a_oth = swap([a0, ax, ay])
+    m2 = send(m, dz=-2)
+    ad, a_oth, m2 = together(ad, a_oth, m2)
+    m0 = jnp.stack([m, m1, m2, m3])
+    attn_w = [a0, ax, ay] + ad, a_oth + swap(ad)
+    m0, x, attn_w = together(m0, x, attn_w)
 
     joined, vec = qkv_call(dims, where, x, *attn_w, devices)
-    bx, by = send(b0, dx=1), send(b0, dy=1)
-    joined, bx, by, c0 = together(joined, bx, by, c0)
-
-    att, lse = attn_call(joined, seg_row, seg_col)
-    bd = send(bx, dy=1)
-    cx, cy = send(c0, dx=1), send(c0, dy=1)
-    b_oth = links.swap([b0, bx, by])
-    att, bd, cx, cy, b_oth = together(att, bd, cx, cy, b_oth)
+    att0, lse0 = attn_call(joined, seg_row, seg_col, 0, 2)
+    mx, my = xy(m0)
+    att0, joined, mx, my = together(att0, joined, mx, my)
+    att1, lse1 = attn_call(joined, seg_row, seg_col, 2, d // 256 - 2)
+    att = att0, att1
 
     middle, normed_two = proj_call(dims, where, x, att, vec, *attn_w)
-    cd = send(cy, dx=1)
-    b_oth = b_oth + links.swap([bd])
-    c_oth = links.swap([c0, cx, cy])
-    normed_two, cd, b_oth, c_oth = together(normed_two, cd, b_oth, c_oth)
-    c_oth = c_oth + links.swap([cd])
-
-    out, gn, gfb, gob, gf_own, gf_oth, go_own, go_oth = mlp_call(
-        dims, where, normed_two, cot, middle, vec, ([b0, bx, by, bd], b_oth), ([c0, cx, cy, cd], c_oth)
+    md = corner(mx, my)
+    m_oth = swap([m0, mx, my])
+    normed_two, md, m_oth = together(normed_two, md, m_oth)
+    mlp_w = [m0, mx, my] + md, m_oth + swap(md)
+
+    out, gn, gfb, gob, m_own, m_oth = mlp_call(dims, where, normed_two, cot, middle, vec, *mlp_w)
+    gm, ga, gw_proj, delta, gg2, gb2, gpb = proj_back_call(dims, where, gn, middle, cot, att, vec, *attn_w)
+    (m_oth,) = swap([m_oth])
+    ga, delta, m_own, m_oth = together(ga, delta, m_own, m_oth)
+    delta = delta[: d // HD].reshape(d // 128, 2, rows)
+    b = links.add_core(m_own, m_oth)
+    b, ga, delta = together(b, ga, delta)
+    stats = (delta, seg_row, seg_col, x, vec, *attn_w)
+    first = send(b[3][:2], dy=1), send(b[3][2:], dx=1), send(b[1][2:], dx=1), send(b[2][:2], dy=1)
+    gn1, qv1, g_own, g_oth = attn_back_call(dims, where, joined, ga, lse0, *stats, 0, 2, (gw_proj,), False, devices)
+    gn1, g_own, g_oth, first = together(gn1, g_own, g_oth, first)
+
+    by_y, by_x, x_high, y_low = first
+    sums = add_all([b[1][:2], by_y]).astype(BF), add_all([b[2][2:], by_x]).astype(BF)
+    sums, gn1, g_own, g_oth = together(sums, gn1, g_own, g_oth)
+    x_low, y_high = send(sums[0], dx=1), send(sums[1], dy=1)
+    (g_oth,) = swap([g_oth])
+    gx, h_own, h_oth = attn_back_call(
+        dims, where, joined, ga, lse1, *stats, 2, d // 256 - 2, (gn1, qv1, gm, gfb, gob, gg2, gb2, gpb), True, devices
     )
-
-    gm, ga, gw_proj, delta, gg2, gb2, gpb = proj_back_call(dims, where, gn, middle, cot, att, vec, *attn_w)
-    delta = delta[: d // HD].reshape(d // 128, 2, rows)
-    gf_oth, go_oth = links.swap([gf_oth, go_oth])
-    fc = links.add_core(gf_own, gf_oth)
-    wo = links.add_core(go_own, go_oth)
-    ga, fc, wo = together(ga, fc, wo)
-
-    shared = (dims, where, joined, ga, lse, delta, seg_row, seg_col, x, vec, *attn_w)
-    gn1, qv1, g_own, g_oth = attn_back_call(*shared, 0, 2, (gw_proj,), False, devices)
-    fd, fy = send(fc[3], dy=1), send(fc[2], dy=1)
-    wd, wx = send(wo[3], dx=1), send(wo[1], dx=1)
-    fcx = add_all([fc[1], fd]).astype(BF)
-    woy = add_all([wo[2], wd]).astype(BF)
-    gn1, g_own, g_oth, fcx, woy, fy, wx = together(gn1, g_own, g_oth, fcx, woy, fy, wx)
-
-    gx, h_own, h_oth = attn_back_call(
-        *shared, 2, d // 256 - 2, (gn1, qv1, gm, gfb, gob, gg2, gb2, gpb), True, devices
-    )
-    fx, wy = send(fcx, dx=1), send(woy, dy=1)
-    (g_oth,) = links.swap([g_oth])
-    fc = links.add_chips(fc[0], [fx, fy])
-    wo = links.add_chips(wo[0], [wx, wy])
-    one = links.add_core(g_own, g_oth)
-    gx, h_own, h_oth, fc, wo, one = together(gx, h_own, h_oth, fc, wo, one)
-
-    fc, wo = links.sum_z(fc), links.sum_z(wo)
-    one = links.add_chips(one[0], [send(one[1], dx=1), send(one[2], dy=1), send(one[3], dx=1, dy=1)])
-    (h_oth,) = links.swap([h_oth])
-    two = links.add_core(h_own, h_oth)
-    two, one, fc, wo = together(two, one, fc, wo)
-    two = links.add_chips(two[0], [send(two[1], dx=1), send(two[2], dy=1), send(two[3], dx=1, dy=1)])
-    one = links.sum_z(one)
-    s_fc = links.rows_back(fc)
-    two, one, s_fc = together(two, one, s_fc)
-    s_two = links.rows_back(links.sum_z(two))
-    s_one = links.rows_back(one)
-    return results(r, start, out, gx, s_fc, wo, s_one, s_two)
+    gx, h_own, h_oth, x_low, y_high, g_oth = together(gx, h_own, h_oth, x_low, y_high, g_oth)
+
+    (h_oth,) = swap([h_oth])
+    column = [add_all([b[0][j], x_low[j], y_low[j]]).astype(BF) for j in range(2)]
+    column += [add_all([b[0][j + 2], x_high[j], y_high[j]]).astype(BF) for j in range(2)]
+    column, h_oth = together(column, h_oth)
+    arrived = [column[0]] + [send(column[j], dz=j) for j in range(1, dims[0])]
+    e = links.add_core(merge_parts(g_own, h_own), merge_parts(g_oth, h_oth))
+    near = send(e[1], dx=1), send(e[2], dy=1), send(e[3], dx=1, dy=1)
+    near, arrived, out, gx = together(near, arrived, out, gx)
+
+    column = [add_all([e[0][j]] + [a[j] for a in near]).astype(BF) for j in range(dims[0])]
+    total = add_all(arrived)
+    s_fc = links.rows_back(total[:, : w_fc.shape[1] // 2])
+    s_out = jnp.concatenate([total[:, -2 * d : -d], total[:, -d:]], axis=0)
+    s_attn = links.rows_back(add_all([column[0]] + [send(column[j], dz=j) for j in range(1, dims[0])]))
+    return results(r, start, out, gx, s_fc, s_out, s_attn)
 
 
 def solution(mesh):

time: 364 us -> 329 us (0.904)
  waiting for transfers between devices: 92.7 us -> 56.4 us
  starting transfers between devices: 61.1 us -> 42 us
  other arithmetic: 29.2 us -> 38 us
  local copies, waits for them, and re-layouts: 11.1 us -> 18.2 us
  Pallas kernels: 158 us -> 163 us
    ppermute x64 -> x46, waiting for transfers between devices: 92.7 us -> 56.4 us  [send(): return lax.ppermute(array, AXES, pairs)]
    ppermute x64 -> x46, starting transfers between devices: 61.1 us -> 42 us  [send(): return lax.ppermute(array, AXES, pairs)]
    slice x10 -> x23, local copies, waits for them, and re-layouts: 1.17 us -> 6.68 us  [the longest x4 1.6 us: corner(): return [send(x_part[:2], dy=1), send(y_part[2:], dx=1)]]
    pallas_call x2 -> x4, Pallas kernels: 74.5 us -> 79.7 us  [the longest x1 54.9 us: mlp_call(): pl.pallas_call(functools.partial(mlp_kernel, dims, len(own)), grid=(block...]
  transfers between devices with their start and end apart: 64 -> 46, of which waited for: 23 -> 13; matrix products, arithmetic and copies ran while one was open for 8% -> 9% of each run, Pallas kernels for 29% -> 33%
where the time goes in v3:
time: 329 us; the launch traced here: 325 us
  Pallas kernels  163 us (50%)
  waiting for transfers between devices  56.4 us (17%)
  starting transfers between devices  42 us (13%)
  other arithmetic  38 us (12%)
  local copies, waits for them, and re-layouts  18.2 us (6%)
  between operations  7.51 us (2%)
    ppermute x46, waiting for transfers between devices, send(): return lax.ppermute(array, AXES, pairs)  56.4 us
    pallas_call x1, Pallas kernels, mlp_call(): pl.pallas_call(functools.partial(mlp_kernel, dims, len(own)), grid=(block...  54.9 us
    pallas_call x2, Pallas kernels, attn_back_call(): pl.pallas_call(functools.partial(attn_back_kernel, dims, arrays, group0,...  50.2 us
    ppermute x46, starting transfers between devices, send(): return lax.ppermute(array, AXES, pairs)  42 us
    pallas_call x2, Pallas kernels, attn_call(): pl.pallas_call(attn_kernel, grid=(2 * groups,), in_specs=[at(0), at(1), a...  23.2 us
    pallas_call x1, Pallas kernels, proj_back_call(): pl.pallas_call(functools.partial(proj_back_kernel, dims, len(own), 3 * d...  13.3 us
    pallas_call x1, Pallas kernels, qkv_call(): pl.pallas_call(functools.partial(qkv_kernel, dims, len(own), devices), gr...  11.9 us
    concatenate x3, other arithmetic, roll_rows(): jnp.concatenate([array, array], axis=0)  11.5 us
  transfers between devices with their start and end apart: 46, of which 13 were waited for; matrix products, arithmetic and copies ran while one was open for 9% of the time, Pallas kernels for 33%

profile of v3, /device:TPU:0, one launch (start us, length us, event | category | flops | bytes accessed | tf_op | source)
XLA Modules:
  0.0 324.8 jit_solution(4871953710324152894)
XLA Ops:
  1.5 1.3 fusion.43.t_ref
  3.4 1.6 cut.1
  7.5 5.0 %collective-permute-start.1 = (bf16[48,1664]{1,0:T(8,128)(2,1)S(1)}, bf16[48,1664]{1,0:T(8,128)(2,1)S(1)}, u32[]{:S(2)}, u32[]{:S(2)}) collective-permute-start(bf16[48,1664]{1,0:T(8,128)(2,1)S(1)} %pad_maximum_fusion.7), channel_id=1, source_target_pairs={{0,24},{1,25},{2,26},{3,27},{4,28},{5,29},{6,30},{7,31},{8,0},{9,1... | collective-permute-start | bytes 479240 | tf_op jit(solution)/shard_map/ppermute | solution.py:897
  13.6 1.4 fusion.55
  22.5 4.1 %fusion.4.x_ref = bf16[1024,768]{1,0:T(8,128)(2,1)} fusion(s32[]{:T(128)S(6)} %select_n.150, bf16[1024,768]{1,0:T(8,128)(2,1)} %param.15), kind=kLoop, calls=%fused_computation.18 | loop fusion | flops 3145728 | bytes 3145732 | tf_op jit(solution)/shard_map/concatenate | solution.py:804
  26.6 2.3 fusion.3.c_ref
  30.6 1.6 collective-permute-start.5
  32.2 1.5 collective-permute-start.6
  33.6 2.9 collective-permute-start.7
  37.1 7.2 %collective-permute-done.7 = bf16[48,3072]{1,0:T(8,128)(2,1)S(1)} collective-permute-done((bf16[48,3072]{1,0:T(8,128)(2,1)}, bf16[48,3072]{1,0:T(8,128)(2,1)S(1)}, u32[]{:S(2)}, u32[]{:S(2)}) %collective-permute-start.7) | collective-permute-done | bytes 294944 | tf_op jit(solution)/shard_map/ppermute | solution.py:897
  44.3 6.2 %collective-permute-done.8 = bf16[48,3072]{1,0:T(8,128)(2,1)S(1)} collective-permute-done((bf16[48,3072]{1,0:T(8,128)(2,1)}, bf16[48,3072]{1,0:T(8,128)(2,1)S(1)}, u32[]{:S(2)}, u32[]{:S(2)}) %collective-permute-start.8) | collective-permute-done | bytes 294944 | tf_op jit(solution)/shard_map/ppermute | solution.py:897
  53.8 2.2 collective-permute-start.14
  56.8 13.4 %collective-permute-done.14 = bf16[48,3072]{1,0:T(8,128)(2,1)} collective-permute-done((bf16[48,3072]{1,0:T(8,128)(2,1)}, bf16[48,3072]{1,0:T(8,128)(2,1)}, u32[]{:S(2)}, u32[]{:S(2)}) %collective-permute-start.14) | collective-permute-done | bytes 294944 | tf_op jit(solution)/shard_map/ppermute | solution.py:897
  70.8 1.4 pad_maximum_fusion.2.refs_0_
  72.6 1.4 collective-permute-start.17
  74.0 1.5 collective-permute-start.18
  75.6 11.9 %qkv.1 = (bf16[1024,2304]{1,0:T(8,128)(2,1)}, f32[8,3072]{1,0:T(8,128)}) custom-call(s32[4]{0:T(128)} %pad_add_fusion.where_ref, bf16[1024,768]{1,0:T(8,128)(2,1)} %fusion.4.x_ref, bf16[4,48,1664]{2,1,0:T(8,128)(2,1)} %copy-done, bf16[4,48,1664]{2,1,0:T(8,128)(2,1)} %copy-done.2, bf16[4,48,1664]{2,1,0:T(8,128)(2,1)} %copy-done.3, ...), custom_call_target="tpu_custom_call" | custom-call | flops 3623878656 | bytes 9830400 | tf_op jit(solution)/shard_map/qkv/pallas_call | solution.py:348
  87.5 14.8 %attn.2 = (bf16[1024,512]{1,0:T(8,128)(2,1)}, f32[4,2,1024]{2,1,0:T(2,128)}) custom-call(bf16[1024,2304]{1,0:T(8,128)(2,1)} %get-tuple-element.175.q_ref.k_ref.v_ref.j_ref, bf16[1024,2304]{1,0:T(8,128)(2,1)} %get-tuple-element.175.q_ref.k_ref.v_ref.j_ref, bf16[1024,2304]{1,0:T(8,128)(2,1)} %get-tuple-element.175.q_ref.k_ref.v_ref.j_ref, s32[1,256]{1,0:T(1,128)} %bitcast.104, ...), custom_call_target="tpu_custom_call" | custom-call | flops 16000000000 | bytes 8000000 | tf_op jit(solution)/shard_map/attn/pallas_call | solution.py:118
  104.5 8.4 %attn.3 = (bf16[1024,256]{1,0:T(8,128)(2,1)}, f32[2,2,1024]{2,1,0:T(2,128)}) custom-call(bf16[1024,2304]{1,0:T(8,128)(2,1)} %get-tuple-element.175.q_ref.k_ref.v_ref.j_ref, bf16[1024,2304]{1,0:T(8,128)(2,1)} %get-tuple-element.175.q_ref.k_ref.v_ref.j_ref, bf16[1024,2304]{1,0:T(8,128)(2,1)} %get-tuple-element.175.q_ref.k_ref.v_ref.j_ref, s32[1,256]{1,0:T(1,128)} %bitcast.105, ...), custom_call_target="tpu_custom_call" | custom-call | flops 8000000000 | bytes 8000000 | tf_op jit(solution)/shard_map/attn/pallas_call | solution.py:118
  112.9 7.5 %proj.1 = (f32[1024,768]{1,0:T(8,128)}, bf16[1024,768]{1,0:T(8,128)(2,1)}) custom-call(s32[4]{0:T(128)} %pad_add_fusion.where_ref, bf16[1024,768]{1,0:T(8,128)(2,1)} %fusion.4.x_ref, bf16[1024,512]{1,0:T(8,128)(2,1)} %get-tuple-element.174.a0_ref, bf16[1024,256]{1,0:T(8,128)(2,1)} %get-tuple-element.176.a1_ref, f32[8,3072]{1,0:T(8,128)} %get-tuple-element.177.vec_ref, ...), custom_call_target="tpu_custom_call" | custom-call | flops 1207959552 | bytes 9043968 | tf_op jit(solution)/shard_map/proj/pallas_call | solution.py:390
  121.0 1.7 collective-permute-done.24.refs_8_
  124.4 54.9 %mlp.1 = (bf16[1024,768]{1,0:T(8,128)(2,1)}, f32[1024,768]{1,0:T(8,128)}, f32[1,3072]{1,0:T(1,128)}, f32[1,768]{1,0:T(1,128)}, bf16[4,4,48,3072]{3,2,1,0:T(8,128)(2,1)}, /*index=5*/bf16[4,4,48,3072]{3,2,1,0:T(8,128)(2,1)}) custom-call(s32[4]{0:T(128)} %pad_add_fusion.where_ref, bf16[1024,768]{1,0:T(8,128)(2,1)} %get-tuple-element.181.n_ref, ...), custom_call_target="tpu_custom_call" | custom-call | flops 28991029248 | bytes 30000000 | tf_op jit(solution)/shard_map/mlp/pallas_call | solution.py:522
  180.2 13.3 %proj_back.1 = (f32[1024,768]{1,0:T(8,128)}, bf16[1024,768]{1,0:T(8,128)(2,1)}, bf16[768,768]{1,0:T(8,128)(2,1)}, f32[16,1024]{1,0:T(8,128)}, f32[1,768]{1,0:T(1...) custom-call(s32[4]{0:T(128)} %pad_add_fusion.where_ref, f32[1024,768]{1,0:T(8,128)} %get-tuple-element.189.gn_ref, ...), custom_call_target="tpu_custom_call" | custom-call | flops 2415919104 | bytes 12582912 | tf_op jit(solution)/shard_map/proj_back/pallas_call | solution.py:598
  193.6 1.5 reshape.210.del_ref
  195.1 4.6 %fusion.8 = (bf16[4,48,3072]{2,1,0:T(8,128)(2,1)S(1)}, bf16[4,48,3072]{2,1,0:T(8,128)(2,1)S(1)}, bf16[4,48,3072]{2,1,0:T(8,128)(2,1)S(1)}, bf16[4,48,3072]{2,1,0:T(8,128)(2,1)S(1)}) fusion(bf16[4,4,48,3072]{3,2,1,0:T(8,128)(2,1)} %collective-permute-done.26, bf16[4,4,48,3072]{3,2,1,0:T(8,128)(2,1)} %get-tuple-element.194), kind=kLoop, calls=%fused_computation.26 | loop fusion | flops 9437184 | bytes 14155776 | tf_op jit(solution)/shard_map/convert_element_type | solution.py:912
  199.6 1.1 fusion.52
  200.7 1.3 collective-permute-start.27
  202.0 1.5 collective-permute-start.28
  206.5 28.0 %attn_back.1 = (f32[1024,768]{1,0:T(8,128)}, f32[1,1536]{1,0:T(1,128)}, bf16[4,4,48,1152]{3,2,1,0:T(8,128)(2,1)}, bf16[4,4,48,1152]{3,2,1,0:T(8,128)(2,1)}) custom-call(s32[4]{0:T(128)} %pad_add_fusion.where_ref, bf16[1024,2304]{1,0:T(8,128)(2,1)} %get-tuple-element.175.q_ref.k_ref.v_ref.j_ref, bf16[1024,768]{1,0:T(8,128)(2,1)} %get-tuple-element.199.do_ref, ...), custom_call_target="tpu_custom_call" | custom-call | flops 40000000000 | bytes 12000000 | tf_op jit(solution)/shard_map/attn_back/pallas_call | solution.py:765
  234.6 1.0 add_convert_fusion.9
  236.6 1.5 collective-permute-start.31
  238.0 1.3 collective-permute-start.32
  239.4 22.2 %attn_back_last.1 = (bf16[1024,768]{1,0:T(8,128)(2,1)}, bf16[4,4,48,512]{3,2,1,0:T(8,128)(2,1)}, bf16[4,4,48,512]{3,2,1,0:T(8,128)(2,1)}) custom-call(s32[4]{0:T(128)} %pad_add_fusion.where_ref, bf16[1024,2304]{1,0:T(8,128)(2,1)} %get-tuple-element.175.q_ref.k_ref.v_ref.j_ref, bf16[1024,768]{1,0:T(8,128)(2,1)} %get-tuple-element.199.do_ref, ...), custom_call_target="tpu_custom_call" | custom-call | flops 20000000000 | bytes 12000000 | tf_op jit(solution)/shard_map/attn_back_last/pallas_call | solution.py:765
  264.4 1.0 copy-done.15
  265.4 2.6 fusion.29
  269.5 1.7 add_convert_fusion.4
  272.5 2.2 collective-permute-start.37
  274.7 2.9 collective-permute-start.39
  277.6 8.9 %collective-permute-done.38 = bf16[48,3072]{1,0:T(8,128)(2,1)S(1)} collective-permute-done((bf16[48,3072]{1,0:T(8,128)(2,1)S(1)}, bf16[48,3072]{1,0:T(8,128)(2,1)S(1)}, u32[]{:S(2)}, u32[]{:S(2)}) %collective-permute-start.38) | collective-permute-done | bytes 294944 | tf_op jit(solution)/shard_map/ppermute | solution.py:897
  287.6 9.9 %collective-permute-done.39 = bf16[48,3072]{1,0:T(8,128)(2,1)} collective-permute-done((bf16[48,3072]{1,0:T(8,128)(2,1)}, bf16[48,3072]{1,0:T(8,128)(2,1)}, u32[]{:S(2)}, u32[]{:S(2)}) %collective-permute-start.39) | collective-permute-done | bytes 294944 | tf_op jit(solution)/shard_map/ppermute | solution.py:897
  297.5 1.3 collective-permute-done.40
  298.8 2.9 collective-permute-done.36
  301.7 1.3 convert_add_fusion
  303.3 2.4 collective-permute-start.43
  306.7 1.4 collective-permute-start.41
  308.1 3.7 %fusion.1 = bf16[1024,768]{1,0:T(8,128)(2,1)} fusion(s32[]{:T(128)S(6)} %select_n.158, bf16[1024,768]{1,0:T(8,128)(2,1)S(1)} %copy-done.8), kind=kLoop, calls=%fused_computation.15 | loop fusion | flops 3145728 | bytes 3145732 | tf_op jit(solution)/shard_map/concatenate | solution.py:804
  312.6 3.7 %fusion = bf16[1024,768]{1,0:T(8,128)(2,1)} fusion(s32[]{:T(128)S(6)} %select_n.158, bf16[1024,768]{1,0:T(8,128)(2,1)S(1)} %copy-done.9), kind=kLoop, calls=%fused_computation.14 | loop fusion | flops 3145728 | bytes 3145732 | tf_op jit(solution)/shard_map/concatenate | solution.py:804
  316.3 3.0 collective-permute-done.42
  (177 shorter events, 36.8 us)
Async XLA Ops:
  5.0 1.6 collective-permute-start
  7.5 22.9 %collective-permute-start.1 = (bf16[48,1664]{1,0:T(8,128)(2,1)S(1)}, bf16[48,1664]{1,0:T(8,128)(2,1)S(1)}, u32[]{:S(2)}, u32[]{:S(2)}) collective-permute-start(bf16[48,1664]{1,0:T(8,128)(2,1)S(1)} %pad_maximum_fusion.7), channel_id=1, source_target_pairs={{0,24},{1,25},{2,26},{3,27},{4,28},{5,29},{6,30},{7,31},{8,0},{9,1... | collective-permute-start | bytes 479240 | tf_op jit(solution)/shard_map/ppermute | solution.py:897
  12.5 17.9 %collective-permute-start.2 = (bf16[48,1664]{1,0:T(8,128)(2,1)S(1)}, bf16[48,1664]{1,0:T(8,128)(2,1)S(1)}, u32[]{:S(2)}, u32[]{:S(2)}) collective-permute-start(bf16[48,1664]{1,0:T(8,128)(2,1)S(1)} %pad_maximum_fusion.7), channel_id=1, source_target_pairs={{0,16},{1,17},{2,18},{3,19},{4,20},{5,21},{6,22},{7,23},{8,24},{9,... | collective-permute-start | bytes 479240 | tf_op jit(solution)/shard_map/ppermute | solution.py:897
  12.5 17.9 %collective-permute-start.3 = (bf16[48,1664]{1,0:T(8,128)(2,1)S(1)}, bf16[48,1664]{1,0:T(8,128)(2,1)S(1)}, u32[]{:S(2)}, u32[]{:S(2)}) collective-permute-start(bf16[48,1664]{1,0:T(8,128)(2,1)S(1)} %pad_maximum_fusion.7), channel_id=1, source_target_pairs={{0,8},{1,9},{2,10},{3,11},{4,12},{5,13},{6,14},{7,15},{8,16},{9,17... | collective-permute-start | bytes 479240 | tf_op jit(solution)/shard_map/ppermute | solution.py:897
  22.4 7.2 %collective-permute-start.4 = (bf16[24,1536]{1,0:T(8,128)(2,1)S(1)}, bf16[24,1536]{1,0:T(8,128)(2,1)S(1)}, u32[]{:S(2)}, u32[]{:S(2)}) collective-permute-start(bf16[24,1536]{1,0:T(8,128)(2,1)S(1)} %broadcast_select_fusion.8), channel_id=1, source_target_pairs={{0,1},{1,0},{2,3},{3,2},{4,5},{5,4},{6,7},{7,6},{8,9},{9,8},{10,11... | collective-permute-start | bytes 221192 | tf_op jit(solution)/shard_map/ppermute | solution.py:897
  29.6 26.4 %copy-start.22 = (s32[256]{0:T(256)}, s32[256]{0:T(256)S(1)}, u32[]{:S(2)}) copy-start(s32[256]{0:T(256)S(1)} %slice.320) | copy-start | bytes 3076
  30.5 41.6 %copy-start = (bf16[4,48,1664]{2,1,0:T(8,128)(2,1)}, bf16[4,48,1664]{2,1,0:T(8,128)(2,1)S(1)}, u32[]{:S(2)}) copy-start(bf16[4,48,1664]{2,1,0:T(8,128)(2,1)S(1)} %pad_maximum_fusion.3.refs_0_) | copy-start | bytes 1916932
  30.6 19.9 %collective-permute-start.5 = (bf16[4,48,1664]{2,1,0:T(8,128)(2,1)S(1)}, bf16[4,48,1664]{2,1,0:T(8,128)(2,1)S(1)}, u32[]{:S(2)}, u32[]{:S(2)}) collective-permute-start(bf16[4,48,1664]{2,1,0:T(8,128)(2,1)S(1)} %pad_maximum_fusion.3.refs_0_), channel_id=1, source_target_pairs={{0,2},{1,3},{2,0},{3,1},{4,6},{5,7},{6,4},{7,5},{8,10},{9,11},{10,... | collective-permute-start | bytes 1916936 | tf_op jit(solution)/shard_map/ppermute | solution.py:897
  32.2 18.3 %collective-permute-start.6 = (bf16[4,48,1664]{2,1,0:T(8,128)(2,1)S(1)}, bf16[4,48,1664]{2,1,0:T(8,128)(2,1)S(1)}, u32[]{:S(2)}, u32[]{:S(2)}) collective-permute-start(bf16[4,48,1664]{2,1,0:T(8,128)(2,1)S(1)} %pad_maximum_fusion.3.refs_0_), channel_id=1, source_target_pairs={{0,4},{1,5},{2,6},{3,7},{4,0},{5,1},{6,2},{7,3},{8,12},{9,13},{10,... | collective-permute-start | bytes 1916936 | tf_op jit(solution)/shard_map/ppermute | solution.py:897
  33.6 10.6 %collective-permute-start.7 = (bf16[48,3072]{1,0:T(8,128)(2,1)}, bf16[48,3072]{1,0:T(8,128)(2,1)S(1)}, u32[]{:S(2)}, u32[]{:S(2)}) collective-permute-start(bf16[48,3072]{1,0:T(8,128)(2,1)} %pad_maximum_fusion.4), channel_id=1, source_target_pairs={{0,24},{1,25},{2,26},{3,27},{4,28},{5,29},{6,30},{7,31},{8,0},{9,1... | collective-permute-start | bytes 884744 | tf_op jit(solution)/shard_map/ppermute | solution.py:897
  36.5 14.0 %collective-permute-start.8 = (bf16[48,3072]{1,0:T(8,128)(2,1)}, bf16[48,3072]{1,0:T(8,128)(2,1)S(1)}, u32[]{:S(2)}, u32[]{:S(2)}) collective-permute-start(bf16[48,3072]{1,0:T(8,128)(2,1)} %pad_maximum_fusion.4), channel_id=1, source_target_pairs={{0,8},{1,9},{2,10},{3,11},{4,12},{5,13},{6,14},{7,15},{8,16},{9,17... | collective-permute-start | bytes 884744 | tf_op jit(solution)/shard_map/ppermute | solution.py:897
  37.0 16.8 %collective-permute-start.11 = (bf16[4,48,1664]{2,1,0:T(8,128)(2,1)S(1)}, bf16[4,48,1664]{2,1,0:T(8,128)(2,1)S(1)}, u32[]{:S(2)}, u32[]{:S(2)}) collective-permute-start(bf16[4,48,1664]{2,1,0:T(8,128)(2,1)S(1)} %pad_maximum_fusion.3.refs_0_), channel_id=1, source_target_pairs={{0,1},{1,0},{2,3},{3,2},{4,5},{5,4},{6,7},{7,6},{8,9},{9,8},{10,11... | collective-permute-start | bytes 1916936 | tf_op jit(solution)/shard_map/ppermute | solution.py:897
  50.5 19.7 %collective-permute-start.12 = (bf16[4,48,1664]{2,1,0:T(8,128)(2,1)S(1)}, bf16[4,48,1664]{2,1,0:T(8,128)(2,1)S(1)}, u32[]{:S(2)}, u32[]{:S(2)}) collective-permute-start(bf16[4,48,1664]{2,1,0:T(8,128)(2,1)S(1)} %collective-permute-done.5.refs_1_), channel_id=1, source_target_pairs={{0,1},{1,0},{2,3},{3,2},{4,5},{5,4},{6,7},{7,6},{8,9},{9,8},{10,11... | collective-permute-start | bytes 1916936 | tf_op jit(solution)/shard_map/ppermute | solution.py:897
  51.2 19.0 %collective-permute-start.13 = (bf16[4,48,1664]{2,1,0:T(8,128)(2,1)S(1)}, bf16[4,48,1664]{2,1,0:T(8,128)(2,1)}, u32[]{:S(2)}, u32[]{:S(2)}) collective-permute-start(bf16[4,48,1664]{2,1,0:T(8,128)(2,1)S(1)} %collective-permute-done.6.refs_2_), channel_id=1, source_target_pairs={{0,1},{1,0},{2,3},{3,2},{4,5},{5,4},{6,7},{7,6},{8,9},{9,8},{10,11... | collective-permute-start | bytes 1916936 | tf_op jit(solution)/shard_map/ppermute | solution.py:897
  52.7 17.5 %collective-permute-start.9 = (bf16[2,48,1664]{2,1,0:T(8,128)(2,1)}, bf16[2,48,1664]{2,1,0:T(8,128)(2,1)}, u32[]{:S(2)}, u32[]{:S(2)}) collective-permute-start(bf16[2,48,1664]{2,1,0:T(8,128)(2,1)} %slice.325), channel_id=1, source_target_pairs={{0,4},{1,5},{2,6},{3,7},{4,0},{5,1},{6,2},{7,3},{8,12},{9,13},{10,... | collective-permute-start | bytes 958472 | tf_op jit(solution)/shard_map/ppermute | solution.py:897
  53.2 17.0 %collective-permute-start.10 = (bf16[2,48,1664]{2,1,0:T(8,128)(2,1)}, bf16[2,48,1664]{2,1,0:T(8,128)(2,1)}, u32[]{:S(2)}, u32[]{:S(2)}) collective-permute-start(bf16[2,48,1664]{2,1,0:T(8,128)(2,1)} %slice.326), channel_id=1, source_target_pairs={{0,2},{1,3},{2,0},{3,1},{4,6},{5,7},{6,4},{7,5},{8,10},{9,11},{10,... | collective-permute-start | bytes 958472 | tf_op jit(solution)/shard_map/ppermute | solution.py:897
  53.8 16.4 %collective-permute-start.14 = (bf16[48,3072]{1,0:T(8,128)(2,1)}, bf16[48,3072]{1,0:T(8,128)(2,1)}, u32[]{:S(2)}, u32[]{:S(2)}) collective-permute-start(bf16[48,3072]{1,0:T(8,128)(2,1)} %pad_maximum_fusion.4), channel_id=1, source_target_pairs={{0,16},{1,17},{2,18},{3,19},{4,20},{5,21},{6,22},{7,23},{8,24},{9,... | collective-permute-start | bytes 884744 | tf_op jit(solution)/shard_map/ppermute | solution.py:897
  70.2 2.0 collective-permute-start.15
  70.3 2.3 collective-permute-start.16
  72.6 29.8 %collective-permute-start.17 = (bf16[4,48,3072]{2,1,0:T(8,128)(2,1)S(1)}, bf16[4,48,3072]{2,1,0:T(8,128)(2,1)S(1)}, u32[]{:S(2)}, u32[]{:S(2)}) collective-permute-start(bf16[4,48,3072]{2,1,0:T(8,128)(2,1)S(1)} %pad_maximum_fusion.2.refs_0_), channel_id=1, source_target_pairs={{0,2},{1,3},{2,0},{3,1},{4,6},{5,7},{6,4},{7,5},{8,10},{9,11},{10,... | collective-permute-start | bytes 3538952 | tf_op jit(solution)/shard_map/ppermute | solution.py:897
  74.0 28.4 %collective-permute-start.18 = (bf16[4,48,3072]{2,1,0:T(8,128)(2,1)S(1)}, bf16[4,48,3072]{2,1,0:T(8,128)(2,1)S(1)}, u32[]{:S(2)}, u32[]{:S(2)}) collective-permute-start(bf16[4,48,3072]{2,1,0:T(8,128)(2,1)S(1)} %pad_maximum_fusion.2.refs_0_), channel_id=1, source_target_pairs={{0,4},{1,5},{2,6},{3,7},{4,0},{5,1},{6,2},{7,3},{8,12},{9,13},{10,... | collective-permute-start | bytes 3538952 | tf_op jit(solution)/shard_map/ppermute | solution.py:897
  75.5 44.9 %collective-permute-start.21 = (bf16[4,48,3072]{2,1,0:T(8,128)(2,1)S(1)}, bf16[4,48,3072]{2,1,0:T(8,128)(2,1)}, u32[]{:S(2)}, u32[]{:S(2)}) collective-permute-start(bf16[4,48,3072]{2,1,0:T(8,128)(2,1)S(1)} %pad_maximum_fusion.2.refs_0_), channel_id=1, source_target_pairs={{0,1},{1,0},{2,3},{3,2},{4,5},{5,4},{6,7},{7,6},{8,9},{9,8},{10,11... | collective-permute-start | bytes 3538952 | tf_op jit(solution)/shard_map/ppermute | solution.py:897
  102.4 18.0 %collective-permute-start.22 = (bf16[4,48,3072]{2,1,0:T(8,128)(2,1)S(1)}, bf16[4,48,3072]{2,1,0:T(8,128)(2,1)S(1)}, u32[]{:S(2)}, u32[]{:S(2)}) collective-permute-start(bf16[4,48,3072]{2,1,0:T(8,128)(2,1)S(1)} %collective-permute-done.17.refs_1_), channel_id=1, source_target_pairs={{0,1},{1,0},{2,3},{3,2},{4,5},{5,4},{6,7},{7,6},{8,9},{9,8},{10,11... | collective-permute-start | bytes 3538952 | tf_op jit(solution)/shard_map/ppermute | solution.py:897
  103.0 17.5 %collective-permute-start.23 = (bf16[4,48,3072]{2,1,0:T(8,128)(2,1)S(1)}, bf16[4,48,3072]{2,1,0:T(8,128)(2,1)}, u32[]{:S(2)}, u32[]{:S(2)}) collective-permute-start(bf16[4,48,3072]{2,1,0:T(8,128)(2,1)S(1)} %collective-permute-done.18.refs_2_), channel_id=1, source_target_pairs={{0,1},{1,0},{2,3},{3,2},{4,5},{5,4},{6,7},{7,6},{8,9},{9,8},{10,11... | collective-permute-start | bytes 3538952 | tf_op jit(solution)/shard_map/ppermute | solution.py:897
  103.1 17.3 %collective-permute-start.19 = (bf16[2,48,3072]{2,1,0:T(8,128)(2,1)S(1)}, bf16[2,48,3072]{2,1,0:T(8,128)(2,1)}, u32[]{:S(2)}, u32[]{:S(2)}) collective-permute-start(bf16[2,48,3072]{2,1,0:T(8,128)(2,1)S(1)} %slice.327), channel_id=1, source_target_pairs={{0,4},{1,5},{2,6},{3,7},{4,0},{5,1},{6,2},{7,3},{8,12},{9,13},{10,... | collective-permute-start | bytes 1769480 | tf_op jit(solution)/shard_map/ppermute | solution.py:897
  103.9 16.5 %collective-permute-start.20 = (bf16[2,48,3072]{2,1,0:T(8,128)(2,1)S(1)}, bf16[2,48,3072]{2,1,0:T(8,128)(2,1)}, u32[]{:S(2)}, u32[]{:S(2)}) collective-permute-start(bf16[2,48,3072]{2,1,0:T(8,128)(2,1)S(1)} %slice.328), channel_id=1, source_target_pairs={{0,2},{1,3},{2,0},{3,1},{4,6},{5,7},{6,4},{7,5},{8,10},{9,11},{10,... | collective-permute-start | bytes 1769480 | tf_op jit(solution)/shard_map/ppermute | solution.py:897
  120.5 2.3 collective-permute-start.24
  120.6 3.0 collective-permute-start.25
  179.3 14.2 %collective-permute-start.26 = (bf16[4,4,48,3072]{3,2,1,0:T(8,128)(2,1)}, bf16[4,4,48,3072]{3,2,1,0:T(8,128)(2,1)}, u32[]{:S(2)}, u32[]{:S(2)}) collective-permute-start(bf16[4,4,48,3072]{3,2,1,0:T(8,128)(2,1)} %get-tuple-element.193), channel_id=1, source_target_pairs={{0,1},{1,0},{2,3},{3,2},{4,5},{5,4},{6,7},{7,6},{8,9},{9,8},{10,11... | collective-permute-start | bytes 14155784 | tf_op jit(solution)/shard_map/ppermute | solution.py:897
  200.7 33.8 %collective-permute-start.27 = (bf16[2,48,3072]{2,1,0:T(8,128)(2,1)}, bf16[2,48,3072]{2,1,0:T(8,128)(2,1)S(1)}, u32[]{:S(2)}, u32[]{:S(2)}) collective-permute-start(bf16[2,48,3072]{2,1,0:T(8,128)(2,1)} %get-tuple-element.272), channel_id=1, source_target_pairs={{0,4},{1,5},{2,6},{3,7},{4,0},{5,1},{6,2},{7,3},{8,12},{9,13},{10,... | collective-permute-start | bytes 1769480 | tf_op jit(solution)/shard_map/ppermute | solution.py:897
  202.0 32.5 %collective-permute-start.28 = (bf16[2,48,3072]{2,1,0:T(8,128)(2,1)}, bf16[2,48,3072]{2,1,0:T(8,128)(2,1)S(1)}, u32[]{:S(2)}, u32[]{:S(2)}) collective-permute-start(bf16[2,48,3072]{2,1,0:T(8,128)(2,1)} %get-tuple-element.271), channel_id=1, source_target_pairs={{0,2},{1,3},{2,0},{3,1},{4,6},{5,7},{6,4},{7,5},{8,10},{9,11},{10,... | collective-permute-start | bytes 1769480 | tf_op jit(solution)/shard_map/ppermute | solution.py:897
  204.4 30.1 %collective-permute-start.29 = (bf16[2,48,3072]{2,1,0:T(8,128)(2,1)}, bf16[2,48,3072]{2,1,0:T(8,128)(2,1)S(1)}, u32[]{:S(2)}, u32[]{:S(2)}) collective-permute-start(bf16[2,48,3072]{2,1,0:T(8,128)(2,1)} %slice.341), channel_id=1, source_target_pairs={{0,2},{1,3},{2,0},{3,1},{4,6},{5,7},{6,4},{7,5},{8,10},{9,11},{10,... | collective-permute-start | bytes 1769480 | tf_op jit(solution)/shard_map/ppermute | solution.py:897
  205.8 28.8 %collective-permute-start.30 = (bf16[2,48,3072]{2,1,0:T(8,128)(2,1)}, bf16[2,48,3072]{2,1,0:T(8,128)(2,1)S(1)}, u32[]{:S(2)}, u32[]{:S(2)}) collective-permute-start(bf16[2,48,3072]{2,1,0:T(8,128)(2,1)} %slice.342), channel_id=1, source_target_pairs={{0,4},{1,5},{2,6},{3,7},{4,0},{5,1},{6,2},{7,3},{8,12},{9,13},{10,... | collective-permute-start | bytes 1769480 | tf_op jit(solution)/shard_map/ppermute | solution.py:897
  236.6 25.2 %collective-permute-start.31 = (bf16[2,48,3072]{2,1,0:T(8,128)(2,1)}, bf16[2,48,3072]{2,1,0:T(8,128)(2,1)}, u32[]{:S(2)}, u32[]{:S(2)}) collective-permute-start(bf16[2,48,3072]{2,1,0:T(8,128)(2,1)} %add_convert_fusion.9), channel_id=1, source_target_pairs={{0,2},{1,3},{2,0},{3,1},{4,6},{5,7},{6,4},{7,5},{8,10},{9,11},{10,... | collective-permute-start | bytes 1769480 | tf_op jit(solution)/shard_map/ppermute | solution.py:897
  238.0 23.7 %collective-permute-start.32 = (bf16[2,48,3072]{2,1,0:T(8,128)(2,1)}, bf16[2,48,3072]{2,1,0:T(8,128)(2,1)}, u32[]{:S(2)}, u32[]{:S(2)}) collective-permute-start(bf16[2,48,3072]{2,1,0:T(8,128)(2,1)} %add_convert_fusion.8), channel_id=1, source_target_pairs={{0,4},{1,5},{2,6},{3,7},{4,0},{5,1},{6,2},{7,3},{8,12},{9,13},{10,... | collective-permute-start | bytes 1769480 | tf_op jit(solution)/shard_map/ppermute | solution.py:897
  239.4 22.4 %collective-permute-start.33 = (bf16[4,4,48,1152]{3,2,1,0:T(8,128)(2,1)}, bf16[4,4,48,1152]{3,2,1,0:T(8,128)(2,1)S(1)}, u32[]{:S(2)}, u32[]{:S(2)}) collective-permute-start(bf16[4,4,48,1152]{3,2,1,0:T(8,128)(2,1)} %get-tuple-element.228), channel_id=1, source_target_pairs={{0,1},{1,0},{2,3},{3,2},{4,5},{5,4},{6,7},{7,6},{8,9},{9,8},{10,11... | collective-permute-start | bytes 5308424 | tf_op jit(solution)/shard_map/ppermute | solution.py:897
  263.6 4.5 %collective-permute-start.34 = (bf16[4,4,48,512]{3,2,1,0:T(8,128)(2,1)S(1)}, bf16[4,4,48,512]{3,2,1,0:T(8,128)(2,1)S(1)}, u32[]{:S(2)}, u32[]{:S(2)}) collective-permute-start(bf16[4,4,48,512]{3,2,1,0:T(8,128)(2,1)S(1)} %copy-done.24), channel_id=1, source_target_pairs={{0,1},{1,0},{2,3},{3,2},{4,5},{5,4},{6,7},{7,6},{8,9},{9,8},{10,11... | collective-permute-start | bytes 2359304 | tf_op jit(solution)/shard_map/ppermute | solution.py:897
  271.2 27.6 %collective-permute-start.35 = (bf16[4,48,1664]{2,1,0:T(8,128)(2,1)}, bf16[4,48,1664]{2,1,0:T(8,128)(2,1)S(1)}, u32[]{:S(2)}, u32[]{:S(2)}) collective-permute-start(bf16[4,48,1664]{2,1,0:T(8,128)(2,1)} %get-tuple-element.261), channel_id=1, source_target_pairs={{0,2},{1,3},{2,0},{3,1},{4,6},{5,7},{6,4},{7,5},{8,10},{9,11},{10,... | collective-permute-start | bytes 1916936 | tf_op jit(solution)/shard_map/ppermute | solution.py:897
  271.8 29.9 %collective-permute-start.36 = (bf16[4,48,1664]{2,1,0:T(8,128)(2,1)}, bf16[4,48,1664]{2,1,0:T(8,128)(2,1)S(1)}, u32[]{:S(2)}, u32[]{:S(2)}) collective-permute-start(bf16[4,48,1664]{2,1,0:T(8,128)(2,1)} %get-tuple-element.260), channel_id=1, source_target_pairs={{0,4},{1,5},{2,6},{3,7},{4,0},{5,1},{6,2},{7,3},{8,12},{9,13},{10,... | collective-permute-start | bytes 1916936 | tf_op jit(solution)/shard_map/ppermute | solution.py:897
  272.5 29.2 %collective-permute-start.37 = (bf16[4,48,1664]{2,1,0:T(8,128)(2,1)}, bf16[4,48,1664]{2,1,0:T(8,128)(2,1)S(1)}, u32[]{:S(2)}, u32[]{:S(2)}) collective-permute-start(bf16[4,48,1664]{2,1,0:T(8,128)(2,1)} %get-tuple-element.259), channel_id=1, source_target_pairs={{0,6},{1,7},{2,4},{3,5},{4,2},{5,3},{6,0},{7,1},{8,14},{9,15},{10,... | collective-permute-start | bytes 1916936 | tf_op jit(solution)/shard_map/ppermute | solution.py:897
  274.7 11.8 %collective-permute-start.38 = (bf16[48,3072]{1,0:T(8,128)(2,1)S(1)}, bf16[48,3072]{1,0:T(8,128)(2,1)S(1)}, u32[]{:S(2)}, u32[]{:S(2)}) collective-permute-start(bf16[48,3072]{1,0:T(8,128)(2,1)S(1)} %get-tuple-element.239), channel_id=1, source_target_pairs={{0,8},{1,9},{2,10},{3,11},{4,12},{5,13},{6,14},{7,15},{8,16},{9,17... | collective-permute-start | bytes 884744 | tf_op jit(solution)/shard_map/ppermute | solution.py:897
  274.7 22.8 %collective-permute-start.39 = (bf16[48,3072]{1,0:T(8,128)(2,1)}, bf16[48,3072]{1,0:T(8,128)(2,1)}, u32[]{:S(2)}, u32[]{:S(2)}) collective-permute-start(bf16[48,3072]{1,0:T(8,128)(2,1)} %get-tuple-element.240), channel_id=1, source_target_pairs={{0,16},{1,17},{2,18},{3,19},{4,20},{5,21},{6,22},{7,23},{8,24},{9,... | collective-permute-start | bytes 884744 | tf_op jit(solution)/shard_map/ppermute | solution.py:897
  287.2 11.6 %collective-permute-start.40 = (bf16[48,3072]{1,0:T(8,128)(2,1)S(1)}, bf16[48,3072]{1,0:T(8,128)(2,1)}, u32[]{:S(2)}, u32[]{:S(2)}) collective-permute-start(bf16[48,3072]{1,0:T(8,128)(2,1)S(1)} %get-tuple-element.241), channel_id=1, source_target_pairs={{0,24},{1,25},{2,26},{3,27},{4,28},{5,29},{6,30},{7,31},{8,0},{9,1... | collective-permute-start | bytes 884744 | tf_op jit(solution)/shard_map/ppermute | solution.py:897
  303.3 13.1 %collective-permute-start.43 = (bf16[48,1664]{1,0:T(8,128)(2,1)S(1)}, bf16[48,1664]{1,0:T(8,128)(2,1)S(1)}, u32[]{:S(2)}, u32[]{:S(2)}) collective-permute-start(bf16[48,1664]{1,0:T(8,128)(2,1)S(1)} %get-tuple-element.263), channel_id=1, source_target_pairs={{0,24},{1,25},{2,26},{3,27},{4,28},{5,29},{6,30},{7,31},{8,0},{9,1... | collective-permute-start | bytes 479240 | tf_op jit(solution)/shard_map/ppermute | solution.py:897
  305.7 13.6 %collective-permute-start.42 = (bf16[48,1664]{1,0:T(8,128)(2,1)S(1)}, bf16[48,1664]{1,0:T(8,128)(2,1)S(1)}, u32[]{:S(2)}, u32[]{:S(2)}) collective-permute-start(bf16[48,1664]{1,0:T(8,128)(2,1)S(1)} %get-tuple-element.264), channel_id=1, source_target_pairs={{0,16},{1,17},{2,18},{3,19},{4,20},{5,21},{6,22},{7,23},{8,24},{9,... | collective-permute-start | bytes 479240 | tf_op jit(solution)/shard_map/ppermute | solution.py:897
  306.7 12.6 %collective-permute-start.41 = (bf16[48,1664]{1,0:T(8,128)(2,1)S(1)}, bf16[48,1664]{1,0:T(8,128)(2,1)S(1)}, u32[]{:S(2)}, u32[]{:S(2)}) collective-permute-start(bf16[48,1664]{1,0:T(8,128)(2,1)S(1)} %get-tuple-element.262), channel_id=1, source_target_pairs={{0,8},{1,9},{2,10},{3,11},{4,12},{5,13},{6,14},{7,15},{8,16},{9,17... | collective-permute-start | bytes 479240 | tf_op jit(solution)/shard_map/ppermute | solution.py:897
  308.1 8.2 %collective-permute-start.45 = (f32[24,1536]{1,0:T(8,128)S(1)}, f32[24,1536]{1,0:T(8,128)S(1)}, u32[]{:S(2)}, u32[]{:S(2)}) collective-permute-start(f32[24,1536]{1,0:T(8,128)S(1)} %slice_select_fusion.2), channel_id=1, source_target_pairs={{0,1},{1,0},{2,3},{3,2},{4,5},{5,4},{6,7},{7,6},{8,9},{9,8},{10,11... | collective-permute-start | bytes 442376 | tf_op jit(solution)/shard_map/ppermute | solution.py:897
  319.5 1.5 collective-permute-start.44
  (27 other events, 178.5 us)

commit v4 on v3

v4 whole, which is shorter than its diff:
```python
import functools
import math

import jax
import jax.numpy as jnp
from jax import lax
from jax.experimental import pallas as pl
from jax.experimental.pallas import tpu as pltpu
from jax.sharding import PartitionSpec as P

HD = 64
LONG = 768
EPS = 1e-05
BS = 1.0 / math.sqrt(48.0)
NEG = -1e30
F32 = jnp.float32
BF = jnp.bfloat16
VMEM_LIMIT = 58 * 1024 * 1024
AXES = ("dp", "fsdp")
GC0 = math.sqrt(2.0 / math.pi)
GC1 = 0.044715


def dot(a, b):
    return lax.dot_general(a, b, (((1,), (0,)), ((), ())), preferred_element_type=F32)


def dot_t(a, b):
    return lax.dot_general(a, b, (((1,), (1,)), ((), ())), preferred_element_type=F32)


def dot_0(a, b):
    return lax.dot_general(a, b, (((0,), (0,)), ((), ())), preferred_element_type=F32)


def params(grid_len=1):
    return pltpu.CompilerParams(
        dimension_semantics=("arbitrary",) * grid_len, vmem_limit_bytes=VMEM_LIMIT
    )


def cost(flops, nbytes, trans=0):
    return pl.CostEstimate(flops=int(flops), bytes_accessed=int(nbytes), transcendentals=int(trans))


def normalize(values):
    centred = values - jnp.mean(values, axis=-1, keepdims=True)
    rstd = lax.rsqrt(jnp.mean(centred * centred, axis=-1, keepdims=True) + EPS)
    return centred * rstd, rstd


def ln_back(dy, xhat, rstd, gain):
    dx = dy * gain
    m1 = jnp.mean(dx, axis=-1, keepdims=True)
    m2 = jnp.mean(dx * xhat, axis=-1, keepdims=True)
    return rstd * (dx - m1 - xhat * m2)


def full_spec(shape):
    return pl.BlockSpec(shape, lambda *_: (0,) * len(shape), pipeline_mode=pl.Buffered(1))


def lane_masks(rows):
    lane = lax.broadcasted_iota(jnp.int32, (rows, 128), 1)
    return lane < HD


def split_heads(block):
    low = lane_masks(block.shape[0])
    zero = jnp.zeros_like(block)
    return jnp.where(low, block, zero), jnp.where(low, zero, block)


def q_tiles(rows):
    tiles = [(r, 0, r + 256, True) for r in range(0, LONG, 256)]
    tiles += [(LONG, LONG, rows, False)]
    return tiles


def diag_allowed(is_long, seg_row, seg_col):
    kv = lax.broadcasted_iota(jnp.int32, (256, 256), 0)
    qp = lax.broadcasted_iota(jnp.int32, (256, 256), 1)
    allowed = kv <= qp
    if not is_long:
        allowed = allowed & (seg_col == seg_row)
    return allowed


def attn_kernel(q_ref, k_ref, v_ref, segr_ref, segc_ref, o_ref, lse_ref):
    rows = q_ref.shape[0]
    ks = split_heads(k_ref[...] * BF(HD**-0.5))
    vt = v_ref[...].T
    items = [(tile, h) for tile in q_tiles(rows) for h in range(2)]

    def score(item):
        (q0, kv0, kv1, _), h = item
        return dot_t(ks[h][kv0:kv1], q_ref[q0 : q0 + 256, :])

    queue = [score(it) for it in items[:3]]
    outs = []
    for n, ((q0, kv0, kv1, is_long), h) in enumerate(items):
        if n + 3 < len(items):
            queue.append(score(items[n + 3]))
        s, queue[n] = queue[n], None
        parts = mask_diagonal(s, q0 - kv0, is_long, segr_ref, segc_ref)
        top = functools.reduce(jnp.maximum, [jnp.max(p, axis=0, keepdims=True) for p in parts])
        exps = [jnp.exp(p - top) for p in parts]
        total = functools.reduce(jnp.add, [jnp.sum(e, axis=0, keepdims=True) for e in exps])
        lse_ref[0, h : h + 1, q0 : q0 + 256] = top + jnp.log(total)
        probs = jnp.concatenate([e.astype(BF) for e in exps], axis=0)
        outs.append(dot(vt[h * HD : (h + 1) * HD, kv0:kv1], probs) * (1.0 / total))
        if h == 1:
            o_ref[q0 : q0 + 256, :] = jnp.concatenate(outs, axis=0).T.astype(BF)
            outs = []


def mask_diagonal(s, at, is_long, segr_ref, segc_ref):
    allowed = diag_allowed(is_long, segr_ref[...], segc_ref[...])
    diag = jnp.where(allowed, s[at:], NEG)
    return [s[:at], diag] if at else [diag]


def attn_call(joined, seg_row, seg_col, group0, groups):
    rows = joined.shape[0]
    pairs = joined.shape[1] // 384
    at = lambda t: pl.BlockSpec((rows, 128), lambda p: (0, pair_block(group0 * 2 + p, pairs) * 3 + t))
    return pl.pallas_call(
        attn_kernel,
        grid=(2 * groups,),
        in_specs=[at(0), at(1), at(2), full_spec((1, 256)), full_spec((256, 1))],
        out_specs=[
            pl.BlockSpec((rows, 128), lambda p: (0, p)),
            pl.BlockSpec((1, 2, rows), lambda p: (p, 0, 0)),
        ],
        out_shape=[
            jax.ShapeDtypeStruct((rows, groups * 256), BF),
            jax.ShapeDtypeStruct((2 * groups, 2, rows), F32),
        ],
        compiler_params=params(),
        cost_estimate=cost(groups * 8e9, 8e6, 5.5e6),
        name="attn",
    )(joined, joined, joined, seg_row, seg_col)


def pair_block(p, pairs):
    return (p % 2) * (pairs // 2) + p // 2


ANY = pl.BlockSpec(memory_space=pl.ANY)
SMEM = pl.BlockSpec(memory_space=pltpu.SMEM)


def local_copy(src, dst, sem):
    return pltpu.make_async_copy(src, dst, sem)


def chips_of(dims, where_ref):
    z_n, y_n, x_n = dims
    zi, yi, xi = [where_ref[i] for i in range(3)]
    for i in range(y_n * x_n):
        for j in range(z_n):
            yield i, j, lax.rem(zi + j, z_n), lax.rem(yi + i // x_n, y_n), lax.rem(xi + i % x_n, x_n)


def piece_at(dims, arrays, i, j):
    at = i * dims[0] + j
    for a in arrays:
        if at < a.shape[0]:
            return a.at[at]
        at -= a.shape[0]


def load_columns(dims, where_ref, own, oth, first, cols, dst, sem):
    ci = where_ref[3]
    for i, j, z, y, x in chips_of(dims, where_ref):
        for half, src in ((ci, own), (1 - ci, oth)):
            block = piece_at(dims, src, i, j).at[:, pl.ds(first, cols)]
            local_copy(block, dst.at[half, z, y, x], sem.at[half, z, y, x]).start()


def wait_columns(dims, dst, sem, half):
    for z in range(dims[0]):
        for y in range(dims[1]):
            for x in range(dims[2]):
                block = dst.at[half, z, y, x]
                local_copy(block, block, sem.at[half, z, y, x]).wait()


def flat2(value):
    return value.reshape(-1, value.shape[-1])


def store_columns(dims, where_ref, src, own, oth, half, first, cols, sem):
    ci = where_ref[3]
    for other, out in ((False, own), (True, oth)):

        @pl.when((half != ci) if other else (half == ci))
        def _():
            for i, j, z, y, x in chips_of(dims, where_ref):
                local_copy(src.at[z, y, x], out.at[i, j, :, pl.ds(first, cols)], sem.at[i, j]).start()


def wait_store(dims, src, out, first, cols, sem):
    for i in range(dims[1] * dims[2]):
        for j in range(dims[0]):
            local_copy(src.at[0, 0, 0], out.at[i, j, :, pl.ds(first, cols)], sem.at[i, j]).wait()


def weight_scratch(dims, n, cols):
    return [
        pltpu.VMEM((2,) + dims + (n, cols), BF),
        pltpu.SemaphoreType.DMA((2,) + dims),
    ]


def vector_plan(d, devices):
    r = d // devices
    return {
        "g1": (0, 0, r), "b1": (0, r, r), "qv": (0, 2 * r, 2 * r), "fb": (1, 0, 4 * r),
        "pb": (2, 0, r), "g2": (2, r, r), "b2": (2, 2 * r, r), "ob": (2, 3 * r, r),
    }


VECTOR_ROWS = {"g1": 0, "b1": 1, "qv": 2, "pb": 3, "g2": 4, "b2": 5, "fb": 6, "ob": 7}


def owner_of(shape, size, axis):
    c = lax.broadcasted_iota(jnp.int32, shape, axis).astype(F32)
    owner = jnp.floor((c + 0.5) * (1.0 / size))
    return owner, c - owner * size


def row_pick(devices, d, row):
    r = d // devices
    at = lax.broadcasted_iota(jnp.int32, (devices, d), 1)
    dev = lax.broadcasted_iota(jnp.int32, (devices, d), 0)
    return (at == dev * r + row).astype(BF)


def vector_maps(devices, n, first, size):
    owner, place = owner_of((devices, n), size, 1)
    mine = owner == lax.broadcasted_iota(jnp.int32, (devices, n), 0).astype(F32)
    _, place = owner_of((128, n), size, 1)
    spot = (place + first == lax.broadcasted_iota(jnp.int32, (128, n), 0).astype(F32)).astype(BF)
    return mine, spot


def unpack_vectors(table, d, devices, out_ref):
    plan = vector_plan(d, devices)
    picked = [dot(row_pick(devices, d, k), table).astype(BF) for k in range(3)]
    for name, i in VECTOR_ROWS.items():
        k, first, size = plan[name]
        n = size * devices
        mine, spot = vector_maps(devices, n, first, size)
        spread = dot(picked[k], spot)
        out_ref[i : i + 1, :n] = jnp.sum(jnp.where(mine, spread, 0.0), axis=0, keepdims=True)


def pack_vectors(rows, d, devices):
    plan = vector_plan(d, devices)
    parts = [None] * 3
    for name in VECTOR_ROWS:
        k, first, size = plan[name]
        n = size * devices
        mine, spot = vector_maps(devices, n, first, size)
        part = dot_t(jnp.where(mine, rows[name], 0.0).astype(BF), spot)
        parts[k] = part if parts[k] is None else parts[k] + part
    total = None
    for k in range(3):
        piece = dot_0(row_pick(devices, d, k), parts[k].astype(BF))
        total = piece if total is None else total + piece
    return total.astype(BF)


def cut_kernel(where_ref, w_ref, t_ref, keep_ref, give_ref):
    ci = where_ref[3]
    pairs = w_ref.shape[1] // 384
    for h in range(2):
        for other, out in ((False, keep_ref), (True, give_ref)):

            @pl.when((ci != h) if other else (ci == h))
            def _():
                at = 0
                for p in range(h, pairs, 2):
                    for t in range(3):
                        first = (t * pairs + p) * 128
                        out[:, at : at + 128] = w_ref[:, first : first + 128]
                        at += 128
                out[:, at:] = t_ref[...]


def cut_call(where, w_qkv, table):
    r = w_qkv.shape[0]
    cols = w_qkv.shape[1] // 2 + 128
    return pl.pallas_call(
        cut_kernel,
        grid=(1,),
        in_specs=[SMEM, full_spec(w_qkv.shape), full_spec(table.shape)],
        out_specs=[full_spec((r, cols))] * 2,
        out_shape=[jax.ShapeDtypeStruct((r, cols), BF)] * 2,
        compiler_params=params(),
        cost_estimate=cost(0, 4 * r * cols),
        name="cut",
    )(where, w_qkv, table)


def qkv_kernel(dims, count, devices, where_ref, x_ref, *refs):
    own, oth = refs[:count], refs[count : 2 * count]
    o_ref, vec_ref, w_scr, w_sem, t_scr, t_sem, n_scr, bias_scr = refs[2 * count :]
    rows, d = x_ref.shape
    cols = w_scr.shape[-1]
    table_at = own[0].shape[-1] - 128
    step = pl.program_id(0)

    @pl.when(step == 0)
    def _():
        for i, j, z, y, x in chips_of(dims, where_ref):
            block = piece_at(dims, own, i, j).at[:, pl.ds(table_at, 128)]
            local_copy(block, t_scr.at[z, y, x], t_sem.at[z, y, x]).start()
        load_columns(dims, where_ref, own, oth, 0, cols, w_scr, w_sem)
        for z in range(dims[0]):
            for y in range(dims[1]):
                for x in range(dims[2]):
                    block = t_scr.at[z, y, x]
                    local_copy(block, block, t_sem.at[z, y, x]).wait()
        vec_ref[...] = jnp.zeros_like(vec_ref)
        unpack_vectors(flat2(t_scr[...]), d, devices, vec_ref)
        zero = jnp.zeros((1, 128), F32)
        pairs = d // 128
        for p in range(pairs):
            at = pair_block(p, pairs) * 384
            half, at = at // cols, at % cols
            bias_scr[half, :, at : at + 128] = vec_ref[2:3, p * 128 : (p + 1) * 128]
            bias_scr[half, :, at + 128 : at + 256] = zero
            bias_scr[half, :, at + 256 : at + 384] = vec_ref[2:3, d + p * 128 : d + (p + 1) * 128]
        for r in range(0, rows, 256):
            xhat, _ = normalize(x_ref[r : r + 256, :].astype(F32))
            n_scr[r : r + 256, :] = (xhat * vec_ref[0:1, :d] + vec_ref[1:2, :d]).astype(BF)
        wait_columns(dims, w_scr, w_sem, 0)

    @pl.when(step == 1)
    def _():
        wait_columns(dims, w_scr, w_sem, 1)

    w = flat2(w_scr[step])
    for r in range(0, rows, 256):
        o_ref[r : r + 256, :] = (dot(n_scr[r : r + 256, :], w) + bias_scr[step]).astype(BF)


def qkv_call(dims, where, x, own, oth, devices):
    rows, d = x.shape
    n = own[0].shape[1]
    cols = 3 * d // 2
    return pl.pallas_call(
        functools.partial(qkv_kernel, dims, len(own), devices),
        grid=(2,),
        in_specs=[SMEM, full_spec((rows, d))] + [ANY] * (2 * len(own)),
        out_specs=[pl.BlockSpec((rows, cols), lambda j: (0, j)), full_spec((8, 4 * d))],
        out_shape=[
            jax.ShapeDtypeStruct((rows, 2 * cols), BF), jax.ShapeDtypeStruct((8, 4 * d), F32)
        ],
        scratch_shapes=weight_scratch(dims, n, cols)
        + [
            pltpu.VMEM(dims + (n, 128), BF), pltpu.SemaphoreType.DMA(dims),
            pltpu.VMEM((rows, d), BF), pltpu.VMEM((2, 1, cols), F32),
        ],
        compiler_params=params(),
        cost_estimate=cost(4 * rows * d * cols, rows * d * 8 + d * cols * 4),
        name="qkv",
    )(where, x, *own, *oth)


def proj_kernel(x_ref, a0_ref, a1_ref, vec_ref, w_ref, mid_ref, n_ref):
    d = x_ref.shape[1]
    a = jnp.concatenate([a0_ref[...], a1_ref[...]], axis=1)
    branch = dot(a, w_ref[...]) + vec_ref[3:4, :d]
    middle = x_ref[...].astype(F32) + BS * branch
    mid_ref[...] = middle
    xhat, _ = normalize(middle)
    n_ref[...] = (xhat * vec_ref[4:5, :d] + vec_ref[5:6, :d]).astype(BF)


def proj_call(x, att, vec, w):
    rows, d = x.shape
    br = 256
    row = pl.BlockSpec((br, d), lambda i: (i, 0))
    return pl.pallas_call(
        proj_kernel,
        grid=(rows // br,),
        in_specs=[row] + [pl.BlockSpec((br, v.shape[1]), lambda i: (i, 0)) for v in att]
        + [full_spec(vec.shape), full_spec((d, d))],
        out_specs=[row, row],
        out_shape=[jax.ShapeDtypeStruct((rows, d), F32), jax.ShapeDtypeStruct((rows, d), BF)],
        compiler_params=params(),
        cost_estimate=cost(2 * rows * d * d, rows * d * 10 + d * d * 2),
        name="proj",
    )(x, *att, vec, w)


def mlp_kernel(dims, count, take, where_ref, n_ref, c_ref, mid_ref, vec_ref, wo_ref, *refs):
    own, oth = refs[:count], refs[count : 2 * count]
    (
        out_ref, gn_ref, gfb_ref, gob_ref, go_ref, g_own, g_oth,
        nt_scr, mg_scr, acc_scr, act_scr, gp_scr, f_scr, f_sem, gf_scr, gf_sem,
    ) = refs[2 * count :]
    j = pl.program_id(0)
    rows, d = n_ref.shape
    wide = f_scr.shape[-1]
    blocks = 2 * wide // d
    br = 512

    @pl.when(j == 0)
    def _():
        load_columns(dims, where_ref, own, oth, 0, wide, f_scr, f_sem)
        nt_scr[...] = n_ref[...].T
        total = jnp.zeros_like(gob_ref)
        for r in range(0, rows, br):
            mg = (BS * c_ref[r : r + br, :].astype(F32)).astype(BF)
            mg_scr[r : r + br, :] = mg
            total += jnp.sum(mg.astype(F32), axis=0, keepdims=True)
        gob_ref[...] = total
        wait_columns(dims, f_scr, f_sem, 0)

    @pl.when(j == blocks // 2)
    def _():
        wait_columns(dims, f_scr, f_sem, 1)

    half = j // (blocks // 2)
    first = pl.multiple_of(lax.rem(j, blocks // 2) * d, 128)
    wf = flat2(f_scr[half, :, :, :, :, pl.ds(first, d)])
    wo = wo_ref[:, :take, :].reshape(d, d)
    fb = vec_ref[6:7, pl.ds(pl.multiple_of(j * d, 128), d)]
    bias_sum = jnp.zeros((1, d), F32)
    starts = list(range(0, rows, br))

    def ahead_of(r):
        return dot(n_ref[r : r + br, :], wf), dot_t(mg_scr[r : r + br, :], wo)

    def behind(r, act, gp):
        rr = slice(r, r + br)
        fwd = dot(act, wo)
        back = dot_t(gp, wf)
        acc_scr[rr, :] = jnp.where(j == 0, fwd, acc_scr[rr, :] + fwd)
        gn_ref[rr, :] = jnp.where(j == 0, back, gn_ref[rr, :] + back)

    queue = [ahead_of(starts[0])]
    waiting = None
    for i, r in enumerate(starts):
        rr = slice(r, r + br)
        if i + 1 < len(starts):
            queue.append(ahead_of(starts[i + 1]))
        (pre, ga), queue[i] = queue[i], None
        pre = pre + fb
        sq = pre * pre
        t = jnp.tanh(GC0 * pre * (1.0 + GC1 * sq))
        half_t = 0.5 * (1.0 + t)
        act = (pre * half_t).astype(BF)
        slope = half_t + (0.5 * GC0) * pre * (1.0 - t * t) * (1.0 + (3.0 * GC1) * sq)
        gp = (slope * ga).astype(BF)
        act_scr[rr, :] = act
        gp_scr[rr, :] = gp
        bias_sum += jnp.sum(gp.astype(F32), axis=0, keepdims=True)
        if waiting is not None:
            behind(*waiting)
        waiting = r, act, gp
    behind(*waiting)

    gfb_ref[...] = bias_sum
    gf_scr[j] = dot(nt_scr[...], gp_scr[...]).astype(BF).reshape(gf_scr.shape[1:])
    store_columns(dims, where_ref, gf_scr.at[j], g_own, g_oth, half, first, d, gf_sem.at[j])
    go_ref[...] = dot_0(act_scr[...], mg_scr[...]).astype(BF)

    @pl.when(j == blocks - 1)
    def _():
        for r in range(0, rows, br):
            rr = slice(r, r + br)
            out_ref[rr, :] = (mid_ref[rr, :] + BS * (acc_scr[rr, :] + vec_ref[7:8, :d])).astype(BF)
        for b in range(blocks):
            wait_store(dims, gf_scr.at[b], g_own, 0, d, gf_sem.at[b])


def mlp_call(dims, where, normed, cot, middle, vec, w_out, take, own, oth):
    rows, d = normed.shape
    n, wide = own[0].shape[1:]
    blocks = 2 * wide // d
    count = dims[1] * dims[2]
    act = full_spec((rows, d))
    piece = jax.ShapeDtypeStruct((count, dims[0], n, wide), BF)
    block = pl.BlockSpec((d, d), lambda j: (j, 0))
    whole = pl.BlockSpec((d // take,) + w_out.shape[1:], lambda j: (j, 0, 0))
    return pl.pallas_call(
        functools.partial(mlp_kernel, dims, len(own), take),
        grid=(blocks,),
        in_specs=[SMEM, act, act, act, full_spec(vec.shape), whole] + [ANY] * (2 * len(own)),
        out_specs=[act, act, pl.BlockSpec((1, d), lambda j: (0, j)), full_spec((1, d)), block] + [ANY] * 2,
        out_shape=[
            jax.ShapeDtypeStruct((rows, d), BF),
            jax.ShapeDtypeStruct((rows, d), F32),
            jax.ShapeDtypeStruct((1, blocks * d), F32),
            jax.ShapeDtypeStruct((1, d), F32),
            jax.ShapeDtypeStruct((blocks * d, d), BF),
            piece, piece,
        ],
        scratch_shapes=[
            pltpu.VMEM((d, rows), BF), pltpu.VMEM((rows, d), BF), pltpu.VMEM((rows, d), F32),
            pltpu.VMEM((rows, d), BF), pltpu.VMEM((rows, d), BF),
        ]
        + weight_scratch(dims, n, wide)
        + [
            pltpu.VMEM((blocks,) + dims + (n, d), BF), pltpu.SemaphoreType.DMA((blocks, count, dims[0])),
        ],
        compiler_params=params(),
        cost_estimate=cost(24 * rows * d * wide, 30e6, 2 * rows * wide),
        name="mlp",
    )(where, normed, cot, middle, vec, w_out, *own, *oth)


def proj_back_kernel(
    gn_ref, mid_ref, c_ref, a0_ref, a1_ref, vec_ref, ind_ref, w_ref,
    gm_ref, ga_ref, gw_ref, del_ref, gg_ref, gb_ref, gpb_ref, gw_acc,
):
    i = pl.program_id(0)
    d = mid_ref.shape[1]

    @pl.when(i == 0)
    def _():
        gw_acc[...] = jnp.zeros_like(gw_acc)
        gg_ref[...] = jnp.zeros_like(gg_ref)
        gb_ref[...] = jnp.zeros_like(gb_ref)
        gpb_ref[...] = jnp.zeros_like(gpb_ref)

    dy = gn_ref[...]
    xhat, rstd = normalize(mid_ref[...])
    gg_ref[...] += jnp.sum(dy * xhat, axis=0, keepdims=True)
    gb_ref[...] += jnp.sum(dy, axis=0, keepdims=True)
    gm = c_ref[...].astype(F32) + ln_back(dy, xhat, rstd, vec_ref[4:5, :d])
    gm_ref[...] = gm
    pg = (BS * gm).astype(BF)
    gpb_ref[...] += jnp.sum(pg.astype(F32), axis=0, keepdims=True)
    a = jnp.concatenate([a0_ref[...], a1_ref[...]], axis=1)
    gw_acc[...] += dot_0(a, pg)
    ga = dot_t(pg, w_ref[...]).astype(BF)
    ga_ref[...] = ga
    prod = ga.astype(F32) * a.astype(F32)
    high = prod.astype(BF)
    low = (prod - high.astype(F32)).astype(BF)
    del_ref[...] = dot_t(ind_ref[...], high) + dot_t(ind_ref[...], low)

    @pl.when(i == pl.num_programs(0) - 1)
    def _():
        gw_ref[...] = gw_acc[...].astype(BF)


def proj_back_call(gn, middle, cot, att, vec, w):
    rows, d = middle.shape
    br = 256
    row = pl.BlockSpec((br, d), lambda i: (i, 0))
    ind = (jnp.arange(16)[:, None] == jnp.arange(d)[None, :] // HD).astype(BF)
    one = full_spec((1, d))
    vshape = jax.ShapeDtypeStruct((1, d), F32)
    return pl.pallas_call(
        proj_back_kernel,
        grid=(rows // br,),
        in_specs=[row, row, row] + [pl.BlockSpec((br, v.shape[1]), lambda i: (i, 0)) for v in att]
        + [full_spec(vec.shape), full_spec((16, d)), full_spec((d, d))],
        out_specs=[row, row, full_spec((d, d)), pl.BlockSpec((16, br), lambda i: (0, i)), one, one, one],
        out_shape=[
            jax.ShapeDtypeStruct((rows, d), F32),
            jax.ShapeDtypeStruct((rows, d), BF),
            jax.ShapeDtypeStruct((d, d), BF),
            jax.ShapeDtypeStruct((16, rows), F32),
            vshape, vshape, vshape,
        ],
        scratch_shapes=[pltpu.VMEM((d, d), F32)],
        compiler_params=params(),
        cost_estimate=cost(4 * rows * d * d, rows * d * 16),
        name="proj_back",
    )(gn, middle, cot, *att, vec, ind, w)


def pair_back(j_ref, do_ref, lse_ref, del_ref, row, segr_ref, segc_ref, pair, dj_ref, dk_acc, dv_acc):
    rows = j_ref.shape[0]
    scale = HD**-0.5
    lanes = slice(pair * 128, (pair + 1) * 128)
    base = pair * 384
    k = j_ref[:, 128:256] * BF(scale)
    ks = split_heads(k)
    kt = k.T
    vs = split_heads(j_ref[:, 256:384])
    qt = j_ref[:, 0:128].T
    dot_do = do_ref[:, lanes].T
    items = [(tile, h) for tile in q_tiles(rows)[::-1] for h in range(2)]

    def ahead_of(item):
        (q0, kv0, kv1, _), h = item
        q = j_ref[q0 : q0 + 256, 0:128]
        do = do_ref[q0 : q0 + 256, lanes]
        return dot_t(ks[h][kv0:kv1], q), dot_t(vs[h][kv0:kv1], do)

    def behind(tile, h, probs, ds):
        q0, kv0, kv1, _ = tile
        hh = slice(h * HD, (h + 1) * HD)
        qq = slice(q0, q0 + 256)
        dv = dot_t(dot_do[hh, qq], probs)
        dk = dot_t(qt[hh, qq], ds)
        if q0 in (LONG, LONG - 256):
            dk_acc[hh, kv0:kv1] = dk
            dv_acc[hh, kv0:kv1] = dv
        else:
            dk_acc[hh, kv0:kv1] += dk
            dv_acc[hh, kv0:kv1] += dv
        return dot(kt[hh, kv0:kv1], ds)

    queue = [ahead_of(it) for it in items[:2]]
    waiting, dqs = None, []

    def settle():
        tile, h = waiting[:2]
        dqs.append(behind(*waiting))
        if h == 1:
            q0 = tile[0]
            dj_ref[q0 : q0 + 256, base : base + 128] = jnp.concatenate(dqs[-2:], axis=0).T.astype(BF)

    for n, (tile, h) in enumerate(items):
        q0, kv0, kv1, is_long = tile
        if n + 2 < len(items):
            queue.append(ahead_of(items[n + 2]))
        (s, dp), queue[n] = queue[n], None
        lse = lse_ref[pair, h : h + 1, q0 : q0 + 256]
        dlt = del_ref[pl.ds(row + h, 1), q0 : q0 + 256]
        parts = mask_diagonal(s, q0 - kv0, is_long, segr_ref, segc_ref)
        probs = jnp.concatenate([jnp.exp(p - lse) for p in parts], axis=0)
        ds = (probs * (dp - dlt)).astype(BF)
        if waiting is not None:
            settle()
        waiting = tile, h, probs.astype(BF), ds
    settle()
    dj_ref[:, base + 128 : base + 256] = (dk_acc[...] * scale).T.astype(BF)
    dj_ref[:, base + 256 : base + 384] = dv_acc[...].T.astype(BF)


def attn_back_kernel(
    dims, count, devices, where_ref, j0_ref, j1_ref, do_ref, lse_ref, del_ref, segr_ref, segc_ref,
    x_ref, vec_ref, gwp_ref, gfb_ref, gob_ref, gg2_ref, gb2_ref, gpb_ref, gm_ref, *refs,
):
    own, oth, refs = refs[:count], refs[count : 2 * count], refs[2 * count :]
    gx_ref, g_own, g_oth = refs[:3]
    (
        w_scr, w_sem, nt_scr, gn_scr, gm_scr, gm_sem, dj_scr, dk_acc, dv_acc, gw_scr, gw_sem,
        p_scr, p_sem, t_scr, t_sem, qv_scr,
    ) = refs[3:]
    i = pl.program_id(0)
    groups = gw_scr.shape[0]
    rows, d = x_ref.shape
    br = 256
    proj_at = groups * 384
    table_at = proj_at + d // 2

    @pl.when(i == 0)
    def _():
        load_columns(dims, where_ref, own, oth, 0, groups * 384, w_scr, w_sem)
        local_copy(gm_ref, gm_scr, gm_sem).start()
        for h in range(2):
            p_scr[h] = gwp_ref[:, h * (d // 2) : (h + 1) * (d // 2)].reshape(p_scr.shape[1:])
            store_columns(dims, where_ref, p_scr.at[h], g_own, g_oth, h, proj_at, d // 2, p_sem.at[h])
        for r in range(0, rows, br):
            xhat, _ = normalize(x_ref[r : r + br, :].astype(F32))
            nt_scr[:, r : r + br] = (xhat * vec_ref[0:1, :d] + vec_ref[1:2, :d]).astype(BF).T

    for h, j_ref in enumerate((j0_ref, j1_ref)):
        row = (i * 2 + h) * 2
        pair_back(j_ref, do_ref, lse_ref, del_ref, row, segr_ref, segc_ref, h, dj_scr, dk_acc, dv_acc)

    @pl.when(i == 0)
    def _():
        for h in range(2):
            wait_columns(dims, w_scr, w_sem, h)

    first = pl.multiple_of(i * 384, 128)
    dj = dj_scr[...]
    for h in range(2):
        for t, off in ((0, 0), (2, d)):
            part = dj[:, h * 384 + t * 128 : h * 384 + (t + 1) * 128].astype(F32)
            qv_scr[:, pl.ds(pl.multiple_of(off + (i * 2 + h) * 128, 128), 128)] = jnp.sum(part, axis=0, keepdims=True)
    gw = dot(nt_scr[...], dj).astype(BF)
    for h in range(2):
        gw_scr[i, h] = gw[:, h * 384 : (h + 1) * 384].reshape(gw_scr.shape[2:])
        store_columns(dims, where_ref, gw_scr.at[i, h], g_own, g_oth, h, first, 384, gw_sem.at[i, h])
    w = jnp.concatenate([flat2(w_scr[h, :, :, :, :, pl.ds(first, 384)]) for h in range(2)], axis=1)
    for r in range(0, rows, br):
        back = dot_t(dj[r : r + br, :], w)
        gn_scr[r : r + br, :] = jnp.where(i == 0, back, gn_scr[r : r + br, :] + back)

    @pl.when(i == groups - 1)
    def _():
        local_copy(gm_ref, gm_scr, gm_sem).wait()
        gg = jnp.zeros((1, d), F32)
        gb = jnp.zeros((1, d), F32)
        for r in range(0, rows, br):
            rr = slice(r, r + br)
            xhat, rstd = normalize(x_ref[rr, :].astype(F32))
            dy = gn_scr[rr, :]
            gg += jnp.sum(dy * xhat, axis=0, keepdims=True)
            gb += jnp.sum(dy, axis=0, keepdims=True)
            gx_ref[rr, :] = (gm_scr[rr, :] + ln_back(dy, xhat, rstd, vec_ref[0:1, :d])).astype(BF)
        table = pack_vectors(
            {
                "g1": gg, "b1": gb, "qv": qv_scr[...], "fb": gfb_ref[...], "pb": gpb_ref[...],
                "g2": gg2_ref[...], "b2": gb2_ref[...], "ob": gob_ref[...],
            },
            d, devices,
        ).reshape(t_scr.shape)
        t_scr[...] = table
        for h in range(2):
            store_columns(dims, where_ref, t_scr, g_own, g_oth, h, table_at, 128, t_sem.at[h])
        for h in range(2):
            for b in range(groups):
                wait_store(dims, gw_scr.at[b, h], g_own, 0, 384, gw_sem.at[b, h])
            wait_store(dims, p_scr.at[h], g_own, proj_at, d // 2, p_sem.at[h])
            wait_store(dims, t_scr, g_own, table_at, 128, t_sem.at[h])


def attn_back_call(dims, where, joined, ga, lse, delta, seg_row, seg_col, x, vec, own, oth, vectors, gm, devices):
    rows, d = x.shape
    n = own[0].shape[1]
    groups = d // 256
    act = full_spec((rows, d))
    count = dims[1] * dims[2]
    piece = jax.ShapeDtypeStruct((count, dims[0], n, groups * 384 + d // 2 + 128), BF)
    return pl.pallas_call(
        functools.partial(attn_back_kernel, dims, len(own), devices),
        grid=(groups,),
        in_specs=[
            SMEM,
            pl.BlockSpec((rows, 384), lambda i: (0, i)),
            pl.BlockSpec((rows, 384), lambda i: (0, groups + i)),
            pl.BlockSpec((rows, 256), lambda i: (0, i)),
            pl.BlockSpec((2, 2, rows), lambda i: (i, 0, 0)),
            full_spec(delta.shape), full_spec((1, 256)), full_spec((256, 1)), act, full_spec(vec.shape),
        ]
        + [full_spec(v.shape) for v in vectors] + [ANY] * (1 + 2 * len(own)),
        out_specs=[act, ANY, ANY],
        out_shape=[jax.ShapeDtypeStruct((rows, d), BF), piece, piece],
        scratch_shapes=weight_scratch(dims, n, groups * 384)
        + [
            pltpu.VMEM((d, rows), BF), pltpu.VMEM((rows, d), F32),
            pltpu.VMEM((rows, d), F32), pltpu.SemaphoreType.DMA(()), pltpu.VMEM((rows, 768), BF),
            pltpu.VMEM((128, rows), F32), pltpu.VMEM((128, rows), F32),
            pltpu.VMEM((groups, 2) + dims + (n, 384), BF), pltpu.SemaphoreType.DMA((groups, 2, count, dims[0])),
            pltpu.VMEM((2,) + dims + (n, d // 2), BF), pltpu.SemaphoreType.DMA((2, count, dims[0])),
            pltpu.VMEM(dims + (n, 128), BF), pltpu.SemaphoreType.DMA((2, count, dims[0])),
            pltpu.VMEM((1, 2 * d), F32),
        ],
        compiler_params=params(),
        cost_estimate=cost(60e9, 20e6, 5.5e6),
        name="attn_back",
    )(where, joined, joined, ga, lse, delta, seg_row, seg_col, x, vec, *vectors, gm, *own, *oth)


def pack_plan(counts, rows):
    c = [counts[i] for i in range(counts.shape[0])]
    ends, run = [], jnp.int32(0)
    for v in c:
        run = run + v
        ends.append(run)
    start = jnp.int32(0)
    for i in range(len(c) - 1):
        start = jnp.where(c[i] == LONG, ends[i] - c[i], start)
    rolled = jnp.arange(rows, dtype=jnp.int32)
    pos = rolled + start
    pos = jnp.where(pos >= rows, pos - rows, pos)
    seg = functools.reduce(jnp.add, [(pos >= e).astype(jnp.int32) for e in ends])
    valid = seg < len(c) - 1
    seg = jnp.where(valid, seg, 1000 + rolled)
    return start, seg[LONG:], valid


def roll_rows(array, shift):
    return lax.dynamic_slice_in_dim(jnp.concatenate([array, array], axis=0), shift, array.shape[0])


def half_columns(w, h, joined=False):
    r, cols = w.shape
    if not joined:
        return w[:, h * (cols // 2) : (h + 1) * (cols // 2)]
    pairs = cols // 384
    starts = [(t * pairs + p) * 128 for p in range(h, pairs, 2) for t in range(3)]
    return jnp.concatenate([w[:, s : s + 128] for s in starts], axis=1)


def join_columns(left, right):
    r, m = left.shape
    both = jnp.stack([v.reshape(r, m // 384, 3, 128) for v in (left, right)], axis=2)
    return both.transpose(0, 3, 1, 2, 4).reshape(r, 2 * m)


def add_all(values):
    return functools.reduce(jnp.add, [v.astype(F32) for v in values])


class Plain:
    def __init__(self, dp, fsdp):
        self.dims = (1, 1, 1)
        index = lax.axis_index("dp") * fsdp + lax.axis_index("fsdp")
        self.ci = index % 2

    def where(self):
        zero = jnp.zeros((), jnp.int32)
        return jnp.stack([zero, zero, zero, self.ci.astype(jnp.int32)])

    def pick(self, pair):
        return jnp.where(self.ci == 0, pair[0], pair[1]), jnp.where(self.ci == 0, pair[1], pair[0])

    def gather(self, w_qkv, table, w_fc):
        whole = lambda v: lax.all_gather(v, AXES, axis=0, tiled=True)
        attn, fc = whole(jnp.concatenate([w_qkv, table], axis=1)), whole(w_fc)
        qkv, table = attn[:, : w_qkv.shape[1]], attn[:, w_qkv.shape[1] :]
        first = [jnp.concatenate([half_columns(qkv, h, True), table], axis=1) for h in range(2)]
        listed = []
        for pair in (first, [half_columns(fc, h) for h in range(2)]):
            own, oth = self.pick(pair)
            listed.append(([own[None]], [oth[None]]))
        return listed

    def scatter(self, own, oth):
        pair = self.pick([own[0, 0], oth[0, 0]])
        m = pair[0].shape[1]
        mine = lax.psum_scatter(jnp.concatenate(pair, axis=1), AXES, scatter_dimension=0, tiled=True).astype(F32)
        return mine[:, :m], mine[:, m:]


class Chips:
    def __init__(self, dp, fsdp):
        x_n, z_n = fsdp // 2, 4
        self.dims = (z_n, dp // z_n, x_n)
        index = lax.axis_index("dp") * fsdp + lax.axis_index("fsdp")
        self.ci = index % 2
        self.at = (index // (2 * x_n * self.dims[1]), (index // (2 * x_n)) % self.dims[1], (index // 2) % x_n, self.ci)

    def where(self):
        return jnp.stack(self.at).astype(jnp.int32)

    def pick(self, pair):
        return jnp.where(self.ci == 0, pair[0], pair[1]), jnp.where(self.ci == 0, pair[1], pair[0])

    def send(self, array, dz=0, dy=0, dx=0, dc=0):
        z_n, y_n, x_n = self.dims
        pairs = []
        for z in range(z_n):
            for y in range(y_n):
                for x in range(x_n):
                    for c in range(2):
                        here = ((z * y_n + y) * x_n + x) * 2 + c
                        there = (((z + dz) % z_n * y_n + (y + dy) % y_n) * x_n + (x + dx) % x_n) * 2 + (c + dc) % 2
                        pairs.append((here, there))
        return lax.ppermute(array, AXES, pairs)

    def trade(self, halves):
        return self.rows_of(*self.pick(halves))

    def rows_of(self, keep, give):
        return jnp.concatenate(self.pick([keep, self.send(give, dc=1)]), axis=0)

    def along_z(self, piece):
        return [piece] + [self.send(piece, dz=-k) for k in range(1, self.dims[0])]

    def swap(self, arrays):
        return [self.send(v, dc=1) for v in arrays]

    def add_core(self, own, theirs):
        return [add_all([own[i], theirs[i]]).astype(BF) for i in range(own.shape[0])]

    def rows_back(self, total):
        n = total.shape[0] // 2
        mine, give = self.pick([total[:n], total[n:]])
        return self.pick([mine, self.send(give, dc=1)])


def together(*trees):
    return lax.optimization_barrier(trees)


def prepare(tokens, lengths, cotangent):
    start, seg, valid = pack_plan(lengths[0], tokens.shape[0])
    x = roll_rows(tokens, start)
    cot = jnp.where(valid[:, None], roll_rows(cotangent, start), BF(0))
    return start, seg[None, :], seg[:, None], x, cot


def vector_table(r, ln1_gain, ln1_bias, qv_bias, proj_bias, ln2_gain, ln2_bias, fc_bias, out_bias):
    flat = [
        jnp.concatenate([ln1_gain, ln1_bias, qv_bias]), fc_bias,
        jnp.concatenate([proj_bias, ln2_gain, ln2_bias, out_bias]),
    ]
    return jnp.pad(jnp.stack(flat), ((0, r - 3), (0, 128 - 4 * r)))


def results(r, out, gx, s_fc, s_out, s_attn):
    d = out.shape[1]
    cut = 3 * d // 2
    s_qkv = join_columns(*[v[:, :cut] for v in s_attn])
    s_proj = jnp.concatenate([v[:, cut:-128] for v in s_attn], axis=1)
    row0, row1, row2 = [s_attn[0][k, -128:][: 4 * r] for k in range(3)]
    return (
        out, gx,
        row0[:r], row0[r : 2 * r], s_qkv, row0[2 * r :], s_proj, row2[:r],
        row2[r : 2 * r], row2[2 * r : 3 * r], jnp.concatenate(s_fc, axis=1), row1, s_out, row2[3 * r :],
    )


def block_plain(
    links, tokens, lengths, ln1_gain, ln1_bias, w_qkv, qv_bias, w_proj, proj_bias, ln2_gain, ln2_bias,
    w_fc, fc_bias, w_out, out_bias, cotangent,
):
    rows, d = tokens.shape
    r = w_qkv.shape[0]
    devices = d // r
    dims, where = links.dims, links.where()
    table = vector_table(r, ln1_gain, ln1_bias, qv_bias, proj_bias, ln2_gain, ln2_bias, fc_bias, out_bias)
    attn_w, fc_w = links.gather(w_qkv, table, w_fc)
    proj = lax.all_gather(w_proj, AXES, axis=0, tiled=True)
    w_out_all = lax.all_gather(w_out, AXES, axis=0, tiled=True).reshape(-1, d, d)
    start, seg_row, seg_col, x, cot = prepare(tokens, lengths, cotangent)
    joined, vec = qkv_call(dims, where, x, *attn_w, devices)
    att0, lse0 = attn_call(joined, seg_row, seg_col, 0, 2)
    att1, lse1 = attn_call(joined, seg_row, seg_col, 2, d // 256 - 2)
    att = att0, att1
    middle, normed_two = proj_call(x, att, vec, proj)
    out, gn, gfb, gob, gw_out, *fc_g = mlp_call(dims, where, normed_two, cot, middle, vec, w_out_all, d, *fc_w)
    s_fc = links.scatter(*fc_g)
    s_out = lax.psum_scatter(gw_out, AXES, scatter_dimension=0, tiled=True).astype(F32)
    gm, ga, gw_proj, delta, gg2, gb2, gpb = proj_back_call(gn, middle, cot, att, vec, proj)
    gx, *g = attn_back_call(
        dims, where, joined, ga, jnp.concatenate([lse0, lse1]), delta, seg_row, seg_col, x, vec, *attn_w,
        (gw_proj, gfb, gob, gg2, gb2, gpb), gm, devices,
    )
    restore = rows - start
    return results(r, roll_rows(out, restore), roll_rows(gx, restore), s_fc, s_out, links.scatter(*g))


def block_chips(
    links, tokens, lengths, ln1_gain, ln1_bias, w_qkv, qv_bias, w_proj, proj_bias, ln2_gain, ln2_bias,
    w_fc, fc_bias, w_out, out_bias, cotangent,
):
    rows, d = tokens.shape
    r = w_qkv.shape[0]
    devices = d // r
    dims, where, send, swap = links.dims, links.where(), links.send, links.swap
    table = vector_table(r, ln1_gain, ln1_bias, qv_bias, proj_bias, ln2_gain, ln2_bias, fc_bias, out_bias)

    def xy(column):
        return send(column, dx=1), send(column, dy=1)

    hidden = w_out.shape[0]
    rest = lax.all_gather(jnp.concatenate([w_out, w_proj], axis=0), AXES, axis=0, tiled=True)
    rest = rest.reshape(devices, hidden + r, d)
    a = links.rows_of(*cut_call(where, w_qkv, table))
    a, tokens, lengths, cotangent, w_fc = together(a, tokens, lengths, cotangent, w_fc)
    a0 = links.along_z(a)
    fc = links.trade([half_columns(w_fc, h) for h in range(2)])
    prep = prepare(tokens, lengths, cotangent)
    a0, prep, fc = together(a0, prep, fc)
    start, seg_row, seg_col, x, cot = prep
    a0 = jnp.stack(a0)
    a_own = [a0, send(a0, dx=1), send(a0, dy=1), send(a0, dx=1, dy=1)]
    fc = links.along_z(fc)
    a_own, fc = together(a_own, fc)
    fc0 = jnp.stack(fc)
    attn_w = a_own, swap(a_own)
    fc0, x, attn_w = together(fc0, x, attn_w)

    joined, vec = qkv_call(dims, where, x, *attn_w, devices)
    att0, lse0 = attn_call(joined, seg_row, seg_col, 0, 2)
    fx, fy = xy(fc0)
    att0, joined, fx, fy = together(att0, joined, fx, fy)
    att1, lse1 = attn_call(joined, seg_row, seg_col, 2, d // 256 - 2)
    att = att0, att1
    proj = rest[:, hidden:].reshape(d, d)
    middle, normed_two = proj_call(x, att, vec, proj)
    fd = [send(fx[:2], dy=1), send(fy[2:], dx=1)]
    f_oth = swap([fc0, fx, fy])
    lse = jnp.concatenate([lse0, lse1])
    normed_two, fd, f_oth, lse = together(normed_two, fd, f_oth, lse)
    fc_w = [fc0, fx, fy] + fd, f_oth + swap(fd)

    out, gn, gfb, gob, gw_out, f_own, f_oth = mlp_call(dims, where, normed_two, cot, middle, vec, rest, hidden, *fc_w)
    s_out = lax.psum_scatter(gw_out, AXES, scatter_dimension=0, tiled=True).astype(F32)
    gm, ga, gw_proj, delta, gg2, gb2, gpb = proj_back_call(gn, middle, cot, att, vec, proj)
    (f_oth,) = swap([f_oth])
    restore = rows - start
    out = roll_rows(out, restore)
    ga, delta, f_own, f_oth, out = together(ga, delta, f_own, f_oth, out)

    def near(b):
        return send(b[1], dx=1), send(b[2], dy=1), send(b[3], dx=1, dy=1)

    def column(b, arrived):
        return [add_all([b[0][j]] + [v[j] for v in arrived]).astype(BF) for j in range(dims[0])]

    def far(parts):
        return [parts[0]] + [send(parts[j], dz=j) for j in range(1, dims[0])]

    b = links.add_core(f_own, f_oth)
    b, ga, delta = together(b, ga, delta)
    b_near = near(b)
    gx, g_own, g_oth = attn_back_call(
        dims, where, joined, ga, lse, delta, seg_row, seg_col, x, vec, *attn_w,
        (gw_proj, gfb, gob, gg2, gb2, gpb), gm, devices,
    )
    gx, g_own, g_oth, b_near, b = together(gx, g_own, g_oth, b_near, b)

    (g_oth,) = swap([g_oth])
    b = column(b, b_near)
    g_oth, b, gx = together(g_oth, b, gx)
    e = links.add_core(g_own, g_oth)
    e_near, b = near(e), far(b)
    gx = roll_rows(gx, restore)
    e_near, b, e, gx = together(e_near, b, e, gx)

    e = far(column(e, e_near))
    s_fc = links.rows_back(add_all(b))
    e, s_fc = together(e, s_fc)
    return results(r, out, gx, s_fc, s_out, links.rows_back(add_all(e)))


def solution(mesh):
    dp, fsdp = mesh.shape["dp"], mesh.shape["fsdp"]

    def per_device(*args):
        if (dp, fsdp) == (8, 4) and args[4].shape[0] % 8 == 0:
            return block_chips(Chips(dp, fsdp), *args)
        return block_plain(Plain(dp, fsdp), *args)

    row, vec = P(AXES, None), P(AXES)
    in_specs = (row, row, vec, vec, row, vec, row, vec, vec, vec, row, vec, row, vec, row)
    out_specs = (row, row, vec, vec, row, vec, row, vec, vec, vec, row, vec, row, vec)
    return jax.shard_map(
        per_device, mesh=mesh, in_specs=in_specs, out_specs=out_specs, check_vma=False
    )
```

time: 329 us -> 313 us (0.951)
  Pallas kernels: 163 us -> 129 us
  waiting for transfers between devices: 56.4 us -> 83.9 us
  between operations: 7.51 us -> 20.7 us
  local copies, waits for them, and re-layouts: 18.2 us -> 8.28 us
  other arithmetic: 38 us -> 29.8 us
  starting transfers between devices: 42 us -> 36.3 us
    reduce_scatter x0 -> x1, waiting for transfers between devices: none -> 23.7 us  [block_chips(): lax.psum_scatter(gw_out, AXES, scatter_dimension=0, tiled=True).astype(F32)]
    pallas_call x6 -> x5, Pallas kernels: 128 us -> 104 us  [the longest x1 46.6 us: mlp_call(): pl.pallas_call(functools.partial(mlp_kernel, dims, len(own), take), grid=...]
    pallas_call x2, Pallas kernels: 23.2 us -> 13.1 us  [attn_call(): pl.pallas_call(attn_kernel, grid=(2 * groups,), in_specs=[at(0), at(1), a...]
    ppermute x46 -> x40, starting transfers between devices: 42 us -> 36.2 us  [send(): return lax.ppermute(array, AXES, pairs)]
    unnamed x54 -> x38, local copies, waits for them, and re-layouts: 4.94 us -> 0.78 us
    convert_element_type x2, other arithmetic: 6.26 us -> 2.29 us  [add_core(): add_all([own[i], theirs[i]]).astype(BF)]
    ppermute x46 -> x40, waiting for transfers between devices: 56.4 us -> 60.2 us  [send(): return lax.ppermute(array, AXES, pairs)]
    slice x19 -> x4, local copies, waits for them, and re-layouts: 6.65 us -> 2.94 us  [the longest x1 2.38 us: block_chips(): proj = rest[:, hidden:].reshape(d, d)]
  transfers between devices with their start and end apart: 46 -> 42, of which waited for: 13 -> 19; matrix products, arithmetic and copies ran while one was open for 9% -> 10% of each run, Pallas kernels for 33% -> 27%
where the time goes in v4:
time: 313 us; the launch traced here: 308 us
  Pallas kernels  129 us (41%)
  waiting for transfers between devices  83.9 us (27%)
  starting transfers between devices  36.3 us (12%)
  other arithmetic  29.8 us (10%)
  between operations  20.7 us (7%)
  local copies, waits for them, and re-layouts  8.28 us (3%)
    ppermute x40, waiting for transfers between devices, send(): return lax.ppermute(array, AXES, pairs)  60.2 us
    pallas_call x1, Pallas kernels, mlp_call(): pl.pallas_call(functools.partial(mlp_kernel, dims, len(own), take), grid=...  46.6 us
    pallas_call x1, Pallas kernels, attn_back_call(): pl.pallas_call(functools.partial(attn_back_kernel, dims, len(own), device...  38.2 us
    ppermute x40, starting transfers between devices, send(): return lax.ppermute(array, AXES, pairs)  36.2 us
    reduce_scatter x1, waiting for transfers between devices, block_chips(): lax.psum_scatter(gw_out, AXES, scatter_dimension=0, tiled=True).astype(F32)  23.7 us
    pallas_call x2, Pallas kernels, attn_call(): pl.pallas_call(attn_kernel, grid=(2 * groups,), in_specs=[at(0), at(1), a...  13.1 us
    pallas_call x1, Pallas kernels, qkv_call(): pl.pallas_call(functools.partial(qkv_kernel, dims, len(own), devices), gr...  11.9 us
    pallas_call x1, Pallas kernels, proj_back_call(): pl.pallas_call(proj_back_kernel, grid=(rows // br,), in_specs=[row, row,...  11.8 us
  transfers between devices with their start and end apart: 42, of which 19 were waited for; matrix products, arithmetic and copies ran while one was open for 10% of the time, Pallas kernels for 27%

profile of v4, /device:TPU:0, one launch (start us, length us, event | category | flops | bytes accessed | tf_op | source)
XLA Modules:
  0.0 308.1 jit_solution(10326123728686537913)
XLA Ops:
  7.2 1.7 pad_maximum_fusion.3
  10.5 1.3 fusion.30.t_ref
  11.8 1.6 cut.1
  13.8 1.1 collective-permute-done
  15.8 5.0 %collective-permute-start.1 = (bf16[48,1280]{1,0:T(8,128)(2,1)S(1)}, bf16[48,1280]{1,0:T(8,128)(2,1)S(1)}, u32[]{:S(2)}, u32[]{:S(2)}) collective-permute-start(bf16[48,1280]{1,0:T(8,128)(2,1)S(1)} %pad_maximum_fusion.5), channel_id=1, source_target_pairs={{0,24},{1,25},{2,26},{3,27},{4,28},{5,29},{6,30},{7,31},{8,0},{9,1... | collective-permute-start | bytes 368648 | tf_op jit(solution)/shard_map/ppermute | solution.py:856
  20.8 1.0 collective-permute-start.3
  21.8 1.4 fusion.39
  30.8 3.8 %fusion.4.x_ref = bf16[1024,768]{1,0:T(8,128)(2,1)} fusion(s32[]{:T(128)S(6)} %select_n.152, bf16[1024,768]{1,0:T(8,128)(2,1)S(1)} %copy-done.3), kind=kLoop, calls=%fused_computation.12 | loop fusion | flops 3145728 | bytes 3145732 | tf_op jit(solution)/shard_map/concatenate | solution.py:779
  34.6 2.3 fusion.3.c_ref
  37.7 1.5 collective-permute-start.5
  39.2 1.6 collective-permute-start.6
  41.3 2.4 collective-permute-start.10
  43.7 1.6 collective-permute-start.8
  45.3 6.3 %collective-permute-done.10 = bf16[48,1536]{1,0:T(8,128)(2,1)S(1)} collective-permute-done((bf16[48,1536]{1,0:T(8,128)(2,1)S(1)}, bf16[48,1536]{1,0:T(8,128)(2,1)S(1)}, u32[]{:S(2)}, u32[]{:S(2)}) %collective-permute-start.10) | collective-permute-done | bytes 147488 | tf_op jit(solution)/shard_map/ppermute | solution.py:856
  51.6 4.4 %collective-permute-done.8 = bf16[48,1536]{1,0:T(8,128)(2,1)S(1)} collective-permute-done((bf16[48,1536]{1,0:T(8,128)(2,1)S(1)}, bf16[48,1536]{1,0:T(8,128)(2,1)S(1)}, u32[]{:S(2)}, u32[]{:S(2)}) %collective-permute-start.8) | collective-permute-done | bytes 147488 | tf_op jit(solution)/shard_map/ppermute | solution.py:856
  56.0 9.8 %collective-permute-done.9 = bf16[48,1536]{1,0:T(8,128)(2,1)S(1)} collective-permute-done((bf16[48,1536]{1,0:T(8,128)(2,1)S(1)}, bf16[48,1536]{1,0:T(8,128)(2,1)S(1)}, u32[]{:S(2)}, u32[]{:S(2)}) %collective-permute-start.9) | collective-permute-done | bytes 147488 | tf_op jit(solution)/shard_map/ppermute | solution.py:856
  65.9 2.3 collective-permute-done.7.refs_3_
  70.9 1.4 collective-permute-done.13.refs_6_
  72.3 1.4 collective-permute-done.14.refs_7_
  74.4 11.9 %qkv.1 = (bf16[1024,2304]{1,0:T(8,128)(2,1)}, f32[8,3072]{1,0:T(8,128)}) custom-call(s32[4]{0:T(128)} %pad_add_fusion.where_ref, bf16[1024,768]{1,0:T(8,128)(2,1)} %fusion.4.x_ref, bf16[4,48,1280]{2,1,0:T(8,128)(2,1)} %copy-done.7, bf16[4,48,1280]{2,1,0:T(8,128)(2,1)} %copy-done.13, bf16[4,48,1280]{2,1,0:T(8,128)(2,1)} %copy-done.14, ...), custom_call_target="tpu_custom_call" | custom-call | flops 3623878656 | bytes 9830400 | tf_op jit(solution)/shard_map/qkv/pallas_call | solution.py:354
  86.4 8.0 %attn.2 = (bf16[1024,512]{1,0:T(8,128)(2,1)}, f32[4,2,1024]{2,1,0:T(2,128)}) custom-call(bf16[1024,2304]{1,0:T(8,128)(2,1)} %get-tuple-element.160.q_ref.k_ref.v_ref.j0_ref.j1_ref, bf16[1024,2304]{1,0:T(8,128)(2,1)} %get-tuple-element.160.q_ref.k_ref.v_ref.j0_ref.j1_ref, bf16[1024,2304]{1,0:T(8,128)(2,1)} %get-tuple-element.160.q_ref.k_ref.v_ref.j0_ref.j1_ref, ...), custom_call_target="tpu_custom_call" | custom-call | flops 16000000000 | bytes 8000000 | tf_op jit(solution)/shard_map/attn/pallas_call | solution.py:127
  94.4 1.4 collective-permute-done.15.refs_1_
  96.5 1.4 collective-permute-start.17
  98.5 5.0 %attn.3 = (bf16[1024,256]{1,0:T(8,128)(2,1)}, f32[2,2,1024]{2,1,0:T(2,128)}) custom-call(bf16[1024,2304]{1,0:T(8,128)(2,1)} %get-tuple-element.160.q_ref.k_ref.v_ref.j0_ref.j1_ref, bf16[1024,2304]{1,0:T(8,128)(2,1)} %get-tuple-element.160.q_ref.k_ref.v_ref.j0_ref.j1_ref, bf16[1024,2304]{1,0:T(8,128)(2,1)} %get-tuple-element.160.q_ref.k_ref.v_ref.j0_ref.j1_ref, ...), custom_call_target="tpu_custom_call" | custom-call | flops 8000000000 | bytes 8000000 | tf_op jit(solution)/shard_map/attn/pallas_call | solution.py:127
  103.6 1.4 pad_maximum_fusion.7.lse_ref
  105.0 2.4 slice.354
  107.4 5.9 %proj.1 = (f32[1024,768]{1,0:T(8,128)}, bf16[1024,768]{1,0:T(8,128)(2,1)}) custom-call(bf16[1024,768]{1,0:T(8,128)(2,1)} %fusion.4.x_ref, bf16[1024,512]{1,0:T(8,128)(2,1)} %get-tuple-element.159.a0_ref, bf16[1024,256]{1,0:T(8,128)(2,1)} %get-tuple-element.161.a1_ref, f32[8,3072]{1,0:T(8,128)} %get-tuple-element.162.vec_ref, bf16[768,768]{1,0:T(8,128)(2,1)} %bitcast.76), custom_call_target="tpu_custom_call" | custom-call | flops 1207959552 | bytes 9043968 | tf_op jit(solution)/shard_map/proj/pallas_call | solution.py:387
  113.9 1.1 collective-permute-done.22.refs_8_
  116.3 46.6 %mlp.1 = (bf16[1024,768]{1,0:T(8,128)(2,1)}, f32[1024,768]{1,0:T(8,128)}, f32[1,3072]{1,0:T(1,128)}, f32[1,768]{1,0:T(1,128)}, bf16[3072,768]{1,0:T(8,128)(2,1)}...) custom-call(s32[4]{0:T(128)} %pad_add_fusion.where_ref, bf16[1024,768]{1,0:T(8,128)(2,1)} %get-tuple-element.168.n_ref, ...), custom_call_target="tpu_custom_call" | custom-call | flops 28991029248 | bytes 30000000 | tf_op jit(solution)/shard_map/mlp/pallas_call | solution.py:491
  163.8 4.0 %fusion.1 = bf16[1024,768]{1,0:T(8,128)(2,1)} fusion(s32[]{:T(128)S(6)} %select_n.160, bf16[1024,768]{1,0:T(8,128)(2,1)} %get-tuple-element.181), kind=kLoop, calls=%fused_computation.9 | loop fusion | flops 3145728 | bytes 3145732 | tf_op jit(solution)/shard_map/concatenate | solution.py:779
  167.9 11.8 %proj_back.1 = (f32[1024,768]{1,0:T(8,128)}, bf16[1024,768]{1,0:T(8,128)(2,1)}, bf16[768,768]{1,0:T(8,128)(2,1)}, f32[16,1024]{1,0:T(8,128)}, f32[1,768]{1,0:T(1...) custom-call(f32[1024,768]{1,0:T(8,128)} %get-tuple-element.176.gn_ref, f32[1024,768]{1,0:T(8,128)} %get-tuple-element.170.mid_ref, ...), custom_call_target="tpu_custom_call" | custom-call | flops 2415919104 | bytes 12582912 | tf_op jit(solution)/shard_map/proj_back/pallas_call | solution.py:561
  179.7 1.7 fusion.12
  181.4 1.5 collective-permute-start.25
  183.4 1.5 collective-permute-start.27
  184.9 38.2 %attn_back.1 = (bf16[1024,768]{1,0:T(8,128)(2,1)}, bf16[4,4,48,1664]{3,2,1,0:T(8,128)(2,1)}, bf16[4,4,48,1664]{3,2,1,0:T(8,128)(2,1)}) custom-call(s32[4]{0:T(128)} %pad_add_fusion.where_ref, bf16[1024,2304]{1,0:T(8,128)(2,1)} %get-tuple-element.160.q_ref.k_ref.v_ref.j0_ref.j1_ref, bf16[1024,2304]{1,0:T(8,128)(2,1)} %get-tuple-element.160.q_ref.k_ref.v_ref.j0_ref.j1_ref, ...), custom_call_target="tpu_custom_call" | custom-call | flops 60000002048 | bytes 20000000 | tf_op jit(solution)/shard_map/attn_back/pallas_call | solution.py:730
  223.5 4.7 %collective-permute-done.28 = bf16[4,4,48,1664]{3,2,1,0:T(8,128)(2,1)S(1)} collective-permute-done((bf16[4,4,48,1664]{3,2,1,0:T(8,128)(2,1)}, bf16[4,4,48,1664]{3,2,1,0:T(8,128)(2,1)S(1)}, u32[]{:S(2)}, u32[]{:S(2)}) %collective-permute-start.28) | collective-permute-done | bytes 2555936 | tf_op jit(solution)/shard_map/ppermute | solution.py:856
  228.8 1.6 collective-permute-start.29
  230.9 1.5 collective-permute-start.31
  232.4 2.8 collective-permute-start.32
  236.2 5.0 %collective-permute-done.32 = bf16[48,1536]{1,0:T(8,128)(2,1)S(1)} collective-permute-done((bf16[48,1536]{1,0:T(8,128)(2,1)S(1)}, bf16[48,1536]{1,0:T(8,128)(2,1)S(1)}, u32[]{:S(2)}, u32[]{:S(2)}) %collective-permute-start.32) | collective-permute-done | bytes 147488 | tf_op jit(solution)/shard_map/ppermute | solution.py:856
  241.6 3.7 %fusion = bf16[1024,768]{1,0:T(8,128)(2,1)} fusion(s32[]{:T(128)S(6)} %select_n.160, bf16[1024,768]{1,0:T(8,128)(2,1)S(1)} %copy-done.4), kind=kLoop, calls=%fused_computation.8 | loop fusion | flops 3145728 | bytes 3145732 | tf_op jit(solution)/shard_map/concatenate | solution.py:779
  245.3 3.0 collective-permute-done.33
  248.4 1.8 collective-permute-done.34
  250.1 14.3 %collective-permute-done.30 = bf16[4,48,1664]{2,1,0:T(8,128)(2,1)S(1)} collective-permute-done((bf16[4,48,1664]{2,1,0:T(8,128)(2,1)S(1)}, bf16[4,48,1664]{2,1,0:T(8,128)(2,1)S(1)}, u32[]{:S(2)}, u32[]{:S(2)}) %collective-permute-start.30) | collective-permute-done | bytes 639008 | tf_op jit(solution)/shard_map/ppermute | solution.py:856
  265.0 2.9 collective-permute-start.35
  268.9 1.6 collective-permute-start.37
  270.5 23.7 %reduce-scatter.2.cloned.1.call-done = bf16[96,768]{1,0:T(8,128)(2,1)} async-done(((bf16[3072,768]{1,0:T(8,128)(2,1)}), bf16[96,768]{1,0:T(8,128)(2,1)}) %reduce-scatter.2.cloned.1.call-update) | async-done | bytes 147472 | tf_op jit(solution)/shard_map/reduce_scatter | solution.py:987
  294.1 1.6 convert_element_type.393
  (135 shorter events, 23.3 us)
Async XLA Ops:
  7.2 23.6 %copy-start.3 = (bf16[1024,768]{1,0:T(8,128)(2,1)S(1)}, bf16[1024,768]{1,0:T(8,128)(2,1)}, u32[]{:S(2)}) copy-start(bf16[1024,768]{1,0:T(8,128)(2,1)} %param.15) | copy-start | bytes 4718596
  7.2 97.8 %all-gather.2.cloned.1.call-start = ((), (), s32[]{:S(2)}) async-start(), calls=%async_computation.1 | async-start | bytes 6082560 | tf_op jit(solution)/shard_map/all_gather | solution.py:955
  9.0 285.2 %reduce-scatter.2.cloned.1.call-start = ((), (), s32[]{:S(2)}) async-start(), calls=%async_computation.2 | async-start | bytes 4866048 | tf_op jit(solution)/shard_map/reduce_scatter | solution.py:987
  13.4 1.6 collective-permute-start
  15.8 21.8 %collective-permute-start.1 = (bf16[48,1280]{1,0:T(8,128)(2,1)S(1)}, bf16[48,1280]{1,0:T(8,128)(2,1)S(1)}, u32[]{:S(2)}, u32[]{:S(2)}) collective-permute-start(bf16[48,1280]{1,0:T(8,128)(2,1)S(1)} %pad_maximum_fusion.5), channel_id=1, source_target_pairs={{0,24},{1,25},{2,26},{3,27},{4,28},{5,29},{6,30},{7,31},{8,0},{9,1... | collective-permute-start | bytes 368648 | tf_op jit(solution)/shard_map/ppermute | solution.py:856
  20.8 16.8 %collective-permute-start.2 = (bf16[48,1280]{1,0:T(8,128)(2,1)S(1)}, bf16[48,1280]{1,0:T(8,128)(2,1)S(1)}, u32[]{:S(2)}, u32[]{:S(2)}) collective-permute-start(bf16[48,1280]{1,0:T(8,128)(2,1)S(1)} %pad_maximum_fusion.5), channel_id=1, source_target_pairs={{0,16},{1,17},{2,18},{3,19},{4,20},{5,21},{6,22},{7,23},{8,24},{9,... | collective-permute-start | bytes 368648 | tf_op jit(solution)/shard_map/ppermute | solution.py:856
  20.8 16.8 %collective-permute-start.3 = (bf16[48,1280]{1,0:T(8,128)(2,1)S(1)}, bf16[48,1280]{1,0:T(8,128)(2,1)S(1)}, u32[]{:S(2)}, u32[]{:S(2)}) collective-permute-start(bf16[48,1280]{1,0:T(8,128)(2,1)S(1)} %pad_maximum_fusion.5), channel_id=1, source_target_pairs={{0,8},{1,9},{2,10},{3,11},{4,12},{5,13},{6,14},{7,15},{8,16},{9,17... | collective-permute-start | bytes 368648 | tf_op jit(solution)/shard_map/ppermute | solution.py:856
  29.4 8.2 %collective-permute-start.4 = (bf16[24,1536]{1,0:T(8,128)(2,1)S(1)}, bf16[24,1536]{1,0:T(8,128)(2,1)S(1)}, u32[]{:S(2)}, u32[]{:S(2)}) collective-permute-start(bf16[24,1536]{1,0:T(8,128)(2,1)S(1)} %broadcast_select_fusion.6), channel_id=1, source_target_pairs={{0,1},{1,0},{2,3},{3,2},{4,5},{5,4},{6,7},{7,6},{8,9},{9,8},{10,11... | collective-permute-start | bytes 221192 | tf_op jit(solution)/shard_map/ppermute | solution.py:856
  37.5 48.8 %copy-start.11 = (s32[256]{0:T(256)}, s32[256]{0:T(256)S(1)}, u32[]{:S(2)}) copy-start(s32[256]{0:T(256)S(1)} %slice.276) | copy-start | bytes 3076
  37.7 36.7 %copy-start.7 = (bf16[4,48,1280]{2,1,0:T(8,128)(2,1)}, bf16[4,48,1280]{2,1,0:T(8,128)(2,1)S(1)}, u32[]{:S(2)}) copy-start(bf16[4,48,1280]{2,1,0:T(8,128)(2,1)S(1)} %pad_maximum_fusion.1.refs_0_) | copy-start | bytes 1474564
  37.7 28.1 %collective-permute-start.5 = (bf16[4,48,1280]{2,1,0:T(8,128)(2,1)S(1)}, bf16[4,48,1280]{2,1,0:T(8,128)(2,1)S(1)}, u32[]{:S(2)}, u32[]{:S(2)}) collective-permute-start(bf16[4,48,1280]{2,1,0:T(8,128)(2,1)S(1)} %pad_maximum_fusion.1.refs_0_), channel_id=1, source_target_pairs={{0,2},{1,3},{2,0},{3,1},{4,6},{5,7},{6,4},{7,5},{8,10},{9,11},{10,... | collective-permute-start | bytes 1474568 | tf_op jit(solution)/shard_map/ppermute | solution.py:856
  39.2 26.6 %collective-permute-start.6 = (bf16[4,48,1280]{2,1,0:T(8,128)(2,1)S(1)}, bf16[4,48,1280]{2,1,0:T(8,128)(2,1)S(1)}, u32[]{:S(2)}, u32[]{:S(2)}) collective-permute-start(bf16[4,48,1280]{2,1,0:T(8,128)(2,1)S(1)} %pad_maximum_fusion.1.refs_0_), channel_id=1, source_target_pairs={{0,4},{1,5},{2,6},{3,7},{4,0},{5,1},{6,2},{7,3},{8,12},{9,13},{10,... | collective-permute-start | bytes 1474568 | tf_op jit(solution)/shard_map/ppermute | solution.py:856
  40.8 27.4 %collective-permute-start.7 = (bf16[4,48,1280]{2,1,0:T(8,128)(2,1)S(1)}, bf16[4,48,1280]{2,1,0:T(8,128)(2,1)S(1)}, u32[]{:S(2)}, u32[]{:S(2)}) collective-permute-start(bf16[4,48,1280]{2,1,0:T(8,128)(2,1)S(1)} %pad_maximum_fusion.1.refs_0_), channel_id=1, source_target_pairs={{0,6},{1,7},{2,4},{3,5},{4,2},{5,3},{6,0},{7,1},{8,14},{9,15},{10,... | collective-permute-start | bytes 1474568 | tf_op jit(solution)/shard_map/ppermute | solution.py:856
  41.3 10.3 %collective-permute-start.10 = (bf16[48,1536]{1,0:T(8,128)(2,1)S(1)}, bf16[48,1536]{1,0:T(8,128)(2,1)S(1)}, u32[]{:S(2)}, u32[]{:S(2)}) collective-permute-start(bf16[48,1536]{1,0:T(8,128)(2,1)S(1)} %pad_maximum_fusion.4), channel_id=1, source_target_pairs={{0,8},{1,9},{2,10},{3,11},{4,12},{5,13},{6,14},{7,15},{8,16},{9,17... | collective-permute-start | bytes 442376 | tf_op jit(solution)/shard_map/ppermute | solution.py:856
  43.7 12.3 %collective-permute-start.8 = (bf16[48,1536]{1,0:T(8,128)(2,1)S(1)}, bf16[48,1536]{1,0:T(8,128)(2,1)S(1)}, u32[]{:S(2)}, u32[]{:S(2)}) collective-permute-start(bf16[48,1536]{1,0:T(8,128)(2,1)S(1)} %pad_maximum_fusion.4), channel_id=1, source_target_pairs={{0,24},{1,25},{2,26},{3,27},{4,28},{5,29},{6,30},{7,31},{8,0},{9,1... | collective-permute-start | bytes 442376 | tf_op jit(solution)/shard_map/ppermute | solution.py:856
  51.6 14.3 %collective-permute-start.9 = (bf16[48,1536]{1,0:T(8,128)(2,1)S(1)}, bf16[48,1536]{1,0:T(8,128)(2,1)S(1)}, u32[]{:S(2)}, u32[]{:S(2)}) collective-permute-start(bf16[48,1536]{1,0:T(8,128)(2,1)S(1)} %pad_maximum_fusion.4), channel_id=1, source_target_pairs={{0,16},{1,17},{2,18},{3,19},{4,20},{5,21},{6,22},{7,23},{8,24},{9,... | collective-permute-start | bytes 442376 | tf_op jit(solution)/shard_map/ppermute | solution.py:856
  68.2 2.0 collective-permute-start.11
  68.2 2.7 collective-permute-start.12
  68.7 3.6 %collective-permute-start.13 = (bf16[4,48,1280]{2,1,0:T(8,128)(2,1)S(1)}, bf16[4,48,1280]{2,1,0:T(8,128)(2,1)}, u32[]{:S(2)}, u32[]{:S(2)}) collective-permute-start(bf16[4,48,1280]{2,1,0:T(8,128)(2,1)S(1)} %collective-permute-done.6.refs_2_), channel_id=1, source_target_pairs={{0,1},{1,0},{2,3},{3,2},{4,5},{5,4},{6,7},{7,6},{8,9},{9,8},{10,11... | collective-permute-start | bytes 1474568 | tf_op jit(solution)/shard_map/ppermute | solution.py:856
  68.7 5.0 %collective-permute-start.14 = (bf16[4,48,1280]{2,1,0:T(8,128)(2,1)S(1)}, bf16[4,48,1280]{2,1,0:T(8,128)(2,1)}, u32[]{:S(2)}, u32[]{:S(2)}) collective-permute-start(bf16[4,48,1280]{2,1,0:T(8,128)(2,1)S(1)} %collective-permute-done.7.refs_3_), channel_id=1, source_target_pairs={{0,1},{1,0},{2,3},{3,2},{4,5},{5,4},{6,7},{7,6},{8,9},{9,8},{10,11... | collective-permute-start | bytes 1474568 | tf_op jit(solution)/shard_map/ppermute | solution.py:856
  70.1 16.3 %copy-start.5 = (bf16[4,48,1536]{2,1,0:T(8,128)(2,1)}, bf16[4,48,1536]{2,1,0:T(8,128)(2,1)S(1)}, u32[]{:S(2)}) copy-start(bf16[4,48,1536]{2,1,0:T(8,128)(2,1)S(1)} %pad_maximum_fusion.refs_0_) | copy-start | bytes 1769476
  73.7 22.1 %collective-permute-start.15 = (bf16[4,48,1536]{2,1,0:T(8,128)(2,1)S(1)}, bf16[4,48,1536]{2,1,0:T(8,128)(2,1)S(1)}, u32[]{:S(2)}, u32[]{:S(2)}) collective-permute-start(bf16[4,48,1536]{2,1,0:T(8,128)(2,1)S(1)} %pad_maximum_fusion.refs_0_), channel_id=1, source_target_pairs={{0,2},{1,3},{2,0},{3,1},{4,6},{5,7},{6,4},{7,5},{8,10},{9,11},{10,... | collective-permute-start | bytes 1769480 | tf_op jit(solution)/shard_map/ppermute | solution.py:856
  74.4 21.4 %collective-permute-start.16 = (bf16[4,48,1536]{2,1,0:T(8,128)(2,1)S(1)}, bf16[4,48,1536]{2,1,0:T(8,128)(2,1)S(1)}, u32[]{:S(2)}, u32[]{:S(2)}) collective-permute-start(bf16[4,48,1536]{2,1,0:T(8,128)(2,1)S(1)} %pad_maximum_fusion.refs_0_), channel_id=1, source_target_pairs={{0,4},{1,5},{2,6},{3,7},{4,0},{5,1},{6,2},{7,3},{8,12},{9,13},{10,... | collective-permute-start | bytes 1769480 | tf_op jit(solution)/shard_map/ppermute | solution.py:856
  74.4 38.8 %collective-permute-start.19 = (bf16[4,48,1536]{2,1,0:T(8,128)(2,1)S(1)}, bf16[4,48,1536]{2,1,0:T(8,128)(2,1)S(1)}, u32[]{:S(2)}, u32[]{:S(2)}) collective-permute-start(bf16[4,48,1536]{2,1,0:T(8,128)(2,1)S(1)} %pad_maximum_fusion.refs_0_), channel_id=1, source_target_pairs={{0,1},{1,0},{2,3},{3,2},{4,5},{5,4},{6,7},{7,6},{8,9},{9,8},{10,11... | collective-permute-start | bytes 1769480 | tf_op jit(solution)/shard_map/ppermute | solution.py:856
  95.8 17.5 %collective-permute-start.20 = (bf16[4,48,1536]{2,1,0:T(8,128)(2,1)S(1)}, bf16[4,48,1536]{2,1,0:T(8,128)(2,1)}, u32[]{:S(2)}, u32[]{:S(2)}) collective-permute-start(bf16[4,48,1536]{2,1,0:T(8,128)(2,1)S(1)} %collective-permute-done.15.refs_1_), channel_id=1, source_target_pairs={{0,1},{1,0},{2,3},{3,2},{4,5},{5,4},{6,7},{7,6},{8,9},{9,8},{10,11... | collective-permute-start | bytes 1769480 | tf_op jit(solution)/shard_map/ppermute | solution.py:856
  96.0 17.4 %collective-permute-start.21 = (bf16[4,48,1536]{2,1,0:T(8,128)(2,1)S(1)}, bf16[4,48,1536]{2,1,0:T(8,128)(2,1)}, u32[]{:S(2)}, u32[]{:S(2)}) collective-permute-start(bf16[4,48,1536]{2,1,0:T(8,128)(2,1)S(1)} %collective-permute-done.16.refs_2_), channel_id=1, source_target_pairs={{0,1},{1,0},{2,3},{3,2},{4,5},{5,4},{6,7},{7,6},{8,9},{9,8},{10,11... | collective-permute-start | bytes 1769480 | tf_op jit(solution)/shard_map/ppermute | solution.py:856
  96.5 16.8 %collective-permute-start.17 = (bf16[2,48,1536]{2,1,0:T(8,128)(2,1)S(1)}, bf16[2,48,1536]{2,1,0:T(8,128)(2,1)S(1)}, u32[]{:S(2)}, u32[]{:S(2)}) collective-permute-start(bf16[2,48,1536]{2,1,0:T(8,128)(2,1)S(1)} %slice.280), channel_id=1, source_target_pairs={{0,4},{1,5},{2,6},{3,7},{4,0},{5,1},{6,2},{7,3},{8,12},{9,13},{10,... | collective-permute-start | bytes 884744 | tf_op jit(solution)/shard_map/ppermute | solution.py:856
  98.0 15.4 %collective-permute-start.18 = (bf16[2,48,1536]{2,1,0:T(8,128)(2,1)S(1)}, bf16[2,48,1536]{2,1,0:T(8,128)(2,1)}, u32[]{:S(2)}, u32[]{:S(2)}) collective-permute-start(bf16[2,48,1536]{2,1,0:T(8,128)(2,1)S(1)} %slice.281), channel_id=1, source_target_pairs={{0,2},{1,3},{2,0},{3,1},{4,6},{5,7},{6,4},{7,5},{8,10},{9,11},{10,... | collective-permute-start | bytes 884744 | tf_op jit(solution)/shard_map/ppermute | solution.py:856
  113.3 1.6 collective-permute-start.22
  113.4 2.2 collective-permute-start.23
  162.9 16.7 %collective-permute-start.24 = (bf16[4,4,48,1536]{3,2,1,0:T(8,128)(2,1)}, bf16[4,4,48,1536]{3,2,1,0:T(8,128)(2,1)S(1)}, u32[]{:S(2)}, u32[]{:S(2)}) collective-permute-start(bf16[4,4,48,1536]{3,2,1,0:T(8,128)(2,1)} %get-tuple-element.180), channel_id=1, source_target_pairs={{0,1},{1,0},{2,3},{3,2},{4,5},{5,4},{6,7},{7,6},{8,9},{9,8},{10,11... | collective-permute-start | bytes 7077896 | tf_op jit(solution)/shard_map/ppermute | solution.py:856
  167.9 11.8 %copy-start.1 = (bf16[4,4,48,1536]{3,2,1,0:T(8,128)(2,1)S(1)}, bf16[4,4,48,1536]{3,2,1,0:T(8,128)(2,1)}, u32[]{:S(2)}) copy-start(bf16[4,4,48,1536]{3,2,1,0:T(8,128)(2,1)} %get-tuple-element.184) | copy-start | bytes 7077892
  181.4 41.7 %collective-permute-start.25 = (bf16[4,48,1536]{2,1,0:T(8,128)(2,1)}, bf16[4,48,1536]{2,1,0:T(8,128)(2,1)S(1)}, u32[]{:S(2)}, u32[]{:S(2)}) collective-permute-start(bf16[4,48,1536]{2,1,0:T(8,128)(2,1)} %get-tuple-element.201), channel_id=1, source_target_pairs={{0,2},{1,3},{2,0},{3,1},{4,6},{5,7},{6,4},{7,5},{8,10},{9,11},{10,... | collective-permute-start | bytes 1769480 | tf_op jit(solution)/shard_map/ppermute | solution.py:856
  182.9 40.2 %collective-permute-start.26 = (bf16[4,48,1536]{2,1,0:T(8,128)(2,1)}, bf16[4,48,1536]{2,1,0:T(8,128)(2,1)S(1)}, u32[]{:S(2)}, u32[]{:S(2)}) collective-permute-start(bf16[4,48,1536]{2,1,0:T(8,128)(2,1)} %get-tuple-element.202), channel_id=1, source_target_pairs={{0,4},{1,5},{2,6},{3,7},{4,0},{5,1},{6,2},{7,3},{8,12},{9,13},{10,... | collective-permute-start | bytes 1769480 | tf_op jit(solution)/shard_map/ppermute | solution.py:856
  183.4 39.8 %collective-permute-start.27 = (bf16[4,48,1536]{2,1,0:T(8,128)(2,1)S(1)}, bf16[4,48,1536]{2,1,0:T(8,128)(2,1)S(1)}, u32[]{:S(2)}, u32[]{:S(2)}) collective-permute-start(bf16[4,48,1536]{2,1,0:T(8,128)(2,1)S(1)} %get-tuple-element.203), channel_id=1, source_target_pairs={{0,6},{1,7},{2,4},{3,5},{4,2},{5,3},{6,0},{7,1},{8,14},{9,15},{10,... | collective-permute-start | bytes 1769480 | tf_op jit(solution)/shard_map/ppermute | solution.py:856
  223.1 5.1 %collective-permute-start.28 = (bf16[4,4,48,1664]{3,2,1,0:T(8,128)(2,1)}, bf16[4,4,48,1664]{3,2,1,0:T(8,128)(2,1)S(1)}, u32[]{:S(2)}, u32[]{:S(2)}) collective-permute-start(bf16[4,4,48,1664]{3,2,1,0:T(8,128)(2,1)} %get-tuple-element.206), channel_id=1, source_target_pairs={{0,1},{1,0},{2,3},{3,2},{4,5},{5,4},{6,7},{7,6},{8,9},{9,8},{10,11... | collective-permute-start | bytes 7667720 | tf_op jit(solution)/shard_map/ppermute | solution.py:856
  228.2 13.3 %copy-start.4 = (bf16[1024,768]{1,0:T(8,128)(2,1)S(1)}, bf16[1024,768]{1,0:T(8,128)(2,1)}, u32[]{:S(2)}) copy-start(bf16[1024,768]{1,0:T(8,128)(2,1)} %get-tuple-element.217) | copy-start | bytes 4718596
  228.8 21.3 %collective-permute-start.29 = (bf16[4,48,1664]{2,1,0:T(8,128)(2,1)S(1)}, bf16[4,48,1664]{2,1,0:T(8,128)(2,1)S(1)}, u32[]{:S(2)}, u32[]{:S(2)}) collective-permute-start(bf16[4,48,1664]{2,1,0:T(8,128)(2,1)S(1)} %get-tuple-element.237), channel_id=1, source_target_pairs={{0,2},{1,3},{2,0},{3,1},{4,6},{5,7},{6,4},{7,5},{8,10},{9,11},{10,... | collective-permute-start | bytes 1916936 | tf_op jit(solution)/shard_map/ppermute | solution.py:856
  230.4 34.0 %collective-permute-start.30 = (bf16[4,48,1664]{2,1,0:T(8,128)(2,1)S(1)}, bf16[4,48,1664]{2,1,0:T(8,128)(2,1)S(1)}, u32[]{:S(2)}, u32[]{:S(2)}) collective-permute-start(bf16[4,48,1664]{2,1,0:T(8,128)(2,1)S(1)} %get-tuple-element.236), channel_id=1, source_target_pairs={{0,4},{1,5},{2,6},{3,7},{4,0},{5,1},{6,2},{7,3},{8,12},{9,13},{10,... | collective-permute-start | bytes 1916936 | tf_op jit(solution)/shard_map/ppermute | solution.py:856
  230.9 33.6 %collective-permute-start.31 = (bf16[4,48,1664]{2,1,0:T(8,128)(2,1)S(1)}, bf16[4,48,1664]{2,1,0:T(8,128)(2,1)S(1)}, u32[]{:S(2)}, u32[]{:S(2)}) collective-permute-start(bf16[4,48,1664]{2,1,0:T(8,128)(2,1)S(1)} %get-tuple-element.235), channel_id=1, source_target_pairs={{0,6},{1,7},{2,4},{3,5},{4,2},{5,3},{6,0},{7,1},{8,14},{9,15},{10,... | collective-permute-start | bytes 1916936 | tf_op jit(solution)/shard_map/ppermute | solution.py:856
  232.4 8.8 %collective-permute-start.32 = (bf16[48,1536]{1,0:T(8,128)(2,1)S(1)}, bf16[48,1536]{1,0:T(8,128)(2,1)S(1)}, u32[]{:S(2)}, u32[]{:S(2)}) collective-permute-start(bf16[48,1536]{1,0:T(8,128)(2,1)S(1)} %get-tuple-element.214), channel_id=1, source_target_pairs={{0,8},{1,9},{2,10},{3,11},{4,12},{5,13},{6,14},{7,15},{8,16},{9,17... | collective-permute-start | bytes 442376 | tf_op jit(solution)/shard_map/ppermute | solution.py:856
  235.2 13.2 %collective-permute-start.33 = (bf16[48,1536]{1,0:T(8,128)(2,1)S(1)}, bf16[48,1536]{1,0:T(8,128)(2,1)S(1)}, u32[]{:S(2)}, u32[]{:S(2)}) collective-permute-start(bf16[48,1536]{1,0:T(8,128)(2,1)S(1)} %get-tuple-element.215), channel_id=1, source_target_pairs={{0,16},{1,17},{2,18},{3,19},{4,20},{5,21},{6,22},{7,23},{8,24},{9,... | collective-permute-start | bytes 442376 | tf_op jit(solution)/shard_map/ppermute | solution.py:856
  241.2 8.9 %collective-permute-start.34 = (bf16[48,1536]{1,0:T(8,128)(2,1)S(1)}, bf16[48,1536]{1,0:T(8,128)(2,1)S(1)}, u32[]{:S(2)}, u32[]{:S(2)}) collective-permute-start(bf16[48,1536]{1,0:T(8,128)(2,1)S(1)} %get-tuple-element.216), channel_id=1, source_target_pairs={{0,24},{1,25},{2,26},{3,27},{4,28},{5,29},{6,30},{7,31},{8,0},{9,1... | collective-permute-start | bytes 442376 | tf_op jit(solution)/shard_map/ppermute | solution.py:856
  264.6 5.9 %collective-permute-start.38 = (f32[24,1536]{1,0:T(8,128)S(1)}, f32[24,1536]{1,0:T(8,128)S(1)}, u32[]{:S(2)}, u32[]{:S(2)}) collective-permute-start(f32[24,1536]{1,0:T(8,128)S(1)} %slice_select_fusion.2), channel_id=1, source_target_pairs={{0,1},{1,0},{2,3},{3,2},{4,5},{5,4},{6,7},{7,6},{8,9},{9,8},{10,11... | collective-permute-start | bytes 442376 | tf_op jit(solution)/shard_map/ppermute | solution.py:856
  265.0 30.8 %collective-permute-start.35 = (bf16[48,1664]{1,0:T(8,128)(2,1)S(1)}, bf16[48,1664]{1,0:T(8,128)(2,1)S(1)}, u32[]{:S(2)}, u32[]{:S(2)}) collective-permute-start(bf16[48,1664]{1,0:T(8,128)(2,1)S(1)} %get-tuple-element.244), channel_id=1, source_target_pairs={{0,8},{1,9},{2,10},{3,11},{4,12},{5,13},{6,14},{7,15},{8,16},{9,17... | collective-permute-start | bytes 479240 | tf_op jit(solution)/shard_map/ppermute | solution.py:856
  267.8 27.9 %collective-permute-start.36 = (bf16[48,1664]{1,0:T(8,128)(2,1)S(1)}, bf16[48,1664]{1,0:T(8,128)(2,1)S(1)}, u32[]{:S(2)}, u32[]{:S(2)}) collective-permute-start(bf16[48,1664]{1,0:T(8,128)(2,1)S(1)} %get-tuple-element.243), channel_id=1, source_target_pairs={{0,16},{1,17},{2,18},{3,19},{4,20},{5,21},{6,22},{7,23},{8,24},{9,... | collective-permute-start | bytes 479240 | tf_op jit(solution)/shard_map/ppermute | solution.py:856
  268.9 26.9 %collective-permute-start.37 = (bf16[48,1664]{1,0:T(8,128)(2,1)S(1)}, bf16[48,1664]{1,0:T(8,128)(2,1)S(1)}, u32[]{:S(2)}, u32[]{:S(2)}) collective-permute-start(bf16[48,1664]{1,0:T(8,128)(2,1)S(1)} %get-tuple-element.242), channel_id=1, source_target_pairs={{0,24},{1,25},{2,26},{3,27},{4,28},{5,29},{6,30},{7,31},{8,0},{9,1... | collective-permute-start | bytes 479240 | tf_op jit(solution)/shard_map/ppermute | solution.py:856
  295.9 1.5 collective-permute-start.39
  (13 other events, 61.8 us)
Sparse Core Ops, SparseCore 0:
  11.5 89.4 all-gather.1
  163.9 130.1 reduce-scatter.1

commit v5 on v4

--- a/solution.py
+++ b/solution.py
@@ -3,6 +3,7 @@
 
 import jax
 import jax.numpy as jnp
+import numpy as np
 from jax import lax
 from jax.experimental import pallas as pl
 from jax.experimental.pallas import tpu as pltpu
@@ -272,9 +273,10 @@
     return total.astype(BF)
 
 
-def cut_kernel(where_ref, w_ref, t_ref, keep_ref, give_ref):
+def cut_kernel(where_ref, w_ref, p_ref, t_ref, keep_ref, give_ref):
     ci = where_ref[3]
     pairs = w_ref.shape[1] // 384
+    half = p_ref.shape[1] // 2
     for h in range(2):
         for other, out in ((False, keep_ref), (True, give_ref)):
 
@@ -286,45 +288,76 @@
                         first = (t * pairs + p) * 128
                         out[:, at : at + 128] = w_ref[:, first : first + 128]
                         at += 128
-                out[:, at:] = t_ref[...]
-
-
-def cut_call(where, w_qkv, table):
+                out[:, at : at + half] = p_ref[:, h * half : (h + 1) * half]
+                out[:, at + half :] = t_ref[...]
+
+
+def cut_call(where, w_qkv, w_proj, table):
     r = w_qkv.shape[0]
-    cols = w_qkv.shape[1] // 2 + 128
+    cols = (w_qkv.shape[1] + w_proj.shape[1]) // 2 + 128
+    shapes = [full_spec(v.shape) for v in (w_qkv, w_proj, table)]
     return pl.pallas_call(
         cut_kernel,
         grid=(1,),
-        in_specs=[SMEM, full_spec(w_qkv.shape), full_spec(table.shape)],
+        in_specs=[SMEM] + shapes,
         out_specs=[full_spec((r, cols))] * 2,
         out_shape=[jax.ShapeDtypeStruct((r, cols), BF)] * 2,
         compiler_params=params(),
         cost_estimate=cost(0, 4 * r * cols),
         name="cut",
-    )(where, w_qkv, table)
-
-
-def qkv_kernel(dims, count, devices, where_ref, x_ref, *refs):
+    )(where, w_qkv, w_proj, table)
+
+
+def first_norm_kernel(dims, count, devices, where_ref, x_ref, *refs):
+    own = refs[:count]
+    n_ref, nt_ref, vec_ref, t_scr, t_sem = refs[count:]
+    rows, d = x_ref.shape
+    table_at = own[0].shape[-1] - 128
+    for i, j, z, y, x in chips_of(dims, where_ref):
+        block = piece_at(dims, own, i, j).at[:, pl.ds(table_at, 128)]
+        local_copy(block, t_scr.at[z, y, x], t_sem.at[z, y, x]).start()
+    for z in range(dims[0]):
+        for y in range(dims[1]):
+            for x in range(dims[2]):
+                block = t_scr.at[z, y, x]
+                local_copy(block, block, t_sem.at[z, y, x]).wait()
+    vec_ref[...] = jnp.zeros_like(vec_ref)
+    unpack_vectors(flat2(t_scr[...]), d, devices, vec_ref)
+    for r in range(0, rows, 256):
+        xhat, _ = normalize(x_ref[r : r + 256, :].astype(F32))
+        normed = (xhat * vec_ref[0:1, :d] + vec_ref[1:2, :d]).astype(BF)
+        n_ref[r : r + 256, :] = normed
+        nt_ref[:, r : r + 256] = normed.T
+
+
+def first_norm_call(dims, where, x, own, devices):
+    rows, d = x.shape
+    return pl.pallas_call(
+        functools.partial(first_norm_kernel, dims, len(own), devices),
+        grid=(1,),
+        in_specs=[SMEM, full_spec((rows, d))] + [ANY] * len(own),
+        out_specs=[full_spec((rows, d)), full_spec((d, rows)), full_spec((8, 4 * d))],
+        out_shape=[
+            jax.ShapeDtypeStruct((rows, d), BF), jax.ShapeDtypeStruct((d, rows), BF),
+            jax.ShapeDtypeStruct((8, 4 * d), F32),
+        ],
+        scratch_shapes=[pltpu.VMEM(dims + (own[0].shape[1], 128), BF), pltpu.SemaphoreType.DMA(dims)],
+        compiler_params=params(),
+        cost_estimate=cost(1e9, rows * d * 6),
+        name="first_norm",
+    )(where, x, *own)
+
+
+def qkv_kernel(dims, count, where_ref, n_ref, vec_ref, *refs):
     own, oth = refs[:count], refs[count : 2 * count]
-    o_ref, vec_ref, w_scr, w_sem, t_scr, t_sem, n_scr, bias_scr = refs[2 * count :]
-    rows, d = x_ref.shape
+    o_ref, w_scr, w_sem, bias_scr = refs[2 * count :]
+    rows, d = n_ref.shape
     cols = w_scr.shape[-1]
-    table_at = own[0].shape[-1] - 128
     step = pl.program_id(0)
 
     @pl.when(step == 0)
     def _():
-        for i, j, z, y, x in chips_of(dims, where_ref):
-            block = piece_at(dims, own, i, j).at[:, pl.ds(table_at, 128)]
-            local_copy(block, t_scr.at[z, y, x], t_sem.at[z, y, x]).start()
         load_columns(dims, where_ref, own, oth, 0, cols, w_scr, w_sem)
-        for z in range(dims[0]):
-            for y in range(dims[1]):
-                for x in range(dims[2]):
-                    block = t_scr.at[z, y, x]
-                    local_copy(block, block, t_sem.at[z, y, x]).wait()
-        vec_ref[...] = jnp.zeros_like(vec_ref)
-        unpack_vectors(flat2(t_scr[...]), d, devices, vec_ref)
         zero = jnp.zeros((1, 128), F32)
         pairs = d // 128
         for p in range(pairs):
@@ -333,9 +366,6 @@
             bias_scr[half, :, at : at + 128] = vec_ref[2:3, p * 128 : (p + 1) * 128]
             bias_scr[half, :, at + 128 : at + 256] = zero
             bias_scr[half, :, at + 256 : at + 384] = vec_ref[2:3, d + p * 128 : d + (p + 1) * 128]
-        for r in range(0, rows, 256):
-            xhat, _ = normalize(x_ref[r : r + 256, :].astype(F32))
-            n_scr[r : r + 256, :] = (xhat * vec_ref[0:1, :d] + vec_ref[1:2, :d]).astype(BF)
         wait_columns(dims, w_scr, w_sem, 0)
 
     @pl.when(step == 1)
@@ -344,74 +374,93 @@
 
     w = flat2(w_scr[step])
     for r in range(0, rows, 256):
-        o_ref[r : r + 256, :] = (dot(n_scr[r : r + 256, :], w) + bias_scr[step]).astype(BF)
-
-
-def qkv_call(dims, where, x, own, oth, devices):
-    rows, d = x.shape
+        o_ref[r : r + 256, :] = (dot(n_ref[r : r + 256, :], w) + bias_scr[step]).astype(BF)
+
+
+def qkv_call(dims, where, normed, vec, own, oth):
+    rows, d = normed.shape
     n = own[0].shape[1]
     cols = 3 * d // 2
     return pl.pallas_call(
-        functools.partial(qkv_kernel, dims, len(own), devices),
+        functools.partial(qkv_kernel, dims, len(own)),
         grid=(2,),
-        in_specs=[SMEM, full_spec((rows, d))] + [ANY] * (2 * len(own)),
-        out_specs=[pl.BlockSpec((rows, cols), lambda j: (0, j)), full_spec((8, 4 * d))],
-        out_shape=[
-            jax.ShapeDtypeStruct((rows, 2 * cols), BF), jax.ShapeDtypeStruct((8, 4 * d), F32)
-        ],
-        scratch_shapes=weight_scratch(dims, n, cols)
-        + [
-            pltpu.VMEM(dims + (n, 128), BF), pltpu.SemaphoreType.DMA(dims),
-            pltpu.VMEM((rows, d), BF), pltpu.VMEM((2, 1, cols), F32),
-        ],
+        in_specs=[SMEM, full_spec((rows, d)), full_spec(vec.shape)] + [ANY] * (2 * len(own)),
+        out_specs=pl.BlockSpec((rows, cols), lambda j: (0, j)),
+        out_shape=jax.ShapeDtypeStruct((rows, 2 * cols), BF),
+        scratch_shapes=weight_scratch(dims, n, cols) + [pltpu.VMEM((2, 1, cols), F32)],
         compiler_params=params(),
         cost_estimate=cost(4 * rows * d * cols, rows * d * 8 + d * cols * 4),
         name="qkv",
-    )(where, x, *own, *oth)
-
-
-def proj_kernel(x_ref, a0_ref, a1_ref, vec_ref, w_ref, mid_ref, n_ref):
+    )(where, normed, vec, *own, *oth)
+
+
+def proj_kernel(dims, count, first, where_ref, x_ref, a0_ref, a1_ref, vec_ref, *refs):
+    own, oth = refs[:count], refs[count : 2 * count]
+    mid_ref, n_ref, w_scr, w_sem = refs[2 * count :]
     d = x_ref.shape[1]
+
+    @pl.when(pl.program_id(0) == 0)
+    def _():
+        load_columns(dims, where_ref, own, oth, first, w_scr.shape[-1], w_scr, w_sem)
+        for h in range(2):
+            wait_columns(dims, w_scr, w_sem, h)
+
     a = jnp.concatenate([a0_ref[...], a1_ref[...]], axis=1)
-    branch = dot(a, w_ref[...]) + vec_ref[3:4, :d]
+    branch = jnp.concatenate([dot(a, flat2(w_scr[h])) for h in range(2)], axis=1) + vec_ref[3:4, :d]
     middle = x_ref[...].astype(F32) + BS * branch
     mid_ref[...] = middle
     xhat, _ = normalize(middle)
     n_ref[...] = (xhat * vec_ref[4:5, :d] + vec_ref[5:6, :d]).astype(BF)
 
 
-def proj_call(x, att, vec, w):
+def proj_call(dims, where, x, att, vec, own, oth):
     rows, d = x.shape
     br = 256
     row = pl.BlockSpec((br, d), lambda i: (i, 0))
     return pl.pallas_call(
-        proj_kernel,
+        functools.partial(proj_kernel, dims, len(own), 3 * d // 2),
         grid=(rows // br,),
-        in_specs=[row] + [pl.BlockSpec((br, v.shape[1]), lambda i: (i, 0)) for v in att]
-        + [full_spec(vec.shape), full_spec((d, d))],
+        in_specs=[SMEM, row] + [pl.BlockSpec((br, v.shape[1]), lambda i: (i, 0)) for v in att]
+        + [full_spec(vec.shape)] + [ANY] * (2 * len(own)),
         out_specs=[row, row],
         out_shape=[jax.ShapeDtypeStruct((rows, d), F32), jax.ShapeDtypeStruct((rows, d), BF)],
+        scratch_shapes=weight_scratch(dims, own[0].shape[1], d // 2),
         compiler_params=params(),
         cost_estimate=cost(2 * rows * d * d, rows * d * 10 + d * d * 2),
         name="proj",
-    )(x, *att, vec, w)
-
-
-def mlp_kernel(dims, count, take, where_ref, n_ref, c_ref, mid_ref, vec_ref, wo_ref, *refs):
+    )(where, x, *att, vec, *own, *oth)
+
+
+def mlp_kernel(dims, count, where_ref, n_ref, c_ref, mid_ref, vec_ref, *refs):
     own, oth = refs[:count], refs[count : 2 * count]
     (
-        out_ref, gn_ref, gfb_ref, gob_ref, go_ref, g_own, g_oth,
-        nt_scr, mg_scr, acc_scr, act_scr, gp_scr, f_scr, f_sem, gf_scr, gf_sem,
+        out_ref, gn_ref, gfb_ref, gob_ref, g_own, g_oth,
+        mid_scr, mid_sem, nt_scr, mg_scr, acc_scr, act_scr, gp_scr, f_scr, f_sem, o_scr, o_sem, gf_scr, gf_sem, go_scr, go_sem,
     ) = refs[2 * count :]
+    z_n, y_n, x_n = dims
+    zi, yi, xi, ci = [where_ref[i] for i in range(4)]
     j = pl.program_id(0)
+    blocks = o_scr.shape[0]
     rows, d = n_ref.shape
+    n = own[0].shape[1]
     wide = f_scr.shape[-1]
-    blocks = 2 * wide // d
+    parts = d // n
     br = 512
 
     @pl.when(j == 0)
     def _():
         load_columns(dims, where_ref, own, oth, 0, wide, f_scr, f_sem)
+        for i, s, z, y, x in chips_of(dims, where_ref):
+            for core, src in ((ci, own), (1 - ci, oth)):
+                for t in range(2):
+                    at = (((z * y_n + y) * x_n + x) * 2 + core) * 2 + t
+                    q = lax.rem(at, parts)
+                    local_copy(
+                        piece_at(dims, src, i, s).at[:, pl.ds(wide + t * d, d)],
+                        o_scr.at[at // parts, pl.ds(pl.multiple_of(q * n, 16), n), :],
+                        o_sem.at[at // parts, q],
+                    ).start()
+        local_copy(mid_ref, mid_scr, mid_sem).start()
         nt_scr[...] = n_ref[...].T
         total = jnp.zeros_like(gob_ref)
         for r in range(0, rows, br):
@@ -425,10 +474,14 @@
     def _():
         wait_columns(dims, f_scr, f_sem, 1)
 
+    for q in range(parts):
+        part = o_scr.at[j, pl.ds(q * n, n), :]
+        local_copy(part, part, o_sem.at[j, q]).wait()
+
     half = j // (blocks // 2)
     first = pl.multiple_of(lax.rem(j, blocks // 2) * d, 128)
     wf = flat2(f_scr[half, :, :, :, :, pl.ds(first, d)])
-    wo = wo_ref[:, :take, :].reshape(d, d)
+    wo = o_scr[j]
     fb = vec_ref[6:7, pl.ds(pl.multiple_of(j * d, 128), d)]
     bias_sum = jnp.zeros((1, d), F32)
     starts = list(range(0, rows, br))
@@ -468,66 +521,90 @@
     gfb_ref[...] = bias_sum
     gf_scr[j] = dot(nt_scr[...], gp_scr[...]).astype(BF).reshape(gf_scr.shape[1:])
     store_columns(dims, where_ref, gf_scr.at[j], g_own, g_oth, half, first, d, gf_sem.at[j])
-    go_ref[...] = dot_0(act_scr[...], mg_scr[...]).astype(BF)
+    go_scr[j] = dot_0(act_scr[...], mg_scr[...]).astype(BF)
+    for q in range(parts):
+        at = j * parts + q
+        dev, t = at // 2, lax.rem(at, 2)
+        core = lax.rem(dev, 2)
+        x = lax.rem(dev // 2, x_n)
+        y = lax.rem(dev // (2 * x_n), y_n)
+        z = dev // (2 * x_n * y_n)
+        piece = lax.rem(y - yi + y_n, y_n) * x_n + lax.rem(x - xi + x_n, x_n)
+        slot = lax.rem(z - zi + z_n, z_n)
+        to = pl.ds(pl.multiple_of(wide + t * d, 128), d)
+        for other, out in ((False, g_own), (True, g_oth)):
+
+            @pl.when((core != ci) if other else (core == ci))
+            def _():
+                local_copy(go_scr.at[j, pl.ds(q * n, n), :], out.at[piece, slot, :, to], go_sem.at[j, q]).start()
 
     @pl.when(j == blocks - 1)
     def _():
+        local_copy(mid_ref, mid_scr, mid_sem).wait()
         for r in range(0, rows, br):
             rr = slice(r, r + br)
-            out_ref[rr, :] = (mid_ref[rr, :] + BS * (acc_scr[rr, :] + vec_ref[7:8, :d])).astype(BF)
+            out_ref[rr, :] = (mid_scr[rr, :] + BS * (acc_scr[rr, :] + vec_ref[7:8, :d])).astype(BF)
         for b in range(blocks):
             wait_store(dims, gf_scr.at[b], g_own, 0, d, gf_sem.at[b])
-
-
-def mlp_call(dims, where, normed, cot, middle, vec, w_out, take, own, oth):
+            for q in range(parts):
+                part = go_scr.at[b, pl.ds(q * n, n), :]
+                local_copy(part, part, go_sem.at[b, q]).wait()
+
+
+def mlp_call(dims, where, normed, cot, middle, vec, own, oth):
     rows, d = normed.shape
-    n, wide = own[0].shape[1:]
+    n, cols = own[0].shape[1:]
+    wide = cols - 2 * d
     blocks = 2 * wide // d
     count = dims[1] * dims[2]
     act = full_spec((rows, d))
-    piece = jax.ShapeDtypeStruct((count, dims[0], n, wide), BF)
-    block = pl.BlockSpec((d, d), lambda j: (j, 0))
-    whole = pl.BlockSpec((d // take,) + w_out.shape[1:], lambda j: (j, 0, 0))
+    piece = jax.ShapeDtypeStruct((count, dims[0], n, cols), BF)
     return pl.pallas_call(
-        functools.partial(mlp_kernel, dims, len(own), take),
+        functools.partial(mlp_kernel, dims, len(own)),
         grid=(blocks,),
-        in_specs=[SMEM, act, act, act, full_spec(vec.shape), whole] + [ANY] * (2 * len(own)),
-        out_specs=[act, act, pl.BlockSpec((1, d), lambda j: (0, j)), full_spec((1, d)), block] + [ANY] * 2,
+        in_specs=[SMEM, act, act, ANY, full_spec(vec.shape)] + [ANY] * (2 * len(own)),
+        out_specs=[act, act, pl.BlockSpec((1, d), lambda j: (0, j)), full_spec((1, d))] + [ANY] * 2,
         out_shape=[
             jax.ShapeDtypeStruct((rows, d), BF),
             jax.ShapeDtypeStruct((rows, d), F32),
             jax.ShapeDtypeStruct((1, blocks * d), F32),
             jax.ShapeDtypeStruct((1, d), F32),
-            jax.ShapeDtypeStruct((blocks * d, d), BF),
             piece, piece,
         ],
         scratch_shapes=[
-            pltpu.VMEM((d, rows), BF), pltpu.VMEM((rows, d), BF), pltpu.VMEM((rows, d), F32),
+            pltpu.VMEM((rows, d), F32), pltpu.SemaphoreType.DMA(()), pltpu.VMEM((d, rows), BF), pltpu.VMEM((rows, d), BF), pltpu.VMEM((rows, d), F32),
             pltpu.VMEM((rows, d), BF), pltpu.VMEM((rows, d), BF),
         ]
         + weight_scratch(dims, n, wide)
         + [
+            pltpu.VMEM((blocks, d, d), BF), pltpu.SemaphoreType.DMA((blocks, d // n)),
             pltpu.VMEM((blocks,) + dims + (n, d), BF), pltpu.SemaphoreType.DMA((blocks, count, dims[0])),
+            pltpu.VMEM((blocks, d, d), BF), pltpu.SemaphoreType.DMA((blocks, d // n)),
         ],
         compiler_params=params(),
         cost_estimate=cost(24 * rows * d * wide, 30e6, 2 * rows * wide),
         name="mlp",
-    )(where, normed, cot, middle, vec, w_out, *own, *oth)
-
-
-def proj_back_kernel(
-    gn_ref, mid_ref, c_ref, a0_ref, a1_ref, vec_ref, ind_ref, w_ref,
-    gm_ref, ga_ref, gw_ref, del_ref, gg_ref, gb_ref, gpb_ref, gw_acc,
-):
+    )(where, normed, cot, middle, vec, *own, *oth)
+
+
+def proj_back_kernel(dims, count, first, where_ref, gn_ref, mid_ref, c_ref, a0_ref, a1_ref, vec_ref, ind_ref, *refs):
+    own, oth = refs[:count], refs[count : 2 * count]
+    (
+        gm_ref, ga_ref, gw_ref, del_ref, gg_ref, gb_ref, gpb_ref, gw_acc, w_scr, w_sem,
+    ) = refs[2 * count :]
     i = pl.program_id(0)
     d = mid_ref.shape[1]
+    m = d // 2
 
     @pl.when(i == 0)
     def _():
+        load_columns(dims, where_ref, own, oth, first, m, w_scr, w_sem)
         gw_acc[...] = jnp.zeros_like(gw_acc)
         gg_ref[...] = jnp.zeros_like(gg_ref)
         gb_ref[...] = jnp.zeros_like(gb_ref)
         gpb_ref[...] = jnp.zeros_like(gpb_ref)
+        for h in range(2):
+            wait_columns(dims, w_scr, w_sem, h)
 
     dy = gn_ref[...]
     xhat, rstd = normalize(mid_ref[...])
@@ -539,7 +616,7 @@
     gpb_ref[...] += jnp.sum(pg.astype(F32), axis=0, keepdims=True)
     a = jnp.concatenate([a0_ref[...], a1_ref[...]], axis=1)
     gw_acc[...] += dot_0(a, pg)
-    ga = dot_t(pg, w_ref[...]).astype(BF)
+    ga = (dot_t(pg[:, :m], flat2(w_scr[0])) + dot_t(pg[:, m:], flat2(w_scr[1]))).astype(BF)
     ga_ref[...] = ga
     prod = ga.astype(F32) * a.astype(F32)
     high = prod.astype(BF)
@@ -551,18 +628,18 @@
         gw_ref[...] = gw_acc[...].astype(BF)
 
 
-def proj_back_call(gn, middle, cot, att, vec, w):
+def proj_back_call(dims, where, gn, middle, cot, att, vec, own, oth):
     rows, d = middle.shape
     br = 256
     row = pl.BlockSpec((br, d), lambda i: (i, 0))
-    ind = (jnp.arange(16)[:, None] == jnp.arange(d)[None, :] // HD).astype(BF)
+    ind = jnp.asarray(np.arange(16)[:, None] == np.arange(d)[None, :] // HD, BF)
     one = full_spec((1, d))
     vshape = jax.ShapeDtypeStruct((1, d), F32)
     return pl.pallas_call(
-        proj_back_kernel,
+        functools.partial(proj_back_kernel, dims, len(own), 3 * d // 2),
         grid=(rows // br,),
-        in_specs=[row, row, row] + [pl.BlockSpec((br, v.shape[1]), lambda i: (i, 0)) for v in att]
-        + [full_spec(vec.shape), full_spec((16, d)), full_spec((d, d))],
+        in_specs=[SMEM, row, row, row] + [pl.BlockSpec((br, v.shape[1]), lambda i: (i, 0)) for v in att]
+        + [full_spec(vec.shape), full_spec((16, d))] + [ANY] * (2 * len(own)),
         out_specs=[row, row, full_spec((d, d)), pl.BlockSpec((16, br), lambda i: (0, i)), one, one, one],
         out_shape=[
             jax.ShapeDtypeStruct((rows, d), F32),
@@ -571,11 +648,11 @@
             jax.ShapeDtypeStruct((16, rows), F32),
             vshape, vshape, vshape,
         ],
-        scratch_shapes=[pltpu.VMEM((d, d), F32)],
+        scratch_shapes=[pltpu.VMEM((d, d), F32)] + weight_scratch(dims, own[0].shape[1], d // 2),
         compiler_params=params(),
         cost_estimate=cost(4 * rows * d * d, rows * d * 16),
         name="proj_back",
-    )(gn, middle, cot, *att, vec, ind, w)
+    )(where, gn, middle, cot, *att, vec, ind, *own, *oth)
 
 
 def pair_back(j_ref, do_ref, lse_ref, del_ref, row, segr_ref, segc_ref, pair, dj_ref, dk_acc, dv_acc):
@@ -641,12 +718,12 @@
 
 def attn_back_kernel(
     dims, count, devices, where_ref, j0_ref, j1_ref, do_ref, lse_ref, del_ref, segr_ref, segc_ref,
-    x_ref, vec_ref, gwp_ref, gfb_ref, gob_ref, gg2_ref, gb2_ref, gpb_ref, gm_ref, *refs,
+    x_ref, vec_ref, gwp_ref, gfb_ref, gob_ref, gg2_ref, gb2_ref, gpb_ref, gm_ref, nt_ref, *refs,
 ):
     own, oth, refs = refs[:count], refs[count : 2 * count], refs[2 * count :]
     gx_ref, g_own, g_oth = refs[:3]
     (
-        w_scr, w_sem, nt_scr, gn_scr, gm_scr, gm_sem, dj_scr, dk_acc, dv_acc, gw_scr, gw_sem,
+        w_scr, w_sem, nt_scr, nt_sem, gn_scr, gm_scr, gm_sem, dj_scr, dk_acc, dv_acc, gw_scr, gw_sem,
         p_scr, p_sem, t_scr, t_sem, qv_scr,
     ) = refs[3:]
     i = pl.program_id(0)
@@ -659,13 +736,11 @@
     @pl.when(i == 0)
     def _():
         load_columns(dims, where_ref, own, oth, 0, groups * 384, w_scr, w_sem)
+        local_copy(nt_ref, nt_scr, nt_sem).start()
         local_copy(gm_ref, gm_scr, gm_sem).start()
         for h in range(2):
             p_scr[h] = gwp_ref[:, h * (d // 2) : (h + 1) * (d // 2)].reshape(p_scr.shape[1:])
             store_columns(dims, where_ref, p_scr.at[h], g_own, g_oth, h, proj_at, d // 2, p_sem.at[h])
-        for r in range(0, rows, br):
-            xhat, _ = normalize(x_ref[r : r + br, :].astype(F32))
-            nt_scr[:, r : r + br] = (xhat * vec_ref[0:1, :d] + vec_ref[1:2, :d]).astype(BF).T
 
     for h, j_ref in enumerate((j0_ref, j1_ref)):
         row = (i * 2 + h) * 2
@@ -673,6 +748,7 @@
 
     @pl.when(i == 0)
     def _():
+        local_copy(nt_ref, nt_scr, nt_sem).wait()
         for h in range(2):
             wait_columns(dims, w_scr, w_sem, h)
 
@@ -720,7 +796,7 @@
             wait_store(dims, t_scr, g_own, table_at, 128, t_sem.at[h])
 
 
-def attn_back_call(dims, where, joined, ga, lse, delta, seg_row, seg_col, x, vec, own, oth, vectors, gm, devices):
+def attn_back_call(dims, where, joined, ga, lse, delta, seg_row, seg_col, x, vec, own, oth, vectors, gm, nt, devices):
     rows, d = x.shape
     n = own[0].shape[1]
     groups = d // 256
@@ -738,12 +814,12 @@
             pl.BlockSpec((2, 2, rows), lambda i: (i, 0, 0)),
             full_spec(delta.shape), full_spec((1, 256)), full_spec((256, 1)), act, full_spec(vec.shape),
         ]
-        + [full_spec(v.shape) for v in vectors] + [ANY] * (1 + 2 * len(own)),
+        + [full_spec(v.shape) for v in vectors] + [ANY] * (2 + 2 * len(own)),
         out_specs=[act, ANY, ANY],
         out_shape=[jax.ShapeDtypeStruct((rows, d), BF), piece, piece],
         scratch_shapes=weight_scratch(dims, n, groups * 384)
         + [
-            pltpu.VMEM((d, rows), BF), pltpu.VMEM((rows, d), F32),
+            pltpu.VMEM((d, rows), BF), pltpu.SemaphoreType.DMA(()), pltpu.VMEM((rows, d), F32),
             pltpu.VMEM((rows, d), F32), pltpu.SemaphoreType.DMA(()), pltpu.VMEM((rows, 768), BF),
             pltpu.VMEM((128, rows), F32), pltpu.VMEM((128, rows), F32),
             pltpu.VMEM((groups, 2) + dims + (n, 384), BF), pltpu.SemaphoreType.DMA((groups, 2, count, dims[0])),
@@ -754,7 +830,7 @@
         compiler_params=params(),
         cost_estimate=cost(60e9, 20e6, 5.5e6),
         name="attn_back",
-    )(where, joined, joined, ga, lse, delta, seg_row, seg_col, x, vec, *vectors, gm, *own, *oth)
+    )(where, joined, joined, ga, lse, delta, seg_row, seg_col, x, vec, *vectors, gm, nt, *own, *oth)
 
 
 def pack_plan(counts, rows):
@@ -811,13 +887,21 @@
     def pick(self, pair):
         return jnp.where(self.ci == 0, pair[0], pair[1]), jnp.where(self.ci == 0, pair[1], pair[0])
 
-    def gather(self, w_qkv, table, w_fc):
+    def gather(self, w_qkv, w_proj, table, w_fc, w_out):
         whole = lambda v: lax.all_gather(v, AXES, axis=0, tiled=True)
-        attn, fc = whole(jnp.concatenate([w_qkv, table], axis=1)), whole(w_fc)
-        qkv, table = attn[:, : w_qkv.shape[1]], attn[:, w_qkv.shape[1] :]
-        first = [jnp.concatenate([half_columns(qkv, h, True), table], axis=1) for h in range(2)]
+        attn = whole(jnp.concatenate([w_qkv, w_proj, table], axis=1))
+        cut = w_qkv.shape[1], w_qkv.shape[1] + w_proj.shape[1]
+        fc, out = whole(w_fc), whole(w_out)
+        d = out.shape[1]
+        lists = [[], []]
+        for h in range(2):
+            qkv, proj, table = attn[:, : cut[0]], attn[:, cut[0] : cut[1]], attn[:, cut[1] :]
+            lists[0].append(jnp.concatenate([half_columns(qkv, h, True), half_columns(proj, h), table], axis=1))
+            lists[1].append(
+                jnp.concatenate([half_columns(fc, h)] + [out[(2 * h + t) * d : (2 * h + t + 1) * d] for t in range(2)], axis=1)
+            )
         listed = []
-        for pair in (first, [half_columns(fc, h) for h in range(2)]):
+        for pair in lists:
             own, oth = self.pick(pair)
             listed.append(([own[None]], [oth[None]]))
         return listed
@@ -827,6 +911,14 @@
         m = pair[0].shape[1]
         mine = lax.psum_scatter(jnp.concatenate(pair, axis=1), AXES, scatter_dimension=0, tiled=True).astype(F32)
         return mine[:, :m], mine[:, m:]
+
+    def scatter_hidden(self, own, oth):
+        pair = self.pick([own[0, 0], oth[0, 0]])
+        d = pair[0].shape[0]
+        wide = pair[0].shape[1] - 2 * d
+        fc = self.scatter(own[..., :wide], oth[..., :wide])
+        out = jnp.concatenate([v[:, wide + t * d : wide + (t + 1) * d] for v in pair for t in range(2)], axis=0)
+        return fc, lax.psum_scatter(out, AXES, scatter_dimension=0, tiled=True).astype(F32)
 
 
 class Chips:
@@ -895,17 +987,21 @@
     return jnp.pad(jnp.stack(flat), ((0, r - 3), (0, 128 - 4 * r)))
 
 
-def results(r, out, gx, s_fc, s_out, s_attn):
+def results(r, out, gx, s_fc, s_out, s_attn, table):
     d = out.shape[1]
     cut = 3 * d // 2
     s_qkv = join_columns(*[v[:, :cut] for v in s_attn])
-    s_proj = jnp.concatenate([v[:, cut:-128] for v in s_attn], axis=1)
-    row0, row1, row2 = [s_attn[0][k, -128:][: 4 * r] for k in range(3)]
+    s_proj = jnp.concatenate([v[:, cut:] for v in s_attn], axis=1)
+    row0, row1, row2 = [table[k, : 4 * r] for k in range(3)]
     return (
         out, gx,
         row0[:r], row0[r : 2 * r], s_qkv, row0[2 * r :], s_proj, row2[:r],
         row2[r : 2 * r], row2[2 * r : 3 * r], jnp.concatenate(s_fc, axis=1), row1, s_out, row2[3 * r :],
     )
+
+
+def split_table(halves):
+    return [v[:, :-128] for v in halves], halves[0][:, -128:]
 
 
 def block_plain(
@@ -917,25 +1013,23 @@
     devices = d // r
     dims, where = links.dims, links.where()
     table = vector_table(r, ln1_gain, ln1_bias, qv_bias, proj_bias, ln2_gain, ln2_bias, fc_bias, out_bias)
-    attn_w, fc_w = links.gather(w_qkv, table, w_fc)
-    proj = lax.all_gather(w_proj, AXES, axis=0, tiled=True)
-    w_out_all = lax.all_gather(w_out, AXES, axis=0, tiled=True).reshape(-1, d, d)
+    attn_w, m_w = links.gather(w_qkv, w_proj, table, w_fc, w_out)
     start, seg_row, seg_col, x, cot = prepare(tokens, lengths, cotangent)
-    joined, vec = qkv_call(dims, where, x, *attn_w, devices)
+    normed, nt, vec = first_norm_call(dims, where, x, attn_w[0], devices)
+    joined = qkv_call(dims, where, normed, vec, *attn_w)
     att0, lse0 = attn_call(joined, seg_row, seg_col, 0, 2)
     att1, lse1 = attn_call(joined, seg_row, seg_col, 2, d // 256 - 2)
     att = att0, att1
-    middle, normed_two = proj_call(x, att, vec, proj)
-    out, gn, gfb, gob, gw_out, *fc_g = mlp_call(dims, where, normed_two, cot, middle, vec, w_out_all, d, *fc_w)
-    s_fc = links.scatter(*fc_g)
-    s_out = lax.psum_scatter(gw_out, AXES, scatter_dimension=0, tiled=True).astype(F32)
-    gm, ga, gw_proj, delta, gg2, gb2, gpb = proj_back_call(gn, middle, cot, att, vec, proj)
+    middle, normed_two = proj_call(dims, where, x, att, vec, *attn_w)
+    out, gn, gfb, gob, *m_g = mlp_call(dims, where, normed_two, cot, middle, vec, *m_w)
+    s_fc, s_out = links.scatter_hidden(*m_g)
+    gm, ga, gw_proj, delta, gg2, gb2, gpb = proj_back_call(dims, where, gn, middle, cot, att, vec, *attn_w)
     gx, *g = attn_back_call(
         dims, where, joined, ga, jnp.concatenate([lse0, lse1]), delta, seg_row, seg_col, x, vec, *attn_w,
-        (gw_proj, gfb, gob, gg2, gb2, gpb), gm, devices,
+        (gw_proj, gfb, gob, gg2, gb2, gpb), gm, nt, devices,
     )
     restore = rows - start
-    return results(r, roll_rows(out, restore), roll_rows(gx, restore), s_fc, s_out, links.scatter(*g))
+    return results(r, roll_rows(out, restore), roll_rows(gx, restore), s_fc, s_out, *split_table(links.scatter(*g)))
 
 
 def block_chips(
@@ -951,76 +1045,98 @@
     def xy(column):
         return send(column, dx=1), send(column, dy=1)
 
-    hidden = w_out.shape[0]
-    rest = lax.all_gather(jnp.concatenate([w_out, w_proj], axis=0), AXES, axis=0, tiled=True)
-    rest = rest.reshape(devices, hidden + r, d)
-    a = links.rows_of(*cut_call(where, w_qkv, table))
+    def corner(x_part, y_part):
+        return [send(x_part[:2], dy=1), send(y_part[2:], dx=1)]
+
+    def near(b):
+        return send(b[1], dx=1), send(b[2], dy=1), send(b[3], dx=1, dy=1)
+
+    def far(parts):
+        return [parts[0]] + [send(parts[j], dz=j) for j in range(1, dims[0])]
+
+    a = links.rows_of(*cut_call(where, w_qkv, w_proj, table))
     a, tokens, lengths, cotangent, w_fc = together(a, tokens, lengths, cotangent, w_fc)
     a0 = links.along_z(a)
     fc = links.trade([half_columns(w_fc, h) for h in range(2)])
+    m = jnp.concatenate([fc, w_out[: 2 * r], w_out[2 * r :]], axis=1)
+    a0, m, tokens, lengths, cotangent = together(a0, m, tokens, lengths, cotangent)
     prep = prepare(tokens, lengths, cotangent)
-    a0, prep, fc = together(a0, prep, fc)
-    start, seg_row, seg_col, x, cot = prep
+    m0 = links.along_z(m)
     a0 = jnp.stack(a0)
     a_own = [a0, send(a0, dx=1), send(a0, dy=1), send(a0, dx=1, dy=1)]
-    fc = links.along_z(fc)
-    a_own, fc = together(a_own, fc)
-    fc0 = jnp.stack(fc)
+    a_own, m0, prep = together(a_own, m0, prep)
+    start, seg_row, seg_col, x, cot = prep
+    m0 = jnp.stack(m0)
+    a_own = [jnp.concatenate(a_own, axis=0)]
+    m0, a_own = together(m0, a_own)
     attn_w = a_own, swap(a_own)
-    fc0, x, attn_w = together(fc0, x, attn_w)
-
-    joined, vec = qkv_call(dims, where, x, *attn_w, devices)
+    mx, my = xy(m0)
+    normed, nt, vec = first_norm_call(dims, where, x, a_own, devices)
+    normed, attn_w = together(normed, attn_w)
+
+    joined = qkv_call(dims, where, normed, vec, *attn_w)
     att0, lse0 = attn_call(joined, seg_row, seg_col, 0, 2)
-    fx, fy = xy(fc0)
-    att0, joined, fx, fy = together(att0, joined, fx, fy)
+    att0, joined, mx, my = together(att0, joined, mx, my)
     att1, lse1 = attn_call(joined, seg_row, seg_col, 2, d // 256 - 2)
     att = att0, att1
-    proj = rest[:, hidden:].reshape(d, d)
-    middle, normed_two = proj_call(x, att, vec, proj)
-    fd = [send(fx[:2], dy=1), send(fy[2:], dx=1)]
-    f_oth = swap([fc0, fx, fy])
+    middle, normed_two = proj_call(dims, where, x, att, vec, *attn_w)
+    md = corner(mx, my)
+    m_oth = swap([m0, mx, my])
     lse = jnp.concatenate([lse0, lse1])
-    normed_two, fd, f_oth, lse = together(normed_two, fd, f_oth, lse)
-    fc_w = [fc0, fx, fy] + fd, f_oth + swap(fd)
-
-    out, gn, gfb, gob, gw_out, f_own, f_oth = mlp_call(dims, where, normed_two, cot, middle, vec, rest, hidden, *fc_w)
-    s_out = lax.psum_scatter(gw_out, AXES, scatter_dimension=0, tiled=True).astype(F32)
-    gm, ga, gw_proj, delta, gg2, gb2, gpb = proj_back_call(gn, middle, cot, att, vec, proj)
-    (f_oth,) = swap([f_oth])
-    restore = rows - start
-    out = roll_rows(out, restore)
-    ga, delta, f_own, f_oth, out = together(ga, delta, f_own, f_oth, out)
-
-    def near(b):
-        return send(b[1], dx=1), send(b[2], dy=1), send(b[3], dx=1, dy=1)
-
-    def column(b, arrived):
-        return [add_all([b[0][j]] + [v[j] for v in arrived]).astype(BF) for j in range(dims[0])]
-
-    def far(parts):
-        return [parts[0]] + [send(parts[j], dz=j) for j in range(1, dims[0])]
-
-    b = links.add_core(f_own, f_oth)
-    b, ga, delta = together(b, ga, delta)
-    b_near = near(b)
+    normed_two, md, m_oth, lse = together(normed_two, md, m_oth, lse)
+    m_w = [m0, mx, my] + md, m_oth + swap(md)
+
+    out, gn, gfb, gob, m_own, m_oth = mlp_call(dims, where, normed_two, cot, middle, vec, *m_w)
+    gm, ga, gw_proj, delta, gg2, gb2, gpb = proj_back_call(dims, where, gn, middle, cot, att, vec, *attn_w)
+    (m_oth,) = swap([m_oth])
+    ga, delta, m_own, m_oth = together(ga, delta, m_own, m_oth)
+
+    def chip_sum(i, part):
+        return add_all([part(m_own[i]), part(m_oth[i])]).astype(BF)
+
+    first = (
+        chip_sum(3, lambda v: v[1:3]), chip_sum(3, lambda v: v[:1]), chip_sum(3, lambda v: v[3:]),
+        chip_sum(1, lambda v: v[1:]), chip_sum(2, lambda v: v[:3]),
+    )
+    first, ga, delta, m_own, m_oth = together(first, ga, delta, m_own, m_oth)
+    first = (
+        send(first[0], dx=1, dy=1), send(first[1], dy=1), send(first[2], dx=1),
+        send(first[3], dx=1), send(first[4], dy=1),
+    )
     gx, g_own, g_oth = attn_back_call(
         dims, where, joined, ga, lse, delta, seg_row, seg_col, x, vec, *attn_w,
-        (gw_proj, gfb, gob, gg2, gb2, gpb), gm, devices,
+        (gw_proj, gfb, gob, gg2, gb2, gpb), gm, nt, devices,
     )
-    gx, g_own, g_oth, b_near, b = together(gx, g_own, g_oth, b_near, b)
+    gx, g_own, g_oth, first, m_own, m_oth, out = together(gx, g_own, g_oth, first, m_own, m_oth, out)
 
     (g_oth,) = swap([g_oth])
-    b = column(b, b_near)
-    g_oth, b, gx = together(g_oth, b, gx)
+    corners, by_y, by_x, from_x, from_y = first
+
+    def chip_total(i, j, arrived):
+        return add_all([m_own[i, j], m_oth[i, j]] + arrived).astype(BF)
+
+    x_one = send(chip_total(1, 0, [by_y[0]]), dx=1)
+    y_one = send(chip_total(2, 3, [by_x[0]]), dy=1)
+    b = {1: send(chip_total(0, 1, [from_x[0], from_y[1], corners[0]]), dz=1)}
     e = links.add_core(g_own, g_oth)
-    e_near, b = near(e), far(b)
-    gx = roll_rows(gx, restore)
-    e_near, b, e, gx = together(e_near, b, e, gx)
-
-    e = far(column(e, e_near))
-    s_fc = links.rows_back(add_all(b))
-    e, s_fc = together(e, s_fc)
-    return results(r, out, gx, s_fc, s_out, links.rows_back(add_all(e)))
+    e, x_one, y_one, gx, out, m_own, m_oth, b = together(e, x_one, y_one, gx, out, m_own, m_oth, b)
+
+    e_near = near(e)
+    b[0] = chip_total(0, 0, [x_one, from_y[0]])
+    b[2] = send(chip_total(0, 2, [from_x[1], from_y[2], corners[1]]), dz=2)
+    b[3] = send(chip_total(0, 3, [from_x[2], y_one]), dz=3)
+    b = [b[j] for j in range(4)]
+    gx, out = roll_rows(gx, rows - start), roll_rows(out, rows - start)
+    e_near, b, e, gx, out = together(e_near, b, e, gx, out)
+
+    e = far([add_all([e[0][j]] + [v[j] for v in e_near]).astype(BF) for j in range(dims[0])])
+    total = add_all(b)
+    s_fc = links.rows_back(total[:, : -2 * d])
+    s_out = jnp.concatenate([total[:, -2 * d : -d], total[:, -d:]], axis=0)
+    e, s_fc, s_out = together(e, s_fc, s_out)
+    total = add_all(e)
+    vectors = jnp.where(links.ci == 0, total[:3, -128:], total[r : r + 3, -128:])
+    return results(r, out, gx, s_fc, s_out, links.rows_back(total[:, :-128]), vectors)
 
 
 def solution(mesh):

time: 313 us -> 304 us (0.971)
  waiting for transfers between devices: 83.9 us -> 63.7 us
  between operations: 20.7 us -> 7.52 us
  other arithmetic: 29.8 us -> 39.4 us
  Pallas kernels: 129 us -> 138 us
  starting transfers between devices: 36.3 us -> 41.1 us
    reduce_scatter x1 -> x0, waiting for transfers between devices: 23.7 us -> none  [block_chips(): lax.psum_scatter(gw_out, AXES, scatter_dimension=0, tiled=True).astype(F32)]
    pallas_call x5 -> x6, Pallas kernels: 77.8 us -> 87.7 us  [the longest x1 49.3 us: mlp_call(): pl.pallas_call(functools.partial(mlp_kernel, dims, len(own)), grid=(block...]
    convert_element_type x2 -> x5, other arithmetic: 2.26 us -> 11.9 us  [the longest x3 7.27 us: chip_sum(): return add_all([part(m_own[i]), part(m_oth[i])]).astype(BF)]
    ppermute x40 -> x41, starting transfers between devices: 36.2 us -> 41.1 us  [send(): return lax.ppermute(array, AXES, pairs)]
    ppermute x40 -> x41, waiting for transfers between devices: 60.2 us -> 63.7 us  [send(): return lax.ppermute(array, AXES, pairs)]
  transfers between devices with their start and end apart: 42 -> 41, of which waited for: 19 -> 18; matrix products, arithmetic and copies ran while one was open for 10% -> 9% of each run, Pallas kernels for 27% -> 29%
where the time goes in v5:
time: 304 us; the launch traced here: 299 us
  Pallas kernels  138 us (45%)
  waiting for transfers between devices  63.7 us (21%)
  starting transfers between devices  41.1 us (14%)
  other arithmetic  39.4 us (13%)
  local copies, waits for them, and re-layouts  10 us (3%)
  between operations  7.52 us (2%)
    ppermute x41, waiting for transfers between devices, send(): return lax.ppermute(array, AXES, pairs)  63.7 us
    pallas_call x1, Pallas kernels, mlp_call(): pl.pallas_call(functools.partial(mlp_kernel, dims, len(own)), grid=(block...  49.3 us
    ppermute x41, starting transfers between devices, send(): return lax.ppermute(array, AXES, pairs)  41.1 us
    pallas_call x1, Pallas kernels, attn_back_call(): pl.pallas_call(functools.partial(attn_back_kernel, dims, len(own), device...  36.9 us
    pallas_call x1, Pallas kernels, proj_back_call(): pl.pallas_call(functools.partial(proj_back_kernel, dims, len(own), 3 * d...  13.4 us
    pallas_call x2, Pallas kernels, attn_call(): pl.pallas_call(attn_kernel, grid=(2 * groups,), in_specs=[at(0), at(1), a...  13 us
    concatenate x3, other arithmetic, roll_rows(): jnp.concatenate([array, array], axis=0)  11.2 us
    pallas_call x1, Pallas kernels, qkv_call(): pl.pallas_call(functools.partial(qkv_kernel, dims, len(own)), grid=(2,),...  9.8 us
  transfers between devices with their start and end apart: 41, of which 18 were waited for; matrix products, arithmetic and copies ran while one was open for 9% of the time, Pallas kernels for 29%

profile of v5, /device:TPU:0, one launch (start us, length us, event | category | flops | bytes accessed | tf_op | source)
XLA Modules:
  0.0 299.3 jit_solution(2108957487808966551)
XLA Ops:
  1.6 1.3 fusion.33.t_ref
  3.4 1.6 cut.1
  10.0 2.8 collective-permute-start.3
  12.8 2.6 collective-permute-start.2
  15.3 1.3 collective-permute-start.1
  16.8 3.1 %collective-permute-done.3 = bf16[48,1664]{1,0:T(8,128)(2,1)S(1)} collective-permute-done((bf16[48,1664]{1,0:T(8,128)(2,1)S(1)}, bf16[48,1664]{1,0:T(8,128)(2,1)S(1)}, u32[]{:S(2)}, u32[]{:S(2)}) %collective-permute-start.3) | collective-permute-done | bytes 159776 | tf_op jit(solution)/shard_map/ppermute | solution.py:948
  19.8 6.5 %collective-permute-done.2 = bf16[48,1664]{1,0:T(8,128)(2,1)S(1)} collective-permute-done((bf16[48,1664]{1,0:T(8,128)(2,1)S(1)}, bf16[48,1664]{1,0:T(8,128)(2,1)S(1)}, u32[]{:S(2)}, u32[]{:S(2)}) %collective-permute-start.2) | collective-permute-done | bytes 159776 | tf_op jit(solution)/shard_map/ppermute | solution.py:948
  26.3 3.9 %collective-permute-start.10 = (bf16[48,3072]{1,0:T(8,128)(2,1)S(1)}, bf16[48,3072]{1,0:T(8,128)(2,1)S(1)}, u32[]{:S(2)}, u32[]{:S(2)}) collective-permute-start(bf16[48,3072]{1,0:T(8,128)(2,1)S(1)} %pad_maximum_fusion.3), channel_id=1, source_target_pairs={{0,8},{1,9},{2,10},{3,11},{4,12},{5,13},{6,14},{7,15},{8,16},{9,17... | collective-permute-start | bytes 884744 | tf_op jit(solution)/shard_map/ppermute | solution.py:948
  30.2 1.6 collective-permute-start.9
  32.0 2.5 collective-permute-start.7
  42.7 3.7 %fusion.4.x_ref = bf16[1024,768]{1,0:T(8,128)(2,1)} fusion(s32[]{:T(128)S(6)} %select_n.151, bf16[1024,768]{1,0:T(8,128)(2,1)S(1)} %copy-done.4), kind=kLoop, calls=%fused_computation.15 | loop fusion | flops 3145728 | bytes 3145732 | tf_op jit(solution)/shard_map/concatenate | solution.py:855
  48.2 2.3 fusion.3.c_ref
  50.9 6.1 %collective-permute-done.8 = bf16[48,3072]{1,0:T(8,128)(2,1)S(1)} collective-permute-done((bf16[48,3072]{1,0:T(8,128)(2,1)S(1)}, bf16[48,3072]{1,0:T(8,128)(2,1)S(1)}, u32[]{:S(2)}, u32[]{:S(2)}) %collective-permute-start.8) | collective-permute-done | bytes 294944 | tf_op jit(solution)/shard_map/ppermute | solution.py:948
  57.0 5.0 %collective-permute-done.6 = bf16[4,48,1664]{2,1,0:T(8,128)(2,1)} collective-permute-done((bf16[4,48,1664]{2,1,0:T(8,128)(2,1)S(1)}, bf16[4,48,1664]{2,1,0:T(8,128)(2,1)}, u32[]{:S(2)}, u32[]{:S(2)}) %collective-permute-start.6) | collective-permute-done | bytes 639008 | tf_op jit(solution)/shard_map/ppermute | solution.py:948
  62.9 2.1 pad_maximum_fusion.1.refs_0_
  65.0 1.7 pad_maximum_fusion.refs_0_
  67.3 1.5 collective-permute-start.13
  70.4 6.1 %first_norm.1 = (bf16[1024,768]{1,0:T(8,128)(2,1)}, bf16[768,1024]{1,0:T(8,128)(2,1)}, f32[8,3072]{1,0:T(8,128)}) custom-call(s32[4]{0:T(128)} %pad_add_fusion.where_ref, bf16[1024,768]{1,0:T(8,128)(2,1)} %fusion.4.x_ref, bf16[16,48,1664]{2,1,0:T(8,128)(2,1)} %copy-done), custom_call_target="tpu_custom_call" | custom-call | flops 1000000000 | bytes 4718592 | tf_op jit(solution)/shard_map/first_norm/pallas_call | solution.py:335
  76.5 9.8 %qkv.1.q_ref.k_ref.v_ref.j0_ref.j1_ref = bf16[1024,2304]{1,0:T(8,128)(2,1)} custom-call(s32[4]{0:T(128)} %pad_add_fusion.where_ref, bf16[1024,768]{1,0:T(8,128)(2,1)} %get-tuple-element.161.n_ref, f32[8,3072]{1,0:T(8,128)} %get-tuple-element.162.vec_ref, bf16[16,48,1664]{2,1,0:T(8,128)(2,1)} %copy-done, bf16[16,48,1664]{2,1,0:T(8,128)(2,1)} %collective-permute-done.11.refs_1_), custom_call_target="tpu_custom_call" | custom-call | flops 3623878656 | bytes 9830400 | tf_op jit(solution)/shard_map/qkv/pallas_call | solution.py:384
  86.3 8.0 %attn.2 = (bf16[1024,512]{1,0:T(8,128)(2,1)}, f32[4,2,1024]{2,1,0:T(2,128)}) custom-call(bf16[1024,2304]{1,0:T(8,128)(2,1)} %qkv.1.q_ref.k_ref.v_ref.j0_ref.j1_ref, bf16[1024,2304]{1,0:T(8,128)(2,1)} %qkv.1.q_ref.k_ref.v_ref.j0_ref.j1_ref, bf16[1024,2304]{1,0:T(8,128)(2,1)} %qkv.1.q_ref.k_ref.v_ref.j0_ref.j1_ref, s32[1,256]{1,0:T(1,128)} %bitcast.120, ...), custom_call_target="tpu_custom_call" | custom-call | flops 16000000000 | bytes 8000000 | tf_op jit(solution)/shard_map/attn/pallas_call | solution.py:128
  94.3 1.2 collective-permute-done.13.refs_2_
  95.5 1.2 collective-permute-done.12.refs_1_
  100.3 1.2 collective-permute-start.14
  101.5 5.0 %attn.3 = (bf16[1024,256]{1,0:T(8,128)(2,1)}, f32[2,2,1024]{2,1,0:T(2,128)}) custom-call(bf16[1024,2304]{1,0:T(8,128)(2,1)} %qkv.1.q_ref.k_ref.v_ref.j0_ref.j1_ref, bf16[1024,2304]{1,0:T(8,128)(2,1)} %qkv.1.q_ref.k_ref.v_ref.j0_ref.j1_ref, bf16[1024,2304]{1,0:T(8,128)(2,1)} %qkv.1.q_ref.k_ref.v_ref.j0_ref.j1_ref, s32[1,256]{1,0:T(1,128)} %bitcast.121, ...), custom_call_target="tpu_custom_call" | custom-call | flops 8000000000 | bytes 8000000 | tf_op jit(solution)/shard_map/attn/pallas_call | solution.py:128
  106.5 7.5 %proj.1 = (f32[1024,768]{1,0:T(8,128)}, bf16[1024,768]{1,0:T(8,128)(2,1)}) custom-call(s32[4]{0:T(128)} %pad_add_fusion.where_ref, bf16[1024,768]{1,0:T(8,128)(2,1)} %fusion.4.x_ref, bf16[1024,512]{1,0:T(8,128)(2,1)} %get-tuple-element.170.a0_ref, bf16[1024,256]{1,0:T(8,128)(2,1)} %get-tuple-element.171.a1_ref, f32[8,3072]{1,0:T(8,128)} %get-tuple-element.162.vec_ref, ...), custom_call_target="tpu_custom_call" | custom-call | flops 1207959552 | bytes 9043968 | tf_op jit(solution)/shard_map/proj/pallas_call | solution.py:420
  115.9 1.5 collective-permute-done.19.refs_8_
  119.0 49.3 %mlp.1 = (bf16[1024,768]{1,0:T(8,128)(2,1)}, f32[1024,768]{1,0:T(8,128)}, f32[1,3072]{1,0:T(1,128)}, f32[1,768]{1,0:T(1,128)}, bf16[4,4,48,3072]{3,2,1,0:T(8,128)(2,1)}, /*index=5*/bf16[4,4,48,3072]{3,2,1,0:T(8,128)(2,1)}) custom-call(s32[4]{0:T(128)} %pad_add_fusion.where_ref, bf16[1024,768]{1,0:T(8,128)(2,1)} %get-tuple-element.177.n_ref, ...), custom_call_target="tpu_custom_call" | custom-call | flops 28991029248 | bytes 30000000 | tf_op jit(solution)/shard_map/mlp/pallas_call | solution.py:562
  168.6 13.4 %proj_back.1 = (f32[1024,768]{1,0:T(8,128)}, bf16[1024,768]{1,0:T(8,128)(2,1)}, bf16[768,768]{1,0:T(8,128)(2,1)}, f32[16,1024]{1,0:T(8,128)}, f32[1,768]{1,0:T(1...) custom-call(s32[4]{0:T(128)} %pad_add_fusion.where_ref, f32[1024,768]{1,0:T(8,128)} %get-tuple-element.185.gn_ref, ...), custom_call_target="tpu_custom_call" | custom-call | flops 2415919104 | bytes 12582912 | tf_op jit(solution)/shard_map/proj_back/pallas_call | solution.py:638
  182.0 2.0 fusion.11
  184.1 1.9 fusion.20
  186.0 3.3 %fusion.6 = (bf16[3,48,3072]{2,1,0:T(8,128)(2,1)}, bf16[3,48,3072]{2,1,0:T(8,128)(2,1)}) fusion(bf16[4,4,48,3072]{3,2,1,0:T(8,128)(2,1)} %collective-permute-done.21, bf16[4,4,48,3072]{3,2,1,0:T(8,128)(2,1)S(1)} %copy-done.1), kind=kLoop, calls=%fused_computation.23 | loop fusion | flops 3538944 | bytes 5308416 | tf_op jit(solution)/shard_map/convert_element_type | solution.py:1095
  189.3 1.2 collective-permute-start.23
  191.0 1.8 collective-permute-start.22
  192.8 1.2 collective-permute-start.25
  194.5 36.9 %attn_back.1 = (bf16[1024,768]{1,0:T(8,128)(2,1)}, bf16[4,4,48,1664]{3,2,1,0:T(8,128)(2,1)}, bf16[4,4,48,1664]{3,2,1,0:T(8,128)(2,1)}) custom-call(s32[4]{0:T(128)} %pad_add_fusion.where_ref, bf16[1024,2304]{1,0:T(8,128)(2,1)} %qkv.1.q_ref.k_ref.v_ref.j0_ref.j1_ref, bf16[1024,2304]{1,0:T(8,128)(2,1)} %qkv.1.q_ref.k_ref.v_ref.j0_ref.j1_ref, ...), custom_call_target="tpu_custom_call" | custom-call | flops 60000002048 | bytes 20000000 | tf_op jit(solution)/shard_map/attn_back/pallas_call | solution.py:806
  232.4 2.4 fusion.16
  235.3 1.5 collective-permute-start.29
  238.2 7.9 %collective-permute-done.30 = bf16[48,3072]{1,0:T(8,128)(2,1)S(1)} collective-permute-done((bf16[48,3072]{1,0:T(8,128)(2,1)S(1)}, bf16[48,3072]{1,0:T(8,128)(2,1)S(1)}, u32[]{:S(2)}, u32[]{:S(2)}) %collective-permute-start.30) | collective-permute-done | bytes 294944 | tf_op jit(solution)/shard_map/ppermute | solution.py:948
  246.1 1.6 collective-permute-start.31
  249.7 2.2 fusion.13
  251.9 3.0 collective-permute-start.35
  254.9 3.8 %fusion.1 = bf16[1024,768]{1,0:T(8,128)(2,1)} fusion(s32[]{:T(128)S(6)} %select_n.153, bf16[1024,768]{1,0:T(8,128)(2,1)S(1)} %copy-done.6), kind=kLoop, calls=%fused_computation.12 | loop fusion | flops 3145728 | bytes 3145732 | tf_op jit(solution)/shard_map/concatenate | solution.py:855
  258.7 3.8 %fusion = bf16[1024,768]{1,0:T(8,128)(2,1)} fusion(s32[]{:T(128)S(6)} %select_n.153, bf16[1024,768]{1,0:T(8,128)(2,1)S(1)} %copy-done.5), kind=kLoop, calls=%fused_computation.11 | loop fusion | flops 3145728 | bytes 3145732 | tf_op jit(solution)/shard_map/concatenate | solution.py:855
  262.4 10.3 %collective-permute-done.34 = bf16[48,3072]{1,0:T(8,128)(2,1)S(1)} collective-permute-done((bf16[48,3072]{1,0:T(8,128)(2,1)S(1)}, bf16[48,3072]{1,0:T(8,128)(2,1)S(1)}, u32[]{:S(2)}, u32[]{:S(2)}) %collective-permute-start.34) | collective-permute-done | bytes 294944 | tf_op jit(solution)/shard_map/ppermute | solution.py:948
  272.7 4.4 %collective-permute-done.32 = bf16[4,48,1664]{2,1,0:T(8,128)(2,1)S(1)} collective-permute-done((bf16[4,48,1664]{2,1,0:T(8,128)(2,1)S(1)}, bf16[4,48,1664]{2,1,0:T(8,128)(2,1)S(1)}, u32[]{:S(2)}, u32[]{:S(2)}) %collective-permute-start.32) | collective-permute-done | bytes 639008 | tf_op jit(solution)/shard_map/ppermute | solution.py:948
  277.8 1.6 collective-permute-start.38
  280.8 3.9 %collective-permute-done.38 = bf16[48,1664]{1,0:T(8,128)(2,1)S(1)} collective-permute-done((bf16[48,1664]{1,0:T(8,128)(2,1)S(1)}, bf16[48,1664]{1,0:T(8,128)(2,1)S(1)}, u32[]{:S(2)}, u32[]{:S(2)}) %collective-permute-start.38) | collective-permute-done | bytes 159776 | tf_op jit(solution)/shard_map/ppermute | solution.py:948
  284.7 9.4 %collective-permute-done.37 = bf16[48,1664]{1,0:T(8,128)(2,1)S(1)} collective-permute-done((bf16[48,1664]{1,0:T(8,128)(2,1)S(1)}, bf16[48,1664]{1,0:T(8,128)(2,1)S(1)}, u32[]{:S(2)}, u32[]{:S(2)}) %collective-permute-start.37) | collective-permute-done | bytes 159776 | tf_op jit(solution)/shard_map/ppermute | solution.py:948
  (143 shorter events, 33.7 us)
Async XLA Ops:
  0.6 16.1 %copy-start.10 = (bf16[24,3072]{1,0:T(8,128)(2,1)S(1)}, bf16[24,3072]{1,0:T(8,128)(2,1)}, u32[]{:S(2)}) copy-start(bf16[24,3072]{1,0:T(8,128)(2,1)} %param.26) | copy-start | bytes 442372
  5.0 1.6 collective-permute-start
  7.5 28.0 %copy-start.15 = (s32[1,5]{1,0:T(1,128)S(1)}, s32[1,5]{1,0:T(1,128)}, u32[]{:S(2)}) copy-start(s32[1,5]{1,0:T(1,128)} %param.17) | copy-start | bytes 64
  7.5 35.1 %copy-start.4 = (bf16[1024,768]{1,0:T(8,128)(2,1)S(1)}, bf16[1024,768]{1,0:T(8,128)(2,1)}, u32[]{:S(2)}) copy-start(bf16[1024,768]{1,0:T(8,128)(2,1)} %param.16) | copy-start | bytes 4718596
  8.6 8.1 %collective-permute-start.4 = (bf16[24,1536]{1,0:T(8,128)(2,1)S(1)}, bf16[24,1536]{1,0:T(8,128)(2,1)S(1)}, u32[]{:S(2)}, u32[]{:S(2)}) collective-permute-start(bf16[24,1536]{1,0:T(8,128)(2,1)S(1)} %broadcast_select_fusion.8), channel_id=1, source_target_pairs={{0,1},{1,0},{2,3},{3,2},{4,5},{5,4},{6,7},{7,6},{8,9},{9,8},{10,11... | collective-permute-start | bytes 221192 | tf_op jit(solution)/shard_map/ppermute | solution.py:948
  10.0 9.9 %collective-permute-start.3 = (bf16[48,1664]{1,0:T(8,128)(2,1)S(1)}, bf16[48,1664]{1,0:T(8,128)(2,1)S(1)}, u32[]{:S(2)}, u32[]{:S(2)}) collective-permute-start(bf16[48,1664]{1,0:T(8,128)(2,1)S(1)} %pad_maximum_fusion.6), channel_id=1, source_target_pairs={{0,8},{1,9},{2,10},{3,11},{4,12},{5,13},{6,14},{7,15},{8,16},{9,17... | collective-permute-start | bytes 479240 | tf_op jit(solution)/shard_map/ppermute | solution.py:948
  12.8 13.6 %collective-permute-start.2 = (bf16[48,1664]{1,0:T(8,128)(2,1)S(1)}, bf16[48,1664]{1,0:T(8,128)(2,1)S(1)}, u32[]{:S(2)}, u32[]{:S(2)}) collective-permute-start(bf16[48,1664]{1,0:T(8,128)(2,1)S(1)} %pad_maximum_fusion.6), channel_id=1, source_target_pairs={{0,16},{1,17},{2,18},{3,19},{4,20},{5,21},{6,22},{7,23},{8,24},{9,... | collective-permute-start | bytes 479240 | tf_op jit(solution)/shard_map/ppermute | solution.py:948
  15.3 11.0 %collective-permute-start.1 = (bf16[48,1664]{1,0:T(8,128)(2,1)S(1)}, bf16[48,1664]{1,0:T(8,128)(2,1)S(1)}, u32[]{:S(2)}, u32[]{:S(2)}) collective-permute-start(bf16[48,1664]{1,0:T(8,128)(2,1)S(1)} %pad_maximum_fusion.6), channel_id=1, source_target_pairs={{0,24},{1,25},{2,26},{3,27},{4,28},{5,29},{6,30},{7,31},{8,0},{9,1... | collective-permute-start | bytes 479240 | tf_op jit(solution)/shard_map/ppermute | solution.py:948
  26.3 20.0 %collective-permute-start.10 = (bf16[48,3072]{1,0:T(8,128)(2,1)S(1)}, bf16[48,3072]{1,0:T(8,128)(2,1)S(1)}, u32[]{:S(2)}, u32[]{:S(2)}) collective-permute-start(bf16[48,3072]{1,0:T(8,128)(2,1)S(1)} %pad_maximum_fusion.3), channel_id=1, source_target_pairs={{0,8},{1,9},{2,10},{3,11},{4,12},{5,13},{6,14},{7,15},{8,16},{9,17... | collective-permute-start | bytes 884744 | tf_op jit(solution)/shard_map/ppermute | solution.py:948
  30.2 20.7 %collective-permute-start.9 = (bf16[48,3072]{1,0:T(8,128)(2,1)S(1)}, bf16[48,3072]{1,0:T(8,128)(2,1)}, u32[]{:S(2)}, u32[]{:S(2)}) collective-permute-start(bf16[48,3072]{1,0:T(8,128)(2,1)S(1)} %pad_maximum_fusion.3), channel_id=1, source_target_pairs={{0,16},{1,17},{2,18},{3,19},{4,20},{5,21},{6,22},{7,23},{8,24},{9,... | collective-permute-start | bytes 884744 | tf_op jit(solution)/shard_map/ppermute | solution.py:948
  32.0 25.0 %collective-permute-start.7 = (bf16[4,48,1664]{2,1,0:T(8,128)(2,1)S(1)}, bf16[4,48,1664]{2,1,0:T(8,128)(2,1)}, u32[]{:S(2)}, u32[]{:S(2)}) collective-permute-start(bf16[4,48,1664]{2,1,0:T(8,128)(2,1)S(1)} %pad_maximum_fusion.2), channel_id=1, source_target_pairs={{0,6},{1,7},{2,4},{3,5},{4,2},{5,3},{6,0},{7,1},{8,14},{9,15},{10,... | collective-permute-start | bytes 1916936 | tf_op jit(solution)/shard_map/ppermute | solution.py:948
  34.5 27.5 %collective-permute-start.6 = (bf16[4,48,1664]{2,1,0:T(8,128)(2,1)S(1)}, bf16[4,48,1664]{2,1,0:T(8,128)(2,1)}, u32[]{:S(2)}, u32[]{:S(2)}) collective-permute-start(bf16[4,48,1664]{2,1,0:T(8,128)(2,1)S(1)} %pad_maximum_fusion.2), channel_id=1, source_target_pairs={{0,4},{1,5},{2,6},{3,7},{4,0},{5,1},{6,2},{7,3},{8,12},{9,13},{10,... | collective-permute-start | bytes 1916936 | tf_op jit(solution)/shard_map/ppermute | solution.py:948
  35.0 27.0 %collective-permute-start.5 = (bf16[4,48,1664]{2,1,0:T(8,128)(2,1)S(1)}, bf16[4,48,1664]{2,1,0:T(8,128)(2,1)S(1)}, u32[]{:S(2)}, u32[]{:S(2)}) collective-permute-start(bf16[4,48,1664]{2,1,0:T(8,128)(2,1)S(1)} %pad_maximum_fusion.2), channel_id=1, source_target_pairs={{0,2},{1,3},{2,0},{3,1},{4,6},{5,7},{6,4},{7,5},{8,10},{9,11},{10,... | collective-permute-start | bytes 1916936 | tf_op jit(solution)/shard_map/ppermute | solution.py:948
  46.4 10.6 %collective-permute-start.8 = (bf16[48,3072]{1,0:T(8,128)(2,1)S(1)}, bf16[48,3072]{1,0:T(8,128)(2,1)S(1)}, u32[]{:S(2)}, u32[]{:S(2)}) collective-permute-start(bf16[48,3072]{1,0:T(8,128)(2,1)S(1)} %pad_maximum_fusion.3), channel_id=1, source_target_pairs={{0,24},{1,25},{2,26},{3,27},{4,28},{5,29},{6,30},{7,31},{8,0},{9,1... | collective-permute-start | bytes 884744 | tf_op jit(solution)/shard_map/ppermute | solution.py:948
  48.2 21.3 %copy-start.16 = (s32[256]{0:T(256)}, s32[256]{0:T(256)S(1)}, u32[]{:S(2)}) copy-start(s32[256]{0:T(256)S(1)} %slice.338) | copy-start | bytes 3076
  66.7 9.8 %collective-permute-start.11 = (bf16[16,48,1664]{2,1,0:T(8,128)(2,1)S(1)}, bf16[16,48,1664]{2,1,0:T(8,128)(2,1)}, u32[]{:S(2)}, u32[]{:S(2)}) collective-permute-start(bf16[16,48,1664]{2,1,0:T(8,128)(2,1)S(1)} %pad_maximum_fusion.refs_0_), channel_id=1, source_target_pairs={{0,1},{1,0},{2,3},{3,2},{4,5},{5,4},{6,7},{7,6},{8,9},{9,8},{10,11... | collective-permute-start | bytes 7667720 | tf_op jit(solution)/shard_map/ppermute | solution.py:948
  66.8 48.0 %collective-permute-start.16 = (bf16[4,48,3072]{2,1,0:T(8,128)(2,1)}, bf16[4,48,3072]{2,1,0:T(8,128)(2,1)}, u32[]{:S(2)}, u32[]{:S(2)}) collective-permute-start(bf16[4,48,3072]{2,1,0:T(8,128)(2,1)} %pad_maximum_fusion.1.refs_0_), channel_id=1, source_target_pairs={{0,1},{1,0},{2,3},{3,2},{4,5},{5,4},{6,7},{7,6},{8,9},{9,8},{10,11... | collective-permute-start | bytes 3538952 | tf_op jit(solution)/shard_map/ppermute | solution.py:948
  67.3 28.3 %collective-permute-start.13 = (bf16[4,48,3072]{2,1,0:T(8,128)(2,1)}, bf16[4,48,3072]{2,1,0:T(8,128)(2,1)}, u32[]{:S(2)}, u32[]{:S(2)}) collective-permute-start(bf16[4,48,3072]{2,1,0:T(8,128)(2,1)} %pad_maximum_fusion.1.refs_0_), channel_id=1, source_target_pairs={{0,4},{1,5},{2,6},{3,7},{4,0},{5,1},{6,2},{7,3},{8,12},{9,13},{10,... | collective-permute-start | bytes 3538952 | tf_op jit(solution)/shard_map/ppermute | solution.py:948
  68.8 28.0 %collective-permute-start.12 = (bf16[4,48,3072]{2,1,0:T(8,128)(2,1)}, bf16[4,48,3072]{2,1,0:T(8,128)(2,1)}, u32[]{:S(2)}, u32[]{:S(2)}) collective-permute-start(bf16[4,48,3072]{2,1,0:T(8,128)(2,1)} %pad_maximum_fusion.1.refs_0_), channel_id=1, source_target_pairs={{0,2},{1,3},{2,0},{3,1},{4,6},{5,7},{6,4},{7,5},{8,10},{9,11},{10,... | collective-permute-start | bytes 3538952 | tf_op jit(solution)/shard_map/ppermute | solution.py:948
  96.8 18.5 %collective-permute-start.17 = (bf16[4,48,3072]{2,1,0:T(8,128)(2,1)}, bf16[4,48,3072]{2,1,0:T(8,128)(2,1)S(1)}, u32[]{:S(2)}, u32[]{:S(2)}) collective-permute-start(bf16[4,48,3072]{2,1,0:T(8,128)(2,1)} %collective-permute-done.12.refs_1_), channel_id=1, source_target_pairs={{0,1},{1,0},{2,3},{3,2},{4,5},{5,4},{6,7},{7,6},{8,9},{9,8},{10,11... | collective-permute-start | bytes 3538952 | tf_op jit(solution)/shard_map/ppermute | solution.py:948
  96.8 18.5 %collective-permute-start.18 = (bf16[4,48,3072]{2,1,0:T(8,128)(2,1)}, bf16[4,48,3072]{2,1,0:T(8,128)(2,1)S(1)}, u32[]{:S(2)}, u32[]{:S(2)}) collective-permute-start(bf16[4,48,3072]{2,1,0:T(8,128)(2,1)} %collective-permute-done.13.refs_2_), channel_id=1, source_target_pairs={{0,1},{1,0},{2,3},{3,2},{4,5},{5,4},{6,7},{7,6},{8,9},{9,8},{10,11... | collective-permute-start | bytes 3538952 | tf_op jit(solution)/shard_map/ppermute | solution.py:948
  99.5 15.3 %collective-permute-start.15 = (bf16[2,48,3072]{2,1,0:T(8,128)(2,1)S(1)}, bf16[2,48,3072]{2,1,0:T(8,128)(2,1)S(1)}, u32[]{:S(2)}, u32[]{:S(2)}) collective-permute-start(bf16[2,48,3072]{2,1,0:T(8,128)(2,1)S(1)} %slice.340), channel_id=1, source_target_pairs={{0,2},{1,3},{2,0},{3,1},{4,6},{5,7},{6,4},{7,5},{8,10},{9,11},{10,... | collective-permute-start | bytes 1769480 | tf_op jit(solution)/shard_map/ppermute | solution.py:948
  100.3 15.0 %collective-permute-start.14 = (bf16[2,48,3072]{2,1,0:T(8,128)(2,1)S(1)}, bf16[2,48,3072]{2,1,0:T(8,128)(2,1)S(1)}, u32[]{:S(2)}, u32[]{:S(2)}) collective-permute-start(bf16[2,48,3072]{2,1,0:T(8,128)(2,1)S(1)} %slice.339), channel_id=1, source_target_pairs={{0,4},{1,5},{2,6},{3,7},{4,0},{5,1},{6,2},{7,3},{8,12},{9,13},{10,... | collective-permute-start | bytes 1769480 | tf_op jit(solution)/shard_map/ppermute | solution.py:948
  115.3 2.1 collective-permute-start.19
  115.4 2.8 collective-permute-start.20
  168.3 13.7 %collective-permute-start.21 = (bf16[4,4,48,3072]{3,2,1,0:T(8,128)(2,1)}, bf16[4,4,48,3072]{3,2,1,0:T(8,128)(2,1)}, u32[]{:S(2)}, u32[]{:S(2)}) collective-permute-start(bf16[4,4,48,3072]{3,2,1,0:T(8,128)(2,1)} %get-tuple-element.189), channel_id=1, source_target_pairs={{0,1},{1,0},{2,3},{3,2},{4,5},{5,4},{6,7},{7,6},{8,9},{9,8},{10,11... | collective-permute-start | bytes 14155784 | tf_op jit(solution)/shard_map/ppermute | solution.py:948
  168.6 13.4 %copy-start.1 = (bf16[4,4,48,3072]{3,2,1,0:T(8,128)(2,1)S(1)}, bf16[4,4,48,3072]{3,2,1,0:T(8,128)(2,1)}, u32[]{:S(2)}) copy-start(bf16[4,4,48,3072]{3,2,1,0:T(8,128)(2,1)} %get-tuple-element.230) | copy-start | bytes 14155780
  189.3 42.1 %collective-permute-start.23 = (bf16[1,48,3072]{2,1,0:T(8,128)(2,1)}, bf16[1,48,3072]{2,1,0:T(8,128)(2,1)S(1)}, u32[]{:S(2)}, u32[]{:S(2)}) collective-permute-start(bf16[1,48,3072]{2,1,0:T(8,128)(2,1)} %get-tuple-element.209), channel_id=1, source_target_pairs={{0,4},{1,5},{2,6},{3,7},{4,0},{5,1},{6,2},{7,3},{8,12},{9,13},{10,... | collective-permute-start | bytes 884744 | tf_op jit(solution)/shard_map/ppermute | solution.py:948
  190.5 40.9 %collective-permute-start.24 = (bf16[1,48,3072]{2,1,0:T(8,128)(2,1)S(1)}, bf16[1,48,3072]{2,1,0:T(8,128)(2,1)S(1)}, u32[]{:S(2)}, u32[]{:S(2)}) collective-permute-start(bf16[1,48,3072]{2,1,0:T(8,128)(2,1)S(1)} %get-tuple-element.210), channel_id=1, source_target_pairs={{0,2},{1,3},{2,0},{3,1},{4,6},{5,7},{6,4},{7,5},{8,10},{9,11},{10,... | collective-permute-start | bytes 884744 | tf_op jit(solution)/shard_map/ppermute | solution.py:948
  191.0 40.5 %collective-permute-start.22 = (bf16[2,48,3072]{2,1,0:T(8,128)(2,1)}, bf16[2,48,3072]{2,1,0:T(8,128)(2,1)S(1)}, u32[]{:S(2)}, u32[]{:S(2)}) collective-permute-start(bf16[2,48,3072]{2,1,0:T(8,128)(2,1)} %fusion.11), channel_id=1, source_target_pairs={{0,6},{1,7},{2,4},{3,5},{4,2},{5,3},{6,0},{7,1},{8,14},{9,15},{10,... | collective-permute-start | bytes 1769480 | tf_op jit(solution)/shard_map/ppermute | solution.py:948
  192.8 38.7 %collective-permute-start.25 = (bf16[3,48,3072]{2,1,0:T(8,128)(2,1)}, bf16[3,48,3072]{2,1,0:T(8,128)(2,1)S(1)}, u32[]{:S(2)}, u32[]{:S(2)}) collective-permute-start(bf16[3,48,3072]{2,1,0:T(8,128)(2,1)} %get-tuple-element.211), channel_id=1, source_target_pairs={{0,2},{1,3},{2,0},{3,1},{4,6},{5,7},{6,4},{7,5},{8,10},{9,11},{10,... | collective-permute-start | bytes 2654216 | tf_op jit(solution)/shard_map/ppermute | solution.py:948
  194.0 37.5 %collective-permute-start.26 = (bf16[3,48,3072]{2,1,0:T(8,128)(2,1)}, bf16[3,48,3072]{2,1,0:T(8,128)(2,1)}, u32[]{:S(2)}, u32[]{:S(2)}) collective-permute-start(bf16[3,48,3072]{2,1,0:T(8,128)(2,1)} %get-tuple-element.212), channel_id=1, source_target_pairs={{0,4},{1,5},{2,6},{3,7},{4,0},{5,1},{6,2},{7,3},{8,12},{9,13},{10,... | collective-permute-start | bytes 2654216 | tf_op jit(solution)/shard_map/ppermute | solution.py:948
  232.4 5.2 %collective-permute-start.27 = (bf16[4,4,48,1664]{3,2,1,0:T(8,128)(2,1)}, bf16[4,4,48,1664]{3,2,1,0:T(8,128)(2,1)S(1)}, u32[]{:S(2)}, u32[]{:S(2)}) collective-permute-start(bf16[4,4,48,1664]{3,2,1,0:T(8,128)(2,1)} %get-tuple-element.217), channel_id=1, source_target_pairs={{0,1},{1,0},{2,3},{3,2},{4,5},{5,4},{6,7},{7,6},{8,9},{9,8},{10,11... | collective-permute-start | bytes 7667720 | tf_op jit(solution)/shard_map/ppermute | solution.py:948
  234.9 11.3 %collective-permute-start.30 = (bf16[48,3072]{1,0:T(8,128)(2,1)S(1)}, bf16[48,3072]{1,0:T(8,128)(2,1)S(1)}, u32[]{:S(2)}, u32[]{:S(2)}) collective-permute-start(bf16[48,3072]{1,0:T(8,128)(2,1)S(1)} %get-tuple-element.259), channel_id=1, source_target_pairs={{0,8},{1,9},{2,10},{3,11},{4,12},{5,13},{6,14},{7,15},{8,16},{9,17... | collective-permute-start | bytes 884744 | tf_op jit(solution)/shard_map/ppermute | solution.py:948
  235.3 10.8 %collective-permute-start.29 = (bf16[48,3072]{1,0:T(8,128)(2,1)S(1)}, bf16[48,3072]{1,0:T(8,128)(2,1)S(1)}, u32[]{:S(2)}, u32[]{:S(2)}) collective-permute-start(bf16[48,3072]{1,0:T(8,128)(2,1)S(1)} %get-tuple-element.260), channel_id=1, source_target_pairs={{0,4},{1,5},{2,6},{3,7},{4,0},{5,1},{6,2},{7,3},{8,12},{9,13},{10,... | collective-permute-start | bytes 884744 | tf_op jit(solution)/shard_map/ppermute | solution.py:948
  236.8 12.9 %copy-start.9 = (bf16[2,48,3072]{2,1,0:T(8,128)(2,1)S(1)}, bf16[2,48,3072]{2,1,0:T(8,128)(2,1)}, u32[]{:S(2)}) copy-start(bf16[2,48,3072]{2,1,0:T(8,128)(2,1)} %copy-done.8) | copy-start | bytes 1769476
  236.8 9.3 %collective-permute-start.28 = (bf16[48,3072]{1,0:T(8,128)(2,1)S(1)}, bf16[48,3072]{1,0:T(8,128)(2,1)S(1)}, u32[]{:S(2)}, u32[]{:S(2)}) collective-permute-start(bf16[48,3072]{1,0:T(8,128)(2,1)S(1)} %get-tuple-element.261), channel_id=1, source_target_pairs={{0,2},{1,3},{2,0},{3,1},{4,6},{5,7},{6,4},{7,5},{8,10},{9,11},{10,... | collective-permute-start | bytes 884744 | tf_op jit(solution)/shard_map/ppermute | solution.py:948
  246.1 8.8 %copy-start.6 = (bf16[1024,768]{1,0:T(8,128)(2,1)S(1)}, bf16[1024,768]{1,0:T(8,128)(2,1)}, u32[]{:S(2)}) copy-start(bf16[1024,768]{1,0:T(8,128)(2,1)} %get-tuple-element.236) | copy-start | bytes 4718596
  246.1 26.6 %collective-permute-start.31 = (bf16[4,48,1664]{2,1,0:T(8,128)(2,1)S(1)}, bf16[4,48,1664]{2,1,0:T(8,128)(2,1)S(1)}, u32[]{:S(2)}, u32[]{:S(2)}) collective-permute-start(bf16[4,48,1664]{2,1,0:T(8,128)(2,1)S(1)} %get-tuple-element.227), channel_id=1, source_target_pairs={{0,2},{1,3},{2,0},{3,1},{4,6},{5,7},{6,4},{7,5},{8,10},{9,11},{10,... | collective-permute-start | bytes 1916936 | tf_op jit(solution)/shard_map/ppermute | solution.py:948
  247.7 29.4 %collective-permute-start.32 = (bf16[4,48,1664]{2,1,0:T(8,128)(2,1)S(1)}, bf16[4,48,1664]{2,1,0:T(8,128)(2,1)S(1)}, u32[]{:S(2)}, u32[]{:S(2)}) collective-permute-start(bf16[4,48,1664]{2,1,0:T(8,128)(2,1)S(1)} %get-tuple-element.228), channel_id=1, source_target_pairs={{0,4},{1,5},{2,6},{3,7},{4,0},{5,1},{6,2},{7,3},{8,12},{9,13},{10,... | collective-permute-start | bytes 1916936 | tf_op jit(solution)/shard_map/ppermute | solution.py:948
  248.5 28.6 %collective-permute-start.33 = (bf16[4,48,1664]{2,1,0:T(8,128)(2,1)S(1)}, bf16[4,48,1664]{2,1,0:T(8,128)(2,1)S(1)}, u32[]{:S(2)}, u32[]{:S(2)}) collective-permute-start(bf16[4,48,1664]{2,1,0:T(8,128)(2,1)S(1)} %get-tuple-element.229), channel_id=1, source_target_pairs={{0,6},{1,7},{2,4},{3,5},{4,2},{5,3},{6,0},{7,1},{8,14},{9,15},{10,... | collective-permute-start | bytes 1916936 | tf_op jit(solution)/shard_map/ppermute | solution.py:948
  251.9 10.5 %collective-permute-start.35 = (bf16[48,3072]{1,0:T(8,128)(2,1)S(1)}, bf16[48,3072]{1,0:T(8,128)(2,1)S(1)}, u32[]{:S(2)}, u32[]{:S(2)}) collective-permute-start(bf16[48,3072]{1,0:T(8,128)(2,1)S(1)} %get-tuple-element.256), channel_id=1, source_target_pairs={{0,24},{1,25},{2,26},{3,27},{4,28},{5,29},{6,30},{7,31},{8,0},{9,1... | collective-permute-start | bytes 884744 | tf_op jit(solution)/shard_map/ppermute | solution.py:948
  254.9 17.8 %collective-permute-start.34 = (bf16[48,3072]{1,0:T(8,128)(2,1)S(1)}, bf16[48,3072]{1,0:T(8,128)(2,1)S(1)}, u32[]{:S(2)}, u32[]{:S(2)}) collective-permute-start(bf16[48,3072]{1,0:T(8,128)(2,1)S(1)} %get-tuple-element.257), channel_id=1, source_target_pairs={{0,16},{1,17},{2,18},{3,19},{4,20},{5,21},{6,22},{7,23},{8,24},{9,... | collective-permute-start | bytes 884744 | tf_op jit(solution)/shard_map/ppermute | solution.py:948
  277.3 3.4 %collective-permute-start.39 = (f32[24,1536]{1,0:T(8,128)S(1)}, f32[24,1536]{1,0:T(8,128)S(1)}, u32[]{:S(2)}, u32[]{:S(2)}) collective-permute-start(f32[24,1536]{1,0:T(8,128)S(1)} %slice_select_fusion.2), channel_id=1, source_target_pairs={{0,1},{1,0},{2,3},{3,2},{4,5},{5,4},{6,7},{7,6},{8,9},{9,8},{10,11... | collective-permute-start | bytes 442376 | tf_op jit(solution)/shard_map/ppermute | solution.py:948
  277.8 6.9 %collective-permute-start.38 = (bf16[48,1664]{1,0:T(8,128)(2,1)S(1)}, bf16[48,1664]{1,0:T(8,128)(2,1)S(1)}, u32[]{:S(2)}, u32[]{:S(2)}) collective-permute-start(bf16[48,1664]{1,0:T(8,128)(2,1)S(1)} %get-tuple-element.270), channel_id=1, source_target_pairs={{0,24},{1,25},{2,26},{3,27},{4,28},{5,29},{6,30},{7,31},{8,0},{9,1... | collective-permute-start | bytes 479240 | tf_op jit(solution)/shard_map/ppermute | solution.py:948
  279.4 14.8 %collective-permute-start.37 = (bf16[48,1664]{1,0:T(8,128)(2,1)S(1)}, bf16[48,1664]{1,0:T(8,128)(2,1)S(1)}, u32[]{:S(2)}, u32[]{:S(2)}) collective-permute-start(bf16[48,1664]{1,0:T(8,128)(2,1)S(1)} %get-tuple-element.271), channel_id=1, source_target_pairs={{0,16},{1,17},{2,18},{3,19},{4,20},{5,21},{6,22},{7,23},{8,24},{9,... | collective-permute-start | bytes 479240 | tf_op jit(solution)/shard_map/ppermute | solution.py:948
  279.4 14.8 %collective-permute-start.36 = (bf16[48,1664]{1,0:T(8,128)(2,1)S(1)}, bf16[48,1664]{1,0:T(8,128)(2,1)S(1)}, u32[]{:S(2)}, u32[]{:S(2)}) collective-permute-start(bf16[48,1664]{1,0:T(8,128)(2,1)S(1)} %get-tuple-element.272), channel_id=1, source_target_pairs={{0,8},{1,9},{2,10},{3,11},{4,12},{5,13},{6,14},{7,15},{8,16},{9,17... | collective-permute-start | bytes 479240 | tf_op jit(solution)/shard_map/ppermute | solution.py:948
  295.5 1.4 collective-permute-start.40
  (16 other events, 50.9 us)

commit v6 on v5

--- a/solution.py
+++ b/solution.py
@@ -155,62 +155,64 @@
     return pltpu.make_async_copy(src, dst, sem)
 
 
-def chips_of(dims, where_ref):
+def places(dims, where_ref):
     z_n, y_n, x_n = dims
     zi, yi, xi = [where_ref[i] for i in range(3)]
-    for i in range(y_n * x_n):
-        for j in range(z_n):
-            yield i, j, lax.rem(zi + j, z_n), lax.rem(yi + i // x_n, y_n), lax.rem(xi + i % x_n, x_n)
-
-
-def piece_at(dims, arrays, i, j):
-    at = i * dims[0] + j
-    for a in arrays:
-        if at < a.shape[0]:
-            return a.at[at]
-        at -= a.shape[0]
-
-
-def load_columns(dims, where_ref, own, oth, first, cols, dst, sem):
+    return [
+        (lax.rem(y - yi + y_n, y_n) * x_n + lax.rem(x - xi + x_n, x_n)) * z_n + lax.rem(z - zi + z_n, z_n)
+        for z in range(z_n)
+        for y in range(y_n)
+        for x in range(x_n)
+    ]
+
+
+def array_spans(arrays):
+    at = 0
+    for k, a in enumerate(arrays):
+        yield k, a, pl.ds(at, a.shape[0])
+        at += a.shape[0]
+
+
+def load_columns(where_ref, own, oth, first, cols, dst, sem):
     ci = where_ref[3]
-    for i, j, z, y, x in chips_of(dims, where_ref):
-        for half, src in ((ci, own), (1 - ci, oth)):
-            block = piece_at(dims, src, i, j).at[:, pl.ds(first, cols)]
-            local_copy(block, dst.at[half, z, y, x], sem.at[half, z, y, x]).start()
-
-
-def wait_columns(dims, dst, sem, half):
-    for z in range(dims[0]):
-        for y in range(dims[1]):
-            for x in range(dims[2]):
-                block = dst.at[half, z, y, x]
-                local_copy(block, block, sem.at[half, z, y, x]).wait()
-
-
-def flat2(value):
-    return value.reshape(-1, value.shape[-1])
-
-
-def store_columns(dims, where_ref, src, own, oth, half, first, cols, sem):
+    for half, arrays in ((ci, own), (1 - ci, oth)):
+        for k, a, span in array_spans(arrays):
+            local_copy(a.at[:, :, pl.ds(first, cols)], dst.at[half, span], sem.at[half, k]).start()
+
+
+def wait_columns(own, dst, sem, half):
+    for k, _, span in array_spans(own):
+        block = dst.at[half, span]
+        local_copy(block, block, sem.at[half, k]).wait()
+
+
+def whole_rows(dims, where_ref, scr, half, cols=slice(None)):
+    return jnp.concatenate([scr[half, p, :, cols] for p in places(dims, where_ref)], axis=0)
+
+
+def put_rows(dims, where_ref, scr, lead, value):
+    n = scr.shape[-2]
+    for i, p in enumerate(places(dims, where_ref)):
+        scr[lead + (p,)] = value[i * n : (i + 1) * n]
+
+
+def store_columns(where_ref, src, own, oth, half, first, cols, sem):
     ci = where_ref[3]
     for other, out in ((False, own), (True, oth)):
 
         @pl.when((half != ci) if other else (half == ci))
         def _():
-            for i, j, z, y, x in chips_of(dims, where_ref):
-                local_copy(src.at[z, y, x], out.at[i, j, :, pl.ds(first, cols)], sem.at[i, j]).start()
-
-
-def wait_store(dims, src, out, first, cols, sem):
-    for i in range(dims[1] * dims[2]):
-        for j in range(dims[0]):
-            local_copy(src.at[0, 0, 0], out.at[i, j, :, pl.ds(first, cols)], sem.at[i, j]).wait()
-
-
-def weight_scratch(dims, n, cols):
+            local_copy(src, out.at[:, :, pl.ds(first, cols)], sem).start()
+
+
+def wait_store(src, sem):
+    local_copy(src, src, sem).wait()
+
+
+def weight_scratch(dims, n, cols, arrays):
     return [
-        pltpu.VMEM((2,) + dims + (n, cols), BF),
-        pltpu.SemaphoreType.DMA((2,) + dims),
+        pltpu.VMEM((2, math.prod(dims), n, cols), BF),
+        pltpu.SemaphoreType.DMA((2, arrays)),
     ]
 
 
@@ -313,16 +315,13 @@
     n_ref, nt_ref, vec_ref, t_scr, t_sem = refs[count:]
     rows, d = x_ref.shape
     table_at = own[0].shape[-1] - 128
-    for i, j, z, y, x in chips_of(dims, where_ref):
-        block = piece_at(dims, own, i, j).at[:, pl.ds(table_at, 128)]
-        local_copy(block, t_scr.at[z, y, x], t_sem.at[z, y, x]).start()
-    for z in range(dims[0]):
-        for y in range(dims[1]):
-            for x in range(dims[2]):
-                block = t_scr.at[z, y, x]
-                local_copy(block, block, t_sem.at[z, y, x]).wait()
+    copies = [local_copy(a.at[:, :, pl.ds(table_at, 128)], t_scr.at[0, span], t_sem.at[i]) for i, a, span in array_spans(own)]
+    for c in copies:
+        c.start()
+    for c in copies:
+        c.wait()
     vec_ref[...] = jnp.zeros_like(vec_ref)
-    unpack_vectors(flat2(t_scr[...]), d, devices, vec_ref)
+    unpack_vectors(whole_rows(dims, where_ref, t_scr, 0), d, devices, vec_ref)
     for r in range(0, rows, 256):
         xhat, _ = normalize(x_ref[r : r + 256, :].astype(F32))
         normed = (xhat * vec_ref[0:1, :d] + vec_ref[1:2, :d]).astype(BF)
@@ -341,7 +340,9 @@
             jax.ShapeDtypeStruct((rows, d), BF), jax.ShapeDtypeStruct((d, rows), BF),
             jax.ShapeDtypeStruct((8, 4 * d), F32),
         ],
-        scratch_shapes=[pltpu.VMEM(dims + (own[0].shape[1], 128), BF), pltpu.SemaphoreType.DMA(dims)],
+        scratch_shapes=[
+            pltpu.VMEM((1, math.prod(dims), own[0].shape[1], 128), BF), pltpu.SemaphoreType.DMA((len(own),)),
+        ],
         compiler_params=params(),
         cost_estimate=cost(1e9, rows * d * 6),
         name="first_norm",
@@ -357,7 +358,7 @@
 
     @pl.when(step == 0)
     def _():
-        load_columns(dims, where_ref, own, oth, 0, cols, w_scr, w_sem)
+        load_columns(where_ref, own, oth, 0, cols, w_scr, w_sem)
         zero = jnp.zeros((1, 128), F32)
         pairs = d // 128
         for p in range(pairs):
@@ -366,13 +367,13 @@
             bias_scr[half, :, at : at + 128] = vec_ref[2:3, p * 128 : (p + 1) * 128]
             bias_scr[half, :, at + 128 : at + 256] = zero
             bias_scr[half, :, at + 256 : at + 384] = vec_ref[2:3, d + p * 128 : d + (p + 1) * 128]
-        wait_columns(dims, w_scr, w_sem, 0)
+        wait_columns(own, w_scr, w_sem, 0)
 
     @pl.when(step == 1)
     def _():
-        wait_columns(dims, w_scr, w_sem, 1)
-
-    w = flat2(w_scr[step])
+        wait_columns(own, w_scr, w_sem, 1)
+
+    w = whole_rows(dims, where_ref, w_scr, step)
     for r in range(0, rows, 256):
         o_ref[r : r + 256, :] = (dot(n_ref[r : r + 256, :], w) + bias_scr[step]).astype(BF)
 
@@ -387,7 +388,7 @@
         in_specs=[SMEM, full_spec((rows, d)), full_spec(vec.shape)] + [ANY] * (2 * len(own)),
         out_specs=pl.BlockSpec((rows, cols), lambda j: (0, j)),
         out_shape=jax.ShapeDtypeStruct((rows, 2 * cols), BF),
-        scratch_shapes=weight_scratch(dims, n, cols) + [pltpu.VMEM((2, 1, cols), F32)],
+        scratch_shapes=weight_scratch(dims, n, cols, len(own)) + [pltpu.VMEM((2, 1, cols), F32)],
         compiler_params=params(),
         cost_estimate=cost(4 * rows * d * cols, rows * d * 8 + d * cols * 4),
         name="qkv",
@@ -401,12 +402,12 @@
 
     @pl.when(pl.program_id(0) == 0)
     def _():
-        load_columns(dims, where_ref, own, oth, first, w_scr.shape[-1], w_scr, w_sem)
+        load_columns(where_ref, own, oth, first, w_scr.shape[-1], w_scr, w_sem)
         for h in range(2):
-            wait_columns(dims, w_scr, w_sem, h)
+            wait_columns(own, w_scr, w_sem, h)
 
     a = jnp.concatenate([a0_ref[...], a1_ref[...]], axis=1)
-    branch = jnp.concatenate([dot(a, flat2(w_scr[h])) for h in range(2)], axis=1) + vec_ref[3:4, :d]
+    branch = jnp.concatenate([dot(a, whole_rows(dims, where_ref, w_scr, h)) for h in range(2)], axis=1) + vec_ref[3:4, :d]
     middle = x_ref[...].astype(F32) + BS * branch
     mid_ref[...] = middle
     xhat, _ = normalize(middle)
@@ -424,7 +425,7 @@
         + [full_spec(vec.shape)] + [ANY] * (2 * len(own)),
         out_specs=[row, row],
         out_shape=[jax.ShapeDtypeStruct((rows, d), F32), jax.ShapeDtypeStruct((rows, d), BF)],
-        scratch_shapes=weight_scratch(dims, own[0].shape[1], d // 2),
+        scratch_shapes=weight_scratch(dims, own[0].shape[1], d // 2, len(own)),
         compiler_params=params(),
         cost_estimate=cost(2 * rows * d * d, rows * d * 10 + d * d * 2),
         name="proj",
@@ -435,31 +436,28 @@
     own, oth = refs[:count], refs[count : 2 * count]
     (
         out_ref, gn_ref, gfb_ref, gob_ref, g_own, g_oth,
-        mid_scr, mid_sem, nt_scr, mg_scr, acc_scr, act_scr, gp_scr, f_scr, f_sem, o_scr, o_sem, gf_scr, gf_sem, go_scr, go_sem,
+        mid_scr, mid_sem, nt_scr, mg_scr, acc_scr, act_scr, gp_scr, w_scr, w_sem, gf_scr, gf_sem, go_scr, go_sem,
     ) = refs[2 * count :]
     z_n, y_n, x_n = dims
     zi, yi, xi, ci = [where_ref[i] for i in range(4)]
     j = pl.program_id(0)
-    blocks = o_scr.shape[0]
     rows, d = n_ref.shape
-    n = own[0].shape[1]
-    wide = f_scr.shape[-1]
+    n, total_cols = w_scr.shape[-2:]
+    wide = total_cols - 2 * d
+    blocks = 2 * wide // d
     parts = d // n
     br = 512
 
+    def hidden_rows(q):
+        at = j * parts + q
+        dev, t = at // 2, lax.rem(at, 2)
+        x, y, z = lax.rem(dev // 2, x_n), lax.rem(dev // (2 * x_n), y_n), dev // (2 * x_n * y_n)
+        piece = lax.rem(y - yi + y_n, y_n) * x_n + lax.rem(x - xi + x_n, x_n)
+        return lax.rem(dev, 2), piece * z_n + lax.rem(z - zi + z_n, z_n), pl.multiple_of(t * d, 128)
+
     @pl.when(j == 0)
     def _():
-        load_columns(dims, where_ref, own, oth, 0, wide, f_scr, f_sem)
-        for i, s, z, y, x in chips_of(dims, where_ref):
-            for core, src in ((ci, own), (1 - ci, oth)):
-                for t in range(2):
-                    at = (((z * y_n + y) * x_n + x) * 2 + core) * 2 + t
-                    q = lax.rem(at, parts)
-                    local_copy(
-                        piece_at(dims, src, i, s).at[:, pl.ds(wide + t * d, d)],
-                        o_scr.at[at // parts, pl.ds(pl.multiple_of(q * n, 16), n), :],
-                        o_sem.at[at // parts, q],
-                    ).start()
+        load_columns(where_ref, own, oth, 0, total_cols, w_scr, w_sem)
         local_copy(mid_ref, mid_scr, mid_sem).start()
         nt_scr[...] = n_ref[...].T
         total = jnp.zeros_like(gob_ref)
@@ -468,20 +466,14 @@
             mg_scr[r : r + br, :] = mg
             total += jnp.sum(mg.astype(F32), axis=0, keepdims=True)
         gob_ref[...] = total
-        wait_columns(dims, f_scr, f_sem, 0)
-
-    @pl.when(j == blocks // 2)
-    def _():
-        wait_columns(dims, f_scr, f_sem, 1)
-
-    for q in range(parts):
-        part = o_scr.at[j, pl.ds(q * n, n), :]
-        local_copy(part, part, o_sem.at[j, q]).wait()
+        for h in range(2):
+            wait_columns(own, w_scr, w_sem, h)
 
     half = j // (blocks // 2)
     first = pl.multiple_of(lax.rem(j, blocks // 2) * d, 128)
-    wf = flat2(f_scr[half, :, :, :, :, pl.ds(first, d)])
-    wo = o_scr[j]
+    wf = whole_rows(dims, where_ref, w_scr, half, pl.ds(first, d))
+    spots = [hidden_rows(q) for q in range(parts)]
+    wo = jnp.concatenate([w_scr[c, p, :, pl.ds(wide + at, d)] for c, p, at in spots], axis=0)
     fb = vec_ref[6:7, pl.ds(pl.multiple_of(j * d, 128), d)]
     bias_sum = jnp.zeros((1, d), F32)
     starts = list(range(0, rows, br))
@@ -519,36 +511,24 @@
     behind(*waiting)
 
     gfb_ref[...] = bias_sum
-    gf_scr[j] = dot(nt_scr[...], gp_scr[...]).astype(BF).reshape(gf_scr.shape[1:])
-    store_columns(dims, where_ref, gf_scr.at[j], g_own, g_oth, half, first, d, gf_sem.at[j])
-    go_scr[j] = dot_0(act_scr[...], mg_scr[...]).astype(BF)
-    for q in range(parts):
-        at = j * parts + q
-        dev, t = at // 2, lax.rem(at, 2)
-        core = lax.rem(dev, 2)
-        x = lax.rem(dev // 2, x_n)
-        y = lax.rem(dev // (2 * x_n), y_n)
-        z = dev // (2 * x_n * y_n)
-        piece = lax.rem(y - yi + y_n, y_n) * x_n + lax.rem(x - xi + x_n, x_n)
-        slot = lax.rem(z - zi + z_n, z_n)
-        to = pl.ds(pl.multiple_of(wide + t * d, 128), d)
-        for other, out in ((False, g_own), (True, g_oth)):
-
-            @pl.when((core != ci) if other else (core == ci))
-            def _():
-                local_copy(go_scr.at[j, pl.ds(q * n, n), :], out.at[piece, slot, :, to], go_sem.at[j, q]).start()
+    put_rows(dims, where_ref, gf_scr, (j,), dot(nt_scr[...], gp_scr[...]).astype(BF))
+    store_columns(where_ref, gf_scr.at[j], g_own, g_oth, half, first, d, gf_sem.at[j])
+    go = dot_0(act_scr[...], mg_scr[...]).astype(BF)
+    for q, (c, p, at) in enumerate(spots):
+        go_scr[c, p, :, pl.ds(at, d)] = go[q * n : (q + 1) * n]
 
     @pl.when(j == blocks - 1)
     def _():
+        for c in range(2):
+            store_columns(where_ref, go_scr.at[c], g_own, g_oth, c, wide, 2 * d, go_sem.at[c])
         local_copy(mid_ref, mid_scr, mid_sem).wait()
         for r in range(0, rows, br):
             rr = slice(r, r + br)
             out_ref[rr, :] = (mid_scr[rr, :] + BS * (acc_scr[rr, :] + vec_ref[7:8, :d])).astype(BF)
         for b in range(blocks):
-            wait_store(dims, gf_scr.at[b], g_own, 0, d, gf_sem.at[b])
-            for q in range(parts):
-                part = go_scr.at[b, pl.ds(q * n, n), :]
-                local_copy(part, part, go_sem.at[b, q]).wait()
+            wait_store(gf_scr.at[b], gf_sem.at[b])
+        for c in range(2):
+            wait_store(go_scr.at[c], go_sem.at[c])
 
 
 def mlp_call(dims, where, normed, cot, middle, vec, own, oth):
@@ -556,9 +536,9 @@
     n, cols = own[0].shape[1:]
     wide = cols - 2 * d
     blocks = 2 * wide // d
-    count = dims[1] * dims[2]
     act = full_spec((rows, d))
-    piece = jax.ShapeDtypeStruct((count, dims[0], n, cols), BF)
+    chips = math.prod(dims)
+    piece = jax.ShapeDtypeStruct((chips, n, cols), BF)
     return pl.pallas_call(
         functools.partial(mlp_kernel, dims, len(own)),
         grid=(blocks,),
@@ -575,11 +555,10 @@
             pltpu.VMEM((rows, d), F32), pltpu.SemaphoreType.DMA(()), pltpu.VMEM((d, rows), BF), pltpu.VMEM((rows, d), BF), pltpu.VMEM((rows, d), F32),
             pltpu.VMEM((rows, d), BF), pltpu.VMEM((rows, d), BF),
         ]
-        + weight_scratch(dims, n, wide)
+        + weight_scratch(dims, n, cols, len(own))
         + [
-            pltpu.VMEM((blocks, d, d), BF), pltpu.SemaphoreType.DMA((blocks, d // n)),
-            pltpu.VMEM((blocks,) + dims + (n, d), BF), pltpu.SemaphoreType.DMA((blocks, count, dims[0])),
-            pltpu.VMEM((blocks, d, d), BF), pltpu.SemaphoreType.DMA((blocks, d // n)),
+            pltpu.VMEM((blocks, chips, n, d), BF), pltpu.SemaphoreType.DMA((blocks,)),
+            pltpu.VMEM((2, chips, n, 2 * d), BF), pltpu.SemaphoreType.DMA((2,)),
         ],
         compiler_params=params(),
         cost_estimate=cost(24 * rows * d * wide, 30e6, 2 * rows * wide),
@@ -598,13 +577,13 @@
 
     @pl.when(i == 0)
     def _():
-        load_columns(dims, where_ref, own, oth, first, m, w_scr, w_sem)
+        load_columns(where_ref, own, oth, first, m, w_scr, w_sem)
         gw_acc[...] = jnp.zeros_like(gw_acc)
         gg_ref[...] = jnp.zeros_like(gg_ref)
         gb_ref[...] = jnp.zeros_like(gb_ref)
         gpb_ref[...] = jnp.zeros_like(gpb_ref)
         for h in range(2):
-            wait_columns(dims, w_scr, w_sem, h)
+            wait_columns(own, w_scr, w_sem, h)
 
     dy = gn_ref[...]
     xhat, rstd = normalize(mid_ref[...])
@@ -616,7 +595,7 @@
     gpb_ref[...] += jnp.sum(pg.astype(F32), axis=0, keepdims=True)
     a = jnp.concatenate([a0_ref[...], a1_ref[...]], axis=1)
     gw_acc[...] += dot_0(a, pg)
-    ga = (dot_t(pg[:, :m], flat2(w_scr[0])) + dot_t(pg[:, m:], flat2(w_scr[1]))).astype(BF)
+    ga = sum(dot_t(pg[:, h * m : (h + 1) * m], whole_rows(dims, where_ref, w_scr, h)) for h in range(2)).astype(BF)
     ga_ref[...] = ga
     prod = ga.astype(F32) * a.astype(F32)
     high = prod.astype(BF)
@@ -648,7 +627,7 @@
             jax.ShapeDtypeStruct((16, rows), F32),
             vshape, vshape, vshape,
         ],
-        scratch_shapes=[pltpu.VMEM((d, d), F32)] + weight_scratch(dims, own[0].shape[1], d // 2),
+        scratch_shapes=[pltpu.VMEM((d, d), F32)] + weight_scratch(dims, own[0].shape[1], d // 2, len(own)),
         compiler_params=params(),
         cost_estimate=cost(4 * rows * d * d, rows * d * 16),
         name="proj_back",
@@ -735,12 +714,12 @@
 
     @pl.when(i == 0)
     def _():
-        load_columns(dims, where_ref, own, oth, 0, groups * 384, w_scr, w_sem)
+        load_columns(where_ref, own, oth, 0, groups * 384, w_scr, w_sem)
         local_copy(nt_ref, nt_scr, nt_sem).start()
         local_copy(gm_ref, gm_scr, gm_sem).start()
         for h in range(2):
-            p_scr[h] = gwp_ref[:, h * (d // 2) : (h + 1) * (d // 2)].reshape(p_scr.shape[1:])
-            store_columns(dims, where_ref, p_scr.at[h], g_own, g_oth, h, proj_at, d // 2, p_sem.at[h])
+            put_rows(dims, where_ref, p_scr, (h,), gwp_ref[:, h * (d // 2) : (h + 1) * (d // 2)])
+            store_columns(where_ref, p_scr.at[h], g_own, g_oth, h, proj_at, d // 2, p_sem.at[h])
 
     for h, j_ref in enumerate((j0_ref, j1_ref)):
         row = (i * 2 + h) * 2
@@ -750,7 +729,7 @@
     def _():
         local_copy(nt_ref, nt_scr, nt_sem).wait()
         for h in range(2):
-            wait_columns(dims, w_scr, w_sem, h)
+            wait_columns(own, w_scr, w_sem, h)
 
     first = pl.multiple_of(i * 384, 128)
     dj = dj_scr[...]
@@ -760,9 +739,9 @@
             qv_scr[:, pl.ds(pl.multiple_of(off + (i * 2 + h) * 128, 128), 128)] = jnp.sum(part, axis=0, keepdims=True)
     gw = dot(nt_scr[...], dj).astype(BF)
     for h in range(2):
-        gw_scr[i, h] = gw[:, h * 384 : (h + 1) * 384].reshape(gw_scr.shape[2:])
-        store_columns(dims, where_ref, gw_scr.at[i, h], g_own, g_oth, h, first, 384, gw_sem.at[i, h])
-    w = jnp.concatenate([flat2(w_scr[h, :, :, :, :, pl.ds(first, 384)]) for h in range(2)], axis=1)
+        put_rows(dims, where_ref, gw_scr, (i, h), gw[:, h * 384 : (h + 1) * 384])
+        store_columns(where_ref, gw_scr.at[i, h], g_own, g_oth, h, first, 384, gw_sem.at[i, h])
+    w = jnp.concatenate([whole_rows(dims, where_ref, w_scr, h, pl.ds(first, 384)) for h in range(2)], axis=1)
     for r in range(0, rows, br):
         back = dot_t(dj[r : r + br, :], w)
         gn_scr[r : r + br, :] = jnp.where(i == 0, back, gn_scr[r : r + br, :] + back)
@@ -785,15 +764,15 @@
                 "g2": gg2_ref[...], "b2": gb2_ref[...], "ob": gob_ref[...],
             },
             d, devices,
-        ).reshape(t_scr.shape)
-        t_scr[...] = table
+        )
+        put_rows(dims, where_ref, t_scr, (), table)
         for h in range(2):
-            store_columns(dims, where_ref, t_scr, g_own, g_oth, h, table_at, 128, t_sem.at[h])
+            store_columns(where_ref, t_scr, g_own, g_oth, h, table_at, 128, t_sem.at[h])
         for h in range(2):
             for b in range(groups):
-                wait_store(dims, gw_scr.at[b, h], g_own, 0, 384, gw_sem.at[b, h])
-            wait_store(dims, p_scr.at[h], g_own, proj_at, d // 2, p_sem.at[h])
-            wait_store(dims, t_scr, g_own, table_at, 128, t_sem.at[h])
+                wait_store(gw_scr.at[b, h], gw_sem.at[b, h])
+            wait_store(p_scr.at[h], p_sem.at[h])
+            wait_store(t_scr, t_sem.at[h])
 
 
 def attn_back_call(dims, where, joined, ga, lse, delta, seg_row, seg_col, x, vec, own, oth, vectors, gm, nt, devices):
@@ -801,8 +780,8 @@
     n = own[0].shape[1]
     groups = d // 256
     act = full_spec((rows, d))
-    count = dims[1] * dims[2]
-    piece = jax.ShapeDtypeStruct((count, dims[0], n, groups * 384 + d // 2 + 128), BF)
+    chips = math.prod(dims)
+    piece = jax.ShapeDtypeStruct((chips, n, groups * 384 + d // 2 + 128), BF)
     return pl.pallas_call(
         functools.partial(attn_back_kernel, dims, len(own), devices),
         grid=(groups,),
@@ -817,14 +796,14 @@
         + [full_spec(v.shape) for v in vectors] + [ANY] * (2 + 2 * len(own)),
         out_specs=[act, ANY, ANY],
         out_shape=[jax.ShapeDtypeStruct((rows, d), BF), piece, piece],
-        scratch_shapes=weight_scratch(dims, n, groups * 384)
+        scratch_shapes=weight_scratch(dims, n, groups * 384, len(own))
         + [
             pltpu.VMEM((d, rows), BF), pltpu.SemaphoreType.DMA(()), pltpu.VMEM((rows, d), F32),
             pltpu.VMEM((rows, d), F32), pltpu.SemaphoreType.DMA(()), pltpu.VMEM((rows, 768), BF),
             pltpu.VMEM((128, rows), F32), pltpu.VMEM((128, rows), F32),
-            pltpu.VMEM((groups, 2) + dims + (n, 384), BF), pltpu.SemaphoreType.DMA((groups, 2, count, dims[0])),
-            pltpu.VMEM((2,) + dims + (n, d // 2), BF), pltpu.SemaphoreType.DMA((2, count, dims[0])),
-            pltpu.VMEM(dims + (n, 128), BF), pltpu.SemaphoreType.DMA((2, count, dims[0])),
+            pltpu.VMEM((groups, 2, chips, n, 384), BF), pltpu.SemaphoreType.DMA((groups, 2)),
+            pltpu.VMEM((2, chips, n, d // 2), BF), pltpu.SemaphoreType.DMA((2,)),
+            pltpu.VMEM((chips, n, 128), BF), pltpu.SemaphoreType.DMA((2,)),
             pltpu.VMEM((1, 2 * d), F32),
         ],
         compiler_params=params(),
@@ -907,13 +886,13 @@
         return listed
 
     def scatter(self, own, oth):
-        pair = self.pick([own[0, 0], oth[0, 0]])
+        pair = self.pick([own[0], oth[0]])
         m = pair[0].shape[1]
         mine = lax.psum_scatter(jnp.concatenate(pair, axis=1), AXES, scatter_dimension=0, tiled=True).astype(F32)
         return mine[:, :m], mine[:, m:]
 
     def scatter_hidden(self, own, oth):
-        pair = self.pick([own[0, 0], oth[0, 0]])
+        pair = self.pick([own[0], oth[0]])
         d = pair[0].shape[0]
         wide = pair[0].shape[1] - 2 * d
         fc = self.scatter(own[..., :wide], oth[..., :wide])
@@ -1090,6 +1069,7 @@
     gm, ga, gw_proj, delta, gg2, gb2, gpb = proj_back_call(dims, where, gn, middle, cot, att, vec, *attn_w)
     (m_oth,) = swap([m_oth])
     ga, delta, m_own, m_oth = together(ga, delta, m_own, m_oth)
+    m_own, m_oth = [v.reshape(-1, dims[0], *v.shape[1:]) for v in (m_own, m_oth)]
 
     def chip_sum(i, part):
         return add_all([part(m_own[i]), part(m_oth[i])]).astype(BF)
@@ -1118,7 +1098,7 @@
     x_one = send(chip_total(1, 0, [by_y[0]]), dx=1)
     y_one = send(chip_total(2, 3, [by_x[0]]), dy=1)
     b = {1: send(chip_total(0, 1, [from_x[0], from_y[1], corners[0]]), dz=1)}
-    e = links.add_core(g_own, g_oth)
+    e = links.add_core(*[v.reshape(-1, dims[0], *v.shape[1:]) for v in (g_own, g_oth)])
     e, x_one, y_one, gx, out, m_own, m_oth, b = together(e, x_one, y_one, gx, out, m_own, m_oth, b)
 
     e_near = near(e)

time: 304 us -> 300 us (0.987)
  Pallas kernels: 138 us -> 129 us
  waiting for transfers between devices: 63.7 us -> 70.4 us
    ppermute x41, waiting for transfers between devices: 63.7 us -> 70.4 us  [send(): return lax.ppermute(array, AXES, pairs)]
    pallas_call x1, Pallas kernels: 36.9 us -> 31.1 us  [attn_back_call(): pl.pallas_call(functools.partial(attn_back_kernel, dims, len(own), device...]
  transfers between devices with their start and end apart: 41 -> 41, of which waited for: 18 -> 20; matrix products, arithmetic and copies ran while one was open for 9% -> 9% of each run, Pallas kernels for 29% -> 27%
where the time goes in v6:
time: 300 us; the launch traced here: 296 us
  Pallas kernels  129 us (43%)
  waiting for transfers between devices  70.4 us (23%)
  starting transfers between devices  40.7 us (14%)
  other arithmetic  39.4 us (13%)
  local copies, waits for them, and re-layouts  9.11 us (3%)
  between operations  7.32 us (2%)
    ppermute x41, waiting for transfers between devices, send(): return lax.ppermute(array, AXES, pairs)  70.4 us
    pallas_call x1, Pallas kernels, mlp_call(): pl.pallas_call(functools.partial(mlp_kernel, dims, len(own)), grid=(block...  47.3 us
    ppermute x41, starting transfers between devices, send(): return lax.ppermute(array, AXES, pairs)  40.7 us
    pallas_call x1, Pallas kernels, attn_back_call(): pl.pallas_call(functools.partial(attn_back_kernel, dims, len(own), device...  31.1 us
    pallas_call x1, Pallas kernels, proj_back_call(): pl.pallas_call(functools.partial(proj_back_kernel, dims, len(own), 3 * d...  13.4 us
    pallas_call x2, Pallas kernels, attn_call(): pl.pallas_call(attn_kernel, grid=(2 * groups,), in_specs=[at(0), at(1), a...  13 us
    concatenate x3, other arithmetic, roll_rows(): jnp.concatenate([array, array], axis=0)  11.2 us
    pallas_call x1, Pallas kernels, qkv_call(): pl.pallas_call(functools.partial(qkv_kernel, dims, len(own)), grid=(2,),...  9.07 us
  transfers between devices with their start and end apart: 41, of which 20 were waited for; matrix products, arithmetic and copies ran while one was open for 9% of the time, Pallas kernels for 27%

profile of v6, /device:TPU:0, one launch (start us, length us, event | category | flops | bytes accessed | tf_op | source)
XLA Modules:
  0.0 295.8 jit_solution(16325228962920432847)
XLA Ops:
  1.6 1.3 fusion.24.t_ref
  3.4 1.6 cut.1
  10.0 2.8 collective-permute-start.3
  12.8 2.6 collective-permute-start.2
  15.3 1.3 collective-permute-start.1
  16.8 3.1 %collective-permute-done.3 = bf16[48,1664]{1,0:T(8,128)(2,1)S(1)} collective-permute-done((bf16[48,1664]{1,0:T(8,128)(2,1)S(1)}, bf16[48,1664]{1,0:T(8,128)(2,1)S(1)}, u32[]{:S(2)}, u32[]{:S(2)}) %collective-permute-start.3) | collective-permute-done | bytes 159776 | tf_op jit(solution)/shard_map/ppermute | solution.py:927
  19.8 6.5 %collective-permute-done.2 = bf16[48,1664]{1,0:T(8,128)(2,1)S(1)} collective-permute-done((bf16[48,1664]{1,0:T(8,128)(2,1)S(1)}, bf16[48,1664]{1,0:T(8,128)(2,1)S(1)}, u32[]{:S(2)}, u32[]{:S(2)}) %collective-permute-start.2) | collective-permute-done | bytes 159776 | tf_op jit(solution)/shard_map/ppermute | solution.py:927
  26.3 3.9 %collective-permute-start.10 = (bf16[48,3072]{1,0:T(8,128)(2,1)S(1)}, bf16[48,3072]{1,0:T(8,128)(2,1)S(1)}, u32[]{:S(2)}, u32[]{:S(2)}) collective-permute-start(bf16[48,3072]{1,0:T(8,128)(2,1)S(1)} %pad_maximum_fusion.3), channel_id=1, source_target_pairs={{0,8},{1,9},{2,10},{3,11},{4,12},{5,13},{6,14},{7,15},{8,16},{9,17... | collective-permute-start | bytes 884744 | tf_op jit(solution)/shard_map/ppermute | solution.py:927
  30.2 1.6 collective-permute-start.9
  32.0 2.5 collective-permute-start.7
  42.7 3.7 %fusion.4.x_ref = bf16[1024,768]{1,0:T(8,128)(2,1)} fusion(s32[]{:T(128)S(6)} %select_n.151, bf16[1024,768]{1,0:T(8,128)(2,1)S(1)} %copy-done.4), kind=kLoop, calls=%fused_computation.15 | loop fusion | flops 3145728 | bytes 3145732 | tf_op jit(solution)/shard_map/concatenate | solution.py:834
  48.0 2.3 fusion.3.c_ref
  50.9 6.1 %collective-permute-done.8 = bf16[48,3072]{1,0:T(8,128)(2,1)S(1)} collective-permute-done((bf16[48,3072]{1,0:T(8,128)(2,1)S(1)}, bf16[48,3072]{1,0:T(8,128)(2,1)S(1)}, u32[]{:S(2)}, u32[]{:S(2)}) %collective-permute-start.8) | collective-permute-done | bytes 294944 | tf_op jit(solution)/shard_map/ppermute | solution.py:927
  57.0 5.0 %collective-permute-done.6 = bf16[4,48,1664]{2,1,0:T(8,128)(2,1)} collective-permute-done((bf16[4,48,1664]{2,1,0:T(8,128)(2,1)S(1)}, bf16[4,48,1664]{2,1,0:T(8,128)(2,1)}, u32[]{:S(2)}, u32[]{:S(2)}) %collective-permute-start.6) | collective-permute-done | bytes 639008 | tf_op jit(solution)/shard_map/ppermute | solution.py:927
  62.9 2.1 pad_maximum_fusion.1.refs_0_
  65.0 1.7 pad_maximum_fusion.refs_0_
  67.3 1.5 collective-permute-start.13
  70.4 6.0 %first_norm.1 = (bf16[1024,768]{1,0:T(8,128)(2,1)}, bf16[768,1024]{1,0:T(8,128)(2,1)}, f32[8,3072]{1,0:T(8,128)}) custom-call(s32[4]{0:T(128)} %pad_add_fusion.where_ref, bf16[1024,768]{1,0:T(8,128)(2,1)} %fusion.4.x_ref, bf16[16,48,1664]{2,1,0:T(8,128)(2,1)} %copy-done), custom_call_target="tpu_custom_call" | custom-call | flops 1000000000 | bytes 4718592 | tf_op jit(solution)/shard_map/first_norm/pallas_call | solution.py:334
  76.4 9.1 %qkv.1.q_ref.k_ref.v_ref.j0_ref.j1_ref = bf16[1024,2304]{1,0:T(8,128)(2,1)} custom-call(s32[4]{0:T(128)} %pad_add_fusion.where_ref, bf16[1024,768]{1,0:T(8,128)(2,1)} %get-tuple-element.161.n_ref, f32[8,3072]{1,0:T(8,128)} %get-tuple-element.162.vec_ref, bf16[16,48,1664]{2,1,0:T(8,128)(2,1)} %copy-done, bf16[16,48,1664]{2,1,0:T(8,128)(2,1)} %collective-permute-done.11.refs_1_), custom_call_target="tpu_custom_call" | custom-call | flops 3623878656 | bytes 9830400 | tf_op jit(solution)/shard_map/qkv/pallas_call | solution.py:385
  85.5 8.0 %attn.2 = (bf16[1024,512]{1,0:T(8,128)(2,1)}, f32[4,2,1024]{2,1,0:T(2,128)}) custom-call(bf16[1024,2304]{1,0:T(8,128)(2,1)} %qkv.1.q_ref.k_ref.v_ref.j0_ref.j1_ref, bf16[1024,2304]{1,0:T(8,128)(2,1)} %qkv.1.q_ref.k_ref.v_ref.j0_ref.j1_ref, bf16[1024,2304]{1,0:T(8,128)(2,1)} %qkv.1.q_ref.k_ref.v_ref.j0_ref.j1_ref, s32[1,256]{1,0:T(1,128)} %bitcast.106, ...), custom_call_target="tpu_custom_call" | custom-call | flops 16000000000 | bytes 8000000 | tf_op jit(solution)/shard_map/attn/pallas_call | solution.py:128
  93.5 2.0 collective-permute-done.13.refs_2_
  95.5 1.2 collective-permute-done.12.refs_1_
  101.5 5.0 %attn.3 = (bf16[1024,256]{1,0:T(8,128)(2,1)}, f32[2,2,1024]{2,1,0:T(2,128)}) custom-call(bf16[1024,2304]{1,0:T(8,128)(2,1)} %qkv.1.q_ref.k_ref.v_ref.j0_ref.j1_ref, bf16[1024,2304]{1,0:T(8,128)(2,1)} %qkv.1.q_ref.k_ref.v_ref.j0_ref.j1_ref, bf16[1024,2304]{1,0:T(8,128)(2,1)} %qkv.1.q_ref.k_ref.v_ref.j0_ref.j1_ref, s32[1,256]{1,0:T(1,128)} %bitcast.107, ...), custom_call_target="tpu_custom_call" | custom-call | flops 8000000000 | bytes 8000000 | tf_op jit(solution)/shard_map/attn/pallas_call | solution.py:128
  106.5 7.3 %proj.1 = (f32[1024,768]{1,0:T(8,128)}, bf16[1024,768]{1,0:T(8,128)(2,1)}) custom-call(s32[4]{0:T(128)} %pad_add_fusion.where_ref, bf16[1024,768]{1,0:T(8,128)(2,1)} %fusion.4.x_ref, bf16[1024,512]{1,0:T(8,128)(2,1)} %get-tuple-element.170.a0_ref, bf16[1024,256]{1,0:T(8,128)(2,1)} %get-tuple-element.171.a1_ref, f32[8,3072]{1,0:T(8,128)} %get-tuple-element.162.vec_ref, ...), custom_call_target="tpu_custom_call" | custom-call | flops 1207959552 | bytes 9043968 | tf_op jit(solution)/shard_map/proj/pallas_call | solution.py:421
  115.9 1.5 collective-permute-done.19.refs_8_
  119.0 47.3 %mlp.1 = (bf16[1024,768]{1,0:T(8,128)(2,1)}, f32[1024,768]{1,0:T(8,128)}, f32[1,3072]{1,0:T(1,128)}, f32[1,768]{1,0:T(1,128)}, bf16[16,48,3072]{2,1,0:T(8,128)(2,1)}, /*index=5*/bf16[16,48,3072]{2,1,0:T(8,128)(2,1)}) custom-call(s32[4]{0:T(128)} %pad_add_fusion.where_ref, bf16[1024,768]{1,0:T(8,128)(2,1)} %get-tuple-element.177.n_ref, ...), custom_call_target="tpu_custom_call" | custom-call | flops 28991029248 | bytes 30000000 | tf_op jit(solution)/shard_map/mlp/pallas_call | solution.py:542
  166.6 13.4 %proj_back.1 = (f32[1024,768]{1,0:T(8,128)}, bf16[1024,768]{1,0:T(8,128)(2,1)}, bf16[768,768]{1,0:T(8,128)(2,1)}, f32[16,1024]{1,0:T(8,128)}, f32[1,768]{1,0:T(1...) custom-call(s32[4]{0:T(128)} %pad_add_fusion.where_ref, f32[1024,768]{1,0:T(8,128)} %get-tuple-element.185.gn_ref, ...), custom_call_target="tpu_custom_call" | custom-call | flops 2415919104 | bytes 12582912 | tf_op jit(solution)/shard_map/proj_back/pallas_call | solution.py:617
  180.1 2.0 add_convert_fusion.6
  182.1 1.9 add_convert_fusion.7
  184.0 3.3 %add_convert_fusion = (bf16[3,48,3072]{2,1,0:T(8,128)(2,1)}, bf16[3,48,3072]{2,1,0:T(8,128)(2,1)}) fusion(bf16[16,48,3072]{2,1,0:T(8,128)(2,1)} %collective-permute-done.21, bf16[16,48,3072]{2,1,0:T(8,128)(2,1)S(1)} %copy-done.1), kind=kLoop, calls=%fused_computation.9 | loop fusion | flops 3538944 | bytes 5308416 | tf_op jit(solution)/shard_map/convert_element_type | solution.py:1075
  189.1 1.7 collective-permute-start.22
  190.9 1.2 collective-permute-start.25
  192.6 31.1 %attn_back.1 = (bf16[1024,768]{1,0:T(8,128)(2,1)}, bf16[16,48,1664]{2,1,0:T(8,128)(2,1)}, bf16[16,48,1664]{2,1,0:T(8,128)(2,1)}) custom-call(s32[4]{0:T(128)} %pad_add_fusion.where_ref, bf16[1024,2304]{1,0:T(8,128)(2,1)} %qkv.1.q_ref.k_ref.v_ref.j0_ref.j1_ref, bf16[1024,2304]{1,0:T(8,128)(2,1)} %qkv.1.q_ref.k_ref.v_ref.j0_ref.j1_ref, ...), custom_call_target="tpu_custom_call" | custom-call | flops 60000002048 | bytes 20000000 | tf_op jit(solution)/shard_map/attn_back/pallas_call | solution.py:785
  223.8 5.4 %collective-permute-done.25 = bf16[3,48,3072]{2,1,0:T(8,128)(2,1)S(1)} collective-permute-done((bf16[3,48,3072]{2,1,0:T(8,128)(2,1)}, bf16[3,48,3072]{2,1,0:T(8,128)(2,1)S(1)}, u32[]{:S(2)}, u32[]{:S(2)}) %collective-permute-start.25) | collective-permute-done | bytes 884768 | tf_op jit(solution)/shard_map/ppermute | solution.py:927
  229.3 2.4 fusion.9
  233.1 1.2 collective-permute-start.28
  235.0 8.2 %collective-permute-done.30 = bf16[48,3072]{1,0:T(8,128)(2,1)S(1)} collective-permute-done((bf16[48,3072]{1,0:T(8,128)(2,1)S(1)}, bf16[48,3072]{1,0:T(8,128)(2,1)S(1)}, u32[]{:S(2)}, u32[]{:S(2)}) %collective-permute-start.30) | collective-permute-done | bytes 294944 | tf_op jit(solution)/shard_map/ppermute | solution.py:927
  243.9 1.5 collective-permute-start.32
  245.3 1.4 collective-permute-start.33
  246.8 2.2 fusion.6
  249.0 2.3 collective-permute-start.35
  251.2 3.8 %fusion.1 = bf16[1024,768]{1,0:T(8,128)(2,1)} fusion(s32[]{:T(128)S(6)} %select_n.153, bf16[1024,768]{1,0:T(8,128)(2,1)S(1)} %copy-done.6), kind=kLoop, calls=%fused_computation.12 | loop fusion | flops 3145728 | bytes 3145732 | tf_op jit(solution)/shard_map/concatenate | solution.py:834
  255.0 3.8 %fusion = bf16[1024,768]{1,0:T(8,128)(2,1)} fusion(s32[]{:T(128)S(6)} %select_n.153, bf16[1024,768]{1,0:T(8,128)(2,1)S(1)} %copy-done.5), kind=kLoop, calls=%fused_computation.11 | loop fusion | flops 3145728 | bytes 3145732 | tf_op jit(solution)/shard_map/concatenate | solution.py:834
  258.8 10.2 %collective-permute-done.34 = bf16[48,3072]{1,0:T(8,128)(2,1)S(1)} collective-permute-done((bf16[48,3072]{1,0:T(8,128)(2,1)S(1)}, bf16[48,3072]{1,0:T(8,128)(2,1)S(1)}, u32[]{:S(2)}, u32[]{:S(2)}) %collective-permute-start.34) | collective-permute-done | bytes 294944 | tf_op jit(solution)/shard_map/ppermute | solution.py:927
  269.0 3.3 %collective-permute-done.32 = bf16[4,48,1664]{2,1,0:T(8,128)(2,1)S(1)} collective-permute-done((bf16[4,48,1664]{2,1,0:T(8,128)(2,1)S(1)}, bf16[4,48,1664]{2,1,0:T(8,128)(2,1)S(1)}, u32[]{:S(2)}, u32[]{:S(2)}) %collective-permute-start.32) | collective-permute-done | bytes 639008 | tf_op jit(solution)/shard_map/ppermute | solution.py:927
  273.9 2.3 collective-permute-start.38
  277.6 3.1 %collective-permute-done.38 = bf16[48,1664]{1,0:T(8,128)(2,1)S(1)} collective-permute-done((bf16[48,1664]{1,0:T(8,128)(2,1)S(1)}, bf16[48,1664]{1,0:T(8,128)(2,1)S(1)}, u32[]{:S(2)}, u32[]{:S(2)}) %collective-permute-start.38) | collective-permute-done | bytes 159776 | tf_op jit(solution)/shard_map/ppermute | solution.py:927
  280.7 10.2 %collective-permute-done.37 = bf16[48,1664]{1,0:T(8,128)(2,1)S(1)} collective-permute-done((bf16[48,1664]{1,0:T(8,128)(2,1)S(1)}, bf16[48,1664]{1,0:T(8,128)(2,1)S(1)}, u32[]{:S(2)}, u32[]{:S(2)}) %collective-permute-start.37) | collective-permute-done | bytes 159776 | tf_op jit(solution)/shard_map/ppermute | solution.py:927
  (143 shorter events, 35.1 us)
Async XLA Ops:
  0.6 16.1 %copy-start.10 = (bf16[24,3072]{1,0:T(8,128)(2,1)S(1)}, bf16[24,3072]{1,0:T(8,128)(2,1)}, u32[]{:S(2)}) copy-start(bf16[24,3072]{1,0:T(8,128)(2,1)} %param.26) | copy-start | bytes 442372
  5.0 1.6 collective-permute-start
  7.5 28.0 %copy-start.15 = (s32[1,5]{1,0:T(1,128)S(1)}, s32[1,5]{1,0:T(1,128)}, u32[]{:S(2)}) copy-start(s32[1,5]{1,0:T(1,128)} %param.17) | copy-start | bytes 64
  7.5 35.1 %copy-start.4 = (bf16[1024,768]{1,0:T(8,128)(2,1)S(1)}, bf16[1024,768]{1,0:T(8,128)(2,1)}, u32[]{:S(2)}) copy-start(bf16[1024,768]{1,0:T(8,128)(2,1)} %param.16) | copy-start | bytes 4718596
  8.6 8.1 %collective-permute-start.4 = (bf16[24,1536]{1,0:T(8,128)(2,1)S(1)}, bf16[24,1536]{1,0:T(8,128)(2,1)S(1)}, u32[]{:S(2)}, u32[]{:S(2)}) collective-permute-start(bf16[24,1536]{1,0:T(8,128)(2,1)S(1)} %broadcast_select_fusion.8), channel_id=1, source_target_pairs={{0,1},{1,0},{2,3},{3,2},{4,5},{5,4},{6,7},{7,6},{8,9},{9,8},{10,11... | collective-permute-start | bytes 221192 | tf_op jit(solution)/shard_map/ppermute | solution.py:927
  10.0 9.9 %collective-permute-start.3 = (bf16[48,1664]{1,0:T(8,128)(2,1)S(1)}, bf16[48,1664]{1,0:T(8,128)(2,1)S(1)}, u32[]{:S(2)}, u32[]{:S(2)}) collective-permute-start(bf16[48,1664]{1,0:T(8,128)(2,1)S(1)} %pad_maximum_fusion.6), channel_id=1, source_target_pairs={{0,8},{1,9},{2,10},{3,11},{4,12},{5,13},{6,14},{7,15},{8,16},{9,17... | collective-permute-start | bytes 479240 | tf_op jit(solution)/shard_map/ppermute | solution.py:927
  12.8 13.6 %collective-permute-start.2 = (bf16[48,1664]{1,0:T(8,128)(2,1)S(1)}, bf16[48,1664]{1,0:T(8,128)(2,1)S(1)}, u32[]{:S(2)}, u32[]{:S(2)}) collective-permute-start(bf16[48,1664]{1,0:T(8,128)(2,1)S(1)} %pad_maximum_fusion.6), channel_id=1, source_target_pairs={{0,16},{1,17},{2,18},{3,19},{4,20},{5,21},{6,22},{7,23},{8,24},{9,... | collective-permute-start | bytes 479240 | tf_op jit(solution)/shard_map/ppermute | solution.py:927
  15.3 11.0 %collective-permute-start.1 = (bf16[48,1664]{1,0:T(8,128)(2,1)S(1)}, bf16[48,1664]{1,0:T(8,128)(2,1)S(1)}, u32[]{:S(2)}, u32[]{:S(2)}) collective-permute-start(bf16[48,1664]{1,0:T(8,128)(2,1)S(1)} %pad_maximum_fusion.6), channel_id=1, source_target_pairs={{0,24},{1,25},{2,26},{3,27},{4,28},{5,29},{6,30},{7,31},{8,0},{9,1... | collective-permute-start | bytes 479240 | tf_op jit(solution)/shard_map/ppermute | solution.py:927
  26.3 20.0 %collective-permute-start.10 = (bf16[48,3072]{1,0:T(8,128)(2,1)S(1)}, bf16[48,3072]{1,0:T(8,128)(2,1)S(1)}, u32[]{:S(2)}, u32[]{:S(2)}) collective-permute-start(bf16[48,3072]{1,0:T(8,128)(2,1)S(1)} %pad_maximum_fusion.3), channel_id=1, source_target_pairs={{0,8},{1,9},{2,10},{3,11},{4,12},{5,13},{6,14},{7,15},{8,16},{9,17... | collective-permute-start | bytes 884744 | tf_op jit(solution)/shard_map/ppermute | solution.py:927
  30.2 20.7 %collective-permute-start.9 = (bf16[48,3072]{1,0:T(8,128)(2,1)S(1)}, bf16[48,3072]{1,0:T(8,128)(2,1)}, u32[]{:S(2)}, u32[]{:S(2)}) collective-permute-start(bf16[48,3072]{1,0:T(8,128)(2,1)S(1)} %pad_maximum_fusion.3), channel_id=1, source_target_pairs={{0,16},{1,17},{2,18},{3,19},{4,20},{5,21},{6,22},{7,23},{8,24},{9,... | collective-permute-start | bytes 884744 | tf_op jit(solution)/shard_map/ppermute | solution.py:927
  32.0 25.0 %collective-permute-start.7 = (bf16[4,48,1664]{2,1,0:T(8,128)(2,1)S(1)}, bf16[4,48,1664]{2,1,0:T(8,128)(2,1)}, u32[]{:S(2)}, u32[]{:S(2)}) collective-permute-start(bf16[4,48,1664]{2,1,0:T(8,128)(2,1)S(1)} %pad_maximum_fusion.2), channel_id=1, source_target_pairs={{0,6},{1,7},{2,4},{3,5},{4,2},{5,3},{6,0},{7,1},{8,14},{9,15},{10,... | collective-permute-start | bytes 1916936 | tf_op jit(solution)/shard_map/ppermute | solution.py:927
  34.5 27.5 %collective-permute-start.6 = (bf16[4,48,1664]{2,1,0:T(8,128)(2,1)S(1)}, bf16[4,48,1664]{2,1,0:T(8,128)(2,1)}, u32[]{:S(2)}, u32[]{:S(2)}) collective-permute-start(bf16[4,48,1664]{2,1,0:T(8,128)(2,1)S(1)} %pad_maximum_fusion.2), channel_id=1, source_target_pairs={{0,4},{1,5},{2,6},{3,7},{4,0},{5,1},{6,2},{7,3},{8,12},{9,13},{10,... | collective-permute-start | bytes 1916936 | tf_op jit(solution)/shard_map/ppermute | solution.py:927
  35.0 27.0 %collective-permute-start.5 = (bf16[4,48,1664]{2,1,0:T(8,128)(2,1)S(1)}, bf16[4,48,1664]{2,1,0:T(8,128)(2,1)S(1)}, u32[]{:S(2)}, u32[]{:S(2)}) collective-permute-start(bf16[4,48,1664]{2,1,0:T(8,128)(2,1)S(1)} %pad_maximum_fusion.2), channel_id=1, source_target_pairs={{0,2},{1,3},{2,0},{3,1},{4,6},{5,7},{6,4},{7,5},{8,10},{9,11},{10,... | collective-permute-start | bytes 1916936 | tf_op jit(solution)/shard_map/ppermute | solution.py:927
  46.4 10.6 %collective-permute-start.8 = (bf16[48,3072]{1,0:T(8,128)(2,1)S(1)}, bf16[48,3072]{1,0:T(8,128)(2,1)S(1)}, u32[]{:S(2)}, u32[]{:S(2)}) collective-permute-start(bf16[48,3072]{1,0:T(8,128)(2,1)S(1)} %pad_maximum_fusion.3), channel_id=1, source_target_pairs={{0,24},{1,25},{2,26},{3,27},{4,28},{5,29},{6,30},{7,31},{8,0},{9,1... | collective-permute-start | bytes 884744 | tf_op jit(solution)/shard_map/ppermute | solution.py:927
  48.0 21.6 %copy-start.16 = (s32[256]{0:T(256)}, s32[256]{0:T(256)S(1)}, u32[]{:S(2)}) copy-start(s32[256]{0:T(256)S(1)} %slice.348) | copy-start | bytes 3076
  66.7 9.7 %collective-permute-start.11 = (bf16[16,48,1664]{2,1,0:T(8,128)(2,1)S(1)}, bf16[16,48,1664]{2,1,0:T(8,128)(2,1)}, u32[]{:S(2)}, u32[]{:S(2)}) collective-permute-start(bf16[16,48,1664]{2,1,0:T(8,128)(2,1)S(1)} %pad_maximum_fusion.refs_0_), channel_id=1, source_target_pairs={{0,1},{1,0},{2,3},{3,2},{4,5},{5,4},{6,7},{7,6},{8,9},{9,8},{10,11... | collective-permute-start | bytes 7667720 | tf_op jit(solution)/shard_map/ppermute | solution.py:927
  66.8 47.7 %collective-permute-start.16 = (bf16[4,48,3072]{2,1,0:T(8,128)(2,1)}, bf16[4,48,3072]{2,1,0:T(8,128)(2,1)}, u32[]{:S(2)}, u32[]{:S(2)}) collective-permute-start(bf16[4,48,3072]{2,1,0:T(8,128)(2,1)} %pad_maximum_fusion.1.refs_0_), channel_id=1, source_target_pairs={{0,1},{1,0},{2,3},{3,2},{4,5},{5,4},{6,7},{7,6},{8,9},{9,8},{10,11... | collective-permute-start | bytes 3538952 | tf_op jit(solution)/shard_map/ppermute | solution.py:927
  67.3 28.3 %collective-permute-start.13 = (bf16[4,48,3072]{2,1,0:T(8,128)(2,1)}, bf16[4,48,3072]{2,1,0:T(8,128)(2,1)}, u32[]{:S(2)}, u32[]{:S(2)}) collective-permute-start(bf16[4,48,3072]{2,1,0:T(8,128)(2,1)} %pad_maximum_fusion.1.refs_0_), channel_id=1, source_target_pairs={{0,4},{1,5},{2,6},{3,7},{4,0},{5,1},{6,2},{7,3},{8,12},{9,13},{10,... | collective-permute-start | bytes 3538952 | tf_op jit(solution)/shard_map/ppermute | solution.py:927
  68.8 28.0 %collective-permute-start.12 = (bf16[4,48,3072]{2,1,0:T(8,128)(2,1)}, bf16[4,48,3072]{2,1,0:T(8,128)(2,1)}, u32[]{:S(2)}, u32[]{:S(2)}) collective-permute-start(bf16[4,48,3072]{2,1,0:T(8,128)(2,1)} %pad_maximum_fusion.1.refs_0_), channel_id=1, source_target_pairs={{0,2},{1,3},{2,0},{3,1},{4,6},{5,7},{6,4},{7,5},{8,10},{9,11},{10,... | collective-permute-start | bytes 3538952 | tf_op jit(solution)/shard_map/ppermute | solution.py:927
  96.8 18.5 %collective-permute-start.17 = (bf16[4,48,3072]{2,1,0:T(8,128)(2,1)}, bf16[4,48,3072]{2,1,0:T(8,128)(2,1)S(1)}, u32[]{:S(2)}, u32[]{:S(2)}) collective-permute-start(bf16[4,48,3072]{2,1,0:T(8,128)(2,1)} %collective-permute-done.12.refs_1_), channel_id=1, source_target_pairs={{0,1},{1,0},{2,3},{3,2},{4,5},{5,4},{6,7},{7,6},{8,9},{9,8},{10,11... | collective-permute-start | bytes 3538952 | tf_op jit(solution)/shard_map/ppermute | solution.py:927
  96.8 18.5 %collective-permute-start.18 = (bf16[4,48,3072]{2,1,0:T(8,128)(2,1)}, bf16[4,48,3072]{2,1,0:T(8,128)(2,1)S(1)}, u32[]{:S(2)}, u32[]{:S(2)}) collective-permute-start(bf16[4,48,3072]{2,1,0:T(8,128)(2,1)} %collective-permute-done.13.refs_2_), channel_id=1, source_target_pairs={{0,1},{1,0},{2,3},{3,2},{4,5},{5,4},{6,7},{7,6},{8,9},{9,8},{10,11... | collective-permute-start | bytes 3538952 | tf_op jit(solution)/shard_map/ppermute | solution.py:927
  99.5 15.3 %collective-permute-start.15 = (bf16[2,48,3072]{2,1,0:T(8,128)(2,1)S(1)}, bf16[2,48,3072]{2,1,0:T(8,128)(2,1)S(1)}, u32[]{:S(2)}, u32[]{:S(2)}) collective-permute-start(bf16[2,48,3072]{2,1,0:T(8,128)(2,1)S(1)} %slice.350), channel_id=1, source_target_pairs={{0,2},{1,3},{2,0},{3,1},{4,6},{5,7},{6,4},{7,5},{8,10},{9,11},{10,... | collective-permute-start | bytes 1769480 | tf_op jit(solution)/shard_map/ppermute | solution.py:927
  100.3 15.0 %collective-permute-start.14 = (bf16[2,48,3072]{2,1,0:T(8,128)(2,1)S(1)}, bf16[2,48,3072]{2,1,0:T(8,128)(2,1)S(1)}, u32[]{:S(2)}, u32[]{:S(2)}) collective-permute-start(bf16[2,48,3072]{2,1,0:T(8,128)(2,1)S(1)} %slice.349), channel_id=1, source_target_pairs={{0,4},{1,5},{2,6},{3,7},{4,0},{5,1},{6,2},{7,3},{8,12},{9,13},{10,... | collective-permute-start | bytes 1769480 | tf_op jit(solution)/shard_map/ppermute | solution.py:927
  115.3 2.1 collective-permute-start.19
  115.4 2.8 collective-permute-start.20
  166.4 13.7 %collective-permute-start.21 = (bf16[16,48,3072]{2,1,0:T(8,128)(2,1)}, bf16[16,48,3072]{2,1,0:T(8,128)(2,1)}, u32[]{:S(2)}, u32[]{:S(2)}) collective-permute-start(bf16[16,48,3072]{2,1,0:T(8,128)(2,1)} %get-tuple-element.189), channel_id=1, source_target_pairs={{0,1},{1,0},{2,3},{3,2},{4,5},{5,4},{6,7},{7,6},{8,9},{9,8},{10,11... | collective-permute-start | bytes 14155784 | tf_op jit(solution)/shard_map/ppermute | solution.py:927
  166.6 13.5 %copy-start.1 = (bf16[16,48,3072]{2,1,0:T(8,128)(2,1)S(1)}, bf16[16,48,3072]{2,1,0:T(8,128)(2,1)}, u32[]{:S(2)}) copy-start(bf16[16,48,3072]{2,1,0:T(8,128)(2,1)} %get-tuple-element.190) | copy-start | bytes 14155780
  187.4 36.4 %collective-permute-start.23 = (bf16[1,48,3072]{2,1,0:T(8,128)(2,1)}, bf16[1,48,3072]{2,1,0:T(8,128)(2,1)S(1)}, u32[]{:S(2)}, u32[]{:S(2)}) collective-permute-start(bf16[1,48,3072]{2,1,0:T(8,128)(2,1)} %get-tuple-element.209), channel_id=1, source_target_pairs={{0,4},{1,5},{2,6},{3,7},{4,0},{5,1},{6,2},{7,3},{8,12},{9,13},{10,... | collective-permute-start | bytes 884744 | tf_op jit(solution)/shard_map/ppermute | solution.py:927
  188.6 35.2 %collective-permute-start.24 = (bf16[1,48,3072]{2,1,0:T(8,128)(2,1)S(1)}, bf16[1,48,3072]{2,1,0:T(8,128)(2,1)S(1)}, u32[]{:S(2)}, u32[]{:S(2)}) collective-permute-start(bf16[1,48,3072]{2,1,0:T(8,128)(2,1)S(1)} %get-tuple-element.210), channel_id=1, source_target_pairs={{0,2},{1,3},{2,0},{3,1},{4,6},{5,7},{6,4},{7,5},{8,10},{9,11},{10,... | collective-permute-start | bytes 884744 | tf_op jit(solution)/shard_map/ppermute | solution.py:927
  189.1 34.6 %collective-permute-start.22 = (bf16[2,48,3072]{2,1,0:T(8,128)(2,1)}, bf16[2,48,3072]{2,1,0:T(8,128)(2,1)S(1)}, u32[]{:S(2)}, u32[]{:S(2)}) collective-permute-start(bf16[2,48,3072]{2,1,0:T(8,128)(2,1)} %add_convert_fusion.6), channel_id=1, source_target_pairs={{0,6},{1,7},{2,4},{3,5},{4,2},{5,3},{6,0},{7,1},{8,14},{9,15},{10,... | collective-permute-start | bytes 1769480 | tf_op jit(solution)/shard_map/ppermute | solution.py:927
  190.9 38.4 %collective-permute-start.25 = (bf16[3,48,3072]{2,1,0:T(8,128)(2,1)}, bf16[3,48,3072]{2,1,0:T(8,128)(2,1)S(1)}, u32[]{:S(2)}, u32[]{:S(2)}) collective-permute-start(bf16[3,48,3072]{2,1,0:T(8,128)(2,1)} %get-tuple-element.211), channel_id=1, source_target_pairs={{0,2},{1,3},{2,0},{3,1},{4,6},{5,7},{6,4},{7,5},{8,10},{9,11},{10,... | collective-permute-start | bytes 2654216 | tf_op jit(solution)/shard_map/ppermute | solution.py:927
  192.1 37.1 %collective-permute-start.26 = (bf16[3,48,3072]{2,1,0:T(8,128)(2,1)}, bf16[3,48,3072]{2,1,0:T(8,128)(2,1)}, u32[]{:S(2)}, u32[]{:S(2)}) collective-permute-start(bf16[3,48,3072]{2,1,0:T(8,128)(2,1)} %get-tuple-element.212), channel_id=1, source_target_pairs={{0,4},{1,5},{2,6},{3,7},{4,0},{5,1},{6,2},{7,3},{8,12},{9,13},{10,... | collective-permute-start | bytes 2654216 | tf_op jit(solution)/shard_map/ppermute | solution.py:927
  229.2 5.1 %collective-permute-start.27 = (bf16[16,48,1664]{2,1,0:T(8,128)(2,1)}, bf16[16,48,1664]{2,1,0:T(8,128)(2,1)S(1)}, u32[]{:S(2)}, u32[]{:S(2)}) collective-permute-start(bf16[16,48,1664]{2,1,0:T(8,128)(2,1)} %get-tuple-element.217), channel_id=1, source_target_pairs={{0,1},{1,0},{2,3},{3,2},{4,5},{5,4},{6,7},{7,6},{8,9},{9,8},{10,11... | collective-permute-start | bytes 7667720 | tf_op jit(solution)/shard_map/ppermute | solution.py:927
  231.8 11.5 %collective-permute-start.30 = (bf16[48,3072]{1,0:T(8,128)(2,1)S(1)}, bf16[48,3072]{1,0:T(8,128)(2,1)S(1)}, u32[]{:S(2)}, u32[]{:S(2)}) collective-permute-start(bf16[48,3072]{1,0:T(8,128)(2,1)S(1)} %get-tuple-element.259), channel_id=1, source_target_pairs={{0,8},{1,9},{2,10},{3,11},{4,12},{5,13},{6,14},{7,15},{8,16},{9,17... | collective-permute-start | bytes 884744 | tf_op jit(solution)/shard_map/ppermute | solution.py:927
  232.3 10.9 %collective-permute-start.29 = (bf16[48,3072]{1,0:T(8,128)(2,1)S(1)}, bf16[48,3072]{1,0:T(8,128)(2,1)S(1)}, u32[]{:S(2)}, u32[]{:S(2)}) collective-permute-start(bf16[48,3072]{1,0:T(8,128)(2,1)S(1)} %get-tuple-element.260), channel_id=1, source_target_pairs={{0,4},{1,5},{2,6},{3,7},{4,0},{5,1},{6,2},{7,3},{8,12},{9,13},{10,... | collective-permute-start | bytes 884744 | tf_op jit(solution)/shard_map/ppermute | solution.py:927
  233.1 13.7 %copy-start.9 = (bf16[2,48,3072]{2,1,0:T(8,128)(2,1)S(1)}, bf16[2,48,3072]{2,1,0:T(8,128)(2,1)}, u32[]{:S(2)}) copy-start(bf16[2,48,3072]{2,1,0:T(8,128)(2,1)} %copy-done.8) | copy-start | bytes 1769476
  233.1 10.1 %collective-permute-start.28 = (bf16[48,3072]{1,0:T(8,128)(2,1)S(1)}, bf16[48,3072]{1,0:T(8,128)(2,1)S(1)}, u32[]{:S(2)}, u32[]{:S(2)}) collective-permute-start(bf16[48,3072]{1,0:T(8,128)(2,1)S(1)} %get-tuple-element.261), channel_id=1, source_target_pairs={{0,2},{1,3},{2,0},{3,1},{4,6},{5,7},{6,4},{7,5},{8,10},{9,11},{10,... | collective-permute-start | bytes 884744 | tf_op jit(solution)/shard_map/ppermute | solution.py:927
  243.2 8.0 %copy-start.6 = (bf16[1024,768]{1,0:T(8,128)(2,1)S(1)}, bf16[1024,768]{1,0:T(8,128)(2,1)}, u32[]{:S(2)}) copy-start(bf16[1024,768]{1,0:T(8,128)(2,1)} %get-tuple-element.236) | copy-start | bytes 4718596
  243.2 25.7 %collective-permute-start.31 = (bf16[4,48,1664]{2,1,0:T(8,128)(2,1)S(1)}, bf16[4,48,1664]{2,1,0:T(8,128)(2,1)S(1)}, u32[]{:S(2)}, u32[]{:S(2)}) collective-permute-start(bf16[4,48,1664]{2,1,0:T(8,128)(2,1)S(1)} %get-tuple-element.227), channel_id=1, source_target_pairs={{0,2},{1,3},{2,0},{3,1},{4,6},{5,7},{6,4},{7,5},{8,10},{9,11},{10,... | collective-permute-start | bytes 1916936 | tf_op jit(solution)/shard_map/ppermute | solution.py:927
  243.9 28.4 %collective-permute-start.32 = (bf16[4,48,1664]{2,1,0:T(8,128)(2,1)S(1)}, bf16[4,48,1664]{2,1,0:T(8,128)(2,1)S(1)}, u32[]{:S(2)}, u32[]{:S(2)}) collective-permute-start(bf16[4,48,1664]{2,1,0:T(8,128)(2,1)S(1)} %get-tuple-element.228), channel_id=1, source_target_pairs={{0,4},{1,5},{2,6},{3,7},{4,0},{5,1},{6,2},{7,3},{8,12},{9,13},{10,... | collective-permute-start | bytes 1916936 | tf_op jit(solution)/shard_map/ppermute | solution.py:927
  245.3 27.9 %collective-permute-start.33 = (bf16[4,48,1664]{2,1,0:T(8,128)(2,1)S(1)}, bf16[4,48,1664]{2,1,0:T(8,128)(2,1)S(1)}, u32[]{:S(2)}, u32[]{:S(2)}) collective-permute-start(bf16[4,48,1664]{2,1,0:T(8,128)(2,1)S(1)} %get-tuple-element.229), channel_id=1, source_target_pairs={{0,6},{1,7},{2,4},{3,5},{4,2},{5,3},{6,0},{7,1},{8,14},{9,15},{10,... | collective-permute-start | bytes 1916936 | tf_op jit(solution)/shard_map/ppermute | solution.py:927
  249.0 9.8 %collective-permute-start.35 = (bf16[48,3072]{1,0:T(8,128)(2,1)S(1)}, bf16[48,3072]{1,0:T(8,128)(2,1)S(1)}, u32[]{:S(2)}, u32[]{:S(2)}) collective-permute-start(bf16[48,3072]{1,0:T(8,128)(2,1)S(1)} %get-tuple-element.256), channel_id=1, source_target_pairs={{0,24},{1,25},{2,26},{3,27},{4,28},{5,29},{6,30},{7,31},{8,0},{9,1... | collective-permute-start | bytes 884744 | tf_op jit(solution)/shard_map/ppermute | solution.py:927
  251.2 17.7 %collective-permute-start.34 = (bf16[48,3072]{1,0:T(8,128)(2,1)S(1)}, bf16[48,3072]{1,0:T(8,128)(2,1)S(1)}, u32[]{:S(2)}, u32[]{:S(2)}) collective-permute-start(bf16[48,3072]{1,0:T(8,128)(2,1)S(1)} %get-tuple-element.257), channel_id=1, source_target_pairs={{0,16},{1,17},{2,18},{3,19},{4,20},{5,21},{6,22},{7,23},{8,24},{9,... | collective-permute-start | bytes 884744 | tf_op jit(solution)/shard_map/ppermute | solution.py:927
  273.4 4.1 %collective-permute-start.39 = (f32[24,1536]{1,0:T(8,128)S(1)}, f32[24,1536]{1,0:T(8,128)S(1)}, u32[]{:S(2)}, u32[]{:S(2)}) collective-permute-start(f32[24,1536]{1,0:T(8,128)S(1)} %slice_select_fusion.2), channel_id=1, source_target_pairs={{0,1},{1,0},{2,3},{3,2},{4,5},{5,4},{6,7},{7,6},{8,9},{9,8},{10,11... | collective-permute-start | bytes 442376 | tf_op jit(solution)/shard_map/ppermute | solution.py:927
  273.9 6.8 %collective-permute-start.38 = (bf16[48,1664]{1,0:T(8,128)(2,1)S(1)}, bf16[48,1664]{1,0:T(8,128)(2,1)S(1)}, u32[]{:S(2)}, u32[]{:S(2)}) collective-permute-start(bf16[48,1664]{1,0:T(8,128)(2,1)S(1)} %get-tuple-element.270), channel_id=1, source_target_pairs={{0,24},{1,25},{2,26},{3,27},{4,28},{5,29},{6,30},{7,31},{8,0},{9,1... | collective-permute-start | bytes 479240 | tf_op jit(solution)/shard_map/ppermute | solution.py:927
  276.2 14.7 %collective-permute-start.37 = (bf16[48,1664]{1,0:T(8,128)(2,1)S(1)}, bf16[48,1664]{1,0:T(8,128)(2,1)S(1)}, u32[]{:S(2)}, u32[]{:S(2)}) collective-permute-start(bf16[48,1664]{1,0:T(8,128)(2,1)S(1)} %get-tuple-element.271), channel_id=1, source_target_pairs={{0,16},{1,17},{2,18},{3,19},{4,20},{5,21},{6,22},{7,23},{8,24},{9,... | collective-permute-start | bytes 479240 | tf_op jit(solution)/shard_map/ppermute | solution.py:927
  276.2 14.7 %collective-permute-start.36 = (bf16[48,1664]{1,0:T(8,128)(2,1)S(1)}, bf16[48,1664]{1,0:T(8,128)(2,1)S(1)}, u32[]{:S(2)}, u32[]{:S(2)}) collective-permute-start(bf16[48,1664]{1,0:T(8,128)(2,1)S(1)} %get-tuple-element.272), channel_id=1, source_target_pairs={{0,8},{1,9},{2,10},{3,11},{4,12},{5,13},{6,14},{7,15},{8,16},{9,17... | collective-permute-start | bytes 479240 | tf_op jit(solution)/shard_map/ppermute | solution.py:927
  292.2 1.4 collective-permute-start.40
  (16 other events, 63.7 us)

commit v7 on v6

--- a/solution.py
+++ b/solution.py
@@ -275,12 +275,13 @@
     return total.astype(BF)
 
 
-def cut_kernel(where_ref, w_ref, p_ref, t_ref, keep_ref, give_ref):
+def cut_kernel(where_ref, w_ref, p_ref, t_ref, f_ref, a_keep, a_give, f_keep, f_give):
     ci = where_ref[3]
     pairs = w_ref.shape[1] // 384
     half = p_ref.shape[1] // 2
+    wide = f_ref.shape[1] // 2
     for h in range(2):
-        for other, out in ((False, keep_ref), (True, give_ref)):
+        for other, out, f_out in ((False, a_keep, f_keep), (True, a_give, f_give)):
 
             @pl.when((ci != h) if other else (ci == h))
             def _():
@@ -292,22 +293,24 @@
                         at += 128
                 out[:, at : at + half] = p_ref[:, h * half : (h + 1) * half]
                 out[:, at + half :] = t_ref[...]
-
-
-def cut_call(where, w_qkv, w_proj, table):
+                f_out[...] = f_ref[:, h * wide : (h + 1) * wide]
+
+
+def cut_call(where, w_qkv, w_proj, table, w_fc):
     r = w_qkv.shape[0]
     cols = (w_qkv.shape[1] + w_proj.shape[1]) // 2 + 128
-    shapes = [full_spec(v.shape) for v in (w_qkv, w_proj, table)]
+    sizes = [cols, cols, w_fc.shape[1] // 2, w_fc.shape[1] // 2]
+    args = (w_qkv, w_proj, table, w_fc)
     return pl.pallas_call(
         cut_kernel,
         grid=(1,),
-        in_specs=[SMEM] + shapes,
-        out_specs=[full_spec((r, cols))] * 2,
-        out_shape=[jax.ShapeDtypeStruct((r, cols), BF)] * 2,
+        in_specs=[SMEM] + [full_spec(v.shape) for v in args],
+        out_specs=[full_spec((r, s)) for s in sizes],
+        out_shape=[jax.ShapeDtypeStruct((r, s), BF) for s in sizes],
         compiler_params=params(),
-        cost_estimate=cost(0, 4 * r * cols),
+        cost_estimate=cost(0, 4 * r * sum(sizes)),
         name="cut",
-    )(where, w_qkv, w_proj, table)
+    )(where, *args)
 
 
 def first_norm_kernel(dims, count, devices, where_ref, x_ref, *refs):
@@ -1033,21 +1036,23 @@
     def far(parts):
         return [parts[0]] + [send(parts[j], dz=j) for j in range(1, dims[0])]
 
-    a = links.rows_of(*cut_call(where, w_qkv, w_proj, table))
-    a, tokens, lengths, cotangent, w_fc = together(a, tokens, lengths, cotangent, w_fc)
+    a_keep, a_give, f_keep, f_give = cut_call(where, w_qkv, w_proj, table, w_fc)
+    a = links.rows_of(a_keep, a_give)
+    a, tokens, lengths, cotangent, f_keep, f_give = together(a, tokens, lengths, cotangent, f_keep, f_give)
     a0 = links.along_z(a)
-    fc = links.trade([half_columns(w_fc, h) for h in range(2)])
+    fc = links.rows_of(f_keep, f_give)
+    a0, fc, w_out, tokens, lengths, cotangent = together(a0, fc, w_out, tokens, lengths, cotangent)
+    prep = prepare(tokens, lengths, cotangent)
+    a0 = jnp.stack(a0)
+    a0, fc, w_out = together(a0, fc, w_out)
     m = jnp.concatenate([fc, w_out[: 2 * r], w_out[2 * r :]], axis=1)
-    a0, m, tokens, lengths, cotangent = together(a0, m, tokens, lengths, cotangent)
-    prep = prepare(tokens, lengths, cotangent)
+    a_own = [a0, send(a0, dx=1), send(a0, dy=1), send(a0, dx=1, dy=1)]
     m0 = links.along_z(m)
-    a0 = jnp.stack(a0)
-    a_own = [a0, send(a0, dx=1), send(a0, dy=1), send(a0, dx=1, dy=1)]
     a_own, m0, prep = together(a_own, m0, prep)
     start, seg_row, seg_col, x, cot = prep
     m0 = jnp.stack(m0)
+    m0, a_own = together(m0, a_own)
     a_own = [jnp.concatenate(a_own, axis=0)]
-    m0, a_own = together(m0, a_own)
     attn_w = a_own, swap(a_own)
     mx, my = xy(m0)
     normed, nt, vec = first_norm_call(dims, where, x, a_own, devices)

time: 300 us -> 298 us (level)
  no operation moved by 1% of the time
where the time goes in v7:
time: 298 us; the launch traced here: 294 us
  Pallas kernels  129 us (43%)
  waiting for transfers between devices  69.9 us (23%)
  starting transfers between devices  40.4 us (14%)
  other arithmetic  36.6 us (12%)
  local copies, waits for them, and re-layouts  10.8 us (4%)
  between operations  7.31 us (2%)
    ppermute x41, waiting for transfers between devices, send(): return lax.ppermute(array, AXES, pairs)  69.9 us
    pallas_call x1, Pallas kernels, mlp_call(): pl.pallas_call(functools.partial(mlp_kernel, dims, len(own)), grid=(block...  47 us
    ppermute x41, starting transfers between devices, send(): return lax.ppermute(array, AXES, pairs)  40.4 us
    pallas_call x1, Pallas kernels, attn_back_call(): pl.pallas_call(functools.partial(attn_back_kernel, dims, len(own), device...  31 us
    pallas_call x1, Pallas kernels, proj_back_call(): pl.pallas_call(functools.partial(proj_back_kernel, dims, len(own), 3 * d...  13.7 us
    pallas_call x2, Pallas kernels, attn_call(): pl.pallas_call(attn_kernel, grid=(2 * groups,), in_specs=[at(0), at(1), a...  13 us
    concatenate x3, other arithmetic, roll_rows(): jnp.concatenate([array, array], axis=0)  11.5 us
    pallas_call x1, Pallas kernels, qkv_call(): pl.pallas_call(functools.partial(qkv_kernel, dims, len(own)), grid=(2,),...  9.07 us
  transfers between devices with their start and end apart: 41, of which 20 were waited for; matrix products, arithmetic and copies ran while one was open for 9% of the time, Pallas kernels for 27%

profile of v7, /device:TPU:0, one launch (start us, length us, event | category | flops | bytes accessed | tf_op | source)
XLA Modules:
  0.0 293.8 jit_solution(2095185755653783373)
XLA Ops:
  1.6 1.3 fusion.24.t_ref
  3.4 1.8 cut.1
  8.1 2.7 collective-permute-start.3
  10.8 2.6 collective-permute-start.2
  13.4 1.3 collective-permute-start.1
  15.7 2.2 collective-permute-done.3
  17.9 6.5 %collective-permute-done.2 = bf16[48,1664]{1,0:T(8,128)(2,1)S(1)} collective-permute-done((bf16[48,1664]{1,0:T(8,128)(2,1)S(1)}, bf16[48,1664]{1,0:T(8,128)(2,1)S(1)}, u32[]{:S(2)}, u32[]{:S(2)}) %collective-permute-start.2) | collective-permute-done | bytes 159776 | tf_op jit(solution)/shard_map/ppermute | solution.py:930
  24.6 4.0 %collective-permute-start.10 = (bf16[48,3072]{1,0:T(8,128)(2,1)S(1)}, bf16[48,3072]{1,0:T(8,128)(2,1)S(1)}, u32[]{:S(2)}, u32[]{:S(2)}) collective-permute-start(bf16[48,3072]{1,0:T(8,128)(2,1)S(1)} %pad_maximum_fusion.2), channel_id=1, source_target_pairs={{0,8},{1,9},{2,10},{3,11},{4,12},{5,13},{6,14},{7,15},{8,16},{9,17... | collective-permute-start | bytes 884744 | tf_op jit(solution)/shard_map/ppermute | solution.py:930
  28.6 1.6 collective-permute-start.9
  30.2 2.4 collective-permute-start.7
  40.8 4.1 %fusion.4.x_ref = bf16[1024,768]{1,0:T(8,128)(2,1)} fusion(s32[]{:T(128)S(6)} %select_n.141, bf16[1024,768]{1,0:T(8,128)(2,1)} %param.16), kind=kLoop, calls=%fused_computation.14 | loop fusion | flops 3145728 | bytes 3145732 | tf_op jit(solution)/shard_map/concatenate | solution.py:837
  46.5 2.3 fusion.3.c_ref
  49.2 6.1 %collective-permute-done.8 = bf16[48,3072]{1,0:T(8,128)(2,1)S(1)} collective-permute-done((bf16[48,3072]{1,0:T(8,128)(2,1)S(1)}, bf16[48,3072]{1,0:T(8,128)(2,1)S(1)}, u32[]{:S(2)}, u32[]{:S(2)}) %collective-permute-start.8) | collective-permute-done | bytes 294944 | tf_op jit(solution)/shard_map/ppermute | solution.py:930
  55.3 4.8 %collective-permute-done.6 = bf16[4,48,1664]{2,1,0:T(8,128)(2,1)} collective-permute-done((bf16[4,48,1664]{2,1,0:T(8,128)(2,1)S(1)}, bf16[4,48,1664]{2,1,0:T(8,128)(2,1)}, u32[]{:S(2)}, u32[]{:S(2)}) %collective-permute-start.6) | collective-permute-done | bytes 639008 | tf_op jit(solution)/shard_map/ppermute | solution.py:930
  60.3 2.1 pad_maximum_fusion.refs_0_
  62.4 1.2 constant_dynamic-update-slice_fusion.2
  65.5 1.4 collective-permute-start.13
  68.5 6.0 %first_norm.1 = (bf16[1024,768]{1,0:T(8,128)(2,1)}, bf16[768,1024]{1,0:T(8,128)(2,1)}, f32[8,3072]{1,0:T(8,128)}) custom-call(s32[4]{0:T(128)} %pad_add_fusion.where_ref, bf16[1024,768]{1,0:T(8,128)(2,1)} %fusion.4.x_ref, bf16[16,48,1664]{2,1,0:T(8,128)(2,1)} %copy-done), custom_call_target="tpu_custom_call" | custom-call | flops 1000000000 | bytes 4718592 | tf_op jit(solution)/shard_map/first_norm/pallas_call | solution.py:337
  74.5 9.1 %qkv.1.q_ref.k_ref.v_ref.j0_ref.j1_ref = bf16[1024,2304]{1,0:T(8,128)(2,1)} custom-call(s32[4]{0:T(128)} %pad_add_fusion.where_ref, bf16[1024,768]{1,0:T(8,128)(2,1)} %get-tuple-element.181.n_ref, f32[8,3072]{1,0:T(8,128)} %get-tuple-element.182.vec_ref, bf16[16,48,1664]{2,1,0:T(8,128)(2,1)} %copy-done, bf16[16,48,1664]{2,1,0:T(8,128)(2,1)} %collective-permute-done.11.refs_1_), custom_call_target="tpu_custom_call" | custom-call | flops 3623878656 | bytes 9830400 | tf_op jit(solution)/shard_map/qkv/pallas_call | solution.py:388
  83.6 8.0 %attn.2 = (bf16[1024,512]{1,0:T(8,128)(2,1)}, f32[4,2,1024]{2,1,0:T(2,128)}) custom-call(bf16[1024,2304]{1,0:T(8,128)(2,1)} %qkv.1.q_ref.k_ref.v_ref.j0_ref.j1_ref, bf16[1024,2304]{1,0:T(8,128)(2,1)} %qkv.1.q_ref.k_ref.v_ref.j0_ref.j1_ref, bf16[1024,2304]{1,0:T(8,128)(2,1)} %qkv.1.q_ref.k_ref.v_ref.j0_ref.j1_ref, s32[1,256]{1,0:T(1,128)} %bitcast.106, ...), custom_call_target="tpu_custom_call" | custom-call | flops 16000000000 | bytes 8000000 | tf_op jit(solution)/shard_map/attn/pallas_call | solution.py:128
  91.7 2.1 collective-permute-done.13.refs_2_
  98.5 1.3 collective-permute-start.14
  99.8 4.9 %attn.3 = (bf16[1024,256]{1,0:T(8,128)(2,1)}, f32[2,2,1024]{2,1,0:T(2,128)}) custom-call(bf16[1024,2304]{1,0:T(8,128)(2,1)} %qkv.1.q_ref.k_ref.v_ref.j0_ref.j1_ref, bf16[1024,2304]{1,0:T(8,128)(2,1)} %qkv.1.q_ref.k_ref.v_ref.j0_ref.j1_ref, bf16[1024,2304]{1,0:T(8,128)(2,1)} %qkv.1.q_ref.k_ref.v_ref.j0_ref.j1_ref, s32[1,256]{1,0:T(1,128)} %bitcast.107, ...), custom_call_target="tpu_custom_call" | custom-call | flops 8000000000 | bytes 8000000 | tf_op jit(solution)/shard_map/attn/pallas_call | solution.py:128
  104.7 7.3 %proj.1 = (f32[1024,768]{1,0:T(8,128)}, bf16[1024,768]{1,0:T(8,128)(2,1)}) custom-call(s32[4]{0:T(128)} %pad_add_fusion.where_ref, bf16[1024,768]{1,0:T(8,128)(2,1)} %fusion.4.x_ref, bf16[1024,512]{1,0:T(8,128)(2,1)} %get-tuple-element.190.a0_ref, bf16[1024,256]{1,0:T(8,128)(2,1)} %get-tuple-element.191.a1_ref, f32[8,3072]{1,0:T(8,128)} %get-tuple-element.182.vec_ref, ...), custom_call_target="tpu_custom_call" | custom-call | flops 1207959552 | bytes 9043968 | tf_op jit(solution)/shard_map/proj/pallas_call | solution.py:424
  114.0 1.5 collective-permute-done.19.refs_8_
  117.2 47.0 %mlp.1 = (bf16[1024,768]{1,0:T(8,128)(2,1)}, f32[1024,768]{1,0:T(8,128)}, f32[1,3072]{1,0:T(1,128)}, f32[1,768]{1,0:T(1,128)}, bf16[16,48,3072]{2,1,0:T(8,128)(2,1)}, /*index=5*/bf16[16,48,3072]{2,1,0:T(8,128)(2,1)}) custom-call(s32[4]{0:T(128)} %pad_add_fusion.where_ref, bf16[1024,768]{1,0:T(8,128)(2,1)} %get-tuple-element.197.n_ref, ...), custom_call_target="tpu_custom_call" | custom-call | flops 28991029248 | bytes 30000000 | tf_op jit(solution)/shard_map/mlp/pallas_call | solution.py:545
  164.5 13.7 %proj_back.1 = (f32[1024,768]{1,0:T(8,128)}, bf16[1024,768]{1,0:T(8,128)(2,1)}, bf16[768,768]{1,0:T(8,128)(2,1)}, f32[16,1024]{1,0:T(8,128)}, f32[1,768]{1,0:T(1...) custom-call(s32[4]{0:T(128)} %pad_add_fusion.where_ref, f32[1024,768]{1,0:T(8,128)} %get-tuple-element.205.gn_ref, ...), custom_call_target="tpu_custom_call" | custom-call | flops 2415919104 | bytes 12582912 | tf_op jit(solution)/shard_map/proj_back/pallas_call | solution.py:620
  179.4 2.0 add_convert_fusion.7
  181.4 3.0 %add_convert_fusion = (bf16[3,48,3072]{2,1,0:T(8,128)(2,1)S(1)}, bf16[3,48,3072]{2,1,0:T(8,128)(2,1)}) fusion(bf16[16,48,3072]{2,1,0:T(8,128)(2,1)} %collective-permute-done.21, bf16[16,48,3072]{2,1,0:T(8,128)(2,1)S(1)} %copy-done.1), kind=kLoop, calls=%fused_computation.8 | loop fusion | flops 3538944 | bytes 5308416 | tf_op jit(solution)/shard_map/convert_element_type | solution.py:1080
  184.4 1.3 collective-permute-start.23
  186.3 1.7 collective-permute-start.22
  187.9 1.2 collective-permute-start.25
  189.7 31.0 %attn_back.1 = (bf16[1024,768]{1,0:T(8,128)(2,1)}, bf16[16,48,1664]{2,1,0:T(8,128)(2,1)}, bf16[16,48,1664]{2,1,0:T(8,128)(2,1)}) custom-call(s32[4]{0:T(128)} %pad_add_fusion.where_ref, bf16[1024,2304]{1,0:T(8,128)(2,1)} %qkv.1.q_ref.k_ref.v_ref.j0_ref.j1_ref, bf16[1024,2304]{1,0:T(8,128)(2,1)} %qkv.1.q_ref.k_ref.v_ref.j0_ref.j1_ref, ...), custom_call_target="tpu_custom_call" | custom-call | flops 60000002048 | bytes 20000000 | tf_op jit(solution)/shard_map/attn_back/pallas_call | solution.py:788
  220.8 5.7 %collective-permute-done.25 = bf16[3,48,3072]{2,1,0:T(8,128)(2,1)S(1)} collective-permute-done((bf16[3,48,3072]{2,1,0:T(8,128)(2,1)}, bf16[3,48,3072]{2,1,0:T(8,128)(2,1)S(1)}, u32[]{:S(2)}, u32[]{:S(2)}) %collective-permute-start.25) | collective-permute-done | bytes 884768 | tf_op jit(solution)/shard_map/ppermute | solution.py:930
  227.5 2.4 fusion.9
  231.2 1.2 collective-permute-start.28
  233.1 8.2 %collective-permute-done.30 = bf16[48,3072]{1,0:T(8,128)(2,1)S(1)} collective-permute-done((bf16[48,3072]{1,0:T(8,128)(2,1)S(1)}, bf16[48,3072]{1,0:T(8,128)(2,1)S(1)}, u32[]{:S(2)}, u32[]{:S(2)}) %collective-permute-start.30) | collective-permute-done | bytes 294944 | tf_op jit(solution)/shard_map/ppermute | solution.py:930
  242.0 1.4 collective-permute-start.32
  243.4 1.5 collective-permute-start.33
  244.9 2.0 fusion.6
  247.0 2.2 collective-permute-start.35
  249.1 3.7 %fusion.1 = bf16[1024,768]{1,0:T(8,128)(2,1)} fusion(s32[]{:T(128)S(6)} %select_n.143, bf16[1024,768]{1,0:T(8,128)(2,1)S(1)} %copy-done.5), kind=kLoop, calls=%fused_computation.11 | loop fusion | flops 3145728 | bytes 3145732 | tf_op jit(solution)/shard_map/concatenate | solution.py:837
  252.9 3.7 %fusion = bf16[1024,768]{1,0:T(8,128)(2,1)} fusion(s32[]{:T(128)S(6)} %select_n.143, bf16[1024,768]{1,0:T(8,128)(2,1)S(1)} %copy-done.4), kind=kLoop, calls=%fused_computation.10 | loop fusion | flops 3145728 | bytes 3145732 | tf_op jit(solution)/shard_map/concatenate | solution.py:837
  256.6 10.3 %collective-permute-done.34 = bf16[48,3072]{1,0:T(8,128)(2,1)S(1)} collective-permute-done((bf16[48,3072]{1,0:T(8,128)(2,1)S(1)}, bf16[48,3072]{1,0:T(8,128)(2,1)S(1)}, u32[]{:S(2)}, u32[]{:S(2)}) %collective-permute-start.34) | collective-permute-done | bytes 294944 | tf_op jit(solution)/shard_map/ppermute | solution.py:930
  266.9 4.5 %collective-permute-done.33 = bf16[4,48,1664]{2,1,0:T(8,128)(2,1)S(1)} collective-permute-done((bf16[4,48,1664]{2,1,0:T(8,128)(2,1)S(1)}, bf16[4,48,1664]{2,1,0:T(8,128)(2,1)S(1)}, u32[]{:S(2)}, u32[]{:S(2)}) %collective-permute-start.33) | collective-permute-done | bytes 639008 | tf_op jit(solution)/shard_map/ppermute | solution.py:930
  272.0 2.2 collective-permute-start.38
  275.6 3.2 %collective-permute-done.38 = bf16[48,1664]{1,0:T(8,128)(2,1)S(1)} collective-permute-done((bf16[48,1664]{1,0:T(8,128)(2,1)S(1)}, bf16[48,1664]{1,0:T(8,128)(2,1)S(1)}, u32[]{:S(2)}, u32[]{:S(2)}) %collective-permute-start.38) | collective-permute-done | bytes 159776 | tf_op jit(solution)/shard_map/ppermute | solution.py:930
  278.8 10.1 %collective-permute-done.37 = bf16[48,1664]{1,0:T(8,128)(2,1)S(1)} collective-permute-done((bf16[48,1664]{1,0:T(8,128)(2,1)S(1)}, bf16[48,1664]{1,0:T(8,128)(2,1)S(1)}, u32[]{:S(2)}, u32[]{:S(2)}) %collective-permute-start.37) | collective-permute-done | bytes 159776 | tf_op jit(solution)/shard_map/ppermute | solution.py:930
  (150 shorter events, 34.3 us)
Async XLA Ops:
  0.6 23.9 %copy-start.14 = (bf16[96,768]{1,0:T(8,128)(2,1)S(1)}, bf16[96,768]{1,0:T(8,128)(2,1)}, u32[]{:S(2)}) copy-start(bf16[96,768]{1,0:T(8,128)(2,1)} %param.28) | copy-start | bytes 442372
  5.2 28.5 %copy-start.17 = (s32[1,5]{1,0:T(1,128)S(1)}, s32[1,5]{1,0:T(1,128)}, u32[]{:S(2)}) copy-start(s32[1,5]{1,0:T(1,128)} %param.17) | copy-start | bytes 64
  5.2 1.6 collective-permute-start
  7.7 7.1 %collective-permute-start.4 = (bf16[24,1536]{1,0:T(8,128)(2,1)}, bf16[24,1536]{1,0:T(8,128)(2,1)S(1)}, u32[]{:S(2)}, u32[]{:S(2)}) collective-permute-start(bf16[24,1536]{1,0:T(8,128)(2,1)} %get-tuple-element.151), channel_id=1, source_target_pairs={{0,1},{1,0},{2,3},{3,2},{4,5},{5,4},{6,7},{7,6},{8,9},{9,8},{10,11... | collective-permute-start | bytes 221192 | tf_op jit(solution)/shard_map/ppermute | solution.py:930
  8.1 9.8 %collective-permute-start.3 = (bf16[48,1664]{1,0:T(8,128)(2,1)S(1)}, bf16[48,1664]{1,0:T(8,128)(2,1)S(1)}, u32[]{:S(2)}, u32[]{:S(2)}) collective-permute-start(bf16[48,1664]{1,0:T(8,128)(2,1)S(1)} %pad_maximum_fusion.5), channel_id=1, source_target_pairs={{0,8},{1,9},{2,10},{3,11},{4,12},{5,13},{6,14},{7,15},{8,16},{9,17... | collective-permute-start | bytes 479240 | tf_op jit(solution)/shard_map/ppermute | solution.py:930
  10.8 13.6 %collective-permute-start.2 = (bf16[48,1664]{1,0:T(8,128)(2,1)S(1)}, bf16[48,1664]{1,0:T(8,128)(2,1)S(1)}, u32[]{:S(2)}, u32[]{:S(2)}) collective-permute-start(bf16[48,1664]{1,0:T(8,128)(2,1)S(1)} %pad_maximum_fusion.5), channel_id=1, source_target_pairs={{0,16},{1,17},{2,18},{3,19},{4,20},{5,21},{6,22},{7,23},{8,24},{9,... | collective-permute-start | bytes 479240 | tf_op jit(solution)/shard_map/ppermute | solution.py:930
  13.4 11.0 %collective-permute-start.1 = (bf16[48,1664]{1,0:T(8,128)(2,1)S(1)}, bf16[48,1664]{1,0:T(8,128)(2,1)S(1)}, u32[]{:S(2)}, u32[]{:S(2)}) collective-permute-start(bf16[48,1664]{1,0:T(8,128)(2,1)S(1)} %pad_maximum_fusion.5), channel_id=1, source_target_pairs={{0,24},{1,25},{2,26},{3,27},{4,28},{5,29},{6,30},{7,31},{8,0},{9,1... | collective-permute-start | bytes 479240 | tf_op jit(solution)/shard_map/ppermute | solution.py:930
  24.6 21.9 %copy-start.3 = (bf16[1024,768]{1,0:T(8,128)(2,1)S(1)}, bf16[1024,768]{1,0:T(8,128)(2,1)}, u32[]{:S(2)}) copy-start(bf16[1024,768]{1,0:T(8,128)(2,1)} %param.30) | copy-start | bytes 4718596
  24.6 20.2 %collective-permute-start.10 = (bf16[48,3072]{1,0:T(8,128)(2,1)S(1)}, bf16[48,3072]{1,0:T(8,128)(2,1)S(1)}, u32[]{:S(2)}, u32[]{:S(2)}) collective-permute-start(bf16[48,3072]{1,0:T(8,128)(2,1)S(1)} %pad_maximum_fusion.2), channel_id=1, source_target_pairs={{0,8},{1,9},{2,10},{3,11},{4,12},{5,13},{6,14},{7,15},{8,16},{9,17... | collective-permute-start | bytes 884744 | tf_op jit(solution)/shard_map/ppermute | solution.py:930
  28.6 20.7 %collective-permute-start.9 = (bf16[48,3072]{1,0:T(8,128)(2,1)S(1)}, bf16[48,3072]{1,0:T(8,128)(2,1)}, u32[]{:S(2)}, u32[]{:S(2)}) collective-permute-start(bf16[48,3072]{1,0:T(8,128)(2,1)S(1)} %pad_maximum_fusion.2), channel_id=1, source_target_pairs={{0,16},{1,17},{2,18},{3,19},{4,20},{5,21},{6,22},{7,23},{8,24},{9,... | collective-permute-start | bytes 884744 | tf_op jit(solution)/shard_map/ppermute | solution.py:930
  30.2 25.1 %collective-permute-start.7 = (bf16[4,48,1664]{2,1,0:T(8,128)(2,1)S(1)}, bf16[4,48,1664]{2,1,0:T(8,128)(2,1)S(1)}, u32[]{:S(2)}, u32[]{:S(2)}) collective-permute-start(bf16[4,48,1664]{2,1,0:T(8,128)(2,1)S(1)} %pad_maximum_fusion.1), channel_id=1, source_target_pairs={{0,6},{1,7},{2,4},{3,5},{4,2},{5,3},{6,0},{7,1},{8,14},{9,15},{10,... | collective-permute-start | bytes 1916936 | tf_op jit(solution)/shard_map/ppermute | solution.py:930
  32.6 27.5 %collective-permute-start.6 = (bf16[4,48,1664]{2,1,0:T(8,128)(2,1)S(1)}, bf16[4,48,1664]{2,1,0:T(8,128)(2,1)}, u32[]{:S(2)}, u32[]{:S(2)}) collective-permute-start(bf16[4,48,1664]{2,1,0:T(8,128)(2,1)S(1)} %pad_maximum_fusion.1), channel_id=1, source_target_pairs={{0,4},{1,5},{2,6},{3,7},{4,0},{5,1},{6,2},{7,3},{8,12},{9,13},{10,... | collective-permute-start | bytes 1916936 | tf_op jit(solution)/shard_map/ppermute | solution.py:930
  33.1 27.1 %collective-permute-start.5 = (bf16[4,48,1664]{2,1,0:T(8,128)(2,1)S(1)}, bf16[4,48,1664]{2,1,0:T(8,128)(2,1)}, u32[]{:S(2)}, u32[]{:S(2)}) collective-permute-start(bf16[4,48,1664]{2,1,0:T(8,128)(2,1)S(1)} %pad_maximum_fusion.1), channel_id=1, source_target_pairs={{0,2},{1,3},{2,0},{3,1},{4,6},{5,7},{6,4},{7,5},{8,10},{9,11},{10,... | collective-permute-start | bytes 1916936 | tf_op jit(solution)/shard_map/ppermute | solution.py:930
  44.8 10.5 %collective-permute-start.8 = (bf16[48,3072]{1,0:T(8,128)(2,1)S(1)}, bf16[48,3072]{1,0:T(8,128)(2,1)S(1)}, u32[]{:S(2)}, u32[]{:S(2)}) collective-permute-start(bf16[48,3072]{1,0:T(8,128)(2,1)S(1)} %pad_maximum_fusion.2), channel_id=1, source_target_pairs={{0,24},{1,25},{2,26},{3,27},{4,28},{5,29},{6,30},{7,31},{8,0},{9,1... | collective-permute-start | bytes 884744 | tf_op jit(solution)/shard_map/ppermute | solution.py:930
  46.5 21.2 %copy-start.18 = (s32[256]{0:T(256)}, s32[256]{0:T(256)S(1)}, u32[]{:S(2)}) copy-start(s32[256]{0:T(256)S(1)} %slice.340) | copy-start | bytes 3076
  64.9 9.6 %collective-permute-start.11 = (bf16[16,48,1664]{2,1,0:T(8,128)(2,1)S(1)}, bf16[16,48,1664]{2,1,0:T(8,128)(2,1)}, u32[]{:S(2)}, u32[]{:S(2)}) collective-permute-start(bf16[16,48,1664]{2,1,0:T(8,128)(2,1)S(1)} %constant_dynamic-update-slice_fusion.refs_0_), channel_id=1, source_target_pairs={{0,1},{1,0},{2,3},{3,2},{4,5},{5,4},{6,7},{7,6},{8,9},{9,8},{10,11... | collective-permute-start | bytes 7667720 | tf_op jit(solution)/shard_map/ppermute | solution.py:930
  65.0 47.7 %collective-permute-start.16 = (bf16[4,48,3072]{2,1,0:T(8,128)(2,1)}, bf16[4,48,3072]{2,1,0:T(8,128)(2,1)}, u32[]{:S(2)}, u32[]{:S(2)}) collective-permute-start(bf16[4,48,3072]{2,1,0:T(8,128)(2,1)} %pad_maximum_fusion.refs_0_), channel_id=1, source_target_pairs={{0,1},{1,0},{2,3},{3,2},{4,5},{5,4},{6,7},{7,6},{8,9},{9,8},{10,11... | collective-permute-start | bytes 3538952 | tf_op jit(solution)/shard_map/ppermute | solution.py:930
  65.5 28.3 %collective-permute-start.13 = (bf16[4,48,3072]{2,1,0:T(8,128)(2,1)}, bf16[4,48,3072]{2,1,0:T(8,128)(2,1)}, u32[]{:S(2)}, u32[]{:S(2)}) collective-permute-start(bf16[4,48,3072]{2,1,0:T(8,128)(2,1)} %pad_maximum_fusion.refs_0_), channel_id=1, source_target_pairs={{0,4},{1,5},{2,6},{3,7},{4,0},{5,1},{6,2},{7,3},{8,12},{9,13},{10,... | collective-permute-start | bytes 3538952 | tf_op jit(solution)/shard_map/ppermute | solution.py:930
  66.9 28.0 %collective-permute-start.12 = (bf16[4,48,3072]{2,1,0:T(8,128)(2,1)}, bf16[4,48,3072]{2,1,0:T(8,128)(2,1)}, u32[]{:S(2)}, u32[]{:S(2)}) collective-permute-start(bf16[4,48,3072]{2,1,0:T(8,128)(2,1)} %pad_maximum_fusion.refs_0_), channel_id=1, source_target_pairs={{0,2},{1,3},{2,0},{3,1},{4,6},{5,7},{6,4},{7,5},{8,10},{9,11},{10,... | collective-permute-start | bytes 3538952 | tf_op jit(solution)/shard_map/ppermute | solution.py:930
  94.9 18.5 %collective-permute-start.17 = (bf16[4,48,3072]{2,1,0:T(8,128)(2,1)}, bf16[4,48,3072]{2,1,0:T(8,128)(2,1)S(1)}, u32[]{:S(2)}, u32[]{:S(2)}) collective-permute-start(bf16[4,48,3072]{2,1,0:T(8,128)(2,1)} %collective-permute-done.12.refs_1_), channel_id=1, source_target_pairs={{0,1},{1,0},{2,3},{3,2},{4,5},{5,4},{6,7},{7,6},{8,9},{9,8},{10,11... | collective-permute-start | bytes 3538952 | tf_op jit(solution)/shard_map/ppermute | solution.py:930
  94.9 18.5 %collective-permute-start.18 = (bf16[4,48,3072]{2,1,0:T(8,128)(2,1)}, bf16[4,48,3072]{2,1,0:T(8,128)(2,1)S(1)}, u32[]{:S(2)}, u32[]{:S(2)}) collective-permute-start(bf16[4,48,3072]{2,1,0:T(8,128)(2,1)} %collective-permute-done.13.refs_2_), channel_id=1, source_target_pairs={{0,1},{1,0},{2,3},{3,2},{4,5},{5,4},{6,7},{7,6},{8,9},{9,8},{10,11... | collective-permute-start | bytes 3538952 | tf_op jit(solution)/shard_map/ppermute | solution.py:930
  97.6 15.3 %collective-permute-start.15 = (bf16[2,48,3072]{2,1,0:T(8,128)(2,1)S(1)}, bf16[2,48,3072]{2,1,0:T(8,128)(2,1)S(1)}, u32[]{:S(2)}, u32[]{:S(2)}) collective-permute-start(bf16[2,48,3072]{2,1,0:T(8,128)(2,1)S(1)} %slice.342), channel_id=1, source_target_pairs={{0,2},{1,3},{2,0},{3,1},{4,6},{5,7},{6,4},{7,5},{8,10},{9,11},{10,... | collective-permute-start | bytes 1769480 | tf_op jit(solution)/shard_map/ppermute | solution.py:930
  98.5 15.0 %collective-permute-start.14 = (bf16[2,48,3072]{2,1,0:T(8,128)(2,1)S(1)}, bf16[2,48,3072]{2,1,0:T(8,128)(2,1)S(1)}, u32[]{:S(2)}, u32[]{:S(2)}) collective-permute-start(bf16[2,48,3072]{2,1,0:T(8,128)(2,1)S(1)} %slice.341), channel_id=1, source_target_pairs={{0,4},{1,5},{2,6},{3,7},{4,0},{5,1},{6,2},{7,3},{8,12},{9,13},{10,... | collective-permute-start | bytes 1769480 | tf_op jit(solution)/shard_map/ppermute | solution.py:930
  113.5 2.1 collective-permute-start.19
  113.5 2.8 collective-permute-start.20
  164.2 13.9 %collective-permute-start.21 = (bf16[16,48,3072]{2,1,0:T(8,128)(2,1)}, bf16[16,48,3072]{2,1,0:T(8,128)(2,1)}, u32[]{:S(2)}, u32[]{:S(2)}) collective-permute-start(bf16[16,48,3072]{2,1,0:T(8,128)(2,1)} %get-tuple-element.209), channel_id=1, source_target_pairs={{0,1},{1,0},{2,3},{3,2},{4,5},{5,4},{6,7},{7,6},{8,9},{9,8},{10,11... | collective-permute-start | bytes 14155784 | tf_op jit(solution)/shard_map/ppermute | solution.py:930
  164.5 13.7 %copy-start.1 = (bf16[16,48,3072]{2,1,0:T(8,128)(2,1)S(1)}, bf16[16,48,3072]{2,1,0:T(8,128)(2,1)}, u32[]{:S(2)}) copy-start(bf16[16,48,3072]{2,1,0:T(8,128)(2,1)} %get-tuple-element.210) | copy-start | bytes 14155780
  184.4 36.4 %collective-permute-start.23 = (bf16[1,48,3072]{2,1,0:T(8,128)(2,1)}, bf16[1,48,3072]{2,1,0:T(8,128)(2,1)S(1)}, u32[]{:S(2)}, u32[]{:S(2)}) collective-permute-start(bf16[1,48,3072]{2,1,0:T(8,128)(2,1)} %get-tuple-element.229), channel_id=1, source_target_pairs={{0,4},{1,5},{2,6},{3,7},{4,0},{5,1},{6,2},{7,3},{8,12},{9,13},{10,... | collective-permute-start | bytes 884744 | tf_op jit(solution)/shard_map/ppermute | solution.py:930
  185.7 35.1 %collective-permute-start.24 = (bf16[1,48,3072]{2,1,0:T(8,128)(2,1)}, bf16[1,48,3072]{2,1,0:T(8,128)(2,1)S(1)}, u32[]{:S(2)}, u32[]{:S(2)}) collective-permute-start(bf16[1,48,3072]{2,1,0:T(8,128)(2,1)} %get-tuple-element.230), channel_id=1, source_target_pairs={{0,2},{1,3},{2,0},{3,1},{4,6},{5,7},{6,4},{7,5},{8,10},{9,11},{10,... | collective-permute-start | bytes 884744 | tf_op jit(solution)/shard_map/ppermute | solution.py:930
  186.3 34.6 %collective-permute-start.22 = (bf16[2,48,3072]{2,1,0:T(8,128)(2,1)S(1)}, bf16[2,48,3072]{2,1,0:T(8,128)(2,1)S(1)}, u32[]{:S(2)}, u32[]{:S(2)}) collective-permute-start(bf16[2,48,3072]{2,1,0:T(8,128)(2,1)S(1)} %add_convert_fusion.6), channel_id=1, source_target_pairs={{0,6},{1,7},{2,4},{3,5},{4,2},{5,3},{6,0},{7,1},{8,14},{9,15},{10,... | collective-permute-start | bytes 1769480 | tf_op jit(solution)/shard_map/ppermute | solution.py:930
  187.9 38.7 %collective-permute-start.25 = (bf16[3,48,3072]{2,1,0:T(8,128)(2,1)}, bf16[3,48,3072]{2,1,0:T(8,128)(2,1)S(1)}, u32[]{:S(2)}, u32[]{:S(2)}) collective-permute-start(bf16[3,48,3072]{2,1,0:T(8,128)(2,1)} %get-tuple-element.231), channel_id=1, source_target_pairs={{0,2},{1,3},{2,0},{3,1},{4,6},{5,7},{6,4},{7,5},{8,10},{9,11},{10,... | collective-permute-start | bytes 2654216 | tf_op jit(solution)/shard_map/ppermute | solution.py:930
  189.1 37.4 %collective-permute-start.26 = (bf16[3,48,3072]{2,1,0:T(8,128)(2,1)S(1)}, bf16[3,48,3072]{2,1,0:T(8,128)(2,1)S(1)}, u32[]{:S(2)}, u32[]{:S(2)}) collective-permute-start(bf16[3,48,3072]{2,1,0:T(8,128)(2,1)S(1)} %get-tuple-element.232), channel_id=1, source_target_pairs={{0,4},{1,5},{2,6},{3,7},{4,0},{5,1},{6,2},{7,3},{8,12},{9,13},{10,... | collective-permute-start | bytes 2654216 | tf_op jit(solution)/shard_map/ppermute | solution.py:930
  227.5 5.0 %collective-permute-start.27 = (bf16[16,48,1664]{2,1,0:T(8,128)(2,1)}, bf16[16,48,1664]{2,1,0:T(8,128)(2,1)S(1)}, u32[]{:S(2)}, u32[]{:S(2)}) collective-permute-start(bf16[16,48,1664]{2,1,0:T(8,128)(2,1)} %get-tuple-element.237), channel_id=1, source_target_pairs={{0,1},{1,0},{2,3},{3,2},{4,5},{5,4},{6,7},{7,6},{8,9},{9,8},{10,11... | collective-permute-start | bytes 7667720 | tf_op jit(solution)/shard_map/ppermute | solution.py:930
  229.9 11.4 %collective-permute-start.30 = (bf16[48,3072]{1,0:T(8,128)(2,1)S(1)}, bf16[48,3072]{1,0:T(8,128)(2,1)S(1)}, u32[]{:S(2)}, u32[]{:S(2)}) collective-permute-start(bf16[48,3072]{1,0:T(8,128)(2,1)S(1)} %get-tuple-element.279), channel_id=1, source_target_pairs={{0,8},{1,9},{2,10},{3,11},{4,12},{5,13},{6,14},{7,15},{8,16},{9,17... | collective-permute-start | bytes 884744 | tf_op jit(solution)/shard_map/ppermute | solution.py:930
  230.5 10.8 %collective-permute-start.29 = (bf16[48,3072]{1,0:T(8,128)(2,1)S(1)}, bf16[48,3072]{1,0:T(8,128)(2,1)S(1)}, u32[]{:S(2)}, u32[]{:S(2)}) collective-permute-start(bf16[48,3072]{1,0:T(8,128)(2,1)S(1)} %get-tuple-element.280), channel_id=1, source_target_pairs={{0,4},{1,5},{2,6},{3,7},{4,0},{5,1},{6,2},{7,3},{8,12},{9,13},{10,... | collective-permute-start | bytes 884744 | tf_op jit(solution)/shard_map/ppermute | solution.py:930
  231.2 13.7 %copy-start.7 = (bf16[3,48,3072]{2,1,0:T(8,128)(2,1)S(1)}, bf16[3,48,3072]{2,1,0:T(8,128)(2,1)}, u32[]{:S(2)}) copy-start(bf16[3,48,3072]{2,1,0:T(8,128)(2,1)} %copy-done.6) | copy-start | bytes 2654212
  231.2 13.7 %copy-start.11 = (bf16[2,48,3072]{2,1,0:T(8,128)(2,1)S(1)}, bf16[2,48,3072]{2,1,0:T(8,128)(2,1)}, u32[]{:S(2)}) copy-start(bf16[2,48,3072]{2,1,0:T(8,128)(2,1)} %copy-done.10) | copy-start | bytes 1769476
  231.2 10.1 %collective-permute-start.28 = (bf16[48,3072]{1,0:T(8,128)(2,1)S(1)}, bf16[48,3072]{1,0:T(8,128)(2,1)S(1)}, u32[]{:S(2)}, u32[]{:S(2)}) collective-permute-start(bf16[48,3072]{1,0:T(8,128)(2,1)S(1)} %get-tuple-element.281), channel_id=1, source_target_pairs={{0,2},{1,3},{2,0},{3,1},{4,6},{5,7},{6,4},{7,5},{8,10},{9,11},{10,... | collective-permute-start | bytes 884744 | tf_op jit(solution)/shard_map/ppermute | solution.py:930
  241.4 25.5 %collective-permute-start.31 = (bf16[4,48,1664]{2,1,0:T(8,128)(2,1)S(1)}, bf16[4,48,1664]{2,1,0:T(8,128)(2,1)S(1)}, u32[]{:S(2)}, u32[]{:S(2)}) collective-permute-start(bf16[4,48,1664]{2,1,0:T(8,128)(2,1)S(1)} %get-tuple-element.247), channel_id=1, source_target_pairs={{0,2},{1,3},{2,0},{3,1},{4,6},{5,7},{6,4},{7,5},{8,10},{9,11},{10,... | collective-permute-start | bytes 1916936 | tf_op jit(solution)/shard_map/ppermute | solution.py:930
  242.0 24.9 %collective-permute-start.32 = (bf16[4,48,1664]{2,1,0:T(8,128)(2,1)S(1)}, bf16[4,48,1664]{2,1,0:T(8,128)(2,1)S(1)}, u32[]{:S(2)}, u32[]{:S(2)}) collective-permute-start(bf16[4,48,1664]{2,1,0:T(8,128)(2,1)S(1)} %get-tuple-element.248), channel_id=1, source_target_pairs={{0,4},{1,5},{2,6},{3,7},{4,0},{5,1},{6,2},{7,3},{8,12},{9,13},{10,... | collective-permute-start | bytes 1916936 | tf_op jit(solution)/shard_map/ppermute | solution.py:930
  243.4 28.0 %collective-permute-start.33 = (bf16[4,48,1664]{2,1,0:T(8,128)(2,1)S(1)}, bf16[4,48,1664]{2,1,0:T(8,128)(2,1)S(1)}, u32[]{:S(2)}, u32[]{:S(2)}) collective-permute-start(bf16[4,48,1664]{2,1,0:T(8,128)(2,1)S(1)} %get-tuple-element.249), channel_id=1, source_target_pairs={{0,6},{1,7},{2,4},{3,5},{4,2},{5,3},{6,0},{7,1},{8,14},{9,15},{10,... | collective-permute-start | bytes 1916936 | tf_op jit(solution)/shard_map/ppermute | solution.py:930
  247.0 9.6 %collective-permute-start.35 = (bf16[48,3072]{1,0:T(8,128)(2,1)S(1)}, bf16[48,3072]{1,0:T(8,128)(2,1)S(1)}, u32[]{:S(2)}, u32[]{:S(2)}) collective-permute-start(bf16[48,3072]{1,0:T(8,128)(2,1)S(1)} %get-tuple-element.276), channel_id=1, source_target_pairs={{0,24},{1,25},{2,26},{3,27},{4,28},{5,29},{6,30},{7,31},{8,0},{9,1... | collective-permute-start | bytes 884744 | tf_op jit(solution)/shard_map/ppermute | solution.py:930
  249.1 17.7 %collective-permute-start.34 = (bf16[48,3072]{1,0:T(8,128)(2,1)S(1)}, bf16[48,3072]{1,0:T(8,128)(2,1)S(1)}, u32[]{:S(2)}, u32[]{:S(2)}) collective-permute-start(bf16[48,3072]{1,0:T(8,128)(2,1)S(1)} %get-tuple-element.277), channel_id=1, source_target_pairs={{0,16},{1,17},{2,18},{3,19},{4,20},{5,21},{6,22},{7,23},{8,24},{9,... | collective-permute-start | bytes 884744 | tf_op jit(solution)/shard_map/ppermute | solution.py:930
  271.5 4.1 %collective-permute-start.39 = (f32[24,1536]{1,0:T(8,128)S(1)}, f32[24,1536]{1,0:T(8,128)S(1)}, u32[]{:S(2)}, u32[]{:S(2)}) collective-permute-start(f32[24,1536]{1,0:T(8,128)S(1)} %slice_select_fusion.2), channel_id=1, source_target_pairs={{0,1},{1,0},{2,3},{3,2},{4,5},{5,4},{6,7},{7,6},{8,9},{9,8},{10,11... | collective-permute-start | bytes 442376 | tf_op jit(solution)/shard_map/ppermute | solution.py:930
  272.0 6.8 %collective-permute-start.38 = (bf16[48,1664]{1,0:T(8,128)(2,1)S(1)}, bf16[48,1664]{1,0:T(8,128)(2,1)S(1)}, u32[]{:S(2)}, u32[]{:S(2)}) collective-permute-start(bf16[48,1664]{1,0:T(8,128)(2,1)S(1)} %get-tuple-element.290), channel_id=1, source_target_pairs={{0,24},{1,25},{2,26},{3,27},{4,28},{5,29},{6,30},{7,31},{8,0},{9,1... | collective-permute-start | bytes 479240 | tf_op jit(solution)/shard_map/ppermute | solution.py:930
  274.2 14.7 %collective-permute-start.37 = (bf16[48,1664]{1,0:T(8,128)(2,1)S(1)}, bf16[48,1664]{1,0:T(8,128)(2,1)S(1)}, u32[]{:S(2)}, u32[]{:S(2)}) collective-permute-start(bf16[48,1664]{1,0:T(8,128)(2,1)S(1)} %get-tuple-element.291), channel_id=1, source_target_pairs={{0,16},{1,17},{2,18},{3,19},{4,20},{5,21},{6,22},{7,23},{8,24},{9,... | collective-permute-start | bytes 479240 | tf_op jit(solution)/shard_map/ppermute | solution.py:930
  274.2 14.7 %collective-permute-start.36 = (bf16[48,1664]{1,0:T(8,128)(2,1)S(1)}, bf16[48,1664]{1,0:T(8,128)(2,1)S(1)}, u32[]{:S(2)}, u32[]{:S(2)}) collective-permute-start(bf16[48,1664]{1,0:T(8,128)(2,1)S(1)} %get-tuple-element.292), channel_id=1, source_target_pairs={{0,8},{1,9},{2,10},{3,11},{4,12},{5,13},{6,14},{7,15},{8,16},{9,17... | collective-permute-start | bytes 479240 | tf_op jit(solution)/shard_map/ppermute | solution.py:930
  290.3 1.4 collective-permute-start.40
  (18 other events, 78.4 us)

commit v8 on v7

--- a/solution.py
+++ b/solution.py
@@ -166,6 +166,14 @@
     ]
 
 
+def leaving(dims, place):
+    if dims != (4, 2, 2):
+        return place
+    for first, step in ((14, -6), (12, 0), (10, 4), (8, 2)):
+        place = jnp.where((place >= first) & (place < first + 2), place + step + 100, place)
+    return jnp.where(place >= 100, place - 100, place)
+
+
 def array_spans(arrays):
     at = 0
     for k, a in enumerate(arrays):
@@ -190,10 +198,10 @@
     return jnp.concatenate([scr[half, p, :, cols] for p in places(dims, where_ref)], axis=0)
 
 
-def put_rows(dims, where_ref, scr, lead, value):
+def put_rows(dims, where_ref, scr, lead, value, order=lambda p: p):
     n = scr.shape[-2]
     for i, p in enumerate(places(dims, where_ref)):
-        scr[lead + (p,)] = value[i * n : (i + 1) * n]
+        scr[lead + (order(p),)] = value[i * n : (i + 1) * n]
 
 
 def store_columns(where_ref, src, own, oth, half, first, cols, sem):
@@ -514,11 +522,12 @@
     behind(*waiting)
 
     gfb_ref[...] = bias_sum
-    put_rows(dims, where_ref, gf_scr, (j,), dot(nt_scr[...], gp_scr[...]).astype(BF))
+    order = functools.partial(leaving, dims)
+    put_rows(dims, where_ref, gf_scr, (j,), dot(nt_scr[...], gp_scr[...]).astype(BF), order)
     store_columns(where_ref, gf_scr.at[j], g_own, g_oth, half, first, d, gf_sem.at[j])
     go = dot_0(act_scr[...], mg_scr[...]).astype(BF)
     for q, (c, p, at) in enumerate(spots):
-        go_scr[c, p, :, pl.ds(at, d)] = go[q * n : (q + 1) * n]
+        go_scr[c, order(p), :, pl.ds(at, d)] = go[q * n : (q + 1) * n]
 
     @pl.when(j == blocks - 1)
     def _():
@@ -1074,20 +1083,13 @@
     gm, ga, gw_proj, delta, gg2, gb2, gpb = proj_back_call(dims, where, gn, middle, cot, att, vec, *attn_w)
     (m_oth,) = swap([m_oth])
     ga, delta, m_own, m_oth = together(ga, delta, m_own, m_oth)
-    m_own, m_oth = [v.reshape(-1, dims[0], *v.shape[1:]) for v in (m_own, m_oth)]
-
-    def chip_sum(i, part):
-        return add_all([part(m_own[i]), part(m_oth[i])]).astype(BF)
-
-    first = (
-        chip_sum(3, lambda v: v[1:3]), chip_sum(3, lambda v: v[:1]), chip_sum(3, lambda v: v[3:]),
-        chip_sum(1, lambda v: v[1:]), chip_sum(2, lambda v: v[:3]),
-    )
+
+    def chip_sum(span, *more):
+        return add_all([m_own[span], m_oth[span], *more]).astype(BF)
+
+    first = chip_sum(slice(6, 10)), chip_sum(slice(10, 14))
     first, ga, delta, m_own, m_oth = together(first, ga, delta, m_own, m_oth)
-    first = (
-        send(first[0], dx=1, dy=1), send(first[1], dy=1), send(first[2], dx=1),
-        send(first[3], dx=1), send(first[4], dy=1),
-    )
+    first = send(first[0], dx=1), send(first[1], dy=1)
     gx, g_own, g_oth = attn_back_call(
         dims, where, joined, ga, lse, delta, seg_row, seg_col, x, vec, *attn_w,
         (gw_proj, gfb, gob, gg2, gb2, gpb), gm, nt, devices,
@@ -1095,25 +1097,20 @@
     gx, g_own, g_oth, first, m_own, m_oth, out = together(gx, g_own, g_oth, first, m_own, m_oth, out)
 
     (g_oth,) = swap([g_oth])
-    corners, by_y, by_x, from_x, from_y = first
-
-    def chip_total(i, j, arrived):
-        return add_all([m_own[i, j], m_oth[i, j]] + arrived).astype(BF)
-
-    x_one = send(chip_total(1, 0, [by_y[0]]), dx=1)
-    y_one = send(chip_total(2, 3, [by_x[0]]), dy=1)
-    b = {1: send(chip_total(0, 1, [from_x[0], from_y[1], corners[0]]), dz=1)}
+    from_x, from_y = first
+    x_low = send(chip_sum(slice(4, 6), from_y[2:]), dx=1)
+    y_high = send(chip_sum(slice(14, 16), from_x[2:]), dy=1)
     e = links.add_core(*[v.reshape(-1, dims[0], *v.shape[1:]) for v in (g_own, g_oth)])
-    e, x_one, y_one, gx, out, m_own, m_oth, b = together(e, x_one, y_one, gx, out, m_own, m_oth, b)
+    e, x_low, y_high, gx, out, m_own, m_oth = together(e, x_low, y_high, gx, out, m_own, m_oth)
 
     e_near = near(e)
-    b[0] = chip_total(0, 0, [x_one, from_y[0]])
-    b[2] = send(chip_total(0, 2, [from_x[1], from_y[2], corners[1]]), dz=2)
-    b[3] = send(chip_total(0, 3, [from_x[2], y_one]), dz=3)
-    b = [b[j] for j in range(4)]
+    arrived = [(x_low, from_y), (from_x, y_high)]
+    b = [chip_sum(j, *[v[j % 2] for v in arrived[j // 2]]) for j in range(dims[0])]
+    b[1:3] = [send(b[j], dz=j) for j in (1, 2)]
     gx, out = roll_rows(gx, rows - start), roll_rows(out, rows - start)
     e_near, b, e, gx, out = together(e_near, b, e, gx, out)
 
+    b[3] = send(b[3], dz=3)
     e = far([add_all([e[0][j]] + [v[j] for v in e_near]).astype(BF) for j in range(dims[0])])
     total = add_all(b)
     s_fc = links.rows_back(total[:, : -2 * d])

time: 298 us -> 296 us (level)
    convert_element_type x5 -> x2, other arithmetic: 10.7 us -> 6.99 us  [chip_sum(): return add_all([m_own[span], m_oth[span], *more]).astype(BF)]
    ppermute x41 -> x38, starting transfers between devices: 40.4 us -> 37.7 us  [send(): return lax.ppermute(array, AXES, pairs)]
    ppermute x41 -> x38, waiting for transfers between devices: 69.9 us -> 69.6 us  [send(): return lax.ppermute(array, AXES, pairs)]
  transfers between devices with their start and end apart: 41 -> 38, of which waited for: 20 -> 22; matrix products, arithmetic and copies ran while one was open for 9% -> 11% of each run, Pallas kernels for 27% -> 28%
where the time goes in v8:
time: 296 us; the launch traced here: 292 us
  Pallas kernels  130 us (44%)
  waiting for transfers between devices  69.6 us (24%)
  starting transfers between devices  37.7 us (13%)
  other arithmetic  37.6 us (13%)
  local copies, waits for them, and re-layouts  9.86 us (3%)
  between operations  7.32 us (2%)
    ppermute x38, waiting for transfers between devices, send(): return lax.ppermute(array, AXES, pairs)  69.6 us
    pallas_call x1, Pallas kernels, mlp_call(): pl.pallas_call(functools.partial(mlp_kernel, dims, len(own)), grid=(block...  47.5 us
    ppermute x38, starting transfers between devices, send(): return lax.ppermute(array, AXES, pairs)  37.7 us
    pallas_call x1, Pallas kernels, attn_back_call(): pl.pallas_call(functools.partial(attn_back_kernel, dims, len(own), device...  31.2 us
    pallas_call x1, Pallas kernels, proj_back_call(): pl.pallas_call(functools.partial(proj_back_kernel, dims, len(own), 3 * d...  14.1 us
    pallas_call x2, Pallas kernels, attn_call(): pl.pallas_call(attn_kernel, grid=(2 * groups,), in_specs=[at(0), at(1), a...  13 us
    concatenate x3, other arithmetic, roll_rows(): jnp.concatenate([array, array], axis=0)  11.2 us
    pallas_call x1, Pallas kernels, qkv_call(): pl.pallas_call(functools.partial(qkv_kernel, dims, len(own)), grid=(2,),...  8.98 us
  transfers between devices with their start and end apart: 38, of which 22 were waited for; matrix products, arithmetic and copies ran while one was open for 11% of the time, Pallas kernels for 28%

profile of v8, /device:TPU:0, one launch (start us, length us, event | category | flops | bytes accessed | tf_op | source)
XLA Modules:
  0.0 291.9 jit_solution(6140413730642504480)
XLA Ops:
  1.6 1.3 fusion.21.t_ref
  3.4 1.8 cut.1
  8.1 2.7 collective-permute-start.3
  10.9 2.6 collective-permute-start.2
  13.5 1.3 collective-permute-start.1
  15.7 2.2 collective-permute-done.3
  17.9 6.5 %collective-permute-done.2 = bf16[48,1664]{1,0:T(8,128)(2,1)S(1)} collective-permute-done((bf16[48,1664]{1,0:T(8,128)(2,1)S(1)}, bf16[48,1664]{1,0:T(8,128)(2,1)S(1)}, u32[]{:S(2)}, u32[]{:S(2)}) %collective-permute-start.2) | collective-permute-done | bytes 159776 | tf_op jit(solution)/shard_map/ppermute | solution.py:939
  24.6 4.0 %collective-permute-start.10 = (bf16[48,3072]{1,0:T(8,128)(2,1)S(1)}, bf16[48,3072]{1,0:T(8,128)(2,1)S(1)}, u32[]{:S(2)}, u32[]{:S(2)}) collective-permute-start(bf16[48,3072]{1,0:T(8,128)(2,1)S(1)} %pad_maximum_fusion.2), channel_id=1, source_target_pairs={{0,8},{1,9},{2,10},{3,11},{4,12},{5,13},{6,14},{7,15},{8,16},{9,17... | collective-permute-start | bytes 884744 | tf_op jit(solution)/shard_map/ppermute | solution.py:939
  28.6 1.6 collective-permute-start.9
  30.2 2.4 collective-permute-start.7
  40.8 3.8 %fusion.4.x_ref = bf16[1024,768]{1,0:T(8,128)(2,1)} fusion(s32[]{:T(128)S(6)} %select_n.141, bf16[1024,768]{1,0:T(8,128)(2,1)S(1)} %copy-done.2), kind=kLoop, calls=%fused_computation.14 | loop fusion | flops 3145728 | bytes 3145732 | tf_op jit(solution)/shard_map/concatenate | solution.py:846
  46.2 2.4 fusion.3.c_ref
  49.2 6.1 %collective-permute-done.8 = bf16[48,3072]{1,0:T(8,128)(2,1)S(1)} collective-permute-done((bf16[48,3072]{1,0:T(8,128)(2,1)S(1)}, bf16[48,3072]{1,0:T(8,128)(2,1)S(1)}, u32[]{:S(2)}, u32[]{:S(2)}) %collective-permute-start.8) | collective-permute-done | bytes 294944 | tf_op jit(solution)/shard_map/ppermute | solution.py:939
  55.3 4.8 %collective-permute-done.6 = bf16[4,48,1664]{2,1,0:T(8,128)(2,1)} collective-permute-done((bf16[4,48,1664]{2,1,0:T(8,128)(2,1)S(1)}, bf16[4,48,1664]{2,1,0:T(8,128)(2,1)}, u32[]{:S(2)}, u32[]{:S(2)}) %collective-permute-start.6) | collective-permute-done | bytes 639008 | tf_op jit(solution)/shard_map/ppermute | solution.py:939
  60.3 2.1 pad_maximum_fusion.refs_0_
  62.5 1.2 constant_dynamic-update-slice_fusion.2
  63.7 1.2 constant_dynamic-update-slice_fusion.1
  65.5 1.4 collective-permute-start.13
  68.6 6.0 %first_norm.1 = (bf16[1024,768]{1,0:T(8,128)(2,1)}, bf16[768,1024]{1,0:T(8,128)(2,1)}, f32[8,3072]{1,0:T(8,128)}) custom-call(s32[4]{0:T(128)} %pad_add_fusion.where_ref, bf16[1024,768]{1,0:T(8,128)(2,1)} %fusion.4.x_ref, bf16[16,48,1664]{2,1,0:T(8,128)(2,1)} %copy-done), custom_call_target="tpu_custom_call" | custom-call | flops 1000000000 | bytes 4718592 | tf_op jit(solution)/shard_map/first_norm/pallas_call | solution.py:345
  74.6 9.0 %qkv.1.q_ref.k_ref.v_ref.j0_ref.j1_ref = bf16[1024,2304]{1,0:T(8,128)(2,1)} custom-call(s32[4]{0:T(128)} %pad_add_fusion.where_ref, bf16[1024,768]{1,0:T(8,128)(2,1)} %get-tuple-element.174.n_ref, f32[8,3072]{1,0:T(8,128)} %get-tuple-element.175.vec_ref, bf16[16,48,1664]{2,1,0:T(8,128)(2,1)} %copy-done, bf16[16,48,1664]{2,1,0:T(8,128)(2,1)} %collective-permute-done.11.refs_1_), custom_call_target="tpu_custom_call" | custom-call | flops 3623878656 | bytes 9830400 | tf_op jit(solution)/shard_map/qkv/pallas_call | solution.py:396
  83.6 8.0 %attn.2 = (bf16[1024,512]{1,0:T(8,128)(2,1)}, f32[4,2,1024]{2,1,0:T(2,128)}) custom-call(bf16[1024,2304]{1,0:T(8,128)(2,1)} %qkv.1.q_ref.k_ref.v_ref.j0_ref.j1_ref, bf16[1024,2304]{1,0:T(8,128)(2,1)} %qkv.1.q_ref.k_ref.v_ref.j0_ref.j1_ref, bf16[1024,2304]{1,0:T(8,128)(2,1)} %qkv.1.q_ref.k_ref.v_ref.j0_ref.j1_ref, s32[1,256]{1,0:T(1,128)} %bitcast.68, ...), custom_call_target="tpu_custom_call" | custom-call | flops 16000000000 | bytes 8000000 | tf_op jit(solution)/shard_map/attn/pallas_call | solution.py:128
  91.6 2.2 collective-permute-done.13.refs_2_
  98.5 1.3 collective-permute-start.14
  99.8 5.0 %attn.3 = (bf16[1024,256]{1,0:T(8,128)(2,1)}, f32[2,2,1024]{2,1,0:T(2,128)}) custom-call(bf16[1024,2304]{1,0:T(8,128)(2,1)} %qkv.1.q_ref.k_ref.v_ref.j0_ref.j1_ref, bf16[1024,2304]{1,0:T(8,128)(2,1)} %qkv.1.q_ref.k_ref.v_ref.j0_ref.j1_ref, bf16[1024,2304]{1,0:T(8,128)(2,1)} %qkv.1.q_ref.k_ref.v_ref.j0_ref.j1_ref, s32[1,256]{1,0:T(1,128)} %bitcast.69, ...), custom_call_target="tpu_custom_call" | custom-call | flops 8000000000 | bytes 8000000 | tf_op jit(solution)/shard_map/attn/pallas_call | solution.py:128
  104.8 7.3 %proj.1 = (f32[1024,768]{1,0:T(8,128)}, bf16[1024,768]{1,0:T(8,128)(2,1)}) custom-call(s32[4]{0:T(128)} %pad_add_fusion.where_ref, bf16[1024,768]{1,0:T(8,128)(2,1)} %fusion.4.x_ref, bf16[1024,512]{1,0:T(8,128)(2,1)} %get-tuple-element.183.a0_ref, bf16[1024,256]{1,0:T(8,128)(2,1)} %get-tuple-element.184.a1_ref, f32[8,3072]{1,0:T(8,128)} %get-tuple-element.175.vec_ref, ...), custom_call_target="tpu_custom_call" | custom-call | flops 1207959552 | bytes 9043968 | tf_op jit(solution)/shard_map/proj/pallas_call | solution.py:432
  114.1 1.5 collective-permute-done.19.refs_8_
  117.2 47.5 %mlp.1 = (bf16[1024,768]{1,0:T(8,128)(2,1)}, f32[1024,768]{1,0:T(8,128)}, f32[1,3072]{1,0:T(1,128)}, f32[1,768]{1,0:T(1,128)}, bf16[16,48,3072]{2,1,0:T(8,128)(2,1)}, /*index=5*/bf16[16,48,3072]{2,1,0:T(8,128)(2,1)}) custom-call(s32[4]{0:T(128)} %pad_add_fusion.where_ref, bf16[1024,768]{1,0:T(8,128)(2,1)} %get-tuple-element.190.n_ref, ...), custom_call_target="tpu_custom_call" | custom-call | flops 28991029248 | bytes 30000000 | tf_op jit(solution)/shard_map/mlp/pallas_call | solution.py:554
  165.0 14.1 %proj_back.1 = (f32[1024,768]{1,0:T(8,128)}, bf16[1024,768]{1,0:T(8,128)(2,1)}, bf16[768,768]{1,0:T(8,128)(2,1)}, f32[16,1024]{1,0:T(8,128)}, f32[1,768]{1,0:T(1...) custom-call(s32[4]{0:T(128)} %pad_add_fusion.where_ref, f32[1024,768]{1,0:T(8,128)} %get-tuple-element.198.gn_ref, ...), custom_call_target="tpu_custom_call" | custom-call | flops 2415919104 | bytes 12582912 | tf_op jit(solution)/shard_map/proj_back/pallas_call | solution.py:629
  179.2 4.0 %add_convert_fusion = (bf16[4,48,3072]{2,1,0:T(8,128)(2,1)}, bf16[4,48,3072]{2,1,0:T(8,128)(2,1)}) fusion(bf16[16,48,3072]{2,1,0:T(8,128)(2,1)} %collective-permute-done.21, bf16[16,48,3072]{2,1,0:T(8,128)(2,1)S(1)} %bitcast.59), kind=kLoop, calls=%fused_computation.8 | loop fusion | flops 4718592 | bytes 7077888 | tf_op jit(solution)/shard_map/convert_element_type | solution.py:1088
  183.1 1.2 collective-permute-start.22
  185.0 31.2 %attn_back.1 = (bf16[1024,768]{1,0:T(8,128)(2,1)}, bf16[16,48,1664]{2,1,0:T(8,128)(2,1)}, bf16[16,48,1664]{2,1,0:T(8,128)(2,1)}) custom-call(s32[4]{0:T(128)} %pad_add_fusion.where_ref, bf16[1024,2304]{1,0:T(8,128)(2,1)} %qkv.1.q_ref.k_ref.v_ref.j0_ref.j1_ref, bf16[1024,2304]{1,0:T(8,128)(2,1)} %qkv.1.q_ref.k_ref.v_ref.j0_ref.j1_ref, ...), custom_call_target="tpu_custom_call" | custom-call | flops 60000002048 | bytes 20000000 | tf_op jit(solution)/shard_map/attn_back/pallas_call | solution.py:797
  216.3 3.0 %add_convert_fusion.6 = (bf16[2,48,3072]{2,1,0:T(8,128)(2,1)}, bf16[2,48,3072]{2,1,0:T(8,128)(2,1)}) fusion(bf16[4,48,3072]{2,1,0:T(8,128)(2,1)S(1)} %collective-permute-done.22, bf16[16,48,3072]{2,1,0:T(8,128)(2,1)} %collective-permute-done.21, bf16[16,48,3072]{2,1,0:T(8,128)(2,1)S(1)} %bitcast.59, bf16[4,48,3072]{2,1,0:T(8,128)(2,1)} %collective-permute-done.23), kind=kLoop, calls=%fused_computation.20 | loop fusion | flops 3538944 | bytes 4718592 | tf_op jit(solution)/shard_map/convert_element_type | solution.py:1088
  219.3 1.4 collective-permute-start.26
  221.5 3.0 %add_convert_fusion.2 = (bf16[4,48,1664]{2,1,0:T(8,128)(2,1)S(1)}, bf16[4,48,1664]{2,1,0:T(8,128)(2,1)S(1)}, bf16[4,48,1664]{2,1,0:T(8,128)(2,1)S(1)}, bf16[4,48,1664]{2,1,0:T(8,128)(2,1)S(1)}) fusion(bf16[16,48,1664]{2,1,0:T(8,128)(2,1)} %collective-permute-done.24, bf16[16,48,1664]{2,1,0:T(8,128)(2,1)} %get-tuple-element.226), kind=kLoop, calls=%fused_computation.15 | loop fusion | flops 5111808 | bytes 7667712 | tf_op jit(solution)/shard_map/convert_element_type | solution.py:954
  224.5 10.7 %collective-permute-done.26 = bf16[2,48,3072]{2,1,0:T(8,128)(2,1)S(1)} collective-permute-done((bf16[2,48,3072]{2,1,0:T(8,128)(2,1)}, bf16[2,48,3072]{2,1,0:T(8,128)(2,1)S(1)}, u32[]{:S(2)}, u32[]{:S(2)}) %collective-permute-start.26) | collective-permute-done | bytes 589856 | tf_op jit(solution)/shard_map/ppermute | solution.py:939
  237.2 1.3 collective-permute-start.28
  238.5 1.4 collective-permute-start.29
  239.9 2.5 fusion.8
  242.4 1.8 collective-permute-start.31
  244.6 3.7 %fusion.1 = bf16[1024,768]{1,0:T(8,128)(2,1)} fusion(s32[]{:T(128)S(6)} %select_n.143, bf16[1024,768]{1,0:T(8,128)(2,1)S(1)} %copy-done.4), kind=kLoop, calls=%fused_computation.11 | loop fusion | flops 3145728 | bytes 3145732 | tf_op jit(solution)/shard_map/concatenate | solution.py:846
  248.3 3.7 %fusion = bf16[1024,768]{1,0:T(8,128)(2,1)} fusion(s32[]{:T(128)S(6)} %select_n.143, bf16[1024,768]{1,0:T(8,128)(2,1)S(1)} %copy-done.3), kind=kLoop, calls=%fused_computation.10 | loop fusion | flops 3145728 | bytes 3145732 | tf_op jit(solution)/shard_map/concatenate | solution.py:846
  252.0 11.3 %collective-permute-done.31 = bf16[48,3072]{1,0:T(8,128)(2,1)S(1)} collective-permute-done((bf16[48,3072]{1,0:T(8,128)(2,1)S(1)}, bf16[48,3072]{1,0:T(8,128)(2,1)S(1)}, u32[]{:S(2)}, u32[]{:S(2)}) %collective-permute-start.31) | collective-permute-done | bytes 294944 | tf_op jit(solution)/shard_map/ppermute | solution.py:939
  263.2 3.0 %collective-permute-done.28 = bf16[4,48,1664]{2,1,0:T(8,128)(2,1)S(1)} collective-permute-done((bf16[4,48,1664]{2,1,0:T(8,128)(2,1)S(1)}, bf16[4,48,1664]{2,1,0:T(8,128)(2,1)S(1)}, u32[]{:S(2)}, u32[]{:S(2)}) %collective-permute-start.28) | collective-permute-done | bytes 639008 | tf_op jit(solution)/shard_map/ppermute | solution.py:939
  266.3 1.6 collective-permute-start.35
  268.1 1.7 collective-permute-start.34
  270.5 5.1 %collective-permute-done.35 = bf16[48,3072]{1,0:T(8,128)(2,1)S(1)} collective-permute-done((bf16[48,3072]{1,0:T(8,128)(2,1)S(1)}, bf16[48,3072]{1,0:T(8,128)(2,1)S(1)}, u32[]{:S(2)}, u32[]{:S(2)}) %collective-permute-start.35) | collective-permute-done | bytes 294944 | tf_op jit(solution)/shard_map/ppermute | solution.py:939
  277.2 1.5 collective-permute-done.34
  278.7 8.2 %collective-permute-done.33 = bf16[48,1664]{1,0:T(8,128)(2,1)S(1)} collective-permute-done((bf16[48,1664]{1,0:T(8,128)(2,1)S(1)}, bf16[48,1664]{1,0:T(8,128)(2,1)S(1)}, u32[]{:S(2)}, u32[]{:S(2)}) %collective-permute-start.33) | collective-permute-done | bytes 159776 | tf_op jit(solution)/shard_map/ppermute | solution.py:939
  (133 shorter events, 31.9 us)
Async XLA Ops:
  0.6 23.9 %copy-start.7 = (bf16[96,768]{1,0:T(8,128)(2,1)S(1)}, bf16[96,768]{1,0:T(8,128)(2,1)}, u32[]{:S(2)}) copy-start(bf16[96,768]{1,0:T(8,128)(2,1)} %param.28) | copy-start | bytes 442372
  5.2 1.6 collective-permute-start
  7.7 26.0 %copy-start.10 = (s32[1,5]{1,0:T(1,128)S(1)}, s32[1,5]{1,0:T(1,128)}, u32[]{:S(2)}) copy-start(s32[1,5]{1,0:T(1,128)} %param.17) | copy-start | bytes 64
  7.7 33.1 %copy-start.2 = (bf16[1024,768]{1,0:T(8,128)(2,1)S(1)}, bf16[1024,768]{1,0:T(8,128)(2,1)}, u32[]{:S(2)}) copy-start(bf16[1024,768]{1,0:T(8,128)(2,1)} %param.16) | copy-start | bytes 4718596
  7.7 7.1 %collective-permute-start.4 = (bf16[24,1536]{1,0:T(8,128)(2,1)}, bf16[24,1536]{1,0:T(8,128)(2,1)S(1)}, u32[]{:S(2)}, u32[]{:S(2)}) collective-permute-start(bf16[24,1536]{1,0:T(8,128)(2,1)} %get-tuple-element.144), channel_id=1, source_target_pairs={{0,1},{1,0},{2,3},{3,2},{4,5},{5,4},{6,7},{7,6},{8,9},{9,8},{10,11... | collective-permute-start | bytes 221192 | tf_op jit(solution)/shard_map/ppermute | solution.py:939
  8.1 9.8 %collective-permute-start.3 = (bf16[48,1664]{1,0:T(8,128)(2,1)S(1)}, bf16[48,1664]{1,0:T(8,128)(2,1)S(1)}, u32[]{:S(2)}, u32[]{:S(2)}) collective-permute-start(bf16[48,1664]{1,0:T(8,128)(2,1)S(1)} %pad_maximum_fusion.5), channel_id=1, source_target_pairs={{0,8},{1,9},{2,10},{3,11},{4,12},{5,13},{6,14},{7,15},{8,16},{9,17... | collective-permute-start | bytes 479240 | tf_op jit(solution)/shard_map/ppermute | solution.py:939
  10.9 13.6 %collective-permute-start.2 = (bf16[48,1664]{1,0:T(8,128)(2,1)S(1)}, bf16[48,1664]{1,0:T(8,128)(2,1)S(1)}, u32[]{:S(2)}, u32[]{:S(2)}) collective-permute-start(bf16[48,1664]{1,0:T(8,128)(2,1)S(1)} %pad_maximum_fusion.5), channel_id=1, source_target_pairs={{0,16},{1,17},{2,18},{3,19},{4,20},{5,21},{6,22},{7,23},{8,24},{9,... | collective-permute-start | bytes 479240 | tf_op jit(solution)/shard_map/ppermute | solution.py:939
  13.5 11.0 %collective-permute-start.1 = (bf16[48,1664]{1,0:T(8,128)(2,1)S(1)}, bf16[48,1664]{1,0:T(8,128)(2,1)S(1)}, u32[]{:S(2)}, u32[]{:S(2)}) collective-permute-start(bf16[48,1664]{1,0:T(8,128)(2,1)S(1)} %pad_maximum_fusion.5), channel_id=1, source_target_pairs={{0,24},{1,25},{2,26},{3,27},{4,28},{5,29},{6,30},{7,31},{8,0},{9,1... | collective-permute-start | bytes 479240 | tf_op jit(solution)/shard_map/ppermute | solution.py:939
  24.6 20.0 %collective-permute-start.10 = (bf16[48,3072]{1,0:T(8,128)(2,1)S(1)}, bf16[48,3072]{1,0:T(8,128)(2,1)S(1)}, u32[]{:S(2)}, u32[]{:S(2)}) collective-permute-start(bf16[48,3072]{1,0:T(8,128)(2,1)S(1)} %pad_maximum_fusion.2), channel_id=1, source_target_pairs={{0,8},{1,9},{2,10},{3,11},{4,12},{5,13},{6,14},{7,15},{8,16},{9,17... | collective-permute-start | bytes 884744 | tf_op jit(solution)/shard_map/ppermute | solution.py:939
  28.6 20.7 %collective-permute-start.9 = (bf16[48,3072]{1,0:T(8,128)(2,1)S(1)}, bf16[48,3072]{1,0:T(8,128)(2,1)}, u32[]{:S(2)}, u32[]{:S(2)}) collective-permute-start(bf16[48,3072]{1,0:T(8,128)(2,1)S(1)} %pad_maximum_fusion.2), channel_id=1, source_target_pairs={{0,16},{1,17},{2,18},{3,19},{4,20},{5,21},{6,22},{7,23},{8,24},{9,... | collective-permute-start | bytes 884744 | tf_op jit(solution)/shard_map/ppermute | solution.py:939
  30.2 25.1 %collective-permute-start.7 = (bf16[4,48,1664]{2,1,0:T(8,128)(2,1)S(1)}, bf16[4,48,1664]{2,1,0:T(8,128)(2,1)S(1)}, u32[]{:S(2)}, u32[]{:S(2)}) collective-permute-start(bf16[4,48,1664]{2,1,0:T(8,128)(2,1)S(1)} %pad_maximum_fusion.1), channel_id=1, source_target_pairs={{0,6},{1,7},{2,4},{3,5},{4,2},{5,3},{6,0},{7,1},{8,14},{9,15},{10,... | collective-permute-start | bytes 1916936 | tf_op jit(solution)/shard_map/ppermute | solution.py:939
  32.6 27.5 %collective-permute-start.6 = (bf16[4,48,1664]{2,1,0:T(8,128)(2,1)S(1)}, bf16[4,48,1664]{2,1,0:T(8,128)(2,1)}, u32[]{:S(2)}, u32[]{:S(2)}) collective-permute-start(bf16[4,48,1664]{2,1,0:T(8,128)(2,1)S(1)} %pad_maximum_fusion.1), channel_id=1, source_target_pairs={{0,4},{1,5},{2,6},{3,7},{4,0},{5,1},{6,2},{7,3},{8,12},{9,13},{10,... | collective-permute-start | bytes 1916936 | tf_op jit(solution)/shard_map/ppermute | solution.py:939
  33.1 27.1 %collective-permute-start.5 = (bf16[4,48,1664]{2,1,0:T(8,128)(2,1)S(1)}, bf16[4,48,1664]{2,1,0:T(8,128)(2,1)}, u32[]{:S(2)}, u32[]{:S(2)}) collective-permute-start(bf16[4,48,1664]{2,1,0:T(8,128)(2,1)S(1)} %pad_maximum_fusion.1), channel_id=1, source_target_pairs={{0,2},{1,3},{2,0},{3,1},{4,6},{5,7},{6,4},{7,5},{8,10},{9,11},{10,... | collective-permute-start | bytes 1916936 | tf_op jit(solution)/shard_map/ppermute | solution.py:939
  40.8 5.4 %copy-start.1 = (bf16[1024,768]{1,0:T(8,128)(2,1)S(1)}, bf16[1024,768]{1,0:T(8,128)(2,1)}, u32[]{:S(2)}) copy-start(bf16[1024,768]{1,0:T(8,128)(2,1)} %param.30) | copy-start | bytes 4718596
  44.6 10.7 %collective-permute-start.8 = (bf16[48,3072]{1,0:T(8,128)(2,1)S(1)}, bf16[48,3072]{1,0:T(8,128)(2,1)S(1)}, u32[]{:S(2)}, u32[]{:S(2)}) collective-permute-start(bf16[48,3072]{1,0:T(8,128)(2,1)S(1)} %pad_maximum_fusion.2), channel_id=1, source_target_pairs={{0,24},{1,25},{2,26},{3,27},{4,28},{5,29},{6,30},{7,31},{8,0},{9,1... | collective-permute-start | bytes 884744 | tf_op jit(solution)/shard_map/ppermute | solution.py:939
  46.2 21.5 %copy-start.11 = (s32[256]{0:T(256)}, s32[256]{0:T(256)S(1)}, u32[]{:S(2)}) copy-start(s32[256]{0:T(256)S(1)} %slice.296) | copy-start | bytes 3076
  65.0 9.6 %collective-permute-start.11 = (bf16[16,48,1664]{2,1,0:T(8,128)(2,1)S(1)}, bf16[16,48,1664]{2,1,0:T(8,128)(2,1)}, u32[]{:S(2)}, u32[]{:S(2)}) collective-permute-start(bf16[16,48,1664]{2,1,0:T(8,128)(2,1)S(1)} %constant_dynamic-update-slice_fusion.refs_0_), channel_id=1, source_target_pairs={{0,1},{1,0},{2,3},{3,2},{4,5},{5,4},{6,7},{7,6},{8,9},{9,8},{10,11... | collective-permute-start | bytes 7667720 | tf_op jit(solution)/shard_map/ppermute | solution.py:939
  65.0 47.7 %collective-permute-start.16 = (bf16[4,48,3072]{2,1,0:T(8,128)(2,1)}, bf16[4,48,3072]{2,1,0:T(8,128)(2,1)}, u32[]{:S(2)}, u32[]{:S(2)}) collective-permute-start(bf16[4,48,3072]{2,1,0:T(8,128)(2,1)} %pad_maximum_fusion.refs_0_), channel_id=1, source_target_pairs={{0,1},{1,0},{2,3},{3,2},{4,5},{5,4},{6,7},{7,6},{8,9},{9,8},{10,11... | collective-permute-start | bytes 3538952 | tf_op jit(solution)/shard_map/ppermute | solution.py:939
  65.5 28.3 %collective-permute-start.13 = (bf16[4,48,3072]{2,1,0:T(8,128)(2,1)}, bf16[4,48,3072]{2,1,0:T(8,128)(2,1)}, u32[]{:S(2)}, u32[]{:S(2)}) collective-permute-start(bf16[4,48,3072]{2,1,0:T(8,128)(2,1)} %pad_maximum_fusion.refs_0_), channel_id=1, source_target_pairs={{0,4},{1,5},{2,6},{3,7},{4,0},{5,1},{6,2},{7,3},{8,12},{9,13},{10,... | collective-permute-start | bytes 3538952 | tf_op jit(solution)/shard_map/ppermute | solution.py:939
  67.0 28.0 %collective-permute-start.12 = (bf16[4,48,3072]{2,1,0:T(8,128)(2,1)}, bf16[4,48,3072]{2,1,0:T(8,128)(2,1)}, u32[]{:S(2)}, u32[]{:S(2)}) collective-permute-start(bf16[4,48,3072]{2,1,0:T(8,128)(2,1)} %pad_maximum_fusion.refs_0_), channel_id=1, source_target_pairs={{0,2},{1,3},{2,0},{3,1},{4,6},{5,7},{6,4},{7,5},{8,10},{9,11},{10,... | collective-permute-start | bytes 3538952 | tf_op jit(solution)/shard_map/ppermute | solution.py:939
  94.9 18.5 %collective-permute-start.17 = (bf16[4,48,3072]{2,1,0:T(8,128)(2,1)}, bf16[4,48,3072]{2,1,0:T(8,128)(2,1)S(1)}, u32[]{:S(2)}, u32[]{:S(2)}) collective-permute-start(bf16[4,48,3072]{2,1,0:T(8,128)(2,1)} %collective-permute-done.12.refs_1_), channel_id=1, source_target_pairs={{0,1},{1,0},{2,3},{3,2},{4,5},{5,4},{6,7},{7,6},{8,9},{9,8},{10,11... | collective-permute-start | bytes 3538952 | tf_op jit(solution)/shard_map/ppermute | solution.py:939
  94.9 18.5 %collective-permute-start.18 = (bf16[4,48,3072]{2,1,0:T(8,128)(2,1)}, bf16[4,48,3072]{2,1,0:T(8,128)(2,1)S(1)}, u32[]{:S(2)}, u32[]{:S(2)}) collective-permute-start(bf16[4,48,3072]{2,1,0:T(8,128)(2,1)} %collective-permute-done.13.refs_2_), channel_id=1, source_target_pairs={{0,1},{1,0},{2,3},{3,2},{4,5},{5,4},{6,7},{7,6},{8,9},{9,8},{10,11... | collective-permute-start | bytes 3538952 | tf_op jit(solution)/shard_map/ppermute | solution.py:939
  97.7 15.3 %collective-permute-start.15 = (bf16[2,48,3072]{2,1,0:T(8,128)(2,1)S(1)}, bf16[2,48,3072]{2,1,0:T(8,128)(2,1)S(1)}, u32[]{:S(2)}, u32[]{:S(2)}) collective-permute-start(bf16[2,48,3072]{2,1,0:T(8,128)(2,1)S(1)} %slice.298), channel_id=1, source_target_pairs={{0,2},{1,3},{2,0},{3,1},{4,6},{5,7},{6,4},{7,5},{8,10},{9,11},{10,... | collective-permute-start | bytes 1769480 | tf_op jit(solution)/shard_map/ppermute | solution.py:939
  98.5 15.0 %collective-permute-start.14 = (bf16[2,48,3072]{2,1,0:T(8,128)(2,1)S(1)}, bf16[2,48,3072]{2,1,0:T(8,128)(2,1)S(1)}, u32[]{:S(2)}, u32[]{:S(2)}) collective-permute-start(bf16[2,48,3072]{2,1,0:T(8,128)(2,1)S(1)} %slice.297), channel_id=1, source_target_pairs={{0,4},{1,5},{2,6},{3,7},{4,0},{5,1},{6,2},{7,3},{8,12},{9,13},{10,... | collective-permute-start | bytes 1769480 | tf_op jit(solution)/shard_map/ppermute | solution.py:939
  104.8 7.3 %copy-start.8 = (f32[4,2,1024]{2,1,0:T(2,128)S(1)}, f32[4,2,1024]{2,1,0:T(2,128)}, u32[]{:S(2)}) copy-start(f32[4,2,1024]{2,1,0:T(2,128)} %get-tuple-element.188) | copy-start | bytes 98308
  104.8 7.3 %copy-start.9 = (f32[2,2,1024]{2,1,0:T(2,128)S(1)}, f32[2,2,1024]{2,1,0:T(2,128)}, u32[]{:S(2)}) copy-start(f32[2,2,1024]{2,1,0:T(2,128)} %get-tuple-element.189) | copy-start | bytes 49156
  113.5 2.1 collective-permute-start.19
  113.6 2.8 collective-permute-start.20
  164.7 14.4 %collective-permute-start.21 = (bf16[16,48,3072]{2,1,0:T(8,128)(2,1)}, bf16[16,48,3072]{2,1,0:T(8,128)(2,1)}, u32[]{:S(2)}, u32[]{:S(2)}) collective-permute-start(bf16[16,48,3072]{2,1,0:T(8,128)(2,1)} %get-tuple-element.202), channel_id=1, source_target_pairs={{0,1},{1,0},{2,3},{3,2},{4,5},{5,4},{6,7},{7,6},{8,9},{9,8},{10,11... | collective-permute-start | bytes 14155784 | tf_op jit(solution)/shard_map/ppermute | solution.py:939
  165.0 14.1 %slice-start = ((s8[4718592]{0:T(1024)(128)(4,1)}), s8[4194304]{0:T(1024)(128)(4,1)S(1)}, s32[]{:S(2)}) async-start(s8[4718592]{0:T(1024)(128)(4,1)} %bitcast.58), calls=%async_computation | async-start | bytes 8388608
  165.0 14.1 %slice-start.1 = ((s8[4718592]{0:T(1024)(128)(4,1)}), s8[524288]{0:T(1024)(128)(4,1)S(1)}, s32[]{:S(2)}) async-start(s8[4718592]{0:T(1024)(128)(4,1)} %bitcast.58), calls=%async_computation.1 | async-start | bytes 1048576
  183.1 33.1 %collective-permute-start.22 = (bf16[4,48,3072]{2,1,0:T(8,128)(2,1)}, bf16[4,48,3072]{2,1,0:T(8,128)(2,1)S(1)}, u32[]{:S(2)}, u32[]{:S(2)}) collective-permute-start(bf16[4,48,3072]{2,1,0:T(8,128)(2,1)} %get-tuple-element.221), channel_id=1, source_target_pairs={{0,2},{1,3},{2,0},{3,1},{4,6},{5,7},{6,4},{7,5},{8,10},{9,11},{10,... | collective-permute-start | bytes 3538952 | tf_op jit(solution)/shard_map/ppermute | solution.py:939
  184.4 31.8 %collective-permute-start.23 = (bf16[4,48,3072]{2,1,0:T(8,128)(2,1)}, bf16[4,48,3072]{2,1,0:T(8,128)(2,1)}, u32[]{:S(2)}, u32[]{:S(2)}) collective-permute-start(bf16[4,48,3072]{2,1,0:T(8,128)(2,1)} %get-tuple-element.222), channel_id=1, source_target_pairs={{0,4},{1,5},{2,6},{3,7},{4,0},{5,1},{6,2},{7,3},{8,12},{9,13},{10,... | collective-permute-start | bytes 3538952 | tf_op jit(solution)/shard_map/ppermute | solution.py:939
  216.2 5.3 %collective-permute-start.24 = (bf16[16,48,1664]{2,1,0:T(8,128)(2,1)}, bf16[16,48,1664]{2,1,0:T(8,128)(2,1)}, u32[]{:S(2)}, u32[]{:S(2)}) collective-permute-start(bf16[16,48,1664]{2,1,0:T(8,128)(2,1)} %get-tuple-element.227), channel_id=1, source_target_pairs={{0,1},{1,0},{2,3},{3,2},{4,5},{5,4},{6,7},{7,6},{8,9},{9,8},{10,11... | collective-permute-start | bytes 7667720 | tf_op jit(solution)/shard_map/ppermute | solution.py:939
  219.3 15.9 %collective-permute-start.26 = (bf16[2,48,3072]{2,1,0:T(8,128)(2,1)}, bf16[2,48,3072]{2,1,0:T(8,128)(2,1)S(1)}, u32[]{:S(2)}, u32[]{:S(2)}) collective-permute-start(bf16[2,48,3072]{2,1,0:T(8,128)(2,1)} %get-tuple-element.268), channel_id=1, source_target_pairs={{0,4},{1,5},{2,6},{3,7},{4,0},{5,1},{6,2},{7,3},{8,12},{9,13},{10,... | collective-permute-start | bytes 1769480 | tf_op jit(solution)/shard_map/ppermute | solution.py:939
  220.7 15.7 %collective-permute-start.25 = (bf16[2,48,3072]{2,1,0:T(8,128)(2,1)}, bf16[2,48,3072]{2,1,0:T(8,128)(2,1)S(1)}, u32[]{:S(2)}, u32[]{:S(2)}) collective-permute-start(bf16[2,48,3072]{2,1,0:T(8,128)(2,1)} %get-tuple-element.269), channel_id=1, source_target_pairs={{0,2},{1,3},{2,0},{3,1},{4,6},{5,7},{6,4},{7,5},{8,10},{9,11},{10,... | collective-permute-start | bytes 1769480 | tf_op jit(solution)/shard_map/ppermute | solution.py:939
  236.4 8.2 %copy-start.4 = (bf16[1024,768]{1,0:T(8,128)(2,1)S(1)}, bf16[1024,768]{1,0:T(8,128)(2,1)}, u32[]{:S(2)}) copy-start(bf16[1024,768]{1,0:T(8,128)(2,1)} %get-tuple-element.242) | copy-start | bytes 4718596
  236.4 26.9 %collective-permute-start.27 = (bf16[4,48,1664]{2,1,0:T(8,128)(2,1)S(1)}, bf16[4,48,1664]{2,1,0:T(8,128)(2,1)S(1)}, u32[]{:S(2)}, u32[]{:S(2)}) collective-permute-start(bf16[4,48,1664]{2,1,0:T(8,128)(2,1)S(1)} %get-tuple-element.234), channel_id=1, source_target_pairs={{0,2},{1,3},{2,0},{3,1},{4,6},{5,7},{6,4},{7,5},{8,10},{9,11},{10,... | collective-permute-start | bytes 1916936 | tf_op jit(solution)/shard_map/ppermute | solution.py:939
  237.2 29.1 %collective-permute-start.28 = (bf16[4,48,1664]{2,1,0:T(8,128)(2,1)S(1)}, bf16[4,48,1664]{2,1,0:T(8,128)(2,1)S(1)}, u32[]{:S(2)}, u32[]{:S(2)}) collective-permute-start(bf16[4,48,1664]{2,1,0:T(8,128)(2,1)S(1)} %get-tuple-element.235), channel_id=1, source_target_pairs={{0,4},{1,5},{2,6},{3,7},{4,0},{5,1},{6,2},{7,3},{8,12},{9,13},{10,... | collective-permute-start | bytes 1916936 | tf_op jit(solution)/shard_map/ppermute | solution.py:939
  238.5 27.8 %collective-permute-start.29 = (bf16[4,48,1664]{2,1,0:T(8,128)(2,1)S(1)}, bf16[4,48,1664]{2,1,0:T(8,128)(2,1)S(1)}, u32[]{:S(2)}, u32[]{:S(2)}) collective-permute-start(bf16[4,48,1664]{2,1,0:T(8,128)(2,1)S(1)} %get-tuple-element.236), channel_id=1, source_target_pairs={{0,6},{1,7},{2,4},{3,5},{4,2},{5,3},{6,0},{7,1},{8,14},{9,15},{10,... | collective-permute-start | bytes 1916936 | tf_op jit(solution)/shard_map/ppermute | solution.py:939
  242.4 20.9 %collective-permute-start.31 = (bf16[48,3072]{1,0:T(8,128)(2,1)S(1)}, bf16[48,3072]{1,0:T(8,128)(2,1)S(1)}, u32[]{:S(2)}, u32[]{:S(2)}) collective-permute-start(bf16[48,3072]{1,0:T(8,128)(2,1)S(1)} %get-tuple-element.263), channel_id=1, source_target_pairs={{0,16},{1,17},{2,18},{3,19},{4,20},{5,21},{6,22},{7,23},{8,24},{9,... | collective-permute-start | bytes 884744 | tf_op jit(solution)/shard_map/ppermute | solution.py:939
  244.2 19.0 %collective-permute-start.30 = (bf16[48,3072]{1,0:T(8,128)(2,1)S(1)}, bf16[48,3072]{1,0:T(8,128)(2,1)S(1)}, u32[]{:S(2)}, u32[]{:S(2)}) collective-permute-start(bf16[48,3072]{1,0:T(8,128)(2,1)S(1)} %get-tuple-element.267), channel_id=1, source_target_pairs={{0,8},{1,9},{2,10},{3,11},{4,12},{5,13},{6,14},{7,15},{8,16},{9,17... | collective-permute-start | bytes 884744 | tf_op jit(solution)/shard_map/ppermute | solution.py:939
  266.3 9.3 %collective-permute-start.35 = (bf16[48,3072]{1,0:T(8,128)(2,1)S(1)}, bf16[48,3072]{1,0:T(8,128)(2,1)S(1)}, u32[]{:S(2)}, u32[]{:S(2)}) collective-permute-start(bf16[48,3072]{1,0:T(8,128)(2,1)S(1)} %get-tuple-element.254), channel_id=1, source_target_pairs={{0,24},{1,25},{2,26},{3,27},{4,28},{5,29},{6,30},{7,31},{8,0},{9,1... | collective-permute-start | bytes 884744 | tf_op jit(solution)/shard_map/ppermute | solution.py:939
  268.1 10.6 %collective-permute-start.34 = (bf16[48,1664]{1,0:T(8,128)(2,1)S(1)}, bf16[48,1664]{1,0:T(8,128)(2,1)S(1)}, u32[]{:S(2)}, u32[]{:S(2)}) collective-permute-start(bf16[48,1664]{1,0:T(8,128)(2,1)S(1)} %get-tuple-element.276), channel_id=1, source_target_pairs={{0,24},{1,25},{2,26},{3,27},{4,28},{5,29},{6,30},{7,31},{8,0},{9,1... | collective-permute-start | bytes 479240 | tf_op jit(solution)/shard_map/ppermute | solution.py:939
  269.9 17.1 %collective-permute-start.33 = (bf16[48,1664]{1,0:T(8,128)(2,1)S(1)}, bf16[48,1664]{1,0:T(8,128)(2,1)S(1)}, u32[]{:S(2)}, u32[]{:S(2)}) collective-permute-start(bf16[48,1664]{1,0:T(8,128)(2,1)S(1)} %get-tuple-element.277), channel_id=1, source_target_pairs={{0,16},{1,17},{2,18},{3,19},{4,20},{5,21},{6,22},{7,23},{8,24},{9,... | collective-permute-start | bytes 479240 | tf_op jit(solution)/shard_map/ppermute | solution.py:939
  270.1 16.8 %collective-permute-start.32 = (bf16[48,1664]{1,0:T(8,128)(2,1)S(1)}, bf16[48,1664]{1,0:T(8,128)(2,1)S(1)}, u32[]{:S(2)}, u32[]{:S(2)}) collective-permute-start(bf16[48,1664]{1,0:T(8,128)(2,1)S(1)} %get-tuple-element.278), channel_id=1, source_target_pairs={{0,8},{1,9},{2,10},{3,11},{4,12},{5,13},{6,14},{7,15},{8,16},{9,17... | collective-permute-start | bytes 479240 | tf_op jit(solution)/shard_map/ppermute | solution.py:939
  275.8 1.4 collective-permute-start.36
  288.2 1.4 collective-permute-start.37
  (10 other events, 29.0 us)
